TPU v7x, 32 devices: a whole 2x2x4 slice. The times are simulated.
32 devices in a mesh: gx: 2 (over core), gy: 16 (over z, y, x).
Axes of the slice: x: 2, y: 2, z: 4, core: 2. Of those that a mesh axis runs over, the one named last changes fastest.
Arguments:
- hidden_in: bfloat16 [2, 8192, 768], P(None, ('gx', 'gy')), may hold values from -6 to 6
- rand_table: int32 [2, 128, 3], P(None, ('gx', 'gy')), may hold values from 0 to 63
- norm1_gain: bfloat16 [768], P(('gx', 'gy')), may hold values from 0.5 to 1.5
- norm1_bias: bfloat16 [768], P(('gx', 'gy')), may hold values from -3 to 3
- w_qkv: bfloat16 [768, 2304], P(('gx', 'gy')), may hold values from -0.21875 to 0.21875
- query_bias: bfloat16 [768], P(('gx', 'gy')), may hold values from -3 to 3
- value_bias: bfloat16 [768], P(('gx', 'gy')), may hold values from -0.59765625 to 0.59765625
- w_out: bfloat16 [768, 768], P(('gx', 'gy')), may hold values from -1.25 to 1.25
- out_bias: bfloat16 [768], P(('gx', 'gy')), may hold values from -2 to 2
- norm2_gain: bfloat16 [768], P(('gx', 'gy')), may hold values from 0.5 to 1.5
- norm2_bias: bfloat16 [768], P(('gx', 'gy')), may hold values from -2 to 2
- w_up: bfloat16 [768, 3072], P(('gx', 'gy')), may hold values from -0.21875 to 0.21875
- up_bias: bfloat16 [3072], P(('gx', 'gy')), may hold values from -3 to 3
- w_down: bfloat16 [3072, 768], P(('gx', 'gy')), may hold values from -0.109375 to 0.109375
- down_bias: bfloat16 [768], P(('gx', 'gy')), may hold values from -2 to 2
- cotangent: bfloat16 [2, 8192, 768], P(None, ('gx', 'gy')), may hold values from -6 to 6
Outputs:
- hidden_out: bfloat16 [2, 8192, 768], P(None, ('gx', 'gy'))
- grad_hidden: float32 [2, 8192, 768], P(None, ('gx', 'gy'))
- grad_norm1_gain: float32 [768], P(('gx', 'gy'))
- grad_norm1_bias: float32 [768], P(('gx', 'gy'))
- grad_w_qkv: float32 [768, 2304], P(('gx', 'gy'))
- grad_query_bias: float32 [768], P(('gx', 'gy'))
- grad_value_bias: float32 [768], P(('gx', 'gy'))
- grad_w_out: float32 [768, 768], P(('gx', 'gy'))
- grad_out_bias: float32 [768], P(('gx', 'gy'))
- grad_norm2_gain: float32 [768], P(('gx', 'gy'))
- grad_norm2_bias: float32 [768], P(('gx', 'gy'))
- grad_w_up: float32 [768, 3072], P(('gx', 'gy'))
- grad_up_bias: float32 [3072], P(('gx', 'gy'))
- grad_w_down: float32 [3072, 768], P(('gx', 'gy'))
- grad_down_bias: float32 [768], P(('gx', 'gy'))
All inputs are finite; a program needn't handle non-finite values.
Results may differ from a plain program's by a relative error of at most 0.012.
Values may be sent and summed in bfloat16 or wider, within the bound.
A program may use at most 320 MiB of HBM per device.

v0:
```python
import jax
import jax.numpy as jnp
from jax import lax
from jax.sharding import PartitionSpec as P

HEADS = 12
HEAD_DIM = 64
D = 768
BLOCK = 64


EPSILON = 1e-05


def norm_core(values_in, norm_gain):
    centre = values_in - jnp.mean(values_in, axis=-1, keepdims=True)
    spread = jnp.mean(centre * centre, axis=-1, keepdims=True)
    return centre * lax.rsqrt(spread + EPSILON) * norm_gain


def gelu_tanh(values_in):
    return jax.nn.gelu(values_in, approximate=True)


def block_allowed(query_ids, random_rows, key_ids, block_total):
    nearby = jnp.abs(query_ids[:, None] - key_ids[None, :]) <= 1
    global_keys = (key_ids == 0) | (key_ids == block_total - 1)
    global_rows = (query_ids == 0) | (query_ids == block_total - 1)
    picked = jnp.any(random_rows[:, :, :, None] == key_ids[None, None, None, :], axis=2)
    return (nearby | global_keys[None, :] | global_rows[:, None])[None] | picked


def key_window(array_in, first_key, key_span):
    return lax.dynamic_slice_in_dim(array_in, first_key, key_span, 1)


def slot_blocks(rand_local, block_ids, block_total):
    base = jnp.broadcast_to(block_ids[None, :], rand_local.shape[:2])
    columns = [base - 1, base, base + 1, jnp.zeros_like(base), jnp.full_like(base, block_total - 1)]
    columns = columns + [rand_local[..., number] for number in range(rand_local.shape[-1])]
    raw_ids = jnp.stack(columns, axis=-1)
    in_range = (raw_ids >= 0) & (raw_ids < block_total)
    valid_list = []
    for place in range(raw_ids.shape[-1]):
        keep_place = in_range[..., place]
        for earlier in range(place):
            keep_place = keep_place & ~(
                valid_list[earlier] & (raw_ids[..., earlier] == raw_ids[..., place])
            )
        valid_list.append(keep_place)
    return (jnp.clip(raw_ids, 0, block_total - 1), jnp.stack(valid_list, axis=-1))


def pick_blocks(window_heads, slot_ids):
    micro_count, seq_len, head_count, head_width = window_heads.shape
    blocks = window_heads.reshape(micro_count, seq_len // BLOCK, BLOCK, head_count, head_width)
    picked = jax.vmap(lambda source, wanted: source[wanted])(blocks, slot_ids)
    return picked.reshape(
        micro_count, slot_ids.shape[1], slot_ids.shape[2] * BLOCK, head_count, head_width
    )


def dense_scores(query_part, key_heads, key_span):
    score_scale = HEAD_DIM ** (-0.5)

    def scores_at(position):
        first_key = position * key_span
        key_part = key_window(key_heads, first_key, key_span)
        scores = (
            jnp.einsum("mqhd,mkhd->mhqk", query_part, key_part, preferred_element_type=jnp.float32)
            * score_scale
        )
        return (scores, jnp.ones((), dtype=bool), first_key)

    return scores_at


def attend_forward(query_heads, value_heads, scores_at, block_count, key_span):
    micro_count, row_count, head_count, head_width = query_heads.shape
    positions = jnp.arange(block_count, dtype=jnp.int32)

    def sweep_top(carry_now, position):
        row_top, row_sum = carry_now
        scores, allowed, first_key = scores_at(position)
        masked = jnp.where(allowed, scores, -1e30)
        new_top = jnp.maximum(row_top, jnp.max(masked, axis=-1))
        powered = jnp.where(allowed, jnp.exp(masked - new_top[..., None]), 0.0)
        return ((new_top, row_sum * jnp.exp(row_top - new_top) + jnp.sum(powered, axis=-1)), None)

    start_state = (
        jnp.full((micro_count, head_count, row_count), -1e30, jnp.float32),
        jnp.zeros((micro_count, head_count, row_count), jnp.float32),
    )
    (row_top, row_sum), _ = lax.scan(sweep_top, start_state, positions)
    log_total = row_top + jnp.log(row_sum)

    def sweep_mix(running, position):
        scores, allowed, first_key = scores_at(position)
        weights_now = jnp.where(allowed, jnp.exp(scores - log_total[..., None]), 0.0).astype(
            jnp.bfloat16
        )
        value_part = key_window(value_heads, first_key, key_span)
        return (
            running
            + jnp.einsum(
                "mhqk,mkhd->mqhd", weights_now, value_part, preferred_element_type=jnp.float32
            ),
            None,
        )

    mixed, _ = lax.scan(
        sweep_mix,
        jnp.zeros((micro_count, row_count, head_count, head_width), jnp.float32),
        positions,
    )
    return (mixed, log_total)


def attend_backward(
    query_heads, key_heads, value_heads, grad_heads, log_total, scores_at, block_count, key_span
):
    micro_count, row_count, head_count, head_width = query_heads.shape
    positions = jnp.arange(block_count, dtype=jnp.int32)

    def weights_at(position):
        scores, allowed, first_key = scores_at(position)
        return (jnp.where(allowed, jnp.exp(scores - log_total[..., None]), 0.0), first_key)

    def sweep_delta(running, position):
        weights_now, first_key = weights_at(position)
        value_part = key_window(value_heads, first_key, key_span)
        grad_weights = jnp.einsum(
            "mqhd,mkhd->mhqk", grad_heads, value_part, preferred_element_type=jnp.float32
        )
        return (running + jnp.sum(weights_now * grad_weights, axis=-1), None)

    row_delta, _ = lax.scan(
        sweep_delta, jnp.zeros((micro_count, head_count, row_count), jnp.float32), positions
    )

    def score_grads(position):
        weights_now, first_key = weights_at(position)
        key_part = key_window(key_heads, first_key, key_span)
        value_part = key_window(value_heads, first_key, key_span)
        grad_weights = jnp.einsum(
            "mqhd,mkhd->mhqk", grad_heads, value_part, preferred_element_type=jnp.float32
        )
        grad_scores = (weights_now * (grad_weights - row_delta[..., None])).astype(jnp.bfloat16)
        query_term = jnp.einsum(
            "mhqk,mkhd->mqhd", grad_scores, key_part, preferred_element_type=jnp.float32
        )
        return (weights_now, grad_scores, query_term, first_key)

    def sweep_query(grad_query, position):
        weights_now, grad_scores, query_term, first_key = score_grads(position)
        return (grad_query + query_term, None)

    grad_query, _ = lax.scan(sweep_query, jnp.zeros(query_heads.shape, jnp.float32), positions)
    return (grad_query, None, None, row_delta)


def attention_forward(
    query_blocks, keys_all, values_all, slot_ids, key_mask, row_glob, select, key_span, span_count
):
    micro_count, local_blocks, block_rows, head_count, head_width = query_blocks.shape
    wide_shape = (micro_count, keys_all.shape[1], head_count, head_width)
    key_heads = keys_all.reshape(wide_shape)
    value_heads = values_all.reshape(wide_shape)
    key_pick = pick_blocks(key_heads, slot_ids)
    value_pick = pick_blocks(value_heads, slot_ids)
    score_scale = HEAD_DIM ** (-0.5)
    scores = (
        jnp.einsum("mbqhd,mbkhd->mbhqk", query_blocks, key_pick, preferred_element_type=jnp.float32)
        * score_scale
    )
    masked = jnp.where(key_mask, scores, -1e30)
    row_top = jnp.max(masked, axis=-1)
    row_sum = jnp.sum(jnp.where(key_mask, jnp.exp(masked - row_top[..., None]), 0.0), axis=-1)
    lse_sparse = row_top + jnp.log(row_sum)
    weights_now = jnp.where(key_mask, jnp.exp(scores - lse_sparse[..., None]), 0.0).astype(
        jnp.bfloat16
    )
    mixed_sparse = jnp.einsum(
        "mbhqk,mbkhd->mbqhd", weights_now, value_pick, preferred_element_type=jnp.float32
    )
    query_pick = lax.dynamic_index_in_dim(query_blocks, select, 1, keepdims=False)
    mixed_dense, lse_dense = attend_forward(
        query_pick, value_heads, dense_scores(query_pick, key_heads, key_span), span_count, key_span
    )
    glob_rows = row_glob[None, :, None, None, None]
    mixed = jnp.where(
        glob_rows,
        lax.dynamic_update_index_in_dim(mixed_sparse, mixed_dense, select, 1),
        mixed_sparse,
    )
    glob_stats = row_glob[None, :, None, None]
    log_rows = jnp.where(
        glob_stats, lax.dynamic_update_index_in_dim(lse_sparse, lse_dense, select, 1), lse_sparse
    )
    return (mixed, log_rows)


def attention_backward(
    query_blocks,
    keys_back,
    values_back,
    grad_blocks,
    log_rows,
    slot_ids,
    key_mask,
    row_glob,
    select,
    key_span,
    span_count,
):
    micro_count, local_blocks, block_rows, head_count, head_width = query_blocks.shape
    seq_len = keys_back.shape[1]
    wide_shape = (micro_count, seq_len, head_count, head_width)
    key_heads = keys_back.reshape(wide_shape)
    value_heads = values_back.reshape(wide_shape)
    key_pick = pick_blocks(key_heads, slot_ids)
    value_pick = pick_blocks(value_heads, slot_ids)
    score_scale = HEAD_DIM ** (-0.5)
    glob_rows = row_glob[None, :, None, None, None]
    grad_sparse = jnp.where(glob_rows, jnp.zeros_like(grad_blocks), grad_blocks)
    scores = (
        jnp.einsum("mbqhd,mbkhd->mbhqk", query_blocks, key_pick, preferred_element_type=jnp.float32)
        * score_scale
    )
    weights_now = jnp.where(key_mask, jnp.exp(scores - log_rows[..., None]), 0.0)
    grad_weights = jnp.einsum(
        "mbqhd,mbkhd->mbhqk", grad_sparse, value_pick, preferred_element_type=jnp.float32
    )
    delta_sparse = jnp.sum(weights_now * grad_weights, axis=-1)
    grad_scores = (weights_now * (grad_weights - delta_sparse[..., None])).astype(jnp.bfloat16)
    grad_query = jnp.einsum(
        "mbhqk,mbkhd->mbqhd", grad_scores, key_pick, preferred_element_type=jnp.float32
    )
    select_glob = jnp.any(row_glob & (jnp.arange(local_blocks, dtype=jnp.int32) == select))
    query_pick = lax.dynamic_index_in_dim(query_blocks, select, 1, keepdims=False)
    grad_pick = lax.dynamic_index_in_dim(grad_blocks, select, 1, keepdims=False)
    grad_pick = jnp.where(select_glob, grad_pick, jnp.zeros_like(grad_pick))
    log_pick = lax.dynamic_index_in_dim(log_rows, select, 1, keepdims=False)
    dense_query, dense_keys, dense_values, delta_dense = attend_backward(
        query_pick,
        key_heads,
        value_heads,
        grad_pick,
        log_pick,
        dense_scores(query_pick, key_heads, key_span),
        span_count,
        key_span,
    )
    query_here = lax.dynamic_index_in_dim(grad_query, select, 1, keepdims=False)
    grad_query = lax.dynamic_update_index_in_dim(grad_query, query_here + dense_query, select, 1)
    glob_stats = row_glob[None, :, None, None]
    delta_rows = jnp.where(
        glob_stats,
        lax.dynamic_update_index_in_dim(delta_sparse, delta_dense, select, 1),
        delta_sparse,
    )
    return (grad_query, None, None, delta_rows)


def key_side(query_all, grad_all, log_all, delta_all, table_all, key_rows, value_rows, first_row):
    micro_count, seq_len, width = query_all.shape
    row_count = key_rows.shape[1]
    block_total = seq_len // BLOCK
    query_span = min(512, seq_len)
    span_blocks = query_span // BLOCK
    score_scale = HEAD_DIM ** (-0.5)
    own_keys = key_rows.reshape(micro_count, row_count, HEADS, HEAD_DIM)
    own_values = value_rows.reshape(micro_count, row_count, HEADS, HEAD_DIM)
    key_ids = (first_row + jnp.arange(row_count, dtype=jnp.int32)) // BLOCK

    def sweep(carry_now, position):
        grad_keys, grad_values = carry_now
        first_query = position * query_span
        first_block = position * span_blocks
        query_part = lax.dynamic_slice_in_dim(query_all, first_query, query_span, 1).reshape(
            micro_count, query_span, HEADS, HEAD_DIM
        )
        grad_part = lax.dynamic_slice_in_dim(grad_all, first_query, query_span, 1).reshape(
            micro_count, query_span, HEADS, HEAD_DIM
        )
        log_part = jnp.moveaxis(
            lax.dynamic_slice_in_dim(log_all, first_block, span_blocks, 1), 1, 2
        ).reshape(micro_count, HEADS, query_span)
        delta_part = jnp.moveaxis(
            lax.dynamic_slice_in_dim(delta_all, first_block, span_blocks, 1), 1, 2
        ).reshape(micro_count, HEADS, query_span)
        table_part = jnp.repeat(
            lax.dynamic_slice_in_dim(table_all, first_block, span_blocks, 1), BLOCK, axis=1
        )
        query_ids = (first_query + jnp.arange(query_span, dtype=jnp.int32)) // BLOCK
        allowed = block_allowed(query_ids, table_part, key_ids, block_total)[:, None]
        scores = (
            jnp.einsum("mqhd,mkhd->mhqk", query_part, own_keys, preferred_element_type=jnp.float32)
            * score_scale
        )
        weights_now = jnp.where(allowed, jnp.exp(scores - log_part[..., None]), 0.0)
        grad_weights = jnp.einsum(
            "mqhd,mkhd->mhqk", grad_part, own_values, preferred_element_type=jnp.float32
        )
        grad_scores = (weights_now * (grad_weights - delta_part[..., None])).astype(jnp.bfloat16)
        grad_keys = grad_keys + jnp.einsum(
            "mhqk,mqhd->mkhd", grad_scores, query_part, preferred_element_type=jnp.float32
        )
        grad_values = grad_values + jnp.einsum(
            "mhqk,mqhd->mkhd",
            weights_now.astype(jnp.bfloat16),
            grad_part,
            preferred_element_type=jnp.float32,
        )
        return ((grad_keys, grad_values), None)

    start_state = (jnp.zeros(own_keys.shape, jnp.float32), jnp.zeros(own_keys.shape, jnp.float32))
    (grad_keys, grad_values), _ = lax.scan(
        sweep, start_state, jnp.arange(seq_len // query_span, dtype=jnp.int32)
    )
    return (
        (grad_keys * score_scale).reshape(micro_count, row_count, width),
        grad_values.reshape(micro_count, row_count, width),
    )


def shards(
    hidden_in,
    rand_table,
    norm1_gain,
    norm1_bias,
    w_qkv,
    query_bias,
    value_bias,
    w_out,
    out_bias,
    norm2_gain,
    norm2_bias,
    w_up,
    up_bias,
    w_down,
    down_bias,
    cotangent,
):
    micro_count, row_count, model_width = hidden_in.shape
    group_size = lax.axis_size("gy")
    group_place = lax.axis_index("gy")
    seq_len = row_count * group_size
    block_total = seq_len // BLOCK
    local_blocks = row_count // BLOCK
    key_span = min(512, seq_len)
    span_count = seq_len // key_span
    score_scale = HEAD_DIM ** (-0.5)
    block_ids = group_place * local_blocks + jnp.arange(local_blocks, dtype=jnp.int32)
    row_glob = (block_ids == 0) | (block_ids == block_total - 1)
    select = jnp.where(group_place == 0, 0, local_blocks - 1).astype(jnp.int32)
    slot_ids, slot_valid = slot_blocks(rand_table, block_ids, block_total)
    key_mask = jnp.repeat(slot_valid, BLOCK, axis=-1)[:, :, None, None, :]
    block_shape = (micro_count, local_blocks, BLOCK, HEADS, HEAD_DIM)
    (
        gain_one,
        shift_one,
        qkv_full,
        query_shift,
        value_shift,
        out_full,
        out_shift,
        gain_two,
        shift_two,
        up_full,
        up_shift,
        down_full,
        down_shift,
    ) = (
        lax.all_gather(norm1_gain, ("gx", "gy"), axis=0, tiled=True),
        lax.all_gather(norm1_bias, ("gx", "gy"), axis=0, tiled=True),
        lax.all_gather(w_qkv, ("gx", "gy"), axis=0, tiled=True),
        lax.all_gather(query_bias, ("gx", "gy"), axis=0, tiled=True),
        lax.all_gather(value_bias, ("gx", "gy"), axis=0, tiled=True),
        lax.all_gather(w_out, ("gx", "gy"), axis=0, tiled=True),
        lax.all_gather(out_bias, ("gx", "gy"), axis=0, tiled=True),
        lax.all_gather(norm2_gain, ("gx", "gy"), axis=0, tiled=True),
        lax.all_gather(norm2_bias, ("gx", "gy"), axis=0, tiled=True),
        lax.all_gather(w_up, ("gx", "gy"), axis=0, tiled=True),
        lax.all_gather(up_bias, ("gx", "gy"), axis=0, tiled=True),
        lax.all_gather(w_down, ("gx", "gy"), axis=0, tiled=True),
        lax.all_gather(down_bias, ("gx", "gy"), axis=0, tiled=True),
    )
    tokens_in = hidden_in.astype(jnp.float32)
    normed = (
        norm_core(tokens_in, gain_one.astype(jnp.float32)) + shift_one.astype(jnp.float32)
    ).astype(jnp.bfloat16)
    packed = jnp.einsum("mtd,de->mte", normed, qkv_full, preferred_element_type=jnp.float32)
    query_rows = (packed[..., :D] + query_shift.astype(jnp.float32)).astype(jnp.bfloat16)
    key_rows = packed[..., D : 2 * D].astype(jnp.bfloat16)
    value_rows = (packed[..., 2 * D :] + value_shift.astype(jnp.float32)).astype(jnp.bfloat16)
    keys_all, values_all = (
        lax.all_gather(key_rows, "gy", axis=1, tiled=True),
        lax.all_gather(value_rows, "gy", axis=1, tiled=True),
    )
    query_blocks = query_rows.reshape(block_shape)
    mixed, log_rows = attention_forward(
        query_blocks,
        keys_all,
        values_all,
        slot_ids,
        key_mask,
        row_glob,
        select,
        key_span,
        span_count,
    )
    mixed_rows = mixed.reshape(micro_count, row_count, D).astype(jnp.bfloat16)
    residual = tokens_in + (
        jnp.einsum("mtd,de->mte", mixed_rows, out_full, preferred_element_type=jnp.float32)
        + out_shift.astype(jnp.float32)
    )
    second = (
        norm_core(residual, gain_two.astype(jnp.float32)) + shift_two.astype(jnp.float32)
    ).astype(jnp.bfloat16)
    upper = jnp.einsum(
        "mtd,df->mtf", second, up_full, preferred_element_type=jnp.float32
    ) + up_shift.astype(jnp.float32)
    active = gelu_tanh(upper).astype(jnp.bfloat16)
    hidden_out = (
        residual
        + (
            jnp.einsum("mtf,fd->mtd", active, down_full, preferred_element_type=jnp.float32)
            + down_shift.astype(jnp.float32)
        )
    ).astype(jnp.bfloat16)
    gain_one_back, qkv_back, out_back, gain_two_back, up_back, down_back = (
        lax.all_gather(norm1_gain, ("gx", "gy"), axis=0, tiled=True),
        lax.all_gather(w_qkv, ("gx", "gy"), axis=0, tiled=True),
        lax.all_gather(w_out, ("gx", "gy"), axis=0, tiled=True),
        lax.all_gather(norm2_gain, ("gx", "gy"), axis=0, tiled=True),
        lax.all_gather(w_up, ("gx", "gy"), axis=0, tiled=True),
        lax.all_gather(w_down, ("gx", "gy"), axis=0, tiled=True),
    )
    keys_back, values_back = (
        lax.all_gather(key_rows, "gy", axis=1, tiled=True),
        lax.all_gather(value_rows, "gy", axis=1, tiled=True),
    )
    grad_w_down = jnp.einsum("mtf,mtd->fd", active, cotangent, preferred_element_type=jnp.float32)
    grad_down_bias = jnp.sum(cotangent.astype(jnp.float32), axis=(0, 1))
    grad_active = jnp.einsum(
        "mtd,fd->mtf", cotangent, down_back, preferred_element_type=jnp.float32
    )
    _, gelu_pull = jax.vjp(gelu_tanh, upper)
    grad_upper = gelu_pull(grad_active)[0].astype(jnp.bfloat16)
    grad_w_up = jnp.einsum("mtd,mtf->df", second, grad_upper, preferred_element_type=jnp.float32)
    grad_up_bias = jnp.sum(grad_upper.astype(jnp.float32), axis=(0, 1))
    grad_second = jnp.einsum("mtf,df->mtd", grad_upper, up_back, preferred_element_type=jnp.float32)
    _, norm_two_pull = jax.vjp(norm_core, residual, gain_two_back.astype(jnp.float32))
    grad_resid_norm, grad_norm2_gain = norm_two_pull(grad_second)
    grad_norm2_bias = jnp.sum(grad_second, axis=(0, 1))
    grad_resid = cotangent.astype(jnp.float32) + grad_resid_norm
    grad_branch = grad_resid.astype(jnp.bfloat16)
    grad_w_out = jnp.einsum(
        "mtd,mte->de", mixed_rows, grad_branch, preferred_element_type=jnp.float32
    )
    grad_out_bias = jnp.sum(grad_branch.astype(jnp.float32), axis=(0, 1))
    grad_mixed = jnp.einsum(
        "mte,de->mtd", grad_branch, out_back, preferred_element_type=jnp.float32
    ).astype(jnp.bfloat16)
    grad_query, unused_keys, unused_values, delta_rows = attention_backward(
        query_blocks,
        keys_back,
        values_back,
        grad_mixed.reshape(block_shape),
        log_rows,
        slot_ids,
        key_mask,
        row_glob,
        select,
        key_span,
        span_count,
    )
    query_all, grad_all = (
        lax.all_gather(query_rows, "gy", axis=1, tiled=True),
        lax.all_gather(grad_mixed, "gy", axis=1, tiled=True),
    )
    log_all, delta_all = (
        lax.all_gather(log_rows, "gy", axis=1, tiled=True),
        lax.all_gather(delta_rows, "gy", axis=1, tiled=True),
    )
    table_all = lax.all_gather(rand_table, "gy", axis=1, tiled=True)
    key_share, value_share = key_side(
        query_all,
        grad_all,
        log_all,
        delta_all,
        table_all,
        key_rows,
        value_rows,
        group_place * row_count,
    )
    grad_query_rows = (
        (grad_query * score_scale).reshape(micro_count, row_count, D).astype(jnp.bfloat16)
    )
    grad_key_rows = key_share.astype(jnp.bfloat16)
    grad_value_rows = value_share.astype(jnp.bfloat16)
    grad_packed = jnp.concatenate([grad_query_rows, grad_key_rows, grad_value_rows], axis=-1)
    grad_w_qkv = jnp.einsum("mtd,mte->de", normed, grad_packed, preferred_element_type=jnp.float32)
    grad_query_bias = jnp.sum(grad_query_rows.astype(jnp.float32), axis=(0, 1))
    grad_value_bias = jnp.sum(grad_value_rows.astype(jnp.float32), axis=(0, 1))
    grad_normed = jnp.einsum(
        "mte,de->mtd", grad_packed, qkv_back, preferred_element_type=jnp.float32
    )
    _, norm_one_pull = jax.vjp(norm_core, tokens_in, gain_one_back.astype(jnp.float32))
    grad_input_norm, grad_norm1_gain = norm_one_pull(grad_normed)
    grad_norm1_bias = jnp.sum(grad_normed, axis=(0, 1))
    grad_hidden = grad_resid + grad_input_norm
    (
        owned_n1g,
        owned_n1b,
        owned_qkv,
        owned_qb,
        owned_vb,
        owned_out,
        owned_ob,
        owned_n2g,
        owned_n2b,
        owned_up,
        owned_ub,
        owned_down,
        owned_db,
    ) = (
        lax.psum_scatter(grad_norm1_gain, ("gx", "gy"), scatter_dimension=0, tiled=True),
        lax.psum_scatter(grad_norm1_bias, ("gx", "gy"), scatter_dimension=0, tiled=True),
        lax.psum_scatter(grad_w_qkv, ("gx", "gy"), scatter_dimension=0, tiled=True),
        lax.psum_scatter(grad_query_bias, ("gx", "gy"), scatter_dimension=0, tiled=True),
        lax.psum_scatter(grad_value_bias, ("gx", "gy"), scatter_dimension=0, tiled=True),
        lax.psum_scatter(grad_w_out, ("gx", "gy"), scatter_dimension=0, tiled=True),
        lax.psum_scatter(grad_out_bias, ("gx", "gy"), scatter_dimension=0, tiled=True),
        lax.psum_scatter(grad_norm2_gain, ("gx", "gy"), scatter_dimension=0, tiled=True),
        lax.psum_scatter(grad_norm2_bias, ("gx", "gy"), scatter_dimension=0, tiled=True),
        lax.psum_scatter(grad_w_up, ("gx", "gy"), scatter_dimension=0, tiled=True),
        lax.psum_scatter(grad_up_bias, ("gx", "gy"), scatter_dimension=0, tiled=True),
        lax.psum_scatter(grad_w_down, ("gx", "gy"), scatter_dimension=0, tiled=True),
        lax.psum_scatter(grad_down_bias, ("gx", "gy"), scatter_dimension=0, tiled=True),
    )
    return (
        hidden_out,
        grad_hidden,
        owned_n1g,
        owned_n1b,
        owned_qkv,
        owned_qb,
        owned_vb,
        owned_out,
        owned_ob,
        owned_n2g,
        owned_n2b,
        owned_up,
        owned_ub,
        owned_down,
        owned_db,
    )


def solution(mesh):
    placed = (
        P(None, ("gx", "gy"), None),
        P(None, ("gx", "gy"), None),
        P(("gx", "gy")),
        P(("gx", "gy")),
        P(("gx", "gy"), None),
        P(("gx", "gy")),
        P(("gx", "gy")),
        P(("gx", "gy"), None),
        P(("gx", "gy")),
        P(("gx", "gy")),
        P(("gx", "gy")),
        P(("gx", "gy"), None),
        P(("gx", "gy")),
        P(("gx", "gy"), None),
        P(("gx", "gy")),
        P(None, ("gx", "gy"), None),
    )
    return jax.shard_map(
        shards,
        mesh=mesh,
        in_specs=placed,
        out_specs=(
            P(None, ("gx", "gy"), None),
            P(None, ("gx", "gy"), None),
            P(("gx", "gy")),
            P(("gx", "gy")),
            P(("gx", "gy"), None),
            P(("gx", "gy")),
            P(("gx", "gy")),
            P(("gx", "gy"), None),
            P(("gx", "gy")),
            P(("gx", "gy")),
            P(("gx", "gy")),
            P(("gx", "gy"), None),
            P(("gx", "gy")),
            P(("gx", "gy"), None),
            P(("gx", "gy")),
        ),
        check_vma=False,
    )
```

profile of v0, /device:TPU:0, one launch (start us, length us, event | category | flops | bytes accessed | tf_op | source)
XLA Modules:
  0.0 1470.6 jit_solution(10344701734852012178)
XLA Ops:
  15.5 42.8 %all-reduce.19 = (bf16[768]{0:T(1024)(128)(2,1)S(1)}, bf16[768]{0:T(1024)(128)(2,1)S(1)}, bf16[768]{0:T(1024)(128)(2,1)S(1)}, bf16[768]{0:T(1024)(128)(2,1)S(1)}...) all-reduce(bf16[768]{0:T(1024)(128)(2,1)S(1)} %dynamic-update-slice, ...), channel_id=1, replica_groups=mesh['gx'=2,'gy'=16] {'gx','gy'}, use_global_device_ids=true, to_apply=%add.1 | all-reduce | flops 9216 | bytes 36864
  61.8 12.1 all-gather.9.cloned.1.call-done
  96.0 136.4 %all-gather.13.cloned.1.call-done = bf16[2,4096,768]{2,1,0:T(8,128)(2,1)} async-done(((bf16[2,256,768]{2,1,0:T(8,128)(2,1)}), bf16[2,4096,768]{2,1,0:T(8,128)(2,1)}) %all-gather.13.cloned.1.call-update) | async-done | bytes 12582928 | tf_op jit(solution)/shard_map/all_gather | solution.py:398
  232.4 38.2 %reshape.676 = bf16[2,64,64,12,64]{4,3,2,1,0:T(8,128)(2,1)} reshape(bf16[2,4096,768]{2,1,0:T(8,128)(2,1)} %all-gather.13.cloned.1.call-done) | data formatting | bytes 25165824 | tf_op jit(solution)/shard_map/reshape;reshape | solution.py:56
  270.7 20.0 %copy.319 = bf16[2,64,64,12,64]{4,2,3,1,0:T(8,128)(2,1)} copy(bf16[2,64,64,12,64]{4,3,2,1,0:T(8,128)(2,1)} %reshape.676) | data formatting | bytes 25165824 | tf_op jit(solution)/shard_map/reshape;reshape | solution.py:56
  290.7 15.9 %gather_fusion.1 = bf16[64,64,12,64]{3,1,2,0:T(8,128)(2,1)} fusion(bf16[2,64,64,12,64]{4,2,3,1,0:T(8,128)(2,1)} %copy.319, s32[64]{0:T(128)S(1)} %reshape.633), kind=kCustom, calls=%fused_computation.1 | custom fusion | bytes 12583424 | tf_op jit(solution)/shard_map/vmap()/gather | solution.py:57
  306.6 18.0 %copy.320 = bf16[64,64,12,64]{1,0,3,2:T(8,128)(2,1)} copy(bf16[64,64,12,64]{3,1,2,0:T(8,128)(2,1)} %gather_fusion.1) | data formatting | bytes 12582912 | tf_op jit(solution)/shard_map/vmap()/gather | solution.py:57
  324.6 17.9 %reshape.627 = bf16[2,4,512,12,64]{2,1,0,4,3:T(4,128)(2,1)} reshape(bf16[64,64,12,64]{1,0,3,2:T(8,128)(2,1)} %copy.320) | data formatting | bytes 12582912 | tf_op jit(solution)/shard_map/reshape | solution.py:58
  342.5 42.9 %all-gather.11.cloned.1.call-done = bf16[2,4096,768]{2,1,0:T(8,128)(2,1)} async-done(((bf16[2,256,768]{2,1,0:T(8,128)(2,1)}), bf16[2,4096,768]{2,1,0:T(8,128)(2,1)}) %all-gather.11.cloned.1.call-update) | async-done | bytes 12582928 | tf_op jit(solution)/shard_map/all_gather | solution.py:399
  385.3 38.2 %reshape.675 = bf16[2,64,64,12,64]{4,3,2,1,0:T(8,128)(2,1)} reshape(bf16[2,4096,768]{2,1,0:T(8,128)(2,1)} %all-gather.11.cloned.1.call-done) | data formatting | bytes 25165824 | tf_op jit(solution)/shard_map/reshape;reshape | solution.py:56
  423.5 20.3 %copy.314 = bf16[2,64,64,12,64]{4,2,3,1,0:T(8,128)(2,1)} copy(bf16[2,64,64,12,64]{4,3,2,1,0:T(8,128)(2,1)} %reshape.675) | data formatting | bytes 25165824 | tf_op jit(solution)/shard_map/reshape;reshape | solution.py:56
  443.8 15.9 %gather_fusion = bf16[64,64,12,64]{3,1,2,0:T(8,128)(2,1)} fusion(bf16[2,64,64,12,64]{4,2,3,1,0:T(8,128)(2,1)} %copy.314, s32[64]{0:T(128)S(1)} %reshape.633), kind=kCustom, calls=%fused_computation | custom fusion | bytes 12583424 | tf_op jit(solution)/shard_map/vmap()/gather | solution.py:57
  459.7 17.7 %copy.315 = bf16[64,64,12,64]{1,0,3,2:T(8,128)(2,1)} copy(bf16[64,64,12,64]{3,1,2,0:T(8,128)(2,1)} %gather_fusion) | data formatting | bytes 12582912 | tf_op jit(solution)/shard_map/vmap()/gather | solution.py:57
  477.4 18.0 %reshape.625 = bf16[2,4,512,12,64]{2,1,0,4,3:T(4,128)(2,1)} reshape(bf16[64,64,12,64]{1,0,3,2:T(8,128)(2,1)} %copy.315) | data formatting | bytes 12582912 | tf_op jit(solution)/shard_map/reshape | solution.py:58
  495.3 8.0 select_reduce_fusion.1
  519.0 16.7 %copy.325 = bf16[2,4096,768]{1,2,0:T(8,128)(2,1)} copy(bf16[2,4096,768]{2,1,0:T(8,128)(2,1)} %all-gather.13.cloned.1.call-done) | data formatting | bytes 25165824 | tf_op jit(solution)/shard_map/all_gather | solution.py:398
  535.7 15.7 %copy.324 = bf16[2,4096,768]{1,2,0:T(8,128)(2,1)} copy(bf16[2,4096,768]{2,1,0:T(8,128)(2,1)} %all-gather.11.cloned.1.call-done) | data formatting | bytes 25165824 | tf_op jit(solution)/shard_map/all_gather | solution.py:399
  552.0 54.6 %while.61 = (s32[]{:T(128)}, f32[2,12,64]{2,1,0:T(8,128)S(1)}, f32[2,12,64]{2,1,0:T(8,128)}, s32[8]{0:T(128)}, bf16[2,4096,12,64]{1,3,2,0:T(8,128)(2,1)}, /*inde...) while((s32[]{:T(128)}, f32[2,12,64]{2,1,0:T(8,128)S(1)}, ...), condition=%wide.region_7.8_spmd.clone, body=%wide.region_4.7_spmd.clone.sunk | while | flops 104603144 | bytes 8190182 | solution.py:94
  608.7 42.9 %while.62 = (s32[]{:T(128)}, f32[2,64,12,64]{1,3,2,0:T(8,128)}, s32[8]{0:T(128)S(1)}, bf16[2,4096,12,64]{1,3,2,0:T(8,128)(2,1)}, bf16[2,4096,12,64]{1,3,2,0:T(8,...) while((s32[]{:T(128)}, f32[2,64,12,64]{1,3,2,0:T(8,128)}, ...), condition=%wide.region_9.10_spmd.clone, body=%wide.region_8.9_spmd.clone.sunk | while | flops 203882496 | bytes 4529840 | solution.py:111
  669.5 9.8 convert_reduce_fusion
  691.2 41.1 %all_gather.84 = s32[2,64,3]{2,0,1:T(2,128)} all-gather(s32[2,4,3]{2,0,1:T(2,128)S(1)} %copy.342), channel_id=1, replica_groups=mesh['gx'=2,'gy'=16] {'gy'}, dimensions={1}, use_global_device_ids=true | all-gather | bytes 1632 | tf_op jit(solution)/shard_map/all_gather | solution.py:487
  755.4 56.2 %while.63 = (s32[]{:T(128)}, f32[2,12,64]{2,1,0:T(8,128)}, s32[8]{0:T(128)S(1)}, bf16[2,4096,12,64]{1,3,2,0:T(8,128)(2,1)}, bf16[2,64,12,64]{3,1,2,0:T(8,128)(2,...) while((s32[]{:T(128)}, f32[2,12,64]{2,1,0:T(8,128)}, ...), condition=%wide.region_18.19_spmd.clone, body=%wide.region_16.18_spmd.clone.sunk | while | flops 204473856 | bytes 10057921 | solution.py:137
  812.8 67.2 %while.64 = (s32[]{:T(128)}, f32[2,64,12,64]{1,3,2,0:T(8,128)}, s32[8]{0:T(128)}, bf16[2,4096,12,64]{1,3,2,0:T(8,128)(2,1)}, bf16[2,64,12,64]{3,1,2,0:T(8,128)(2...) while((s32[]{:T(128)}, f32[2,64,12,64]{1,3,2,0:T(8,128)}, ...), condition=%wide.region_20.21_spmd.clone, body=%wide.region_19.20_spmd.clone.sunk | while | flops 306118656 | bytes 12803780 | solution.py:158
  883.6 13.8 multiply_reduce_fusion.1
  897.4 13.7 fusion.79
  916.5 44.9 %all_gather.87 = f32[2,64,12,64]{3,0,2,1:T(2,128)} all-gather(f32[2,4,12,64]{3,0,2,1:T(2,128)S(1)} %copy.348), channel_id=1, replica_groups=mesh['gx'=2,'gy'=16] {'gy'}, dimensions={1}, use_global_device_ids=true | all-gather | bytes 417792 | tf_op jit(solution)/shard_map/all_gather | solution.py:485
  961.4 44.4 %all_gather.85 = f32[2,64,12,64]{3,0,2,1:T(2,128)} all-gather(f32[2,4,12,64]{3,0,2,1:T(2,128)S(1)} %copy-done.30), channel_id=1, replica_groups=mesh['gx'=2,'gy'=16] {'gy'}, dimensions={1}, use_global_device_ids=true | all-gather | bytes 417792 | tf_op jit(solution)/shard_map/all_gather | solution.py:484
  1005.8 10.4 convolution_bitcast_fusion.1
  1016.9 320.8 %while.65 = (s32[]{:T(128)}, f32[2,256,12,64]{1,3,2,0:T(8,128)}, f32[2,256,12,64]{1,3,2,0:T(8,128)}, s32[8]{0:T(128)S(1)}, bf16[2,4096,768]{2,1,0:T(8,128)(2,1)}...) while((s32[]{:T(128)}, f32[2,256,12,64]{1,3,2,0:T(8,128)}, ...), condition=%wide.region_23.24_spmd.clone, body=%wide.region_21.23_spmd.clone.sunk | while | flops 1645897984 | bytes 73368968 | solution.py:318
  1036.5 7.9 bitcast_add_fusion.6
  1044.6 11.3 bitcast_add_fusion.5
  1075.2 8.7 bitcast_add_fusion.6
  1084.0 12.3 bitcast_add_fusion.5
  1115.6 8.5 bitcast_add_fusion.6
  1124.3 11.8 bitcast_add_fusion.5
  1155.9 9.1 bitcast_add_fusion.6
  1165.1 12.5 bitcast_add_fusion.5
  1197.3 8.7 bitcast_add_fusion.6
  1206.1 12.3 bitcast_add_fusion.5
  1237.8 8.6 bitcast_add_fusion.6
  1246.6 11.8 bitcast_add_fusion.5
  1277.6 8.4 bitcast_add_fusion.6
  1286.2 11.8 bitcast_add_fusion.5
  1317.2 8.4 bitcast_add_fusion.6
  1325.7 11.8 bitcast_add_fusion.5
  1349.4 9.4 add_convert_fusion
  1367.1 38.0 %all-reduce.18 = (f32[768]{0:T(1024)S(1)}, f32[768]{0:T(1024)S(1)}, f32[768]{0:T(1024)S(1)}, f32[768]{0:T(1024)S(1)}, f32[768]{0:T(1024)S(1)}, /*index=5*/f32[76...) all-reduce(f32[768]{0:T(1024)S(1)} %get-tuple-element.707, ...), channel_id=2, replica_groups=mesh['gx'=2,'gy'=16] {'gx','gy'}, use_global_device_ids=true, to_apply=%region_27.28.clone | all-reduce | flops 9216 | bytes 73728
  1410.4 53.1 %reduce-scatter.5.cloned.1.call-done = f32[24,2304]{1,0:T(8,128)} async-done(((f32[768,2304]{1,0:T(8,128)}), f32[24,2304]{1,0:T(8,128)}) %reduce-scatter.5.cloned.1.call-update) | async-done | bytes 221200 | tf_op jit(solution)/shard_map/reduce_scatter | solution.py:531
  (650 shorter events, 484.8 us)
Async XLA Ops:
  7.2 66.7 %all-gather.9.cloned.1.call-start = ((), (), s32[]{:S(2)}) async-start(), calls=%async_computation.4 | async-start | bytes 3649536 | tf_op jit(solution)/shard_map/all_gather | solution.py:377
  7.9 224.5 %all-gather.13.cloned.1.call-start = ((), (), s32[]{:S(2)}) async-start(), calls=%async_computation.6 | async-start | bytes 13369344 | tf_op jit(solution)/shard_map/all_gather | solution.py:398
  58.3 19.9 %copy-start.34 = (f32[768]{0:T(1024)}, f32[768]{0:T(1024)S(1)}, u32[]{:S(2)}) copy-start(f32[768]{0:T(1024)S(1)} %convert_element_type.128) | copy-start | bytes 9220
  58.3 19.9 %copy-start.51 = (f32[768]{0:T(1024)}, f32[768]{0:T(1024)S(1)}, u32[]{:S(2)}) copy-start(f32[768]{0:T(1024)S(1)} %convert_element_type.129) | copy-start | bytes 9220
  59.7 18.6 %copy-start.36 = (f32[2,256]{1,0:T(2,128)}, f32[2,256]{1,0:T(2,128)S(1)}, u32[]{:S(2)}) copy-start(f32[2,256]{1,0:T(2,128)S(1)} %broadcast_multiply_fusion.1) | copy-start | bytes 6148
  61.8 16.5 %copy-start.38 = (f32[2,256]{1,0:T(2,128)}, f32[2,256]{1,0:T(2,128)S(1)}, u32[]{:S(2)}) copy-start(f32[2,256]{1,0:T(2,128)S(1)} %fusion.149) | copy-start | bytes 6148
  81.4 303.9 %all-gather.11.cloned.1.call-start = ((), (), s32[]{:S(2)}) async-start(), calls=%async_computation.5 | async-start | bytes 13369344 | tf_op jit(solution)/shard_map/all_gather | solution.py:399
  84.8 574.6 %all-gather.15.cloned.1.call-start = ((), (), s32[]{:S(2)}) async-start(), calls=%async_computation.7 | async-start | bytes 1216512 | tf_op jit(solution)/shard_map/all_gather | solution.py:380
  85.4 576.9 %all-gather.17.cloned.1.call-start = ((), (), s32[]{:S(2)}) async-start(), calls=%async_computation.8 | async-start | bytes 4866048 | tf_op jit(solution)/shard_map/all_gather | solution.py:384
  86.0 583.5 %all-gather.19.cloned.1.call-start = ((), (), s32[]{:S(2)}) async-start(), calls=%async_computation.9 | async-start | bytes 4866048 | tf_op jit(solution)/shard_map/all_gather | solution.py:386
  86.5 929.8 %all-gather.21.cloned.1.call-start = ((), (), s32[]{:S(2)}) async-start(), calls=%async_computation.10 | async-start | bytes 13369344 | tf_op jit(solution)/shard_map/all_gather | solution.py:480
  87.3 929.1 %all-gather.23.cloned.1.call-start = ((), (), s32[]{:S(2)}) async-start(), calls=%async_computation.11 | async-start | bytes 13369344 | tf_op jit(solution)/shard_map/all_gather | solution.py:481
  88.6 418.7 %copy-start.28 = (pred[2,4,512]{2,1,0:T(4,128)(4,1)}, pred[2,4,512]{2,1,0:T(4,128)(4,1)S(1)}, u32[]{:S(2)}) copy-start(pred[2,4,512]{2,1,0:T(4,128)(4,1)S(1)} %broadcast_in_dim.187) | copy-start | bytes 12292
  503.4 6.4 copy-start
  503.4 7.3 copy-start.2
  510.7 6.0 copy-start.21
  608.7 42.9 %copy-start.10 = (bf16[2,4,64,12,64]{2,4,3,1,0:T(8,128)(2,1)S(1)}, bf16[2,4,64,12,64]{2,4,3,1,0:T(8,128)(2,1)}, u32[]{:S(2)}) copy-start(bf16[2,4,64,12,64]{2,4,3,1,0:T(8,128)(2,1)} %copy.460) | copy-start | bytes 2359300
  653.8 5.7 copy-start.5
  653.8 5.7 copy-start.53
  661.9 86.0 %copy-start.11 = (f32[2,256,768]{2,1,0:T(8,128)}, f32[2,256,768]{2,1,0:T(8,128)S(1)}, u32[]{:S(2)}) copy-start(f32[2,256,768]{2,1,0:T(8,128)S(1)} %get-tuple-element.849) | copy-start | bytes 4718596
  661.9 20.9 %copy-start.40 = (f32[2,256]{1,0:T(2,128)}, f32[2,256]{1,0:T(2,128)S(1)}, u32[]{:S(2)}) copy-start(f32[2,256]{1,0:T(2,128)S(1)} %broadcast_multiply_fusion) | copy-start | bytes 6148
  662.2 20.6 %copy-start.50 = (f32[2,256]{1,0:T(2,128)}, f32[2,256]{1,0:T(2,128)S(1)}, u32[]{:S(2)}) copy-start(f32[2,256]{1,0:T(2,128)S(1)} %fusion.150) | copy-start | bytes 6148
  662.2 7.2 copy-start.14
  662.2 7.2 copy-start.47
  669.5 9.8 copy-start.57
  687.2 47.1 %copy-start.9 = (bf16[2,256,768]{2,1,0:T(8,128)(2,1)S(1)}, bf16[2,256,768]{2,1,0:T(8,128)(2,1)}, u32[]{:S(2)}) copy-start(bf16[2,256,768]{2,1,0:T(8,128)(2,1)} %get-tuple-element.842) | copy-start | bytes 2359300
  687.2 48.3 %copy-start.8 = (bf16[2,256,768]{2,1,0:T(8,128)(2,1)S(1)}, bf16[2,256,768]{2,1,0:T(8,128)(2,1)}, u32[]{:S(2)}) copy-start(bf16[2,256,768]{2,1,0:T(8,128)(2,1)} %slice.129) | copy-start | bytes 2359300
  687.2 723.1 %reduce-scatter.7.cloned.1.call-start = ((), (), s32[]{:S(2)}) async-start(), calls=%async_computation.13 | async-start | bytes 2433024 | tf_op jit(solution)/shard_map/reduce_scatter | solution.py:534
  691.0 719.4 %reduce-scatter.9.cloned.1.call-start = ((), (), s32[]{:S(2)}) async-start(), calls=%async_computation.14 | async-start | bytes 9732096 | tf_op jit(solution)/shard_map/reduce_scatter | solution.py:538
  741.7 13.6 copy-start.7
  755.4 655.0 %reduce-scatter.11.cloned.1.call-start = ((), (), s32[]{:S(2)}) async-start(), calls=%async_computation.15 | async-start | bytes 9732096 | tf_op jit(solution)/shard_map/reduce_scatter | solution.py:540
  755.4 56.3 %copy-start.22 = (f32[2,4,12,64]{3,2,1,0:T(8,128)S(1)}, f32[2,4,12,64]{3,2,1,0:T(8,128)}, u32[]{:S(2)}) copy-start(f32[2,4,12,64]{3,2,1,0:T(8,128)} %get-tuple-element.822) | copy-start | bytes 73732
  912.0 49.4 %copy-start.30 = (f32[2,4,12,64]{3,0,2,1:T(2,128)S(1)}, f32[2,4,12,64]{3,0,2,1:T(2,128)}, u32[]{:S(2)}) copy-start(f32[2,4,12,64]{3,0,2,1:T(2,128)} %copy.344) | copy-start | bytes 73732
  913.1 92.7 %copy-start.15 = (bf16[2,256,768]{2,1,0:T(8,128)(2,1)S(1)}, bf16[2,256,768]{2,1,0:T(8,128)(2,1)}, u32[]{:S(2)}) copy-start(bf16[2,256,768]{2,1,0:T(8,128)(2,1)} %param.41) | copy-start | bytes 2359300
  913.1 92.7 %copy-start.48 = (f32[3072]{0:T(1024)S(1)}, f32[3072]{0:T(1024)}, u32[]{:S(2)}) copy-start(f32[3072]{0:T(1024)} %convert_element_type.142) | copy-start | bytes 36868
  1016.2 447.3 %reduce-scatter.5.cloned.1.call-start = ((), (), s32[]{:S(2)}) async-start(), calls=%async_computation.12 | async-start | bytes 7299072 | tf_op jit(solution)/shard_map/reduce_scatter | solution.py:531
  1036.5 8.1 copy-start.1
  1075.2 8.8 copy-start.1
  1115.6 8.7 copy-start.1
  1155.9 9.2 copy-start.1
  1197.3 8.8 copy-start.1
  1237.8 8.8 copy-start.1
  1277.6 8.5 copy-start.1
  1317.2 8.5 copy-start.1
  1341.2 6.7 copy-start.25
  1349.4 9.5 copy-start.24
  1358.8 5.8 copy-start.16
  1358.8 5.8 copy-start.44
  (45 other events, 83.3 us)
Sparse Core Ops, SparseCore 0:
  10.9 62.8 all-gather.8
  81.5 150.8 all-gather.12
  235.1 150.2 all-gather.10
  388.1 52.2 all-gather.14
  443.1 62.4 all-gather.16
  508.4 62.3 all-gather.18
  573.4 151.4 all-gather.20
  727.6 150.3 all-gather.22
  883.8 99.6 reduce-scatter.6
  990.8 134.7 reduce-scatter.8
  1132.0 134.5 reduce-scatter.10
  1348.1 115.3 reduce-scatter.4
where the time goes:
time: 1480 us; the launch traced here: 1470 us
  matrix products  480 us (32%)
  local copies, waits for them, and re-layouts  414 us (28%)
  waiting for transfers between devices  247 us (17%)
  blocking collectives  211 us (14%)
  other arithmetic  69.2 us (5%)
  loops' own time  33.4 us (2%)
  between operations  15.5 us (1%)
    all_gather x1, waiting for transfers between devices, shards(): lax.all_gather(key_rows, 'gy', axis=1, tiled=True)  136 us
    another operation x4, local copies, waits for them, and re-layouts, pick_blocks(): window_heads.reshape(micro_count, seq_len // BLOCK, BLOCK, head_count, he...  117 us
    dot_general x8, matrix products, sweep(): jnp.einsum('mhqk,mqhd->mkhd', grad_scores, query_part, preferred_element_...  95.6 us
    unnamed x2, blocking collectives  80.8 us
    dot_general x8, matrix products, sweep(): jnp.einsum('mhqk,mqhd->mkhd', weights_now.astype(jnp.bfloat16), grad_part...  68.2 us
    gather x6, local copies, waits for them, and re-layouts, pick_blocks(): picked = jax.vmap(lambda source, wanted: source[wanted])(blocks, slot_ids)  67.6 us
    dot_general x8, matrix products, sweep(): jnp.einsum('mqhd,mkhd->mhqk', query_part, own_keys, preferred_element_typ...  60.7 us
    reduce_scatter x1, waiting for transfers between devices, shards(): lax.psum_scatter(grad_w_qkv, ('gx', 'gy'), scatter_dimension=0, tiled=True)  53.1 us
  transfers between devices with their start and end apart: 12, of which 4 were waited for; matrix products, arithmetic and copies ran while one was open for 64% of the time, Pallas kernels for 0%

commit v1 on v0

v1 whole, which is shorter than its diff:
```python
import functools

import jax
import jax.numpy as jnp
from jax import lax
from jax.experimental import pallas as pl
from jax.experimental.pallas import tpu as pltpu
from jax.sharding import PartitionSpec as P

HEADS = 12
HEAD_DIM = 64
D = 768
FF = 3072
BLOCK = 64
RANDOM = 3
LANES = 2 * HEAD_DIM
EPSILON = 1e-05
NEGATIVE = -1e30
SCALE = HEAD_DIM**-0.5
CHUNK = 256
SPAN = 8

F32 = jnp.float32
BF16 = jnp.bfloat16
VMEM = pltpu.VMEM


def whole(space=VMEM):
    return pl.BlockSpec(memory_space=space)


def params_of(megabytes):
    return pltpu.CompilerParams(vmem_limit_bytes=megabytes * 1024 * 1024)


def head_place(head):
    return (head // 3) * 4 + head % 3


def dot(left, right):
    return lax.dot_general(left, right, (((1,), (0,)), ((), ())), preferred_element_type=F32)


def dot_rt(left, right):
    return lax.dot_general(left, right, (((1,), (1,)), ((), ())), preferred_element_type=F32)


def dot_lt(left, right):
    return lax.dot_general(left, right, (((0,), (0,)), ((), ())), preferred_element_type=F32)


def swap_halves(tile):
    return pltpu.roll(tile, HEAD_DIM, axis=tile.ndim - 1)


def low_lanes(rows):
    return lax.broadcasted_iota(jnp.int32, (rows, LANES), 1) < HEAD_DIM


def norm_parts(values):
    centre = values - jnp.mean(values, axis=-1, keepdims=True)
    spread = jnp.mean(centre * centre, axis=-1, keepdims=True)
    inverse = lax.rsqrt(spread + EPSILON)
    return centre * inverse, inverse


def norm_pull(grad, normal, inverse, gain):
    scaled = grad * gain
    return inverse * (
        scaled
        - jnp.mean(scaled, axis=-1, keepdims=True)
        - normal * jnp.mean(scaled * normal, axis=-1, keepdims=True)
    )


def qkv_kernel(x_ref, gain_ref, shift_ref, w_ref, bias_ref, normed_ref, send_ref):
    micro, rows, _ = x_ref.shape
    values = x_ref[...].reshape(micro * rows, D).astype(F32)
    normal, _ = norm_parts(values)
    normed_ref[...] = (normal * gain_ref[...] + shift_ref[...]).astype(BF16)
    low = low_lanes(rows)
    for chunk in range(3 * D // CHUNK):
        columns = slice(chunk * CHUNK, (chunk + 1) * CHUNK)
        packed = dot(normed_ref[...], w_ref[:, columns]) + bias_ref[:, columns]
        if chunk < D // CHUNK:
            packed = packed.astype(BF16).astype(F32) * SCALE
        for tile in range(CHUNK // LANES):
            part = packed[:, tile * LANES : (tile + 1) * LANES]
            first, second = part[:rows], part[rows:]
            if chunk < D // CHUNK:
                head = (chunk * CHUNK // LANES + tile) * 2
                even = jnp.where(low, first, swap_halves(second))
                odd = jnp.where(low, swap_halves(first), second)
                send_ref[head_place(head), 0] = even.astype(BF16)
                send_ref[head_place(head + 1), 0] = odd.astype(BF16)
            else:
                head = (chunk * CHUNK - D) // LANES + tile
                send_ref[head_place(head), 1] = first.astype(BF16)
                send_ref[head_place(head), 2] = swap_halves(second).astype(BF16)


def qkv_forward(x, gain, shift, w, bias, groups):
    micro, rows, _ = x.shape
    return pl.pallas_call(
        qkv_kernel,
        out_shape=(
            jax.ShapeDtypeStruct((micro * rows, D), BF16),
            jax.ShapeDtypeStruct((groups, 3, rows, LANES), BF16),
        ),
        in_specs=[whole()] * 5,
        out_specs=(whole(), whole()),
        compiler_params=params_of(48),
        name="qkv_forward",
    )(x, gain, shift, w, bias)


def half_mask(low_half):
    lane = lax.broadcasted_iota(jnp.int32, (1, LANES), 1)
    keep = (lane < HEAD_DIM) if low_half else (lane >= HEAD_DIM)
    return jnp.where(keep, 1.0, 0.0).astype(BF16)


def slots_of(table_ref, micro, block, blocks):
    picks = [table_ref[micro, block * RANDOM + number] for number in range(RANDOM)]
    last = blocks - 1
    ids = [block - 1, block, block + 1, 0, last] + picks
    dropped = [None, None, None, block == 1, block == last - 1]
    for number in range(RANDOM):
        pick = picks[number]
        bad = (jnp.abs(pick - block) <= 1) | (pick == 0) | (pick == last)
        for earlier in range(number):
            bad = bad | (pick == picks[earlier])
        dropped.append(bad)
    lane = lax.broadcasted_iota(jnp.int32, (1, LANES), 1)
    tiles = []
    for pair in range(len(ids) // 2):
        level = [
            0.0 if bad is None else jnp.where(bad, NEGATIVE, 0.0).astype(F32)
            for bad in dropped[2 * pair : 2 * pair + 2]
        ]
        tiles.append(jnp.where(lane < HEAD_DIM, level[0], level[1]))
    return ids, jnp.concatenate(tiles, axis=1)


def attend_kernel(table_ref, qkv_ref, out_ref, lse_ref, s_ref):
    groups, _, local, _, _ = qkv_ref.shape
    blocks = groups * local
    low = low_lanes(BLOCK)
    masks = [half_mask(True), half_mask(False)]

    def load(component, block):
        return qkv_ref[block // local, component, block % local]

    def sparse(block, carry):
        mixed, logs = [], []
        for micro in range(2):
            ids, bias = slots_of(table_ref, micro, block, blocks)
            keys = jnp.concatenate([load(1 + micro, spot) for spot in ids], axis=0)
            query = load(0, block) * masks[micro]
            scores = dot_rt(query, keys) + bias
            top = jnp.max(scores, axis=1, keepdims=True)
            powered = jnp.exp(scores - top)
            total = jnp.sum(powered, axis=1, keepdims=True)
            mixed.append(dot(powered.astype(BF16), keys) * (1.0 / total))
            logs.append(top + jnp.log(total))
        out_ref[block // local, block % local] = jnp.where(low, mixed[1], mixed[0]).astype(BF16)
        lse_ref[block] = jnp.where(low, logs[0], logs[1])
        return carry

    lax.fori_loop(1, blocks - 1, sparse, 0)

    spans = blocks // SPAN
    ends = (0, blocks - 1)
    results = []
    for micro in range(2):
        query = jnp.concatenate([load(0, end) for end in ends], axis=0) * masks[micro]

        def keys_at(span, micro=micro):
            return jnp.concatenate(
                [load(1 + micro, span * SPAN + spot) for spot in range(SPAN)], axis=0
            )

        def first_pass(span, top, query=query, keys_at=keys_at):
            scores = dot_rt(query, keys_at(span))
            s_ref[span] = scores
            return jnp.maximum(top, jnp.max(scores, axis=1, keepdims=True))

        top = lax.fori_loop(0, spans, first_pass, jnp.full((2 * BLOCK, 1), NEGATIVE, F32))

        def second_pass(span, carry, top=top, keys_at=keys_at):
            total, mixed = carry
            powered = jnp.exp(s_ref[span] - top)
            return (
                total + jnp.sum(powered, axis=1, keepdims=True),
                mixed + dot(powered.astype(BF16), keys_at(span)),
            )

        total, mixed = lax.fori_loop(
            0,
            spans,
            second_pass,
            (jnp.zeros((2 * BLOCK, 1), F32), jnp.zeros((2 * BLOCK, LANES), F32)),
        )
        results.append((mixed * (1.0 / total), top + jnp.log(total)))
    for place, end in enumerate(ends):
        rows = slice(place * BLOCK, (place + 1) * BLOCK)
        out_ref[end // local, end % local] = jnp.where(
            low, results[1][0][rows], results[0][0][rows]
        ).astype(BF16)
        lse_ref[end] = jnp.where(low, results[0][1][rows], results[1][1][rows])


def attention_forward(table, qkv):
    groups, _, local, _, _ = qkv.shape
    blocks = groups * local
    return pl.pallas_call(
        attend_kernel,
        out_shape=(
            jax.ShapeDtypeStruct((groups, local, BLOCK, LANES), BF16),
            jax.ShapeDtypeStruct((blocks, BLOCK, LANES), F32),
        ),
        in_specs=[whole(pltpu.SMEM), whole()],
        out_specs=(whole(), whole()),
        scratch_shapes=[VMEM((blocks // SPAN, 2 * BLOCK, SPAN * BLOCK), F32)],
        compiler_params=params_of(48),
        name="attention_forward",
    )(table, qkv)


def attend_back_kernel(table_ref, qkv_ref, grad_ref, lse_ref, out_ref, sums_ref, p_ref, dp_ref):
    groups, _, local, _, _ = qkv_ref.shape
    blocks = groups * local
    low = low_lanes(BLOCK)
    masks = [half_mask(True), half_mask(False)]

    def load(component, block):
        return qkv_ref[block // local, component, block % local]

    def load_grad(block):
        return grad_ref[block // local, block % local]

    def clear(block, carry):
        for micro in range(2):
            sums_ref[micro, block] = jnp.zeros((BLOCK, LANES), F32)
        return carry

    lax.fori_loop(0, blocks, clear, 0)

    def sparse(block, carry):
        grads = []
        for micro in range(2):
            ids, bias = slots_of(table_ref, micro, block, blocks)
            keys = jnp.concatenate([load(1 + micro, spot) for spot in ids], axis=0)
            both = jnp.concatenate(
                [load(0, block) * masks[micro], load_grad(block) * masks[1 - micro]], axis=0
            )
            products = dot_rt(both, keys)
            logs = lse_ref[block][:, micro * HEAD_DIM : micro * HEAD_DIM + 1]
            weights = jnp.exp(products[:BLOCK] + bias - logs)
            grad_weights = products[BLOCK:]
            delta = jnp.sum(weights * grad_weights, axis=1, keepdims=True)
            grad_scores = weights * (grad_weights - delta)
            stacked = jnp.concatenate([grad_scores, weights], axis=0).astype(BF16)
            grads.append(dot(stacked[:BLOCK], keys))
            shares = dot_lt(stacked, both)
            for place, spot in enumerate(ids):
                sums_ref[micro, spot] += shares[place * BLOCK : (place + 1) * BLOCK]
        out_ref[block // local, 0, block % local] = (
            jnp.where(low, grads[0], grads[1]) * SCALE
        ).astype(BF16)
        return carry

    lax.fori_loop(1, blocks - 1, sparse, 0)

    spans = blocks // SPAN
    ends = (0, blocks - 1)
    results = []
    for micro in range(2):
        query = jnp.concatenate([load(0, end) for end in ends], axis=0) * masks[micro]
        grad = jnp.concatenate([load_grad(end) for end in ends], axis=0) * masks[1 - micro]
        both = jnp.concatenate([query, grad], axis=0)
        logs = jnp.concatenate(
            [lse_ref[end][:, micro * HEAD_DIM : micro * HEAD_DIM + 1] for end in ends], axis=0
        )

        def keys_at(span, micro=micro):
            return jnp.concatenate(
                [load(1 + micro, span * SPAN + spot) for spot in range(SPAN)], axis=0
            )

        def first_pass(span, delta, both=both, logs=logs, keys_at=keys_at):
            products = dot_rt(both, keys_at(span))
            weights = jnp.exp(products[: 2 * BLOCK] - logs)
            grad_weights = products[2 * BLOCK :]
            p_ref[span] = weights
            dp_ref[span] = grad_weights
            return delta + jnp.sum(weights * grad_weights, axis=1, keepdims=True)

        delta = lax.fori_loop(0, spans, first_pass, jnp.zeros((2 * BLOCK, 1), F32))

        def second_pass(span, carry, delta=delta, both=both, keys_at=keys_at, micro=micro):
            weights = p_ref[span]
            grad_scores = weights * (dp_ref[span] - delta)
            stacked = jnp.concatenate([grad_scores, weights], axis=0).astype(BF16)
            shares = dot_lt(stacked, both)
            for spot in range(SPAN):
                sums_ref[micro, span * SPAN + spot] += shares[spot * BLOCK : (spot + 1) * BLOCK]
            return carry + dot(stacked[: 2 * BLOCK], keys_at(span))

        results.append(
            lax.fori_loop(0, spans, second_pass, jnp.zeros((2 * BLOCK, LANES), F32))
        )
    for place, end in enumerate(ends):
        rows = slice(place * BLOCK, (place + 1) * BLOCK)
        out_ref[end // local, 0, end % local] = (
            jnp.where(low, results[0][rows], results[1][rows]) * SCALE
        ).astype(BF16)

    def finish(block, carry):
        for micro in range(2):
            out_ref[block // local, 1 + micro, block % local] = sums_ref[micro, block].astype(BF16)
        return carry

    lax.fori_loop(0, blocks, finish, 0)


def attention_backward(table, qkv, grad, lse):
    groups, _, local, _, _ = qkv.shape
    blocks = groups * local
    spans = VMEM((blocks // SPAN, 2 * BLOCK, SPAN * BLOCK), F32)
    return pl.pallas_call(
        attend_back_kernel,
        out_shape=jax.ShapeDtypeStruct(qkv.shape, BF16),
        in_specs=[whole(pltpu.SMEM), whole(), whole(), whole()],
        out_specs=whole(),
        scratch_shapes=[VMEM((2, blocks, BLOCK, LANES), F32), spans, spans],
        compiler_params=params_of(48),
        name="attention_backward",
    )(table, qkv, grad, lse)


def middle_kernel(
    mixed_in_ref,
    x_ref,
    dy_ref,
    w_out_ref,
    out_shift_ref,
    gain_ref,
    shift_ref,
    up_shift_ref,
    down_shift_ref,
    w_up_ref,
    w_down_ref,
    hidden_ref,
    send_ref,
    dres_ref,
    g_out_ref,
    g_up_ref,
    g_down_ref,
    g_up_bias_ref,
    g_small_ref,
    mixed_ref,
    residual_ref,
    second_ref,
    second_t_ref,
    total_ref,
    dsecond_ref,
):
    micro, rows, _ = x_ref.shape
    step = pl.program_id(0)
    low = low_lanes(rows)

    @pl.when(step == 0)
    def _():
        for pair in range(HEADS // 2):
            even = mixed_in_ref[head_place(2 * pair)].astype(F32)
            odd = mixed_in_ref[head_place(2 * pair + 1)].astype(F32)
            columns = slice(pair * LANES, (pair + 1) * LANES)
            mixed_ref[:rows, columns] = jnp.where(low, swap_halves(even), odd).astype(BF16)
            mixed_ref[rows:, columns] = jnp.where(low, even, swap_halves(odd)).astype(BF16)
        residual = x_ref[...].reshape(micro * rows, D).astype(F32) + (
            dot(mixed_ref[...], w_out_ref[...]) + out_shift_ref[...]
        )
        residual_ref[...] = residual
        normal, _ = norm_parts(residual)
        second = normal * gain_ref[...] + shift_ref[...]
        second_ref[...] = second.astype(BF16)
        second_t_ref[...] = second.T.astype(BF16)
        total_ref[...] = jnp.zeros_like(total_ref)
        dsecond_ref[...] = jnp.zeros_like(dsecond_ref)

    upper = dot(second_ref[...], w_up_ref[...]) + up_shift_ref[...]
    factor = 0.7978845608028654
    square = upper * upper
    bent = jnp.tanh(factor * (upper + 0.044715 * (upper * square)))
    half = 0.5 * (1.0 + bent)
    active = (upper * half).astype(BF16)
    slope = half + 0.5 * upper * (1.0 - bent * bent) * (
        factor + (3.0 * 0.044715 * factor) * square
    )
    dy = dy_ref[...]
    total_ref[...] += dot(active, w_down_ref[...])
    g_down_ref[...] = dot_lt(active, dy).astype(g_down_ref.dtype)
    dupper = (dot_rt(dy, w_down_ref[...]) * slope).astype(BF16)
    g_up_bias_ref[...] = jnp.sum(dupper.astype(F32), axis=0, keepdims=True)
    g_up_ref[...] = dot(second_t_ref[...], dupper).astype(g_up_ref.dtype)
    dsecond_ref[...] += dot_rt(dupper, w_up_ref[...])

    @pl.when(step == pl.num_programs(0) - 1)
    def _():
        residual = residual_ref[...]
        hidden_ref[...] = (
            (residual + (total_ref[...] + down_shift_ref[...])).astype(BF16).reshape(x_ref.shape)
        )
        normal, inverse = norm_parts(residual)
        dsecond = dsecond_ref[...]
        grad_out = dy_ref[...].astype(F32)
        g_small_ref[0:1] = jnp.sum(dsecond * normal, axis=0, keepdims=True)
        g_small_ref[1:2] = jnp.sum(dsecond, axis=0, keepdims=True)
        g_small_ref[2:3] = jnp.sum(grad_out, axis=0, keepdims=True)
        dres = grad_out + norm_pull(dsecond, normal, inverse, gain_ref[...])
        dres_ref[...] = dres
        branch = dres.astype(BF16)
        g_small_ref[3:4] = jnp.sum(branch.astype(F32), axis=0, keepdims=True)
        g_out_ref[...] = dot_lt(mixed_ref[...], branch).astype(g_out_ref.dtype)
        dmixed = dot_rt(branch, w_out_ref[...])
        for pair in range(HEADS // 2):
            part = dmixed[:, pair * LANES : (pair + 1) * LANES]
            first, last = part[:rows], part[rows:]
            even = jnp.where(low, last, swap_halves(first))
            odd = jnp.where(low, swap_halves(last), first)
            send_ref[head_place(2 * pair)] = even.astype(BF16)
            send_ref[head_place(2 * pair + 1)] = odd.astype(BF16)


def middle(mixed_in, x, dy, w_out, out_shift, gain, shift, up_shift, down_shift, w_up, w_down, kind):
    micro, rows, _ = x.shape
    tokens = micro * rows
    groups = mixed_in.shape[0]

    def fixed(shape):
        return pl.BlockSpec(shape, lambda step: (0,) * len(shape))

    vector = fixed((1, D))
    steps = FF // CHUNK
    return pl.pallas_call(
        middle_kernel,
        grid=(steps,),
        out_shape=(
            jax.ShapeDtypeStruct(x.shape, BF16),
            jax.ShapeDtypeStruct((groups, rows, LANES), BF16),
            jax.ShapeDtypeStruct((tokens, D), F32),
            jax.ShapeDtypeStruct((D, D), kind),
            jax.ShapeDtypeStruct((D, FF), kind),
            jax.ShapeDtypeStruct((FF, D), kind),
            jax.ShapeDtypeStruct((1, FF), F32),
            jax.ShapeDtypeStruct((4, D), F32),
        ),
        in_specs=[
            fixed(mixed_in.shape),
            fixed(x.shape),
            fixed((tokens, D)),
            fixed((D, D)),
            vector,
            vector,
            vector,
            pl.BlockSpec((1, CHUNK), lambda step: (0, step)),
            vector,
            pl.BlockSpec((D, CHUNK), lambda step: (0, step)),
            pl.BlockSpec((CHUNK, D), lambda step: (step, 0)),
        ],
        out_specs=(
            fixed(x.shape),
            fixed((groups, rows, LANES)),
            fixed((tokens, D)),
            fixed((D, D)),
            pl.BlockSpec((D, CHUNK), lambda step: (0, step)),
            pl.BlockSpec((CHUNK, D), lambda step: (step, 0)),
            pl.BlockSpec((1, CHUNK), lambda step: (0, step)),
            fixed((4, D)),
        ),
        scratch_shapes=[
            VMEM((tokens, D), BF16),
            VMEM((tokens, D), F32),
            VMEM((tokens, D), BF16),
            VMEM((D, tokens), BF16),
            VMEM((tokens, D), F32),
            VMEM((tokens, D), F32),
        ],
        compiler_params=params_of(56),
        name="middle",
    )(mixed_in, x, dy, w_out, out_shift, gain, shift, up_shift, down_shift, w_up, w_down)


def qkv_back_kernel(
    recv_ref,
    normed_ref,
    x_ref,
    dres_ref,
    gain_ref,
    w_ref,
    grad_ref,
    g_qkv_ref,
    g_bias_ref,
    g_small_ref,
    packed_ref,
    normed_t_ref,
    dnormed_ref,
):
    micro, rows, _ = x_ref.shape
    step = pl.program_id(0)
    low = low_lanes(rows)

    @pl.when(step == 0)
    def _():
        for pair in range(HEADS // 2):
            even = recv_ref[head_place(2 * pair), 0].astype(F32)
            odd = recv_ref[head_place(2 * pair + 1), 0].astype(F32)
            spot, columns = pair // 2, slice((pair % 2) * LANES, (pair % 2 + 1) * LANES)
            packed_ref[spot, :rows, columns] = jnp.where(low, even, swap_halves(odd)).astype(BF16)
            packed_ref[spot, rows:, columns] = jnp.where(low, swap_halves(even), odd).astype(BF16)
        for head in range(HEADS):
            spot = D // CHUNK + head // 2
            columns = slice((head % 2) * LANES, (head % 2 + 1) * LANES)
            packed_ref[spot, :rows, columns] = recv_ref[head_place(head), 1]
            packed_ref[spot, rows:, columns] = swap_halves(
                recv_ref[head_place(head), 2].astype(F32)
            ).astype(BF16)
        normed_t_ref[...] = normed_ref[...].astype(F32).T.astype(BF16)
        dnormed_ref[...] = jnp.zeros_like(dnormed_ref)

    packed = packed_ref[step]
    g_bias_ref[...] = jnp.sum(packed.astype(F32), axis=0, keepdims=True)
    g_qkv_ref[...] = dot(normed_t_ref[...], packed).astype(g_qkv_ref.dtype)
    dnormed_ref[...] += dot_rt(packed, w_ref[...])

    @pl.when(step == pl.num_programs(0) - 1)
    def _():
        normal, inverse = norm_parts(x_ref[...].reshape(micro * rows, D).astype(F32))
        dnormed = dnormed_ref[...]
        g_small_ref[0:1] = jnp.sum(dnormed * normal, axis=0, keepdims=True)
        g_small_ref[1:2] = jnp.sum(dnormed, axis=0, keepdims=True)
        grad = dres_ref[...] + norm_pull(dnormed, normal, inverse, gain_ref[...])
        grad_ref[...] = grad.reshape(x_ref.shape)


def qkv_backward(recv, normed, x, dres, gain, w, kind):
    micro, rows, _ = x.shape
    tokens = micro * rows

    def fixed(shape):
        return pl.BlockSpec(shape, lambda step: (0,) * len(shape))

    steps = 3 * D // CHUNK
    return pl.pallas_call(
        qkv_back_kernel,
        grid=(steps,),
        out_shape=(
            jax.ShapeDtypeStruct(x.shape, F32),
            jax.ShapeDtypeStruct((D, 3 * D), kind),
            jax.ShapeDtypeStruct((1, 3 * D), F32),
            jax.ShapeDtypeStruct((2, D), F32),
        ),
        in_specs=[
            fixed(recv.shape),
            fixed((tokens, D)),
            fixed(x.shape),
            fixed((tokens, D)),
            fixed((1, D)),
            pl.BlockSpec((D, CHUNK), lambda step: (0, step)),
        ],
        out_specs=(
            fixed(x.shape),
            pl.BlockSpec((D, CHUNK), lambda step: (0, step)),
            pl.BlockSpec((1, CHUNK), lambda step: (0, step)),
            fixed((2, D)),
        ),
        scratch_shapes=[
            VMEM((steps, tokens, CHUNK), BF16),
            VMEM((D, tokens), BF16),
            VMEM((tokens, D), F32),
        ],
        compiler_params=params_of(56),
        name="qkv_backward",
    )(recv, normed, x, dres, gain, w)


AXES = ("gx", "gy")


def gather(array):
    return lax.all_gather(array, AXES, axis=0, tiled=True)


def scatter(array):
    return lax.psum_scatter(array, AXES, scatter_dimension=0, tiled=True)


def exchange(array):
    return lax.all_to_all(array, "gy", 0, 0, tiled=True)


def by_heads(w_qkv):
    rows = w_qkv.shape[0]
    sides = w_qkv[:, D:].reshape(rows, 2, HEADS, HEAD_DIM)
    return jnp.concatenate([w_qkv[:, :D], jnp.swapaxes(sides, 1, 2).reshape(rows, 2 * D)], axis=1)


def by_parts(w_qkv):
    rows = w_qkv.shape[0]
    sides = w_qkv[:, D:].reshape(rows, HEADS, 2, HEAD_DIM)
    return jnp.concatenate([w_qkv[:, :D], jnp.swapaxes(sides, 1, 2).reshape(rows, 2 * D)], axis=1)


def shards(
    hidden_in,
    rand_table,
    norm1_gain,
    norm1_bias,
    w_qkv,
    query_bias,
    value_bias,
    w_out,
    out_bias,
    norm2_gain,
    norm2_bias,
    w_up,
    up_bias,
    w_down,
    down_bias,
    cotangent,
):
    micro, rows, _ = hidden_in.shape
    groups = lax.axis_size("gy")
    local = rows // BLOCK
    own = norm1_gain.shape[0]

    vectors = jnp.concatenate(
        [
            norm1_gain,
            norm1_bias,
            query_bias,
            value_bias,
            out_bias,
            norm2_gain,
            norm2_bias,
            down_bias,
            up_bias,
        ]
    )
    table = lax.all_gather(rand_table, "gy", axis=1, tiled=True)
    table = table.reshape(micro, groups * local * RANDOM)
    vectors = gather(vectors[None]).astype(F32)
    gain_one, shift_one, query_shift, value_shift, out_shift, gain_two, shift_two, down_shift = (
        vectors[:, number * own : (number + 1) * own].reshape(1, D) for number in range(8)
    )
    up_shift = vectors[:, 8 * own :].reshape(1, FF)
    w_qkv_full = gather(by_heads(w_qkv))
    w_out_full, w_up_full, w_down_full = gather(w_out), gather(w_up), gather(w_down)
    packed_bias = by_heads(
        jnp.concatenate([query_shift, jnp.zeros_like(query_shift), value_shift], axis=1)
    )

    normed, send = qkv_forward(hidden_in, gain_one, shift_one, w_qkv_full, packed_bias, groups)
    qkv = exchange(send).reshape(groups, 3, local, BLOCK, LANES)
    mixed, lse = attention_forward(table, qkv)
    mixed_back = exchange(mixed.reshape(groups, rows, LANES))
    hidden_out, grad_send, dres, g_out, g_up, g_down, g_up_bias, g_mid = middle(
        mixed_back,
        hidden_in,
        cotangent.reshape(micro * rows, D),
        w_out_full,
        out_shift,
        gain_two,
        shift_two,
        up_shift,
        down_shift,
        w_up_full,
        w_down_full,
        F32,
    )
    grad_mixed = exchange(grad_send).reshape(groups, local, BLOCK, LANES)
    dqkv = attention_backward(table, qkv, grad_mixed, lse)
    dqkv_back = exchange(dqkv.reshape(groups, 3, rows, LANES))
    grad_hidden, g_qkv, g_packed, g_first = qkv_backward(
        dqkv_back, normed, hidden_in, dres, gain_one, w_qkv_full, F32
    )

    g_packed = by_parts(g_packed)
    small = [
        g_first[0],
        g_first[1],
        g_packed[0, :D],
        g_packed[0, 2 * D :],
        g_mid[3],
        g_mid[0],
        g_mid[1],
        g_mid[2],
    ]
    ranks = D // own
    small = jnp.concatenate(
        [item.reshape(ranks, own) for item in small] + [g_up_bias.reshape(ranks, 4 * own)], axis=1
    )
    small = scatter(small)[0]
    parts = [small[number * own : (number + 1) * own] for number in range(8)]
    return (
        hidden_out,
        grad_hidden,
        parts[0],
        parts[1],
        by_parts(scatter(g_qkv)),
        parts[2],
        parts[3],
        scatter(g_out),
        parts[4],
        parts[5],
        parts[6],
        scatter(g_up),
        small[8 * own :],
        scatter(g_down),
        parts[7],
    )


def solution(mesh):
    tokens = P(None, AXES, None)
    vector = P(AXES)
    matrix = P(AXES, None)
    placed = (
        tokens,
        tokens,
        vector,
        vector,
        matrix,
        vector,
        vector,
        matrix,
        vector,
        vector,
        vector,
        matrix,
        vector,
        matrix,
        vector,
        tokens,
    )
    returned = (
        tokens,
        tokens,
        vector,
        vector,
        matrix,
        vector,
        vector,
        matrix,
        vector,
        vector,
        vector,
        matrix,
        vector,
        matrix,
        vector,
    )
    return jax.shard_map(
        shards, mesh=mesh, in_specs=placed, out_specs=returned, check_vma=False
    )
```

time: 1480 us -> 1030 us (0.70)
  matrix products: 480 us -> 0 us
  local copies, waits for them, and re-layouts: 414 us -> 20.9 us
  waiting for transfers between devices: 247 us -> 527 us
  Pallas kernels: 0 us -> 163 us
  other arithmetic: 69.2 us -> 2.04 us
  blocking collectives: 211 us -> 276 us
  loops' own time: 33.4 us -> 0 us
  starting transfers between devices: 0.66 us -> 22.4 us
    dot_general x88 -> x0, matrix products: 480 us -> none  [the longest x8 95.6 us: sweep(): jnp.einsum('mhqk,mqhd->mkhd', grad_scores, query_part, preferred_element_...]
    reduce_scatter x4, waiting for transfers between devices: 53.1 us -> 458 us  [scatter(): return lax.psum_scatter(array, AXES, scatter_dimension=0, tiled=True)]
    pallas_call x0 -> x5, Pallas kernels: none -> 163 us  [the longest x1 53.2 us: attention_backward(): pl.pallas_call(attend_back_kernel, out_shape=jax.ShapeDtypeStruct(qkv.sha...]
    all_gather x8 -> x4, waiting for transfers between devices: 191 us -> 65.6 us  [gather(): return lax.all_gather(array, AXES, axis=0, tiled=True)]
    another operation x7 -> x8, local copies, waits for them, and re-layouts: 117 us -> 0.64 us  [shards(): item.reshape(ranks, own)]
    all_to_all x0 -> x2, blocking collectives: none -> 106 us  [exchange(): return lax.all_to_all(array, 'gy', 0, 0, tiled=True)]
    dynamic_slice x100 -> x0, local copies, waits for them, and re-layouts: 97.9 us -> none  [the longest x16 39.5 us: sweep(): lax.dynamic_slice_in_dim(grad_all, first_query, query_span, 1)]
    gather x6 -> x0, local copies, waits for them, and re-layouts: 67.6 us -> none  [pick_blocks(): picked = jax.vmap(lambda source, wanted: source[wanted])(blocks, slot_ids)]
  transfers between devices with their start and end apart: 12 -> 10, of which waited for: 4 -> 6; matrix products, arithmetic and copies ran while one was open for 64% -> 2% of each run, Pallas kernels for 0% -> 6%
where the time goes in v1:
time: 1030 us
  waiting for transfers between devices  527 us (51%)
  blocking collectives  276 us (27%)
  Pallas kernels  163 us (16%)
  starting transfers between devices  22.4 us (2%)
  local copies, waits for them, and re-layouts  20.9 us (2%)
  between operations  14.5 us (1%)
    reduce_scatter x4, waiting for transfers between devices, scatter(): return lax.psum_scatter(array, AXES, scatter_dimension=0, tiled=True)  458 us
    all_to_all x2, blocking collectives, exchange(): return lax.all_to_all(array, 'gy', 0, 0, tiled=True)  106 us
    all_gather x1, blocking collectives, shards(): table = lax.all_gather(rand_table, 'gy', axis=1, tiled=True)  88.7 us
    unnamed x2, blocking collectives  81.8 us
    all_gather x4, waiting for transfers between devices, gather(): return lax.all_gather(array, AXES, axis=0, tiled=True)  65.6 us
    pallas_call x1, Pallas kernels, attention_backward(): pl.pallas_call(attend_back_kernel, out_shape=jax.ShapeDtypeStruct(qkv.sha...  53.2 us
    pallas_call x1, Pallas kernels, attention_forward(): pl.pallas_call(attend_kernel, out_shape=(jax.ShapeDtypeStruct((groups, lo...  52.2 us
    pallas_call x1, Pallas kernels, middle(): pl.pallas_call(middle_kernel, grid=(steps,), out_shape=(jax.ShapeDtypeStr...  36.4 us
  transfers between devices with their start and end apart: 10, of which 6 were waited for; matrix products, arithmetic and copies ran while one was open for 2% of the time, Pallas kernels for 6%

profile of v1, /device:TPU:0, one launch (start us, length us, event | category | flops | bytes accessed | tf_op | source)
XLA Modules:
  0.0 1026.1 jit_solution(11837411179122223930)
XLA Ops:
  7.2 0.9 slice.123
  8.1 0.8 slice.122
  8.9 0.2 reshape.114
  9.2 0.2 reshape.115
  9.4 0.7 pad_maximum_fusion.1
  10.1 0.7 all-gather.8.cloned.1.call-update
  10.8 0.7 all-gather.10.cloned.1.call-update
  11.6 0.5 all-gather.12.cloned.1.call-update
  12.1 6.1 concatenate.18
  18.2 0.2 dynamic-update-slice
  18.5 42.4 %all-reduce.1 = bf16[9216]{0:T(1024)(128)(2,1)S(1)} all-reduce(bf16[9216]{0:T(1024)(128)(2,1)S(1)} %dynamic-update-slice), channel_id=2, replica_groups=mesh['gx'=2,'gy'=16] {'gx','gy'}, use_global_device_ids=true, to_apply=%add.1 | all-reduce | flops 9216 | bytes 36864
  61.7 12.9 %all-gather.6.cloned.1.call-done.w_ref = bf16[768,2304]{1,0:T(8,128)(2,1)} async-done(((bf16[24,2304]{1,0:T(8,128)(2,1)}), bf16[768,2304]{1,0:T(8,128)(2,1)}) %all-gather.6.cloned.1.call-update) | async-done | bytes 3538960 | tf_op jit(solution)/shard_map/all_gather | solution.py:592
  74.5 1.1 copy-done
  75.7 6.1 qkv_forward.1
  81.8 0.9 copy-done.1
  82.7 4.8 all-to-all-start
  87.6 88.7 %all_gather.18 = s32[2,64,3]{2,0,1:T(2,128)S(1)} all-gather(s32[2,4,3]{2,0,1:T(2,128)S(1)} %copy.39), channel_id=1, replica_groups=mesh['gx'=2,'gy'=16] {'gy'}, dimensions={1}, use_global_device_ids=true | all-gather | bytes 1632 | tf_op jit(solution)/shard_map/all_gather | solution.py:651
  176.5 52.2 %attention_forward.1 = (bf16[16,4,64,128]{3,2,1,0:T(8,128)(2,1)}, f32[64,64,128]{2,1,0:T(8,128)S(1)}) custom-call(s32[2,192]{1,0:T(2,128)S(1)} %reshape.111.table_ref, bf16[16,3,4,64,128]{4,3,2,1,0:T(8,128)(2,1)} %bitcast.2.qkv_ref), custom_call_target="tpu_custom_call" | custom-call | tf_op jit(solution)/shard_map/attention_forward/pallas_call | solution.py:216
  228.7 17.1 %all-to-all-start.1 = ((bf16[16,256,128]{2,1,0:T(8,128)(2,1)}), bf16[16,256,128]{2,1,0:T(8,128)(2,1)S(1)}, u32[]{:S(2)}, u32[]{:S(2)}) async-start(bf16[16,256,128]{2,1,0:T(8,128)(2,1)} %bitcast.3), calls=%async_computation.1 | async-start | bytes 2097152 | tf_op jit(solution)/shard_map/all_to_all | solution.py:600
  245.8 0.2 reduce-scatter.5.cloned.1.call-start
  246.1 0.7 reshape.123.out_shift_ref
  246.8 0.7 reshape.124.gain_ref
  247.4 0.7 reshape.125.shift_ref
  248.1 0.7 reshape.127.down_shift_ref
  248.8 0.7 reshape.126.up_shift_ref
  249.5 52.8 %all-gather.12.cloned.1.call-done.w_down_ref = bf16[3072,768]{1,0:T(8,128)(2,1)} async-done(((bf16[96,768]{1,0:T(8,128)(2,1)}), bf16[3072,768]{1,0:T(8,128)(2,1)}) %all-gather.12.cloned.1.call-update) | async-done | bytes 4718608 | tf_op jit(solution)/shard_map/all_gather | solution.py:592
  302.2 1.0 copy-done.3
  303.2 36.4 %middle.1 = (bf16[2,256,768]{2,1,0:T(8,128)(2,1)}, bf16[16,256,128]{2,1,0:T(8,128)(2,1)}, f32[512,768]{1,0:T(8,128)}, f32[768,768]{1,0:T(8,128)}, f32[768,3072]{...) custom-call(bf16[16,256,128]{2,1,0:T(8,128)(2,1)} %copy-done.3, ...), custom_call_target="tpu_custom_call" | custom-call | tf_op jit(solution)/shard_map/middle/pallas_call | solution.py:446
  339.6 31.2 %all_to_all.20 = bf16[16,256,128]{2,1,0:T(8,128)(2,1)S(1)} all-to-all(bf16[16,256,128]{2,1,0:T(8,128)(2,1)} %get-tuple-element.34), channel_id=1, replica_groups=mesh['gx'=2,'gy'=16] {'gy'}, dimensions={0} | all-to-all | bytes 2097152 | tf_op jit(solution)/shard_map/all_to_all | solution.py:600
  370.8 53.2 %attention_backward.1 = bf16[16,3,4,64,128]{4,3,2,1,0:T(8,128)(2,1)} custom-call(s32[2,192]{1,0:T(2,128)S(1)} %reshape.111.table_ref, bf16[16,3,4,64,128]{4,3,2,1,0:T(8,128)(2,1)} %bitcast.2.qkv_ref, bf16[16,4,64,128]{3,2,1,0:T(8,128)(2,1)S(1)} %bitcast.31, f32[64,64,128]{2,1,0:T(8,128)S(1)} %get-tuple-element.35.lse_ref), custom_call_target="tpu_custom_call" | custom-call | tf_op jit(solution)/shard_map/attention_backward/pallas_call | solution.py:331
  424.0 74.7 %all_to_all.21.recv_ref = bf16[16,3,256,128]{3,2,1,0:T(8,128)(2,1)} all-to-all(bf16[16,3,256,128]{3,2,1,0:T(8,128)(2,1)} %bitcast.32), channel_id=1, replica_groups=mesh['gx'=2,'gy'=16] {'gy'}, dimensions={0} | all-to-all | bytes 6291456 | tf_op jit(solution)/shard_map/all_to_all | solution.py:600
  498.7 14.6 %qkv_backward.1 = (f32[2,256,768]{2,1,0:T(8,128)}, f32[768,2304]{1,0:T(8,128)}, f32[1,2304]{1,0:T(1,128)}, f32[2,768]{1,0:T(2,128)}) custom-call(bf16[16,3,256,128]{3,2,1,0:T(8,128)(2,1)} %all_to_all.21.recv_ref, bf16[512,768]{1,0:T(8,128)(2,1)} %copy-done.1, bf16[2,256,768]{2,1,0:T(8,128)(2,1)} %x_ref.5, f32[512,768]{1,0:T(8,128)} %get-tuple-element.37.dres_ref, ...), custom_call_target="tpu_custom_call" | custom-call | tf_op jit(solution)/shard_map/qkv_backward/pallas_call | solution.py:555
  513.4 0.5 reduce-scatter.7.cloned.1.call-update
  514.0 0.7 reduce-scatter.11.cloned.1.call-update
  514.8 0.7 reduce-scatter.9.cloned.1.call-update
  515.8 0.5 broadcast.16
  516.3 0.7 reduce.23
  517.8 39.4 %all-reduce.2 = f32[32,288]{1,0:T(8,128)S(1)} all-reduce(f32[32,288]{1,0:T(8,128)S(1)} %concatenate.22), channel_id=3, replica_groups=mesh['gx'=2,'gy'=16] {'gx','gy'}, use_global_device_ids=true, to_apply=%region_0.0.clone | all-reduce | flops 9216 | bytes 73728
  557.2 0.6 dynamic-slice_bitcast_fusion.1
  557.8 0.6 dynamic-slice_bitcast_fusion
  558.4 72.7 %reduce-scatter.5.cloned.1.call-done = f32[24,2304]{1,0:T(8,128)} async-done(((f32[768,2304]{1,0:T(8,128)}), f32[24,2304]{1,0:T(8,128)}) %reduce-scatter.5.cloned.1.call-update) | async-done | bytes 221200 | tf_op jit(solution)/shard_map/reduce_scatter | solution.py:596
  631.1 0.9 slice.171
  632.0 0.2 reshape.133
  632.4 0.9 slice.170
  633.3 0.7 pad_maximum_fusion
  634.0 102.0 %reduce-scatter.7.cloned.1.call-done = f32[24,768]{1,0:T(8,128)} async-done(((f32[768,768]{1,0:T(8,128)}), f32[24,768]{1,0:T(8,128)}) %reduce-scatter.7.cloned.1.call-update) | async-done | bytes 73744 | tf_op jit(solution)/shard_map/reduce_scatter | solution.py:596
  736.0 141.0 %reduce-scatter.11.cloned.1.call-done = f32[96,768]{1,0:T(8,128)} async-done(((f32[3072,768]{1,0:T(8,128)}), f32[96,768]{1,0:T(8,128)}) %reduce-scatter.11.cloned.1.call-update) | async-done | bytes 294928 | tf_op jit(solution)/shard_map/reduce_scatter | solution.py:596
  877.0 142.2 %reduce-scatter.9.cloned.1.call-done = f32[24,3072]{1,0:T(8,128)} async-done(((f32[768,3072]{1,0:T(8,128)}), f32[24,3072]{1,0:T(8,128)}) %reduce-scatter.9.cloned.1.call-update) | async-done | bytes 294928 | tf_op jit(solution)/shard_map/reduce_scatter | solution.py:596
  (64 shorter events, 2.8 us)
Async XLA Ops:
  7.2 67.3 %all-gather.6.cloned.1.call-start = ((), (), s32[]{:S(2)}) async-start(), calls=%async_computation.8 | async-start | bytes 3649536 | tf_op jit(solution)/shard_map/all_gather | solution.py:592
  10.0 239.4 %all-gather.8.cloned.1.call-start = ((), (), s32[]{:S(2)}) async-start(), calls=%async_computation.9 | async-start | bytes 1216512 | tf_op jit(solution)/shard_map/all_gather | solution.py:592
  10.8 238.7 %all-gather.10.cloned.1.call-start = ((), (), s32[]{:S(2)}) async-start(), calls=%async_computation.10 | async-start | bytes 4866048 | tf_op jit(solution)/shard_map/all_gather | solution.py:592
  11.5 290.7 %all-gather.12.cloned.1.call-start = ((), (), s32[]{:S(2)}) async-start(), calls=%async_computation.11 | async-start | bytes 4866048 | tf_op jit(solution)/shard_map/all_gather | solution.py:592
  61.5 21.1 %copy-start.2 = (f32[1,768]{1,0:T(1,128)}, f32[1,768]{1,0:T(1,128)S(1)}, u32[]{:S(2)}) copy-start(f32[1,768]{1,0:T(1,128)S(1)} %reshape.112.gain_ref) | copy-start | bytes 9220
  74.5 1.1 copy-start
  81.8 0.9 copy-start.1
  82.7 4.8 copy-start.8
  82.7 93.8 %all-to-all-start = ((bf16[16,3,256,128]{3,2,1,0:T(8,128)(2,1)}), bf16[16,3,256,128]{3,2,1,0:T(8,128)(2,1)}, u32[]{:S(2)}, u32[]{:S(2)}) async-start(bf16[16,3,256,128]{3,2,1,0:T(8,128)(2,1)} %get-tuple-element.31), calls=%async_computation | async-start | bytes 6291456 | tf_op jit(solution)/shard_map/all_to_all | solution.py:600
  228.7 73.6 %all-to-all-start.1 = ((bf16[16,256,128]{2,1,0:T(8,128)(2,1)}), bf16[16,256,128]{2,1,0:T(8,128)(2,1)S(1)}, u32[]{:S(2)}, u32[]{:S(2)}) async-start(bf16[16,256,128]{2,1,0:T(8,128)(2,1)} %bitcast.3), calls=%async_computation.1 | async-start | bytes 2097152 | tf_op jit(solution)/shard_map/all_to_all | solution.py:600
  245.8 385.3 %reduce-scatter.5.cloned.1.call-start = ((), (), s32[]{:S(2)}) async-start(), calls=%async_computation.12 | async-start | bytes 7299072 | tf_op jit(solution)/shard_map/reduce_scatter | solution.py:596
  302.2 1.0 copy-start.3
  513.4 222.7 %reduce-scatter.7.cloned.1.call-start = ((), (), s32[]{:S(2)}) async-start(), calls=%async_computation.13 | async-start | bytes 2433024 | tf_op jit(solution)/shard_map/reduce_scatter | solution.py:596
  513.9 363.1 %reduce-scatter.11.cloned.1.call-start = ((), (), s32[]{:S(2)}) async-start(), calls=%async_computation.15 | async-start | bytes 9732096 | tf_op jit(solution)/shard_map/reduce_scatter | solution.py:596
  514.7 504.5 %reduce-scatter.9.cloned.1.call-start = ((), (), s32[]{:S(2)}) async-start(), calls=%async_computation.14 | async-start | bytes 9732096 | tf_op jit(solution)/shard_map/reduce_scatter | solution.py:596
  514.7 0.7 copy-start.4
  514.7 1.6 copy-start.5
  514.7 2.4 copy-start.6
  514.8 2.7 copy-start.7
Sparse Core Ops, SparseCore 0:
  11.5 63.0 all-gather.5
  77.4 87.4 all-gather.7
  167.8 65.0 all-gather.9
  235.6 66.5 all-gather.11
  513.5 117.5 reduce-scatter.4
  637.7 98.2 reduce-scatter.6
  742.5 134.4 reduce-scatter.10
  884.5 134.6 reduce-scatter.8

commit v2 on v1

--- a/solution.py
+++ b/solution.py
@@ -612,7 +612,7 @@
     return jnp.concatenate([w_qkv[:, :D], jnp.swapaxes(sides, 1, 2).reshape(rows, 2 * D)], axis=1)
 
 
-def shards(
+def general_shards(
     hidden_in,
     rand_table,
     norm1_gain,
@@ -722,6 +722,1492 @@
     )
 
 
+MESH = pl.DeviceIdType.MESH
+ANY = pl.ANY
+PLANES = 4
+SPOTS = 4
+PIECES = 2
+RANKS = 2 * PLANES * SPOTS
+TILES = 3 * D // LANES
+HALF_TILES = TILES // 2
+QUERY_ORDER = (0, 2, 3, 5, 6, 8, 9, 11, 1, 4, 7, 10)
+
+
+def column_order():
+    order = [("q", head) for head in QUERY_ORDER]
+    for spot in range(SPOTS):
+        for place in (2 * 3 * spot, 2 * 3 * spot + 2):
+            order += [("k", place // 2), ("v", place // 2)]
+        order += [("v", 3 * spot + 2), ("k", 3 * spot + 2)]
+    return order
+
+
+def natural_block(entry):
+    return "qkv".index(entry[0]) * HEADS + entry[1]
+
+
+def take_blocks(array, order):
+    parts = []
+    start = 0
+    while start < len(order):
+        stop = start + 1
+        while stop < len(order) and order[stop] == order[stop - 1] + 1:
+            stop += 1
+        parts.append(array[..., order[start] * HEAD_DIM : (order[start] + stop - start) * HEAD_DIM])
+        start = stop
+    return jnp.concatenate(parts, axis=-1)
+
+
+def flip(value, bits):
+    if bits == 0:
+        return value
+    if bits == 1:
+        return value + 1 - 2 * lax.rem(value, 2)
+    if bits == 2:
+        return value + 2 - 4 * lax.div(value, 2)
+    return 3 - value
+
+
+def place_here():
+    core, rank = lax.axis_index("gx"), lax.axis_index("gy")
+    return core, lax.div(rank, SPOTS), lax.rem(rank, SPOTS)
+
+
+def rank_of(plane, spot):
+    return plane * SPOTS + spot
+
+
+def greet(partners):
+    barrier = pltpu.get_barrier_semaphore()
+    for partner in partners:
+        pl.semaphore_signal(barrier, inc=1, device_id=partner, device_id_type=MESH)
+    pl.semaphore_wait(barrier, len(partners))
+
+
+def remote(source, target, send_sem, recv_sem, device):
+    return pltpu.make_async_remote_copy(
+        src_ref=source,
+        dst_ref=target,
+        send_sem=send_sem,
+        recv_sem=recv_sem,
+        device_id=device,
+        device_id_type=MESH,
+    )
+
+
+def column_partners(core, plane, spot):
+    partners = [(1 - core, rank_of(plane, spot))]
+    for bits in range(1, PLANES):
+        for other in (core, 1 - core):
+            partners.append((other, rank_of(flip(plane, bits), spot)))
+    return partners
+
+
+def all_partners(core, plane, spot):
+    return column_partners(core, plane, spot) + [
+        (core, rank_of(plane, flip(spot, 1))),
+        (core, rank_of(plane, flip(spot, 2))),
+    ]
+
+
+def to_planes(source, target, send_sem, recv_sem, local_sem):
+    core, plane, spot = place_here()
+    half, odd = lax.div(plane, 2), lax.rem(plane, 2)
+    sends, keeps = [], []
+    for micro in range(2):
+        goal = 2 * micro + core
+        here = (goal == plane) & (half == core)
+        send = remote(
+            source.at[micro],
+            target.at[odd],
+            send_sem.at[micro],
+            recv_sem.at[odd],
+            (half, rank_of(goal, spot)),
+        )
+        keep = pltpu.make_async_copy(source.at[micro], target.at[odd], local_sem.at[micro])
+
+        @pl.when(jnp.logical_not(here))
+        def _(send=send):
+            send.start()
+
+        @pl.when(here)
+        def _(keep=keep):
+            keep.start()
+
+        sends.append((here, send))
+        keeps.append((here, keep))
+
+    def finish():
+        for piece in range(PIECES):
+            mine = (odd == core) & (plane == 2 * core + piece)
+            arrival = remote(
+                source.at[0],
+                target.at[piece],
+                send_sem.at[0],
+                recv_sem.at[piece],
+                (core, rank_of(plane, spot)),
+            )
+
+            @pl.when(jnp.logical_not(mine))
+            def _(arrival=arrival):
+                arrival.wait_recv()
+
+        for (here, send), (_, keep) in zip(sends, keeps):
+
+            @pl.when(jnp.logical_not(here))
+            def _(send=send):
+                send.wait_send()
+
+            @pl.when(here)
+            def _(keep=keep):
+                keep.wait()
+
+    return finish
+
+
+def from_planes(source, target, send_sem, recv_sem, local_sem):
+    core, plane, spot = place_here()
+    micro, odd = lax.div(plane, 2), lax.rem(plane, 2)
+    sends, keeps = [], []
+    for piece in range(PIECES):
+        goal = 2 * core + piece
+        here = (goal == plane) & (odd == core)
+        send = remote(
+            source.at[piece],
+            target.at[micro],
+            send_sem.at[piece],
+            recv_sem.at[micro],
+            (odd, rank_of(goal, spot)),
+        )
+        keep = pltpu.make_async_copy(source.at[piece], target.at[micro], local_sem.at[piece])
+
+        @pl.when(jnp.logical_not(here))
+        def _(send=send):
+            send.start()
+
+        @pl.when(here)
+        def _(keep=keep):
+            keep.start()
+
+        sends.append((here, send))
+        keeps.append((here, keep))
+
+    def finish():
+        for number in range(2):
+            mine = (2 * number + core == plane) & (micro == core)
+            arrival = remote(
+                source.at[0],
+                target.at[number],
+                send_sem.at[0],
+                recv_sem.at[number],
+                (core, rank_of(plane, spot)),
+            )
+
+            @pl.when(jnp.logical_not(mine))
+            def _(arrival=arrival):
+                arrival.wait_recv()
+
+        for (here, send), (_, keep) in zip(sends, keeps):
+
+            @pl.when(jnp.logical_not(here))
+            def _(send=send):
+                send.wait_send()
+
+            @pl.when(here)
+            def _(keep=keep):
+                keep.wait()
+
+    return finish
+
+
+class Gather:
+    SENDS = 31
+
+    def __init__(self, source, target, send_sem, recv_sem, local_sem):
+        self.source, self.target = source, target
+        self.send_sem, self.recv_sem = send_sem, recv_sem
+        self.core, self.plane, self.spot = place_here()
+        self.sends = []
+        self.own = pltpu.make_async_copy(
+            source, target.at[self.core, self.plane, self.spot], local_sem
+        )
+        self.own.start()
+
+    def send(self, source, plane, spot, device):
+        copy = remote(
+            source,
+            self.target.at[self.core, plane, spot],
+            self.send_sem.at[len(self.sends)],
+            self.recv_sem.at[self.core, plane, spot],
+            device,
+        )
+        copy.start()
+        self.sends.append(copy)
+
+    def arrive(self, core, plane, spot):
+        shard = self.target.at[core, plane, spot]
+        remote(
+            shard,
+            shard,
+            self.send_sem.at[0],
+            self.recv_sem.at[core, plane, spot],
+            (self.core, rank_of(self.plane, self.spot)),
+        ).wait_recv()
+
+    def neighbour(self, bits):
+        return (self.core, rank_of(self.plane, flip(self.spot, bits)))
+
+    def sibling(self):
+        return (1 - self.core, rank_of(self.plane, self.spot))
+
+    def start(self):
+        for bits in range(1, PLANES):
+            goal = (self.core, rank_of(flip(self.plane, bits), self.spot))
+            self.send(self.source, self.plane, self.spot, goal)
+        for goal in (self.neighbour(1), self.neighbour(2), self.sibling()):
+            self.send(self.source, self.plane, self.spot, goal)
+
+    def column(self):
+        for bits in range(1, PLANES):
+            plane = flip(self.plane, bits)
+            self.arrive(self.core, plane, self.spot)
+            shard = self.target.at[self.core, plane, self.spot]
+            for goal in (self.neighbour(1), self.neighbour(2), self.sibling()):
+                self.send(shard, plane, self.spot, goal)
+
+    def across(self):
+        for bits in range(PLANES):
+            plane = flip(self.plane, bits)
+            for side in (1, 2):
+                spot = flip(self.spot, side)
+                self.arrive(self.core, plane, spot)
+                shard = self.target.at[self.core, plane, spot]
+                if (side == 1) == (bits < 2):
+                    self.send(shard, plane, spot, self.neighbour(3 - side))
+                self.send(shard, plane, spot, self.sibling())
+
+    def corner(self):
+        spot = flip(self.spot, 3)
+        for bits in range(PLANES):
+            plane = flip(self.plane, bits)
+            self.arrive(self.core, plane, spot)
+            self.send(self.target.at[self.core, plane, spot], plane, spot, self.sibling())
+
+    def finish(self):
+        for bits in range(PLANES):
+            for side in range(SPOTS):
+                self.arrive(1 - self.core, flip(self.plane, bits), flip(self.spot, side))
+        self.own.wait()
+        for copy in self.sends:
+            copy.wait_send()
+
+
+def settle(shards_ref, out_ref, tiles_of):
+    rows = shards_ref.shape[3] // 2
+    width = shards_ref.shape[4]
+
+    def pair(number, carry):
+        core, plane, side = (
+            lax.div(number, 2 * PLANES),
+            lax.rem(lax.div(number, 2), PLANES),
+            lax.rem(number, 2),
+        )
+        goal = pl.ds(pl.multiple_of(number * 2 * rows, 16), 2 * rows)
+        for tile in range(width // LANES):
+            columns = slice(tile * LANES, (tile + 1) * LANES)
+            first = shards_ref[core, plane, 2 * side, :, columns].astype(F32)
+            second = shards_ref[core, plane, 2 * side + 1, :, columns].astype(F32)
+            left, right = tiles_of(tile)
+            out_ref[goal, left * LANES : (left + 1) * LANES] = jnp.concatenate(
+                [first[:rows], second[:rows]], axis=0
+            ).astype(BF16)
+            out_ref[goal, right * LANES : (right + 1) * LANES] = jnp.concatenate(
+                [first[rows:], second[rows:]], axis=0
+            ).astype(BF16)
+        return carry
+
+    lax.fori_loop(0, RANKS // 2, pair, 0)
+
+
+def alternate(tile):
+    return 2 * tile, 2 * tile + 1
+
+
+def in_order(tile):
+    return tile, D // LANES // 2 + tile
+
+
+def collect_kernel(
+    x_ref,
+    dy_ref,
+    vec_ref,
+    s_qkv_ref,
+    s_out_ref,
+    s_up_ref,
+    s_down_ref,
+    xs_ref,
+    dys_ref,
+    vecs_ref,
+    w_qkv_ref,
+    w_out_ref,
+    w_up_ref,
+    w_down_ref,
+    g_qkv_ref,
+    g_out_ref,
+    g_up_ref,
+    send_sem,
+    recv_sem,
+    local_sem,
+    move_send,
+    move_recv,
+    move_local,
+):
+    core, plane, spot = place_here()
+    greet(all_partners(core, plane, spot))
+    pairs = (
+        (vec_ref, vecs_ref),
+        (s_qkv_ref, g_qkv_ref),
+        (s_out_ref, g_out_ref),
+        (s_up_ref, g_up_ref),
+        (s_down_ref, w_down_ref),
+    )
+    finish_x = to_planes(x_ref, xs_ref, move_send.at[0], move_recv.at[0], move_local.at[0])
+    gathers = []
+    for number, (source, target) in enumerate(pairs):
+        one = Gather(
+            source, target, send_sem.at[number], recv_sem.at[number], local_sem.at[number]
+        )
+        one.start()
+        gathers.append(one)
+    finish_dy = to_planes(dy_ref, dys_ref, move_send.at[1], move_recv.at[1], move_local.at[1])
+    for one in gathers:
+        one.column()
+    for one in gathers:
+        one.across()
+    for one in gathers:
+        one.corner()
+    for one in gathers:
+        one.finish()
+    settle(g_qkv_ref, w_qkv_ref, alternate)
+    settle(g_out_ref, w_out_ref, in_order)
+    settle(g_up_ref, w_up_ref, alternate)
+    finish_x()
+    finish_dy()
+
+
+def collect(x, dy, vec, s_qkv, s_out, s_up, s_down):
+    grid = (2, PLANES, SPOTS)
+    count = 5
+    return pl.pallas_call(
+        collect_kernel,
+        out_shape=(
+            jax.ShapeDtypeStruct(x.shape, BF16),
+            jax.ShapeDtypeStruct(dy.shape, BF16),
+            jax.ShapeDtypeStruct(grid + vec.shape, BF16),
+            jax.ShapeDtypeStruct((D, 3 * D), BF16),
+            jax.ShapeDtypeStruct((D, D), BF16),
+            jax.ShapeDtypeStruct((D, FF), BF16),
+            jax.ShapeDtypeStruct(grid + s_down.shape, BF16),
+        ),
+        in_specs=[whole(ANY)] * 7,
+        out_specs=(whole(ANY), whole(ANY), whole(ANY), whole(), whole(), whole(), whole(ANY)),
+        scratch_shapes=[
+            VMEM(grid + s_qkv.shape, BF16),
+            VMEM(grid + s_out.shape, BF16),
+            VMEM(grid + s_up.shape, BF16),
+            pltpu.SemaphoreType.DMA((count, Gather.SENDS)),
+            pltpu.SemaphoreType.DMA((count,) + grid),
+            pltpu.SemaphoreType.DMA((count,)),
+            pltpu.SemaphoreType.DMA((2, 2)),
+            pltpu.SemaphoreType.DMA((2, 2)),
+            pltpu.SemaphoreType.DMA((2, 2)),
+        ],
+        compiler_params=pltpu.CompilerParams(
+            vmem_limit_bytes=56 * 1024 * 1024, collective_id=1, has_side_effects=True
+        ),
+        name="collect",
+    )(x, dy, vec, s_qkv, s_out, s_up, s_down)
+
+
+def plane_partners(core, plane, spot):
+    partners = []
+    for other in (core, 1 - core):
+        for side in range(SPOTS):
+            if other is core and side == 0:
+                continue
+            partners.append((other, rank_of(plane, flip(spot, side))))
+    return partners
+
+
+def outward_kernel(source_ref, target_ref, send_sem, recv_sem, local_sem):
+    core, plane, spot = place_here()
+    greet(plane_partners(core, plane, spot))
+    sends, keeps = [], []
+    for side in (3, 1, 2, 0):
+        for other in (core, 1 - core):
+            goal = flip(spot, side)
+            for piece in range(PIECES):
+                source = source_ref.at[other, goal, piece]
+                target = target_ref.at[2 * core + piece, spot]
+                if side == 0 and other is core:
+                    copy = pltpu.make_async_copy(source, target, local_sem.at[piece])
+                    keeps.append(copy)
+                else:
+                    copy = remote(
+                        source,
+                        target,
+                        send_sem.at[len(sends)],
+                        recv_sem.at[2 * core + piece, spot],
+                        (other, rank_of(plane, goal)),
+                    )
+                    sends.append(copy)
+                copy.start()
+    for side in range(SPOTS):
+        for other in (core, 1 - core):
+            if side == 0 and other is core:
+                continue
+            for piece in range(PIECES):
+                target = target_ref.at[2 * other + piece, flip(spot, side)]
+                remote(
+                    target,
+                    target,
+                    send_sem.at[0],
+                    recv_sem.at[2 * other + piece, flip(spot, side)],
+                    (core, rank_of(plane, spot)),
+                ).wait_recv()
+    for copy in sends:
+        copy.wait_send()
+    for copy in keeps:
+        copy.wait()
+
+
+def inward_kernel(source_ref, target_ref, send_sem, recv_sem, local_sem):
+    core, plane, spot = place_here()
+    greet(plane_partners(core, plane, spot))
+    sends, keeps = [], []
+    for side in (3, 1, 2, 0):
+        for other in (core, 1 - core):
+            goal = flip(spot, side)
+            for piece in range(PIECES):
+                source = source_ref.at[2 * other + piece, goal]
+                target = target_ref.at[core, spot, piece]
+                if side == 0 and other is core:
+                    copy = pltpu.make_async_copy(source, target, local_sem.at[piece])
+                    keeps.append(copy)
+                else:
+                    copy = remote(
+                        source,
+                        target,
+                        send_sem.at[len(sends)],
+                        recv_sem.at[core, spot, piece],
+                        (other, rank_of(plane, goal)),
+                    )
+                    sends.append(copy)
+                copy.start()
+    for side in range(SPOTS):
+        for other in (core, 1 - core):
+            if side == 0 and other is core:
+                continue
+            for piece in range(PIECES):
+                target = target_ref.at[other, flip(spot, side), piece]
+                remote(
+                    target,
+                    target,
+                    send_sem.at[0],
+                    recv_sem.at[other, flip(spot, side), piece],
+                    (core, rank_of(plane, spot)),
+                ).wait_recv()
+    for copy in sends:
+        copy.wait_send()
+    for copy in keeps:
+        copy.wait()
+
+
+def plane_exchange(kernel, source, shape, recv_shape, collective, name):
+    return pl.pallas_call(
+        kernel,
+        out_shape=jax.ShapeDtypeStruct(shape, source.dtype),
+        in_specs=[whole(ANY)],
+        out_specs=whole(ANY),
+        scratch_shapes=[
+            pltpu.SemaphoreType.DMA((14,)),
+            pltpu.SemaphoreType.DMA(recv_shape),
+            pltpu.SemaphoreType.DMA((PIECES,)),
+        ],
+        compiler_params=pltpu.CompilerParams(
+            vmem_limit_bytes=16 * 1024 * 1024, collective_id=collective, has_side_effects=True
+        ),
+        name=name,
+    )(source)
+
+
+def outward(source, collective, name):
+    shape = (PLANES, SPOTS) + source.shape[3:]
+    return plane_exchange(outward_kernel, source, shape, (PLANES, SPOTS), collective, name)
+
+
+def inward(source, collective, name):
+    shape = (2, SPOTS, PIECES) + source.shape[2:]
+    return plane_exchange(
+        inward_kernel, source, shape, (2, SPOTS, PIECES), collective, name
+    )
+
+
+def plane_qkv_kernel(x_ref, vec_ref, w_ref, bias_ref, normed_ref, send_ref):
+    pieces, rows, _ = x_ref.shape
+    values = x_ref[...].reshape(pieces * rows, D).astype(F32)
+    normal, _ = norm_parts(values)
+    normed_ref[...] = (normal * vec_ref[0:1] + vec_ref[1:2]).astype(BF16)
+    low = low_lanes(rows)
+    queries = D // LANES
+    for chunk in range(HALF_TILES):
+        columns = slice(chunk * CHUNK, (chunk + 1) * CHUNK)
+        packed = dot(normed_ref[...], w_ref[:, columns]) + bias_ref[:, columns]
+        for side in range(2):
+            tile = chunk + side * HALF_TILES
+            whole_tile = packed[:, side * LANES : (side + 1) * LANES]
+            if tile < queries:
+                whole_tile = whole_tile.astype(BF16).astype(F32) * SCALE
+            for piece in range(pieces):
+                part = whole_tile[piece * rows : (piece + 1) * rows]
+                if tile < SPOTS:
+                    send_ref[0, tile, piece, 0] = part.astype(BF16)
+                elif tile < queries:
+                    first = 2 * (tile - SPOTS)
+                    shared = send_ref[0, first, piece, 0].astype(F32)
+                    send_ref[1, first, piece, 0] = jnp.where(low, part, shared).astype(BF16)
+                    shared = send_ref[0, first + 1, piece, 0].astype(F32)
+                    send_ref[1, first + 1, piece, 0] = jnp.where(
+                        low, swap_halves(part), shared
+                    ).astype(BF16)
+                else:
+                    spot, role = (tile - queries) // 3, (tile - queries) % 3
+                    if role < 2:
+                        send_ref[role, spot, piece, 1] = part.astype(BF16)
+                    else:
+                        send_ref[0, spot, piece, 2] = part.astype(BF16)
+                        send_ref[1, spot, piece, 2] = part.astype(BF16)
+
+
+def plane_qkv(x, vec, w, bias):
+    pieces, rows, _ = x.shape
+    return pl.pallas_call(
+        plane_qkv_kernel,
+        out_shape=(
+            jax.ShapeDtypeStruct((pieces * rows, D), BF16),
+            jax.ShapeDtypeStruct((2, SPOTS, PIECES, 3, rows, LANES), BF16),
+        ),
+        in_specs=[whole()] * 4,
+        out_specs=(whole(), whole()),
+        compiler_params=params_of(48),
+        name="plane_qkv",
+    )(x, vec, w, bias)
+
+
+def plane_attend_kernel(table_ref, qkv_ref, out_ref, lse_ref, s_ref, t_ref):
+    groups, _, local, _, _ = qkv_ref.shape
+    blocks = groups * local
+    half = blocks // 2
+    core = lax.axis_index("gx")
+    low = low_lanes(BLOCK)
+    masks = [half_mask(True), half_mask(False)]
+
+    def load(component, block):
+        return qkv_ref[lax.div(block, local), component, lax.rem(block, local)]
+
+    def store(block, value):
+        out_ref[lax.div(block, local), lax.rem(block, local)] = value.astype(BF16)
+
+    def one(block, slot, ids, bias):
+        keys = jnp.concatenate([load(1 + slot, spot) for spot in ids], axis=0)
+        scores = dot_rt(load(0, block) * masks[slot], keys) + bias
+        top = jnp.max(scores, axis=1, keepdims=True)
+        powered = jnp.exp(scores - top)
+        total = jnp.sum(powered, axis=1, keepdims=True)
+        mixed = dot(powered.astype(BF16), keys) * (1.0 / total)
+        return mixed, top + jnp.log(total)
+
+    def sparse(step, carry):
+        mine = 1 + step + core * (half - 1)
+        other = 1 + step + (1 - core) * (half - 1)
+        ids, bias = slots_of(table_ref, 0, mine, blocks)
+        far_ids, far_bias = slots_of(table_ref, 0, other, blocks)
+        mixed_a, log_a = one(mine, 0, ids, bias)
+        mixed_b, log_b = one(mine, 1, ids, bias)
+        mixed_c, log_c = one(other, 0, far_ids, far_bias)
+        store(mine, jnp.where(low, mixed_b, mixed_a))
+        store(other, mixed_c)
+        lse_ref[mine] = jnp.where(low, log_a, log_b)
+        lse_ref[other] = jnp.where(low, log_c, 0.0)
+        return carry
+
+    lax.fori_loop(0, half - 1, sparse, 0)
+
+    spans = blocks // SPAN
+    ends = (0, blocks - 1)
+    end = core * (blocks - 1)
+    query_a = jnp.concatenate([load(0, number) for number in ends], axis=0) * masks[0]
+    query_b = load(0, end) * masks[1]
+
+    def keys_at(span, slot):
+        return jnp.concatenate(
+            [load(1 + slot, span * SPAN + number) for number in range(SPAN)], axis=0
+        )
+
+    def first_pass(span, carry):
+        top_a, top_b = carry
+        scores_a = dot_rt(query_a, keys_at(span, 0))
+        scores_b = dot_rt(query_b, keys_at(span, 1))
+        s_ref[span] = scores_a
+        t_ref[span] = scores_b
+        return (
+            jnp.maximum(top_a, jnp.max(scores_a, axis=1, keepdims=True)),
+            jnp.maximum(top_b, jnp.max(scores_b, axis=1, keepdims=True)),
+        )
+
+    top_a, top_b = lax.fori_loop(
+        0,
+        spans,
+        first_pass,
+        (jnp.full((2 * BLOCK, 1), NEGATIVE, F32), jnp.full((BLOCK, 1), NEGATIVE, F32)),
+    )
+
+    def second_pass(span, carry):
+        total_a, mixed_a, total_b, mixed_b = carry
+        powered_a = jnp.exp(s_ref[span] - top_a)
+        powered_b = jnp.exp(t_ref[span] - top_b)
+        return (
+            total_a + jnp.sum(powered_a, axis=1, keepdims=True),
+            mixed_a + dot(powered_a.astype(BF16), keys_at(span, 0)),
+            total_b + jnp.sum(powered_b, axis=1, keepdims=True),
+            mixed_b + dot(powered_b.astype(BF16), keys_at(span, 1)),
+        )
+
+    total_a, mixed_a, total_b, mixed_b = lax.fori_loop(
+        0,
+        spans,
+        second_pass,
+        (
+            jnp.zeros((2 * BLOCK, 1), F32),
+            jnp.zeros((2 * BLOCK, LANES), F32),
+            jnp.zeros((BLOCK, 1), F32),
+            jnp.zeros((BLOCK, LANES), F32),
+        ),
+    )
+    mixed_a = mixed_a * (1.0 / total_a)
+    mixed_b = mixed_b * (1.0 / total_b)
+    log_a = top_a + jnp.log(total_a)
+    log_b = top_b + jnp.log(total_b)
+    for place, number in enumerate(ends):
+        rows = slice(place * BLOCK, (place + 1) * BLOCK)
+        store(number, jnp.where(low, mixed_b, mixed_a[rows]))
+        lse_ref[number] = jnp.where(low, log_a[rows], log_b)
+
+
+def plane_attention(table, qkv):
+    groups, _, local, _, _ = qkv.shape
+    blocks = groups * local
+    spans = blocks // SPAN
+    return pl.pallas_call(
+        plane_attend_kernel,
+        out_shape=(
+            jax.ShapeDtypeStruct((groups, local, BLOCK, LANES), BF16),
+            jax.ShapeDtypeStruct((blocks, BLOCK, LANES), F32),
+        ),
+        in_specs=[whole(pltpu.SMEM), whole()],
+        out_specs=(whole(), whole()),
+        scratch_shapes=[
+            VMEM((spans, 2 * BLOCK, SPAN * BLOCK), F32),
+            VMEM((spans, BLOCK, SPAN * BLOCK), F32),
+        ],
+        compiler_params=params_of(48),
+        name="plane_attention",
+    )(table, qkv)
+
+
+def plane_attend_back_kernel(
+    table_ref, qkv_ref, grad_ref, lse_ref, out_ref, sums_ref, pa_ref, da_ref, pb_ref, db_ref
+):
+    groups, _, local, _, _ = qkv_ref.shape
+    blocks = groups * local
+    half = blocks // 2
+    core = lax.axis_index("gx")
+    low = low_lanes(BLOCK)
+    masks = [half_mask(True), half_mask(False)]
+
+    def load(component, block):
+        return qkv_ref[lax.div(block, local), component, lax.rem(block, local)]
+
+    def load_grad(block):
+        return grad_ref[lax.div(block, local), lax.rem(block, local)]
+
+    def store(component, block, value):
+        out_ref[lax.div(block, local), component, lax.rem(block, local)] = value.astype(BF16)
+
+    def clear(block, carry):
+        for slot in range(2):
+            sums_ref[slot, block] = jnp.zeros((BLOCK, LANES), F32)
+        return carry
+
+    lax.fori_loop(0, blocks, clear, 0)
+
+    def one(block, slot, ids, bias):
+        keys = jnp.concatenate([load(1 + slot, spot) for spot in ids], axis=0)
+        both = jnp.concatenate(
+            [load(0, block) * masks[slot], load_grad(block) * masks[1 - slot]], axis=0
+        )
+        products = dot_rt(both, keys)
+        logs = lse_ref[block][:, slot * HEAD_DIM : slot * HEAD_DIM + 1]
+        weights = jnp.exp(products[:BLOCK] + bias - logs)
+        grad_weights = products[BLOCK:]
+        delta = jnp.sum(weights * grad_weights, axis=1, keepdims=True)
+        grad_scores = weights * (grad_weights - delta)
+        stacked = jnp.concatenate([grad_scores, weights], axis=0).astype(BF16)
+        return dot(stacked[:BLOCK], keys), dot_lt(stacked, both)
+
+    def add(slot, ids, shares):
+        for place, spot in enumerate(ids):
+            sums_ref[slot, spot] += shares[place * BLOCK : (place + 1) * BLOCK]
+
+    def sparse(step, carry):
+        mine = 1 + step + core * (half - 1)
+        other = 1 + step + (1 - core) * (half - 1)
+        ids, bias = slots_of(table_ref, 0, mine, blocks)
+        far_ids, far_bias = slots_of(table_ref, 0, other, blocks)
+        query_a, shares_a = one(mine, 0, ids, bias)
+        query_b, shares_b = one(mine, 1, ids, bias)
+        query_c, shares_c = one(other, 0, far_ids, far_bias)
+        store(0, mine, jnp.where(low, query_a, query_b) * SCALE)
+        store(0, other, query_c * SCALE)
+        add(0, ids, shares_a)
+        add(1, ids, shares_b)
+        add(0, far_ids, shares_c)
+        return carry
+
+    lax.fori_loop(0, half - 1, sparse, 0)
+
+    spans = blocks // SPAN
+    ends = (0, blocks - 1)
+    end = core * (blocks - 1)
+    both_a = jnp.concatenate(
+        [load(0, number) * masks[0] for number in ends]
+        + [load_grad(number) * masks[1] for number in ends],
+        axis=0,
+    )
+    both_b = jnp.concatenate([load(0, end) * masks[1], load_grad(end) * masks[0]], axis=0)
+    logs_a = jnp.concatenate([lse_ref[number][:, 0:1] for number in ends], axis=0)
+    logs_b = lse_ref[end][:, HEAD_DIM : HEAD_DIM + 1]
+
+    def keys_at(span, slot):
+        return jnp.concatenate(
+            [load(1 + slot, span * SPAN + number) for number in range(SPAN)], axis=0
+        )
+
+    def first_pass(span, carry):
+        deltas = []
+        for slot, both, logs, p_ref, d_ref in (
+            (0, both_a, logs_a, pa_ref, da_ref),
+            (1, both_b, logs_b, pb_ref, db_ref),
+        ):
+            rows = both.shape[0] // 2
+            products = dot_rt(both, keys_at(span, slot))
+            weights = jnp.exp(products[:rows] - logs)
+            grad_weights = products[rows:]
+            p_ref[span] = weights
+            d_ref[span] = grad_weights
+            deltas.append(carry[slot] + jnp.sum(weights * grad_weights, axis=1, keepdims=True))
+        return tuple(deltas)
+
+    deltas = lax.fori_loop(
+        0, spans, first_pass, (jnp.zeros((2 * BLOCK, 1), F32), jnp.zeros((BLOCK, 1), F32))
+    )
+
+    def second_pass(span, carry):
+        totals = []
+        for slot, both, p_ref, d_ref in (
+            (0, both_a, pa_ref, da_ref),
+            (1, both_b, pb_ref, db_ref),
+        ):
+            rows = both.shape[0] // 2
+            weights = p_ref[span]
+            grad_scores = weights * (d_ref[span] - deltas[slot])
+            stacked = jnp.concatenate([grad_scores, weights], axis=0).astype(BF16)
+            add(slot, [span * SPAN + number for number in range(SPAN)], dot_lt(stacked, both))
+            totals.append(carry[slot] + dot(stacked[:rows], keys_at(span, slot)))
+        return tuple(totals)
+
+    query_a, query_b = lax.fori_loop(
+        0,
+        spans,
+        second_pass,
+        (jnp.zeros((2 * BLOCK, LANES), F32), jnp.zeros((BLOCK, LANES), F32)),
+    )
+    for place, number in enumerate(ends):
+        rows = slice(place * BLOCK, (place + 1) * BLOCK)
+        store(0, number, jnp.where(low, query_a[rows], query_b) * SCALE)
+
+    def finish(block, carry):
+        for slot in range(2):
+            store(1 + slot, block, sums_ref[slot, block])
+        return carry
+
+    lax.fori_loop(0, blocks, finish, 0)
+
+
+def plane_attention_back(table, qkv, grad, lse):
+    groups, _, local, _, _ = qkv.shape
+    blocks = groups * local
+    spans = blocks // SPAN
+    wide = VMEM((spans, 2 * BLOCK, SPAN * BLOCK), F32)
+    thin = VMEM((spans, BLOCK, SPAN * BLOCK), F32)
+    return pl.pallas_call(
+        plane_attend_back_kernel,
+        out_shape=jax.ShapeDtypeStruct(qkv.shape, BF16),
+        in_specs=[whole(pltpu.SMEM), whole(), whole(), whole()],
+        out_specs=whole(),
+        scratch_shapes=[VMEM((2, blocks, BLOCK, LANES), F32), wide, wide, thin, thin],
+        compiler_params=params_of(48),
+        name="plane_attention_back",
+    )(table, qkv, grad, lse)
+
+
+def by_owner(out_ref, values):
+    rows = D // RANKS
+    width = values.shape[1] // 2
+    for owner in range(RANKS):
+        part = values[owner * rows : (owner + 1) * rows]
+        out_ref[owner] = jnp.concatenate([part[:, :width], part[:, width:]], axis=0).astype(BF16)
+
+
+def plane_middle_kernel(
+    mixed_in_ref,
+    x_ref,
+    dy_ref,
+    vec_ref,
+    w_out_ref,
+    up_shift_ref,
+    w_up_ref,
+    w_down_ref,
+    hidden_ref,
+    send_ref,
+    dres_ref,
+    g_out_ref,
+    g_up_ref,
+    g_down_ref,
+    g_up_bias_ref,
+    g_small_ref,
+    mixed_ref,
+    residual_ref,
+    second_ref,
+    second_t_ref,
+    total_ref,
+    dsecond_ref,
+):
+    pieces, rows, _ = x_ref.shape
+    tokens = pieces * rows
+    step = pl.program_id(0)
+    low = low_lanes(rows)
+    out_shift, gain, shift, down_shift = (vec_ref[number : number + 1] for number in (4, 5, 6, 7))
+
+    @pl.when(step == 0)
+    def _():
+        core = lax.axis_index("gx")
+        for piece in range(pieces):
+            span = slice(piece * rows, (piece + 1) * rows)
+            for spot in (0, 2):
+                first = [mixed_in_ref[side, spot, piece].astype(F32) for side in range(2)]
+                last = [mixed_in_ref[side, spot + 1, piece].astype(F32) for side in range(2)]
+                own_first = jnp.where(core == 0, first[0], first[1])
+                own_last = jnp.where(core == 0, last[0], last[1])
+                tiles = (
+                    jnp.where(low, swap_halves(first[0]), first[1]),
+                    jnp.where(low, own_first, last[0]),
+                    swap_halves(jnp.where(low, own_last, last[1])),
+                )
+                for number, tile in enumerate(tiles):
+                    spread = 3 * (spot // 2) + number
+                    mixed_ref[span, spread * LANES : (spread + 1) * LANES] = tile.astype(BF16)
+        residual = x_ref[...].reshape(tokens, D).astype(F32) + (
+            dot(mixed_ref[...], w_out_ref[...]) + out_shift
+        )
+        residual_ref[...] = residual
+        normal, _ = norm_parts(residual)
+        second = normal * gain + shift
+        second_ref[...] = second.astype(BF16)
+        second_t_ref[...] = second.T.astype(BF16)
+        total_ref[...] = jnp.zeros_like(total_ref)
+        dsecond_ref[...] = jnp.zeros_like(dsecond_ref)
+
+    w_down = w_down_ref[...].reshape(CHUNK, D)
+    upper = dot(second_ref[...], w_up_ref[...]) + up_shift_ref[0]
+    factor = 0.7978845608028654
+    square = upper * upper
+    bent = jnp.tanh(factor * (upper + 0.044715 * (upper * square)))
+    middle_half = 0.5 * (1.0 + bent)
+    active = (upper * middle_half).astype(BF16)
+    slope = middle_half + 0.5 * upper * (1.0 - bent * bent) * (
+        factor + (3.0 * 0.044715 * factor) * square
+    )
+    dy = dy_ref[...]
+    total_ref[...] += dot(active, w_down)
+    g_down_ref[...] = dot_lt(active, dy).astype(BF16).reshape(g_down_ref.shape)
+    dupper = (dot_rt(dy, w_down) * slope).astype(BF16)
+    g_up_bias_ref[0] = jnp.sum(dupper.astype(F32), axis=0, keepdims=True)
+    by_owner(g_up_ref, dot(second_t_ref[...], dupper))
+    dsecond_ref[...] += dot_rt(dupper, w_up_ref[...])
+
+    @pl.when(step == pl.num_programs(0) - 1)
+    def _():
+        residual = residual_ref[...]
+        hidden_ref[...] = (
+            (residual + (total_ref[...] + down_shift)).astype(BF16).reshape(x_ref.shape)
+        )
+        normal, inverse = norm_parts(residual)
+        dsecond = dsecond_ref[...]
+        grad_out = dy_ref[...].astype(F32)
+        g_small_ref[0:1] = jnp.sum(dsecond * normal, axis=0, keepdims=True)
+        g_small_ref[1:2] = jnp.sum(dsecond, axis=0, keepdims=True)
+        g_small_ref[2:3] = jnp.sum(grad_out, axis=0, keepdims=True)
+        dres = grad_out + norm_pull(dsecond, normal, inverse, gain)
+        dres_ref[...] = dres
+        branch = dres.astype(BF16)
+        g_small_ref[3:4] = jnp.sum(branch.astype(F32), axis=0, keepdims=True)
+        by_owner(g_out_ref, dot_lt(mixed_ref[...], branch))
+        dmixed = dot_rt(branch, w_out_ref[...])
+        for piece in range(pieces):
+            span = slice(piece * rows, (piece + 1) * rows)
+            for spot in (0, 2):
+                tiles = [
+                    dmixed[span, number * LANES : (number + 1) * LANES]
+                    for number in range(3 * (spot // 2), 3 * (spot // 2) + 3)
+                ]
+                flipped = [swap_halves(tile) for tile in tiles]
+                send_ref[0, spot, piece] = jnp.where(low, tiles[1], flipped[0]).astype(BF16)
+                send_ref[1, spot, piece] = jnp.where(low, tiles[1], tiles[0]).astype(BF16)
+                send_ref[0, spot + 1, piece] = jnp.where(low, flipped[2], tiles[1]).astype(BF16)
+                send_ref[1, spot + 1, piece] = flipped[2].astype(BF16)
+
+
+def plane_middle(mixed_in, x, dy, vec, w_out, up_shift, w_up, w_down):
+    pieces, rows, _ = x.shape
+    tokens = pieces * rows
+    shard = D // RANKS
+
+    def fixed(shape):
+        return pl.BlockSpec(shape, lambda step: (0,) * len(shape))
+
+    steps = FF // CHUNK
+    down = pl.BlockSpec((2, LANES, D), lambda step: (0, step, 0))
+    return pl.pallas_call(
+        plane_middle_kernel,
+        grid=(steps,),
+        out_shape=(
+            jax.ShapeDtypeStruct(x.shape, BF16),
+            jax.ShapeDtypeStruct(mixed_in.shape, BF16),
+            jax.ShapeDtypeStruct((tokens, D), F32),
+            jax.ShapeDtypeStruct((RANKS, 2 * shard, D // 2), BF16),
+            jax.ShapeDtypeStruct((RANKS, 2 * shard, FF // 2), BF16),
+            jax.ShapeDtypeStruct((2, FF // 2, D), BF16),
+            jax.ShapeDtypeStruct((steps, 1, CHUNK), F32),
+            jax.ShapeDtypeStruct((4, D), F32),
+        ),
+        in_specs=[
+            fixed(mixed_in.shape),
+            fixed(x.shape),
+            fixed((tokens, D)),
+            fixed(vec.shape),
+            fixed((D, D)),
+            pl.BlockSpec((1, 1, CHUNK), lambda step: (step, 0, 0)),
+            pl.BlockSpec((D, CHUNK), lambda step: (0, step)),
+            down,
+        ],
+        out_specs=(
+            fixed(x.shape),
+            fixed(mixed_in.shape),
+            fixed((tokens, D)),
+            fixed((RANKS, 2 * shard, D // 2)),
+            pl.BlockSpec((RANKS, 2 * shard, LANES), lambda step: (0, 0, step)),
+            down,
+            pl.BlockSpec((1, 1, CHUNK), lambda step: (step, 0, 0)),
+            fixed((4, D)),
+        ),
+        scratch_shapes=[
+            VMEM((tokens, D), BF16),
+            VMEM((tokens, D), F32),
+            VMEM((tokens, D), BF16),
+            VMEM((D, tokens), BF16),
+            VMEM((tokens, D), F32),
+            VMEM((tokens, D), F32),
+        ],
+        compiler_params=params_of(56),
+        name="plane_middle",
+    )(mixed_in, x, dy, vec, w_out, up_shift, w_up, w_down)
+
+
+def plane_qkv_back_kernel(
+    recv_ref,
+    normed_ref,
+    x_ref,
+    dres_ref,
+    vec_ref,
+    w_ref,
+    grad_ref,
+    g_qkv_ref,
+    g_bias_ref,
+    g_small_ref,
+    packed_ref,
+    normed_t_ref,
+    dnormed_ref,
+):
+    pieces, rows, _ = x_ref.shape
+    step = pl.program_id(0)
+    low = low_lanes(rows)
+
+    @pl.when(step == 0)
+    def _():
+        core = lax.axis_index("gx")
+
+        def put(tile, piece, value):
+            side, chunk = tile // HALF_TILES, tile % HALF_TILES
+            packed_ref[
+                chunk, piece * rows : (piece + 1) * rows, side * LANES : (side + 1) * LANES
+            ] = value.astype(BF16)
+
+        for piece in range(pieces):
+            seconds = []
+            for spot in range(SPOTS):
+                first = recv_ref[0, spot, piece, 0].astype(F32)
+                second = recv_ref[1, spot, piece, 0].astype(F32)
+                put(spot, piece, jnp.where(low, first, jnp.where(core == 0, first, second)))
+                seconds.append(second)
+                base = D // LANES + 3 * spot
+                put(base, piece, recv_ref[0, spot, piece, 1])
+                put(base + 1, piece, recv_ref[1, spot, piece, 1])
+                shared = recv_ref[0, spot, piece, 2].astype(F32) + recv_ref[
+                    1, spot, piece, 2
+                ].astype(F32)
+                put(base + 2, piece, shared)
+            for number in range(2):
+                put(
+                    SPOTS + number,
+                    piece,
+                    jnp.where(low, seconds[2 * number], swap_halves(seconds[2 * number + 1])),
+                )
+        normed_t_ref[...] = normed_ref[...].astype(F32).T.astype(BF16)
+        dnormed_ref[...] = jnp.zeros_like(dnormed_ref)
+
+    packed = packed_ref[step]
+    g_bias_ref[0] = jnp.sum(packed.astype(F32), axis=0, keepdims=True)
+    by_owner(g_qkv_ref, dot(normed_t_ref[...], packed))
+    dnormed_ref[...] += dot_rt(packed, w_ref[...])
+
+    @pl.when(step == pl.num_programs(0) - 1)
+    def _():
+        normal, inverse = norm_parts(x_ref[...].reshape(pieces * rows, D).astype(F32))
+        dnormed = dnormed_ref[...]
+        g_small_ref[0:1] = jnp.sum(dnormed * normal, axis=0, keepdims=True)
+        g_small_ref[1:2] = jnp.sum(dnormed, axis=0, keepdims=True)
+        grad = dres_ref[...] + norm_pull(dnormed, normal, inverse, vec_ref[0:1])
+        grad_ref[...] = grad.astype(BF16).reshape(x_ref.shape)
+
+
+def plane_qkv_back(recv, normed, x, dres, vec, w):
+    pieces, rows, _ = x.shape
+    tokens = pieces * rows
+    shard = D // RANKS
+
+    def fixed(shape):
+        return pl.BlockSpec(shape, lambda step: (0,) * len(shape))
+
+    return pl.pallas_call(
+        plane_qkv_back_kernel,
+        grid=(HALF_TILES,),
+        out_shape=(
+            jax.ShapeDtypeStruct(x.shape, BF16),
+            jax.ShapeDtypeStruct((RANKS, 2 * shard, 3 * D // 2), BF16),
+            jax.ShapeDtypeStruct((HALF_TILES, 1, CHUNK), F32),
+            jax.ShapeDtypeStruct((2, D), F32),
+        ),
+        in_specs=[
+            fixed(recv.shape),
+            fixed((tokens, D)),
+            fixed(x.shape),
+            fixed((tokens, D)),
+            fixed(vec.shape),
+            pl.BlockSpec((D, CHUNK), lambda step: (0, step)),
+        ],
+        out_specs=(
+            fixed(x.shape),
+            pl.BlockSpec((RANKS, 2 * shard, LANES), lambda step: (0, 0, step)),
+            pl.BlockSpec((1, 1, CHUNK), lambda step: (step, 0, 0)),
+            fixed((2, D)),
+        ),
+        scratch_shapes=[
+            VMEM((HALF_TILES, tokens, CHUNK), BF16),
+            VMEM((D, tokens), BF16),
+            VMEM((tokens, D), F32),
+        ],
+        compiler_params=params_of(56),
+        name="plane_qkv_back",
+    )(recv, normed, x, dres, vec, w)
+
+
+class Reduce:
+    SENDS = 4 + 2 + 2 + 3
+    RECVS = SENDS
+
+    def __init__(self, source, total, near, corner_x, corner_y, side_x, side_y, far, out, sems):
+        self.source, self.total, self.near = source, total, near
+        self.corner = {1: corner_x, 2: corner_y}
+        self.side = {1: side_x, 2: side_y}
+        self.far, self.out = far, out
+        self.send_sem, self.recv_sem, self.local_sem = sems
+        self.core, self.plane, self.spot = place_here()
+        self.copies = []
+        self.locals = []
+
+    def start(self):
+        sibling = (1 - self.core, rank_of(self.plane, self.spot))
+        for number, side in enumerate((3, 1, 2, 0)):
+            spot = flip(self.spot, side)
+            copy = remote(
+                self.source.at[1 - self.core, :, spot],
+                self.near.at[:, spot],
+                self.send_sem.at[number],
+                self.recv_sem.at[number],
+                sibling,
+            )
+            copy.start()
+            self.copies.append(copy)
+            keep = pltpu.make_async_copy(
+                self.source.at[self.core, :, spot],
+                self.total.at[:, spot],
+                self.local_sem.at[number],
+            )
+            keep.start()
+            self.locals.append(keep)
+
+    def take(self, number, side):
+        self.copies[number].wait_recv()
+        self.locals[number].wait()
+        spot = flip(self.spot, side)
+
+        def add(plane, carry):
+            self.total[plane, spot] = (
+                self.total[plane, spot].astype(F32) + self.near[plane, spot].astype(F32)
+            ).astype(self.total.dtype)
+            return carry
+
+        lax.fori_loop(0, PLANES, add, 0)
+
+    def corners(self):
+        self.take(0, 3)
+        spot = flip(self.spot, 3)
+        index = 4
+        self.corner_copies = []
+        for bits in range(PLANES):
+            side = 2 if bits < 2 else 1
+            self.corner_copies.append(None)
+            plane = flip(self.plane, bits)
+            copy = remote(
+                self.total.at[plane, spot],
+                self.corner[side].at[bits % 2],
+                self.send_sem.at[index + bits],
+                self.recv_sem.at[index + bits],
+                (self.core, rank_of(self.plane, flip(self.spot, side))),
+            )
+            copy.start()
+            self.corner_copies[bits] = copy
+
+    def sides(self):
+        self.take(1, 1)
+        self.take(2, 2)
+        self.side_copies = {}
+        for side in (1, 2):
+            spot = flip(self.spot, side)
+            came = 3 - side
+            for bits in (0, 1) if came == 2 else (2, 3):
+                self.corner_copies[bits].wait_recv()
+                plane = flip(self.plane, bits)
+                self.total[plane, spot] = (
+                    self.total[plane, spot].astype(F32)
+                    + self.corner[came][bits % 2].astype(F32)
+                ).astype(self.total.dtype)
+            copy = remote(
+                self.total.at[:, spot],
+                self.side[side],
+                self.send_sem.at[7 + side],
+                self.recv_sem.at[7 + side],
+                (self.core, rank_of(self.plane, spot)),
+            )
+            copy.start()
+            self.side_copies[side] = copy
+
+    def columns(self):
+        self.take(3, 0)
+        for side in (1, 2):
+            self.side_copies[side].wait_recv()
+
+        def add(plane, carry):
+            self.total[plane, self.spot] = (
+                self.total[plane, self.spot].astype(F32)
+                + self.side[1][plane].astype(F32)
+                + self.side[2][plane].astype(F32)
+            ).astype(self.total.dtype)
+            return carry
+
+        lax.fori_loop(0, PLANES, add, 0)
+        self.far_copies = []
+        for bits in range(1, PLANES):
+            plane = flip(self.plane, bits)
+            copy = remote(
+                self.total.at[plane, self.spot],
+                self.far.at[bits - 1],
+                self.send_sem.at[9 + bits],
+                self.recv_sem.at[9 + bits],
+                (self.core, rank_of(plane, self.spot)),
+            )
+            copy.start()
+            self.far_copies.append(copy)
+
+    def finish(self):
+        value = self.total[self.plane, self.spot].astype(F32)
+        for bits in range(1, PLANES):
+            self.far_copies[bits - 1].wait_recv()
+            value = value + self.far[bits - 1].astype(F32)
+        self.out[...] = value
+        for copy in self.copies + self.corner_copies + self.far_copies:
+            copy.wait_send()
+        for side in (1, 2):
+            self.side_copies[side].wait_send()
+
+
+REDUCE_SEMS = 13
+
+
+def reduce_scratch(shape, kind):
+    tail = shape[3:]
+    return [
+        VMEM((PLANES, SPOTS) + tail, kind),
+        VMEM((PLANES, SPOTS) + tail, kind),
+        VMEM((2,) + tail, kind),
+        VMEM((2,) + tail, kind),
+        VMEM((PLANES,) + tail, kind),
+        VMEM((PLANES,) + tail, kind),
+        VMEM((PLANES - 1,) + tail, kind),
+    ]
+
+
+def spread_kernel(count, *refs):
+    hidden_ref, grad_ref = refs[:2]
+    sources = refs[2 : 2 + count]
+    hidden_out_ref, grad_out_ref = refs[2 + count : 4 + count]
+    outs = refs[4 + count : 4 + 2 * count]
+    scratch = refs[4 + 2 * count :]
+    buffers = scratch[: 7 * count]
+    send_sem, recv_sem, local_sem, move_send, move_recv, move_local = scratch[7 * count :]
+    core, plane, spot = place_here()
+    greet(all_partners(core, plane, spot))
+    sums = [
+        Reduce(
+            source,
+            *buffers[7 * number : 7 * number + 7],
+            out,
+            (send_sem.at[number], recv_sem.at[number], local_sem.at[number]),
+        )
+        for number, (source, out) in enumerate(zip(sources, outs))
+    ]
+    for one in sums:
+        one.start()
+    finish_grad = from_planes(grad_ref, grad_out_ref, move_send.at[0], move_recv.at[0], move_local.at[0])
+    finish_hidden = from_planes(
+        hidden_ref, hidden_out_ref, move_send.at[1], move_recv.at[1], move_local.at[1]
+    )
+    for one in sums:
+        one.corners()
+    for one in sums:
+        one.sides()
+    for one in sums:
+        one.columns()
+    for one in sums:
+        one.finish()
+    finish_grad()
+    finish_hidden()
+
+
+def spread(hidden, grad, sources):
+    count = len(sources)
+    buffers = []
+    for source in sources:
+        buffers += reduce_scratch(source.shape, source.dtype)
+    return pl.pallas_call(
+        functools.partial(spread_kernel, count),
+        out_shape=(
+            jax.ShapeDtypeStruct(hidden.shape, BF16),
+            jax.ShapeDtypeStruct(grad.shape, BF16),
+        )
+        + tuple(jax.ShapeDtypeStruct(source.shape[3:], F32) for source in sources),
+        in_specs=[whole(ANY)] * (2 + count),
+        out_specs=(whole(ANY), whole(ANY)) + (whole(),) * count,
+        scratch_shapes=buffers
+        + [
+            pltpu.SemaphoreType.DMA((count, REDUCE_SEMS)),
+            pltpu.SemaphoreType.DMA((count, REDUCE_SEMS)),
+            pltpu.SemaphoreType.DMA((count, 4)),
+            pltpu.SemaphoreType.DMA((2, 2)),
+            pltpu.SemaphoreType.DMA((2, 2)),
+            pltpu.SemaphoreType.DMA((2, 2)),
+        ],
+        compiler_params=pltpu.CompilerParams(
+            vmem_limit_bytes=56 * 1024 * 1024, collective_id=2, has_side_effects=True
+        ),
+        name="spread",
+    )(hidden, grad, *sources)
+
+
+def fold_columns(array):
+    half = array.shape[1] // 2
+    return jnp.concatenate([array[:, :half], array[:, half:]], axis=0)
+
+
+def unfold_columns(array):
+    half = array.shape[0] // 2
+    return jnp.concatenate([array[:half], array[half:]], axis=1)
+
+
+def plane_shards(
+    hidden_in,
+    rand_table,
+    norm1_gain,
+    norm1_bias,
+    w_qkv,
+    query_bias,
+    value_bias,
+    w_out,
+    out_bias,
+    norm2_gain,
+    norm2_bias,
+    w_up,
+    up_bias,
+    w_down,
+    down_bias,
+    cotangent,
+):
+    micro, rows, _ = hidden_in.shape
+    local = rows // BLOCK
+    own = norm1_gain.shape[0]
+    order = [natural_block(entry) for entry in column_order()]
+    inverse = [order.index(number) for number in range(len(order))]
+    small = (8 + FF // D) * own
+    entries = rand_table.size
+
+    vec = jnp.concatenate(
+        [
+            norm1_gain,
+            norm1_bias,
+            query_bias,
+            value_bias,
+            out_bias,
+            norm2_gain,
+            norm2_bias,
+            down_bias,
+            up_bias,
+            rand_table.reshape(entries).astype(BF16),
+            jnp.zeros((16 * LANES - small - entries,), BF16),
+        ]
+    ).reshape(16, LANES)
+    x, dy, vecs, w_qkv_all, w_out_all, w_up_all, w_down_all = collect(
+        hidden_in,
+        cotangent,
+        vec,
+        fold_columns(take_blocks(w_qkv, order)),
+        fold_columns(w_out),
+        fold_columns(w_up),
+        w_down,
+    )
+    vecs = vecs.reshape(RANKS, 16 * LANES)
+    vectors = vecs[:, : 8 * own].reshape(RANKS, 8, own).swapaxes(0, 1).reshape(8, D).astype(F32)
+    up_shift = vecs[:, 8 * own : small].astype(F32).reshape(2, FF // CHUNK, LANES)
+    up_shift = up_shift.swapaxes(0, 1).reshape(FF // CHUNK, 1, CHUNK)
+    bias = jnp.concatenate([vectors[2:3], jnp.zeros((1, D), F32), vectors[3:4]], axis=1)
+    bias = take_blocks(bias, order).reshape(2, HALF_TILES, LANES)
+    bias = bias.swapaxes(0, 1).reshape(1, 3 * D)
+    plane = lax.div(lax.axis_index("gy"), SPOTS)
+    tables = vecs[:, small : small + entries].reshape(2, PLANES * SPOTS, 2, local * RANDOM)
+    tables = tables.astype(jnp.int32).transpose(2, 0, 1, 3).reshape(PLANES, 1, -1)
+    table = lax.dynamic_index_in_dim(tables, plane, 0, keepdims=False)
+
+    normed, send = plane_qkv(x, vectors, w_qkv_all, bias)
+    qkv = outward(send, 3, "exchange_qkv")
+    qkv = qkv.reshape(PLANES * SPOTS, 3, local, BLOCK, LANES)
+    mixed, lse = plane_attention(table, qkv)
+    mixed = inward(mixed.reshape(PLANES, SPOTS, rows, LANES), 4, "exchange_mixed")
+    hidden, grad_send, dres, g_out, g_up, g_down, g_up_bias, g_mid = plane_middle(
+        mixed,
+        x,
+        dy.reshape(micro * rows, D),
+        vectors,
+        w_out_all,
+        up_shift,
+        w_up_all,
+        w_down_all.reshape(2, FF // 2, D),
+    )
+    grad_mixed = outward(grad_send, 5, "exchange_dmixed")
+    grad_mixed = grad_mixed.reshape(PLANES * SPOTS, local, BLOCK, LANES)
+    dqkv = plane_attention_back(table, qkv, grad_mixed, lse)
+    dqkv = inward(dqkv.reshape(PLANES, SPOTS, 3, rows, LANES), 6, "exchange_dqkv")
+    grad, g_qkv, g_bias, g_first = plane_qkv_back(dqkv, normed, x, dres, vectors, w_qkv_all)
+
+    g_bias = g_bias.reshape(HALF_TILES, 2, LANES).swapaxes(0, 1).reshape(1, 3 * D)
+    g_bias = take_blocks(g_bias, inverse)
+    singles = jnp.concatenate(
+        [g_first, g_bias[:, :D], g_bias[:, 2 * D :], g_mid[3:4], g_mid[0:3]], axis=0
+    )
+    singles = singles.reshape(8, RANKS, own).swapaxes(0, 1).reshape(RANKS, 8 * own)
+    g_up_bias = g_up_bias.reshape(FF // CHUNK, 2, LANES).swapaxes(0, 1).reshape(RANKS, FF // RANKS)
+    singles = jnp.concatenate(
+        [singles, g_up_bias, jnp.zeros((RANKS, 8 * LANES - small), F32)], axis=1
+    )
+    grid = (2, PLANES, SPOTS)
+    hidden_out, grad_hidden, singles, t_qkv, t_out, t_up, t_down = spread(
+        hidden,
+        grad,
+        [
+            singles.reshape(grid + (8, LANES)),
+            g_qkv.reshape(grid + g_qkv.shape[1:]),
+            g_out.reshape(grid + g_out.shape[1:]),
+            g_up.reshape(grid + g_up.shape[1:]),
+            g_down.reshape(grid + (FF // RANKS, D)),
+        ],
+    )
+    singles = singles.reshape(8 * LANES)
+    parts = [singles[number * own : (number + 1) * own] for number in range(8)]
+    return (
+        hidden_out,
+        grad_hidden.astype(F32),
+        parts[0],
+        parts[1],
+        take_blocks(unfold_columns(t_qkv), inverse),
+        parts[2],
+        parts[3],
+        unfold_columns(t_out),
+        parts[4],
+        parts[5],
+        parts[6],
+        unfold_columns(t_up),
+        singles[8 * own : small],
+        t_down,
+        parts[7],
+    )
+
+
+def shards(*arrays):
+    micro, rows, _ = arrays[0].shape
+    fits = lax.axis_size("gx") == 2 and lax.axis_size("gy") == PLANES * SPOTS
+    fits = fits and micro == 2 and rows % BLOCK == 0
+    return (plane_shards if fits else general_shards)(*arrays)
+
+
 def solution(mesh):
     tokens = P(None, AXES, None)
     vector = P(AXES)

time: 1030 us -> 469 us (0.46)
  waiting for transfers between devices: 527 us -> 0 us
  blocking collectives: 276 us -> 0 us
  Pallas kernels: 163 us -> 429 us
  starting transfers between devices: 22.4 us -> 0 us
  between operations: 14.5 us -> 1 us
  local copies, waits for them, and re-layouts: 20.9 us -> 32.3 us
    reduce_scatter x4 -> x0, waiting for transfers between devices: 458 us -> none  [scatter(): return lax.psum_scatter(array, AXES, scatter_dimension=0, tiled=True)]
    pallas_call x5 -> x11, Pallas kernels: 163 us -> 429 us  [the longest x1 109 us: collect(): pl.pallas_call(collect_kernel, out_shape=(jax.ShapeDtypeStruct(x.shape, B...]
    all_to_all x2 -> x0, blocking collectives: 106 us -> none  [exchange(): return lax.all_to_all(array, 'gy', 0, 0, tiled=True)]
    all_gather x1 -> x0, blocking collectives: 88.7 us -> none  [shards(): table = lax.all_gather(rand_table, 'gy', axis=1, tiled=True)]
    unnamed x2 -> x0, blocking collectives: 81.8 us -> none
    all_gather x4 -> x0, waiting for transfers between devices: 65.6 us -> none  [gather(): return lax.all_gather(array, AXES, axis=0, tiled=True)]
    all_to_all x2 -> x0, starting transfers between devices: 21.9 us -> none  [exchange(): return lax.all_to_all(array, 'gy', 0, 0, tiled=True)]
  transfers between devices with their start and end apart: 10 -> 0, of which waited for: 6 -> 0; matrix products, arithmetic and copies ran while one was open for 2% -> 0% of each run, Pallas kernels for 6% -> 0%
where the time goes in v2:
time: 469 us; the launch traced here: 468 us
  Pallas kernels  429 us (91%)
  local copies, waits for them, and re-layouts  32.3 us (7%)
  other arithmetic  6.44 us (1%)
    pallas_call x1, Pallas kernels, collect(): pl.pallas_call(collect_kernel, out_shape=(jax.ShapeDtypeStruct(x.shape, B...  109 us
    pallas_call x4, Pallas kernels, plane_exchange(): pl.pallas_call(kernel, out_shape=jax.ShapeDtypeStruct(shape, source.dtype...  106 us
    pallas_call x1, Pallas kernels, spread(): pl.pallas_call(functools.partial(spread_kernel, count), out_shape=(jax.Sh...  78.9 us
    pallas_call x1, Pallas kernels, plane_attention_back(): pl.pallas_call(plane_attend_back_kernel, out_shape=jax.ShapeDtypeStruct(q...  47.6 us
    pallas_call x1, Pallas kernels, plane_middle(): pl.pallas_call(plane_middle_kernel, grid=(steps,), out_shape=(jax.ShapeDt...  35.6 us
    pallas_call x1, Pallas kernels, plane_attention(): pl.pallas_call(plane_attend_kernel, out_shape=(jax.ShapeDtypeStruct((grou...  34.2 us
    pallas_call x1, Pallas kernels, plane_qkv_back(): pl.pallas_call(plane_qkv_back_kernel, grid=(HALF_TILES,), out_shape=(jax....  13.5 us
    unnamed x33, local copies, waits for them, and re-layouts  11.9 us

profile of v2, /device:TPU:0, one launch (start us, length us, event | category | flops | bytes accessed | tf_op | source)
XLA Modules:
  0.0 468.3 jit_solution(9515596610684021179)
XLA Ops:
  0.6 0.9 fusion.6
  1.6 0.9 fusion.5
  2.8 0.7 pad_maximum_fusion.2.s_qkv_ref
  3.5 0.9 fusion.4
  4.4 0.7 pad_maximum_fusion.1.s_up_ref
  5.1 0.7 fusion.8
  5.8 0.6 pad_maximum_fusion.4.s_out_ref
  6.4 0.7 convert_element_type.23
  7.1 0.1 copy.45
  7.3 6.7 %concatenate.48 = bf16[2048]{0:T(1024)(128)(2,1)} concatenate(bf16[24]{0:T(256)(128)(2,1)} %param.18, bf16[24]{0:T(256)(128)(2,1)} %param.19, bf16[24]{0:T(256)(128)(2,1)} %param.21, bf16[24]{0:T(256)(128)(2,1)} %param.22, bf16[24]{0:T(256)(128)(2,1)} %param.24, bf16[24]{0:T(256)(128)(2,1)} %param.25, bf16[24]{0:T(256)(128)(2,1)} %param.26, bf16[24]{0:T(256)(128)(2,1)} %param.30, ...), dimensions={0} | concatenate | bytes 8192 | tf_op jit(solution)/shard_map/concatenate | solution.py:2104
  14.0 108.7 %collect.1 = (bf16[2,256,768]{2,1,0:T(8,128)(2,1)}, bf16[2,256,768]{2,1,0:T(8,128)(2,1)}, bf16[2,4,4,16,128]{4,3,2,1,0:T(8,128)(2,1)}, bf16[768,2304]{1,0:T(8,12...) custom-call(bf16[2,256,768]{2,1,0:T(8,128)(2,1)} %x_ref.1, ...), custom_call_target="tpu_custom_call" | custom-call | tf_op jit(solution)/shard_map/collect/pallas_call | solution.py:1101
  122.8 0.9 copy.60
  123.9 0.1 reshape.151.vec_ref
  124.1 0.1 concatenate.54
  124.3 1.1 copy-done.3
  125.5 4.4 plane_qkv.1
  129.9 39.0 %exchange_qkv.1 = bf16[4,4,3,256,128]{4,3,2,1,0:T(8,128)(2,1)S(1)} custom-call(bf16[2,4,2,3,256,128]{5,4,3,2,1,0:T(8,128)(2,1)S(1)} %get-tuple-element.48.source_ref), custom_call_target="tpu_custom_call" | custom-call | tf_op jit(solution)/shard_map/exchange_qkv/pallas_call | solution.py:1227
  168.9 1.7 copy-done
  171.1 34.2 %plane_attention.1 = (bf16[16,4,64,128]{3,2,1,0:T(8,128)(2,1)S(1)}, f32[64,64,128]{2,1,0:T(8,128)S(1)}) custom-call(s32[1,192]{1,0:T(1,128)S(1)} %dynamic-slice_bitcast_fusion.table_ref, bf16[16,3,4,64,128]{4,3,2,1,0:T(8,128)(2,1)} %bitcast.43), custom_call_target="tpu_custom_call" | custom-call | tf_op jit(solution)/shard_map/plane_attention/pallas_call | solution.py:1411
  205.3 14.2 %exchange_mixed.1.mixed_in_ref = bf16[2,4,2,256,128]{4,3,2,1,0:T(8,128)(2,1)S(1)} custom-call(bf16[4,4,256,128]{3,2,1,0:T(8,128)(2,1)S(1)} %bitcast.47), custom_call_target="tpu_custom_call" | custom-call | tf_op jit(solution)/shard_map/exchange_mixed/pallas_call | solution.py:1227
  219.5 1.0 copy-done.4
  220.7 0.6 copy.50
  221.3 35.6 %plane_middle.1 = (bf16[2,256,768]{2,1,0:T(8,128)(2,1)}, bf16[2,4,2,256,128]{4,3,2,1,0:T(8,128)(2,1)}, f32[512,768]{1,0:T(8,128)}, bf16[32,48,384]{2,1,0:T(8,128...) custom-call(bf16[2,4,2,256,128]{4,3,2,1,0:T(8,128)(2,1)} %copy-done., ...), custom_call_target="tpu_custom_call" | custom-call | tf_op jit(solution)/shard_map/plane_middle/pallas_call | solution.py:1701
  256.9 1.2 copy-done.5
  258.2 15.8 %exchange_dmixed.1 = bf16[4,4,256,128]{3,2,1,0:T(8,128)(2,1)S(1)} custom-call(bf16[2,4,2,256,128]{4,3,2,1,0:T(8,128)(2,1)S(1)} %copy-done.5), custom_call_target="tpu_custom_call" | custom-call | tf_op jit(solution)/shard_map/exchange_dmixed/pallas_call | solution.py:1227
  274.0 47.6 %plane_attention_back.1 = bf16[16,3,4,64,128]{4,3,2,1,0:T(8,128)(2,1)} custom-call(s32[1,192]{1,0:T(1,128)S(1)} %dynamic-slice_bitcast_fusion.table_ref, bf16[16,3,4,64,128]{4,3,2,1,0:T(8,128)(2,1)} %bitcast.44, bf16[16,4,64,128]{3,2,1,0:T(8,128)(2,1)S(1)} %bitcast.46, f32[64,64,128]{2,1,0:T(8,128)S(1)} %get-tuple-element.56.lse_ref), custom_call_target="tpu_custom_call" | custom-call | tf_op jit(solution)/shard_map/plane_attention_back/pallas_call | solution.py:1563
  321.6 1.9 copy-done.1
  323.4 36.6 %exchange_dqkv.1.recv_ref = bf16[2,4,2,3,256,128]{5,4,3,2,1,0:T(8,128)(2,1)S(1)} custom-call(bf16[4,4,3,256,128]{4,3,2,1,0:T(8,128)(2,1)S(1)} %bitcast.45), custom_call_target="tpu_custom_call" | custom-call | tf_op jit(solution)/shard_map/exchange_dqkv/pallas_call | solution.py:1227
  360.1 1.6 copy-done.2
  361.7 13.5 %plane_qkv_back.1 = (bf16[2,256,768]{2,1,0:T(8,128)(2,1)}, bf16[32,48,1152]{2,1,0:T(8,128)(2,1)}, f32[9,1,256]{2,1,0:T(1,128)}, f32[2,768]{1,0:T(2,128)}) custom-call(bf16[2,4,2,3,256,128]{5,4,3,2,1,0:T(8,128)(2,1)} %copy-done.2, bf16[512,768]{1,0:T(8,128)(2,1)} %copy-done.6, bf16[2,256,768]{2,1,0:T(8,128)(2,1)} %get-tuple-element.46.x_ref, ...), custom_call_target="tpu_custom_call" | custom-call | tf_op jit(solution)/shard_map/plane_qkv_back/pallas_call | solution.py:1822
  375.2 0.7 copy.62
  376.3 0.7 concatenate.57
  377.0 0.1 reshape.139
  377.6 0.7 copy.56
  378.3 78.9 %spread.1 = (bf16[2,256,768]{2,1,0:T(8,128)(2,1)}, bf16[2,256,768]{2,1,0:T(8,128)(2,1)}, f32[8,128]{1,0:T(8,128)}, f32[48,1152]{1,0:T(8,128)}, f32[48,384]{1,0:T...) custom-call(bf16[2,256,768]{2,1,0:T(8,128)(2,1)} %get-tuple-element.54.refs_0_, ...), custom_call_target="tpu_custom_call" | custom-call | tf_op jit(solution)/shard_map/spread/pallas_call | solution.py:2043
  457.2 1.1 fusion
  458.3 0.7 pad_maximum_fusion
  459.1 0.8 fusion.7
  459.9 0.6 pad_maximum_fusion.3
  460.6 1.0 fusion.3
  461.5 1.0 fusion.1
  462.5 1.0 fusion.2
  463.5 0.8 concatenate.60
  464.3 1.3 convert_element_type.30
  465.6 0.6 fusion.13
  466.2 0.6 slice.492
  466.8 0.9 copy.65
  467.6 0.7 copy.66
  (60 shorter events, 2.1 us)
Async XLA Ops:
  124.0 44.9 %copy-start.7 = (f32[8,768]{1,0:T(8,128)}, f32[8,768]{1,0:T(8,128)S(1)}, u32[]{:S(2)}) copy-start(f32[8,768]{1,0:T(8,128)S(1)} %reshape.151.vec_ref) | copy-start | bytes 73732
  124.3 1.1 copy-start.3
  129.9 39.0 %copy-start.6 = (bf16[512,768]{1,0:T(8,128)(2,1)}, bf16[512,768]{1,0:T(8,128)(2,1)S(1)}, u32[]{:S(2)}) copy-start(bf16[512,768]{1,0:T(8,128)(2,1)S(1)} %get-tuple-element.57.normed_ref) | copy-start | bytes 2359300
  168.9 1.7 copy-start
  219.5 1.0 copy-start.4
  256.9 1.2 copy-start.5
  321.6 1.9 copy-start.1
  360.1 1.6 copy-start.2
  361.7 14.6 %copy-start.11 = (f32[4,768]{1,0:T(4,128)S(1)}, f32[4,768]{1,0:T(4,128)}, u32[]{:S(2)}) copy-start(f32[4,768]{1,0:T(4,128)} %get-tuple-element.62) | copy-start | bytes 36868
  361.7 15.6 %copy-start.12 = (f32[12,1,256]{2,1,0:T(1,128)S(1)}, f32[12,1,256]{2,1,0:T(1,128)}, u32[]{:S(2)}) copy-start(f32[12,1,256]{2,1,0:T(1,128)} %get-tuple-element.63) | copy-start | bytes 36868
  457.2 7.1 %copy-start.9 = (bf16[2,256,768]{2,1,0:T(8,128)(2,1)S(1)}, bf16[2,256,768]{2,1,0:T(8,128)(2,1)}, u32[]{:S(2)}) copy-start(bf16[2,256,768]{2,1,0:T(8,128)(2,1)} %get-tuple-element.69) | copy-start | bytes 2359300
  457.2 8.4 %copy-start.13 = (f32[8,128]{1,0:T(8,128)S(1)}, f32[8,128]{1,0:T(8,128)}, u32[]{:S(2)}) copy-start(f32[8,128]{1,0:T(8,128)} %get-tuple-element.70) | copy-start | bytes 12292
  457.2 9.5 %copy-start.8 = (bf16[2,256,768]{2,1,0:T(8,128)(2,1)S(1)}, bf16[2,256,768]{2,1,0:T(8,128)(2,1)}, u32[]{:S(2)}) copy-start(bf16[2,256,768]{2,1,0:T(8,128)(2,1)} %get-tuple-element.194) | copy-start | bytes 2359300
  459.1 8.6 %copy-start.10 = (f32[96,768]{1,0:T(8,128)S(1)}, f32[96,768]{1,0:T(8,128)}, u32[]{:S(2)}) copy-start(f32[96,768]{1,0:T(8,128)} %get-tuple-element.207) | copy-start | bytes 884740

commit v3 on v2

--- a/solution.py
+++ b/solution.py
@@ -1002,9 +1002,8 @@
             copy.wait_send()
 
 
-def settle(shards_ref, out_ref, tiles_of):
+def settle(shards_ref, plan):
     rows = shards_ref.shape[3] // 2
-    width = shards_ref.shape[4]
 
     def pair(number, carry):
         core, plane, side = (
@@ -1013,11 +1012,10 @@
             lax.rem(number, 2),
         )
         goal = pl.ds(pl.multiple_of(number * 2 * rows, 16), 2 * rows)
-        for tile in range(width // LANES):
+        for tile, out_ref, (left, right) in plan:
             columns = slice(tile * LANES, (tile + 1) * LANES)
             first = shards_ref[core, plane, 2 * side, :, columns].astype(F32)
             second = shards_ref[core, plane, 2 * side + 1, :, columns].astype(F32)
-            left, right = tiles_of(tile)
             out_ref[goal, left * LANES : (left + 1) * LANES] = jnp.concatenate(
                 [first[:rows], second[:rows]], axis=0
             ).astype(BF16)
@@ -1033,28 +1031,14 @@
     return 2 * tile, 2 * tile + 1
 
 
-def in_order(tile):
-    return tile, D // LANES // 2 + tile
-
-
 def collect_kernel(
     x_ref,
-    dy_ref,
     vec_ref,
     s_qkv_ref,
-    s_out_ref,
-    s_up_ref,
-    s_down_ref,
     xs_ref,
-    dys_ref,
     vecs_ref,
     w_qkv_ref,
-    w_out_ref,
-    w_up_ref,
-    w_down_ref,
     g_qkv_ref,
-    g_out_ref,
-    g_up_ref,
     send_sem,
     recv_sem,
     local_sem,
@@ -1064,22 +1048,14 @@
 ):
     core, plane, spot = place_here()
     greet(all_partners(core, plane, spot))
-    pairs = (
-        (vec_ref, vecs_ref),
-        (s_qkv_ref, g_qkv_ref),
-        (s_out_ref, g_out_ref),
-        (s_up_ref, g_up_ref),
-        (s_down_ref, w_down_ref),
-    )
-    finish_x = to_planes(x_ref, xs_ref, move_send.at[0], move_recv.at[0], move_local.at[0])
     gathers = []
-    for number, (source, target) in enumerate(pairs):
+    for number, (source, target) in enumerate(((vec_ref, vecs_ref), (s_qkv_ref, g_qkv_ref))):
         one = Gather(
             source, target, send_sem.at[number], recv_sem.at[number], local_sem.at[number]
         )
         one.start()
         gathers.append(one)
-    finish_dy = to_planes(dy_ref, dys_ref, move_send.at[1], move_recv.at[1], move_local.at[1])
+    finish_x = to_planes(x_ref, xs_ref, move_send, move_recv, move_local)
     for one in gathers:
         one.column()
     for one in gathers:
@@ -1088,45 +1064,35 @@
         one.corner()
     for one in gathers:
         one.finish()
-    settle(g_qkv_ref, w_qkv_ref, alternate)
-    settle(g_out_ref, w_out_ref, in_order)
-    settle(g_up_ref, w_up_ref, alternate)
+    settle(g_qkv_ref, [(tile, w_qkv_ref, alternate(tile)) for tile in range(HALF_TILES)])
     finish_x()
-    finish_dy()
-
-
-def collect(x, dy, vec, s_qkv, s_out, s_up, s_down):
+
+
+def collect(x, vec, s_qkv):
     grid = (2, PLANES, SPOTS)
-    count = 5
     return pl.pallas_call(
         collect_kernel,
         out_shape=(
             jax.ShapeDtypeStruct(x.shape, BF16),
-            jax.ShapeDtypeStruct(dy.shape, BF16),
             jax.ShapeDtypeStruct(grid + vec.shape, BF16),
             jax.ShapeDtypeStruct((D, 3 * D), BF16),
-            jax.ShapeDtypeStruct((D, D), BF16),
-            jax.ShapeDtypeStruct((D, FF), BF16),
-            jax.ShapeDtypeStruct(grid + s_down.shape, BF16),
         ),
-        in_specs=[whole(ANY)] * 7,
-        out_specs=(whole(ANY), whole(ANY), whole(ANY), whole(), whole(), whole(), whole(ANY)),
+        in_specs=[whole(ANY)] * 3,
+        out_specs=(whole(ANY), whole(ANY), whole()),
         scratch_shapes=[
             VMEM(grid + s_qkv.shape, BF16),
-            VMEM(grid + s_out.shape, BF16),
-            VMEM(grid + s_up.shape, BF16),
-            pltpu.SemaphoreType.DMA((count, Gather.SENDS)),
-            pltpu.SemaphoreType.DMA((count,) + grid),
-            pltpu.SemaphoreType.DMA((count,)),
-            pltpu.SemaphoreType.DMA((2, 2)),
-            pltpu.SemaphoreType.DMA((2, 2)),
-            pltpu.SemaphoreType.DMA((2, 2)),
+            pltpu.SemaphoreType.DMA((2, Gather.SENDS)),
+            pltpu.SemaphoreType.DMA((2,) + grid),
+            pltpu.SemaphoreType.DMA((2,)),
+            pltpu.SemaphoreType.DMA((2,)),
+            pltpu.SemaphoreType.DMA((2,)),
+            pltpu.SemaphoreType.DMA((2,)),
         ],
         compiler_params=pltpu.CompilerParams(
-            vmem_limit_bytes=56 * 1024 * 1024, collective_id=1, has_side_effects=True
+            vmem_limit_bytes=48 * 1024 * 1024, collective_id=1, has_side_effects=True
         ),
         name="collect",
-    )(x, dy, vec, s_qkv, s_out, s_up, s_down)
+    )(x, vec, s_qkv)
 
 
 def plane_partners(core, plane, spot):
@@ -1139,9 +1105,12 @@
     return partners
 
 
-def outward_kernel(source_ref, target_ref, send_sem, recv_sem, local_sem):
+def both_partners(core, plane, spot):
+    return plane_partners(core, plane, spot) + column_partners(core, plane, spot)[1:]
+
+
+def outward_send(source_ref, target_ref, send_sem, recv_sem, local_sem):
     core, plane, spot = place_here()
-    greet(plane_partners(core, plane, spot))
     sends, keeps = [], []
     for side in (3, 1, 2, 0):
         for other in (core, 1 - core):
@@ -1162,28 +1131,31 @@
                     )
                     sends.append(copy)
                 copy.start()
-    for side in range(SPOTS):
-        for other in (core, 1 - core):
-            if side == 0 and other is core:
-                continue
-            for piece in range(PIECES):
-                target = target_ref.at[2 * other + piece, flip(spot, side)]
-                remote(
-                    target,
-                    target,
-                    send_sem.at[0],
-                    recv_sem.at[2 * other + piece, flip(spot, side)],
-                    (core, rank_of(plane, spot)),
-                ).wait_recv()
-    for copy in sends:
-        copy.wait_send()
-    for copy in keeps:
-        copy.wait()
-
-
-def inward_kernel(source_ref, target_ref, send_sem, recv_sem, local_sem):
+
+    def finish():
+        for side in range(SPOTS):
+            for other in (core, 1 - core):
+                if side == 0 and other is core:
+                    continue
+                for piece in range(PIECES):
+                    target = target_ref.at[2 * other + piece, flip(spot, side)]
+                    remote(
+                        target,
+                        target,
+                        send_sem.at[0],
+                        recv_sem.at[2 * other + piece, flip(spot, side)],
+                        (core, rank_of(plane, spot)),
+                    ).wait_recv()
+        for copy in sends:
+            copy.wait_send()
+        for copy in keeps:
+            copy.wait()
+
+    return finish
+
+
+def inward_send(source_ref, target_ref, send_sem, recv_sem, local_sem):
     core, plane, spot = place_here()
-    greet(plane_partners(core, plane, spot))
     sends, keeps = [], []
     for side in (3, 1, 2, 0):
         for other in (core, 1 - core):
@@ -1204,23 +1176,45 @@
                     )
                     sends.append(copy)
                 copy.start()
-    for side in range(SPOTS):
-        for other in (core, 1 - core):
-            if side == 0 and other is core:
-                continue
-            for piece in range(PIECES):
-                target = target_ref.at[other, flip(spot, side), piece]
-                remote(
-                    target,
-                    target,
-                    send_sem.at[0],
-                    recv_sem.at[other, flip(spot, side), piece],
-                    (core, rank_of(plane, spot)),
-                ).wait_recv()
-    for copy in sends:
-        copy.wait_send()
-    for copy in keeps:
-        copy.wait()
+
+    def finish():
+        for side in range(SPOTS):
+            for other in (core, 1 - core):
+                if side == 0 and other is core:
+                    continue
+                for piece in range(PIECES):
+                    target = target_ref.at[other, flip(spot, side), piece]
+                    remote(
+                        target,
+                        target,
+                        send_sem.at[0],
+                        recv_sem.at[other, flip(spot, side), piece],
+                        (core, rank_of(plane, spot)),
+                    ).wait_recv()
+        for copy in sends:
+            copy.wait_send()
+        for copy in keeps:
+            copy.wait()
+
+    return finish
+
+
+def exchange_sems(recv_shape):
+    return [
+        pltpu.SemaphoreType.DMA((14,)),
+        pltpu.SemaphoreType.DMA(recv_shape),
+        pltpu.SemaphoreType.DMA((PIECES,)),
+    ]
+
+
+def outward_kernel(source_ref, target_ref, send_sem, recv_sem, local_sem):
+    greet(plane_partners(*place_here()))
+    outward_send(source_ref, target_ref, send_sem, recv_sem, local_sem)()
+
+
+def inward_kernel(source_ref, target_ref, send_sem, recv_sem, local_sem):
+    greet(plane_partners(*place_here()))
+    inward_send(source_ref, target_ref, send_sem, recv_sem, local_sem)()
 
 
 def plane_exchange(kernel, source, shape, recv_shape, collective, name):
@@ -1229,11 +1223,7 @@
         out_shape=jax.ShapeDtypeStruct(shape, source.dtype),
         in_specs=[whole(ANY)],
         out_specs=whole(ANY),
-        scratch_shapes=[
-            pltpu.SemaphoreType.DMA((14,)),
-            pltpu.SemaphoreType.DMA(recv_shape),
-            pltpu.SemaphoreType.DMA((PIECES,)),
-        ],
+        scratch_shapes=exchange_sems(recv_shape),
         compiler_params=pltpu.CompilerParams(
             vmem_limit_bytes=16 * 1024 * 1024, collective_id=collective, has_side_effects=True
         ),
@@ -1251,6 +1241,165 @@
     return plane_exchange(
         inward_kernel, source, shape, (2, SPOTS, PIECES), collective, name
     )
+
+
+def column_send(source, target, send_sem, recv_sem, local_sem):
+    core, plane, spot = place_here()
+    keep = pltpu.make_async_copy(source, target.at[plane], local_sem)
+    keep.start()
+    copies = []
+    for bits in range(1, PLANES):
+        copy = remote(
+            source,
+            target.at[plane],
+            send_sem.at[bits - 1],
+            recv_sem.at[plane],
+            (core, rank_of(flip(plane, bits), spot)),
+        )
+        copy.start()
+        copies.append(copy)
+
+    def finish():
+        for bits in range(1, PLANES):
+            other = flip(plane, bits)
+            remote(
+                source,
+                target.at[other],
+                send_sem.at[0],
+                recv_sem.at[other],
+                (core, rank_of(plane, spot)),
+            ).wait_recv()
+        for copy in copies:
+            copy.wait_send()
+        keep.wait()
+
+    return finish
+
+
+def exchange_qkv_kernel(
+    source_ref,
+    s_ou_ref,
+    s_down_ref,
+    target_ref,
+    c_ou_ref,
+    c_down_ref,
+    send_sem,
+    recv_sem,
+    local_sem,
+    column_send_sem,
+    column_recv_sem,
+    column_local_sem,
+):
+    greet(both_partners(*place_here()))
+    finish = outward_send(source_ref, target_ref, send_sem, recv_sem, local_sem)
+    finishes = [
+        column_send(
+            source,
+            target,
+            column_send_sem.at[number],
+            column_recv_sem.at[number],
+            column_local_sem.at[number],
+        )
+        for number, (source, target) in enumerate(
+            ((s_ou_ref, c_ou_ref), (s_down_ref, c_down_ref))
+        )
+    ]
+    finish()
+    for one in finishes:
+        one()
+
+
+def exchange_qkv(source, s_ou, s_down):
+    return pl.pallas_call(
+        exchange_qkv_kernel,
+        out_shape=(
+            jax.ShapeDtypeStruct((PLANES, SPOTS) + source.shape[3:], BF16),
+            jax.ShapeDtypeStruct((PLANES,) + s_ou.shape, BF16),
+            jax.ShapeDtypeStruct((PLANES,) + s_down.shape, BF16),
+        ),
+        in_specs=[whole(ANY)] * 3,
+        out_specs=(whole(ANY),) * 3,
+        scratch_shapes=exchange_sems((PLANES, SPOTS))
+        + [
+            pltpu.SemaphoreType.DMA((2, PLANES - 1)),
+            pltpu.SemaphoreType.DMA((2, PLANES)),
+            pltpu.SemaphoreType.DMA((2,)),
+        ],
+        compiler_params=pltpu.CompilerParams(
+            vmem_limit_bytes=16 * 1024 * 1024, collective_id=3, has_side_effects=True
+        ),
+        name="exchange_qkv",
+    )(source, s_ou, s_down)
+
+
+class PlaneGather:
+    SENDS = 3 + 4 + 2
+
+    def __init__(self, column, target, send_sem, recv_sem, local_sem):
+        self.column, self.target = column, target
+        self.send_sem, self.recv_sem = send_sem, recv_sem
+        self.core, self.plane, self.spot = place_here()
+        self.sends = []
+        self.own = pltpu.make_async_copy(column, target.at[self.core, :, self.spot], local_sem)
+        self.own.start()
+        for goal in (self.neighbour(1), self.neighbour(2), self.sibling()):
+            self.send(column, slice(0, PLANES), self.spot, 0, goal)
+
+    def neighbour(self, bits):
+        return (self.core, rank_of(self.plane, flip(self.spot, bits)))
+
+    def sibling(self):
+        return (1 - self.core, rank_of(self.plane, self.spot))
+
+    def piece(self, core, planes, spot):
+        return self.target.at[core, planes, spot]
+
+    def send(self, source, planes, spot, part, goal):
+        copy = remote(
+            source,
+            self.piece(self.core, planes, spot),
+            self.send_sem.at[len(self.sends)],
+            self.recv_sem.at[self.core, spot, part],
+            goal,
+        )
+        copy.start()
+        self.sends.append(copy)
+
+    def arrive(self, core, planes, spot, part):
+        piece = self.piece(core, planes, spot)
+        remote(
+            piece,
+            piece,
+            self.send_sem.at[0],
+            self.recv_sem.at[core, spot, part],
+            (self.core, rank_of(self.plane, self.spot)),
+        ).wait_recv()
+
+    def forward(self):
+        for side in (1, 2):
+            spot = flip(self.spot, side)
+            everything = slice(0, PLANES)
+            self.arrive(self.core, everything, spot, 0)
+            half = slice(0, 2) if side == 1 else slice(2, 4)
+            self.send(
+                self.piece(self.core, half, spot), half, spot, side - 1, self.neighbour(3 - side)
+            )
+            self.send(self.piece(self.core, everything, spot), everything, spot, 0, self.sibling())
+
+    def corner(self):
+        spot = flip(self.spot, 3)
+        for part, half in enumerate((slice(0, 2), slice(2, 4))):
+            self.arrive(self.core, half, spot, part)
+            self.send(self.piece(self.core, half, spot), half, spot, part, self.sibling())
+
+    def finish(self):
+        for side in range(3):
+            self.arrive(1 - self.core, slice(0, PLANES), flip(self.spot, side), 0)
+        for part, half in enumerate((slice(0, 2), slice(2, 4))):
+            self.arrive(1 - self.core, half, flip(self.spot, 3), part)
+        self.own.wait()
+        for copy in self.sends:
+            copy.wait_send()
 
 
 def plane_qkv_kernel(x_ref, vec_ref, w_ref, bias_ref, normed_ref, send_ref):
@@ -1304,7 +1453,46 @@
     )(x, vec, w, bias)
 
 
-def plane_attend_kernel(table_ref, qkv_ref, out_ref, lse_ref, s_ref, t_ref):
+def plane_attend_kernel(
+    table_ref,
+    qkv_ref,
+    dy_ref,
+    c_ou_ref,
+    c_down_ref,
+    back_ref,
+    lse_ref,
+    dys_ref,
+    w_out_ref,
+    w_up_ref,
+    w_down_ref,
+    g_ou_ref,
+    out_ref,
+    s_ref,
+    t_ref,
+    send_sem,
+    recv_sem,
+    local_sem,
+    gather_send,
+    gather_recv,
+    gather_local,
+    move_send,
+    move_recv,
+    move_local,
+):
+    greet(both_partners(*place_here()))
+    gathers = [
+        PlaneGather(
+            column,
+            target,
+            gather_send.at[number],
+            gather_recv.at[number],
+            gather_local.at[number],
+        )
+        for number, (column, target) in enumerate(
+            ((c_ou_ref, g_ou_ref), (c_down_ref, w_down_ref))
+        )
+    ]
+    finish_dy = to_planes(dy_ref, dys_ref, move_send, move_recv, move_local)
     groups, _, local, _, _ = qkv_ref.shape
     blocks = groups * local
     half = blocks // 2
@@ -1316,7 +1504,8 @@
         return qkv_ref[lax.div(block, local), component, lax.rem(block, local)]
 
     def store(block, value):
-        out_ref[lax.div(block, local), lax.rem(block, local)] = value.astype(BF16)
+        rank = lax.div(block, local)
+        out_ref[lax.div(rank, SPOTS), lax.rem(rank, SPOTS), lax.rem(block, local)] = value.astype(BF16)
 
     def one(block, slot, ids, bias):
         keys = jnp.concatenate([load(1 + slot, spot) for spot in ids], axis=0)
@@ -1341,7 +1530,9 @@
         lse_ref[other] = jnp.where(low, log_c, 0.0)
         return carry
 
-    lax.fori_loop(0, half - 1, sparse, 0)
+    lax.fori_loop(0, half // 2, sparse, 0)
+    gathers[0].forward()
+    lax.fori_loop(half // 2, half - 1, sparse, 0)
 
     spans = blocks // SPAN
     ends = (0, blocks - 1)
@@ -1403,26 +1594,60 @@
         store(number, jnp.where(low, mixed_b, mixed_a[rows]))
         lse_ref[number] = jnp.where(low, log_a[rows], log_b)
 
-
-def plane_attention(table, qkv):
+    gathers[1].forward()
+    finish_mixed = inward_send(out_ref, back_ref, send_sem, recv_sem, local_sem)
+    gathers[0].corner()
+    gathers[0].finish()
+    outs = D // LANES // 2
+    settle(
+        g_ou_ref,
+        [(tile, w_out_ref, (tile, outs + tile)) for tile in range(outs)]
+        + [(outs + tile, w_up_ref, alternate(tile)) for tile in range(FF // CHUNK)],
+    )
+    gathers[1].corner()
+    gathers[1].finish()
+    finish_dy()
+    finish_mixed()
+
+
+def plane_attention(table, qkv, dy, c_ou, c_down):
     groups, _, local, _, _ = qkv.shape
     blocks = groups * local
     spans = blocks // SPAN
+    grid = (2, PLANES, SPOTS)
+    tile = (local, BLOCK, LANES)
     return pl.pallas_call(
         plane_attend_kernel,
         out_shape=(
-            jax.ShapeDtypeStruct((groups, local, BLOCK, LANES), BF16),
+            jax.ShapeDtypeStruct((2, SPOTS, PIECES) + tile, BF16),
             jax.ShapeDtypeStruct((blocks, BLOCK, LANES), F32),
+            jax.ShapeDtypeStruct(dy.shape, BF16),
+            jax.ShapeDtypeStruct((D, D), BF16),
+            jax.ShapeDtypeStruct((D, FF), BF16),
+            jax.ShapeDtypeStruct(grid + c_down.shape[1:], BF16),
         ),
-        in_specs=[whole(pltpu.SMEM), whole()],
-        out_specs=(whole(), whole()),
+        in_specs=[whole(pltpu.SMEM), whole(), whole(ANY), whole(ANY), whole(ANY)],
+        out_specs=(whole(ANY), whole(), whole(ANY), whole(), whole(), whole(ANY)),
         scratch_shapes=[
+            VMEM(grid + c_ou.shape[1:], BF16),
+            VMEM((PLANES, SPOTS) + tile, BF16),
             VMEM((spans, 2 * BLOCK, SPAN * BLOCK), F32),
             VMEM((spans, BLOCK, SPAN * BLOCK), F32),
+        ]
+        + exchange_sems((2, SPOTS, PIECES))
+        + [
+            pltpu.SemaphoreType.DMA((2, PlaneGather.SENDS)),
+            pltpu.SemaphoreType.DMA((2, 2, SPOTS, 2)),
+            pltpu.SemaphoreType.DMA((2,)),
+            pltpu.SemaphoreType.DMA((2,)),
+            pltpu.SemaphoreType.DMA((2,)),
+            pltpu.SemaphoreType.DMA((2,)),
         ],
-        compiler_params=params_of(48),
+        compiler_params=pltpu.CompilerParams(
+            vmem_limit_bytes=56 * 1024 * 1024, collective_id=4, has_side_effects=True
+        ),
         name="plane_attention",
-    )(table, qkv)
+    )(table, qkv, dy, c_ou, c_down)
 
 
 def plane_attend_back_kernel(
@@ -2116,15 +2341,7 @@
             jnp.zeros((16 * LANES - small - entries,), BF16),
         ]
     ).reshape(16, LANES)
-    x, dy, vecs, w_qkv_all, w_out_all, w_up_all, w_down_all = collect(
-        hidden_in,
-        cotangent,
-        vec,
-        fold_columns(take_blocks(w_qkv, order)),
-        fold_columns(w_out),
-        fold_columns(w_up),
-        w_down,
-    )
+    x, vecs, w_qkv_all = collect(hidden_in, vec, fold_columns(take_blocks(w_qkv, order)))
     vecs = vecs.reshape(RANKS, 16 * LANES)
     vectors = vecs[:, : 8 * own].reshape(RANKS, 8, own).swapaxes(0, 1).reshape(8, D).astype(F32)
     up_shift = vecs[:, 8 * own : small].astype(F32).reshape(2, FF // CHUNK, LANES)
@@ -2138,10 +2355,13 @@
     table = lax.dynamic_index_in_dim(tables, plane, 0, keepdims=False)
 
     normed, send = plane_qkv(x, vectors, w_qkv_all, bias)
-    qkv = outward(send, 3, "exchange_qkv")
+    s_ou = jnp.concatenate([fold_columns(w_out), fold_columns(w_up)], axis=1)
+    qkv, c_ou, c_down = exchange_qkv(send, s_ou, w_down)
     qkv = qkv.reshape(PLANES * SPOTS, 3, local, BLOCK, LANES)
-    mixed, lse = plane_attention(table, qkv)
-    mixed = inward(mixed.reshape(PLANES, SPOTS, rows, LANES), 4, "exchange_mixed")
+    mixed, lse, dy, w_out_all, w_up_all, w_down_all = plane_attention(
+        table, qkv, cotangent, c_ou, c_down
+    )
+    mixed = mixed.reshape(2, SPOTS, PIECES, rows, LANES)
     hidden, grad_send, dres, g_out, g_up, g_down, g_up_bias, g_mid = plane_middle(
         mixed,
         x,

time: 469 us -> 409 us (0.87)
  Pallas kernels: 429 us -> 371 us
    pallas_call x1, Pallas kernels: 109 us -> 35.5 us  [collect(): pl.pallas_call(collect_kernel, out_shape=(jax.ShapeDtypeStruct(x.shape, B...]
    pallas_call x1 -> x2, Pallas kernels: 34.2 us -> 103 us  [the longest x1 63.8 us: plane_attention(): pl.pallas_call(plane_attend_kernel, out_shape=(jax.ShapeDtypeStruct((2, S...]
    pallas_call x4 -> x2, Pallas kernels: 106 us -> 52.1 us  [plane_exchange(): pl.pallas_call(kernel, out_shape=jax.ShapeDtypeStruct(shape, source.dtype...]
    unnamed x33 -> x49, local copies, waits for them, and re-layouts: 11.9 us -> 13.7 us
where the time goes in v3:
time: 409 us
  Pallas kernels  371 us (91%)
  local copies, waits for them, and re-layouts  32.4 us (8%)
  other arithmetic  4.53 us (1%)
    pallas_call x1, Pallas kernels, spread(): pl.pallas_call(functools.partial(spread_kernel, count), out_shape=(jax.Sh...  78.9 us
    pallas_call x1, Pallas kernels, plane_attention(): pl.pallas_call(plane_attend_kernel, out_shape=(jax.ShapeDtypeStruct((2, S...  63.8 us
    pallas_call x2, Pallas kernels, plane_exchange(): pl.pallas_call(kernel, out_shape=jax.ShapeDtypeStruct(shape, source.dtype...  52.1 us
    pallas_call x1, Pallas kernels, plane_attention_back(): pl.pallas_call(plane_attend_back_kernel, out_shape=jax.ShapeDtypeStruct(q...  47.6 us
    pallas_call x1, Pallas kernels, exchange_qkv(): pl.pallas_call(exchange_qkv_kernel, out_shape=(jax.ShapeDtypeStruct((PLAN...  39 us
    pallas_call x1, Pallas kernels, plane_middle(): pl.pallas_call(plane_middle_kernel, grid=(steps,), out_shape=(jax.ShapeDt...  35.7 us
    pallas_call x1, Pallas kernels, collect(): pl.pallas_call(collect_kernel, out_shape=(jax.ShapeDtypeStruct(x.shape, B...  35.5 us
    unnamed x49, local copies, waits for them, and re-layouts  13.7 us

profile of v3, /device:TPU:0, one launch (start us, length us, event | category | flops | bytes accessed | tf_op | source)
XLA Modules:
  0.0 408.5 jit_solution(520892398915295632)
XLA Ops:
  0.6 0.9 fusion.6
  1.6 0.9 fusion.5
  2.5 0.1 concatenate.52
  2.8 0.7 convert_element_type.23
  3.5 0.1 copy.45
  3.7 6.1 %concatenate.51 = bf16[2048]{0:T(1024)(128)(2,1)S(1)} concatenate(bf16[24]{0:T(256)(128)(2,1)} %param.18, bf16[24]{0:T(256)(128)(2,1)} %param.19, bf16[24]{0:T(256)(128)(2,1)} %param.21, bf16[24]{0:T(256)(128)(2,1)} %param.22, bf16[24]{0:T(256)(128)(2,1)} %param.24, bf16[24]{0:T(256)(128)(2,1)} %param.25, bf16[24]{0:T(256)(128)(2,1)} %param.26, bf16[24]{0:T(256)(128)(2,1)} %param.30, ...), dimensions={0} | concatenate | bytes 8192 | tf_op jit(solution)/shard_map/concatenate | solution.py:2329
  9.8 1.1 copy-done.7
  11.0 35.5 %collect.1 = (bf16[2,256,768]{2,1,0:T(8,128)(2,1)S(1)}, bf16[2,4,4,16,128]{4,3,2,1,0:T(8,128)(2,1)S(1)}, bf16[768,2304]{1,0:T(8,128)(2,1)S(1)}) custom-call(bf16[2,256,768]{2,1,0:T(8,128)(2,1)S(1)} %copy-done.7, bf16[16,128]{1,0:T(8,128)(2,1)S(1)} %bitcast.49, bf16[48,1152]{1,0:T(8,128)(2,1)S(1)} %pad_maximum_fusion.1.s_qkv_ref), custom_call_target="tpu_custom_call" | custom-call | tf_op jit(solution)/shard_map/collect/pallas_call | solution.py:1073
  46.5 1.8 copy-done
  48.5 0.1 reshape.151.vec_ref
  48.8 0.1 concatenate.55
  49.0 4.4 %plane_qkv.1 = (bf16[512,768]{1,0:T(8,128)(2,1)S(1)}, bf16[2,4,2,3,256,128]{5,4,3,2,1,0:T(8,128)(2,1)S(1)}) custom-call(bf16[2,256,768]{2,1,0:T(8,128)(2,1)S(1)} %get-tuple-element.49.x_ref, f32[8,768]{1,0:T(8,128)S(1)} %reshape.151.vec_ref, bf16[768,2304]{1,0:T(8,128)(2,1)} %copy-done, f32[1,2304]{1,0:T(1,128)S(1)} %bitcast.48), custom_call_target="tpu_custom_call" | custom-call | tf_op jit(solution)/shard_map/plane_qkv/pallas_call | solution.py:1443
  53.4 39.0 %exchange_qkv.1 = (bf16[4,4,3,256,128]{4,3,2,1,0:T(8,128)(2,1)S(1)}, bf16[4,48,1920]{2,1,0:T(8,128)(2,1)S(1)}, bf16[4,96,768]{2,1,0:T(8,128)(2,1)S(1)}) custom-call(bf16[2,4,2,3,256,128]{5,4,3,2,1,0:T(8,128)(2,1)S(1)} %get-tuple-element.51.source_ref, bf16[48,1920]{1,0:T(8,128)(2,1)S(1)} %maximum_maximum_fusion.s_ou_ref, bf16[96,768]{1,0:T(8,128)(2,1)S(1)} %copy-done.12), custom_call_target="tpu_custom_call" | custom-call | tf_op jit(solution)/shard_map/exchange_qkv/pallas_call | solution.py:1313
  92.5 1.7 copy-done.1
  94.1 0.9 copy-done.9
  95.0 0.8 copy-done.10
  96.1 0.1 copy.47
  96.3 0.6 dynamic-slice_bitcast_fusion.table_ref
  96.9 63.8 %plane_attention.1 = (bf16[2,4,2,4,64,128]{5,4,3,2,1,0:T(8,128)(2,1)}, f32[64,64,128]{2,1,0:T(8,128)}, bf16[2,256,768]{2,1,0:T(8,128)(2,1)}, bf16[768,768]{1,0:T...) custom-call(s32[1,192]{1,0:T(1,128)} %dynamic-slice_bitcast_fusion.table_ref, ...), custom_call_target="tpu_custom_call" | custom-call | tf_op jit(solution)/shard_map/plane_attention/pallas_call | solution.py:1619
  160.9 0.6 copy.50
  161.5 35.7 %plane_middle.1 = (bf16[2,256,768]{2,1,0:T(8,128)(2,1)}, bf16[2,4,2,256,128]{4,3,2,1,0:T(8,128)(2,1)}, f32[512,768]{1,0:T(8,128)}, bf16[32,48,384]{2,1,0:T(8,128...) custom-call(bf16[2,4,2,256,128]{4,3,2,1,0:T(8,128)(2,1)} %bitcast.55, ...), custom_call_target="tpu_custom_call" | custom-call | tf_op jit(solution)/shard_map/plane_middle/pallas_call | solution.py:1926
  197.2 1.4 copy-done.6
  198.5 15.4 %exchange_dmixed.1 = bf16[4,4,256,128]{3,2,1,0:T(8,128)(2,1)S(1)} custom-call(bf16[2,4,2,256,128]{4,3,2,1,0:T(8,128)(2,1)S(1)} %copy-done.6), custom_call_target="tpu_custom_call" | custom-call | tf_op jit(solution)/shard_map/exchange_dmixed/pallas_call | solution.py:1221
  214.0 47.6 %plane_attention_back.1 = bf16[16,3,4,64,128]{4,3,2,1,0:T(8,128)(2,1)} custom-call(s32[1,192]{1,0:T(1,128)S(1)} %copy-done.13, bf16[16,3,4,64,128]{4,3,2,1,0:T(8,128)(2,1)} %bitcast.44, bf16[16,4,64,128]{3,2,1,0:T(8,128)(2,1)S(1)} %bitcast.46, f32[64,64,128]{2,1,0:T(8,128)S(1)} %copy-done.5), custom_call_target="tpu_custom_call" | custom-call | tf_op jit(solution)/shard_map/plane_attention_back/pallas_call | solution.py:1788
  261.6 1.9 copy-done.2
  263.5 36.7 %exchange_dqkv.1.recv_ref = bf16[2,4,2,3,256,128]{5,4,3,2,1,0:T(8,128)(2,1)S(1)} custom-call(bf16[4,4,3,256,128]{4,3,2,1,0:T(8,128)(2,1)S(1)} %bitcast.45), custom_call_target="tpu_custom_call" | custom-call | tf_op jit(solution)/shard_map/exchange_dqkv/pallas_call | solution.py:1221
  300.2 1.6 copy-done.3
  301.9 13.5 %plane_qkv_back.1 = (bf16[2,256,768]{2,1,0:T(8,128)(2,1)}, bf16[32,48,1152]{2,1,0:T(8,128)(2,1)}, f32[9,1,256]{2,1,0:T(1,128)}, f32[2,768]{1,0:T(2,128)}) custom-call(bf16[2,4,2,3,256,128]{5,4,3,2,1,0:T(8,128)(2,1)} %copy-done.3, bf16[512,768]{1,0:T(8,128)(2,1)} %copy-done.8, bf16[2,256,768]{2,1,0:T(8,128)(2,1)} %copy-done.4, ...), custom_call_target="tpu_custom_call" | custom-call | tf_op jit(solution)/shard_map/plane_qkv_back/pallas_call | solution.py:2047
  315.4 0.7 copy.62
  316.3 0.1 concatenate.60
  316.4 0.1 concatenate.59
  316.5 0.7 concatenate.61
  317.2 0.1 reshape.139
  317.8 0.7 copy.56
  318.4 78.9 %spread.1 = (bf16[2,256,768]{2,1,0:T(8,128)(2,1)}, bf16[2,256,768]{2,1,0:T(8,128)(2,1)}, f32[8,128]{1,0:T(8,128)}, f32[48,1152]{1,0:T(8,128)}, f32[48,384]{1,0:T...) custom-call(bf16[2,256,768]{2,1,0:T(8,128)(2,1)} %get-tuple-element.60.refs_0_, ...), custom_call_target="tpu_custom_call" | custom-call | tf_op jit(solution)/shard_map/spread/pallas_call | solution.py:2268
  397.4 1.1 fusion
  398.5 0.7 pad_maximum_fusion
  399.3 0.8 fusion.7
  400.1 0.6 pad_maximum_fusion.2
  400.7 1.0 fusion.3
  401.7 1.0 fusion.1
  402.7 1.0 fusion.2
  403.7 0.8 concatenate.64
  404.5 1.3 convert_element_type.30
  405.7 0.6 fusion.13
  406.3 0.6 slice.492
  406.9 0.9 copy.65
  407.8 0.7 copy.66
  (74 shorter events, 1.8 us)
Async XLA Ops:
  9.8 1.1 copy-start.7
  11.0 42.4 %copy-start.17 = (bf16[24,3072]{1,0:T(8,128)(2,1)S(1)}, bf16[24,3072]{1,0:T(8,128)(2,1)}, u32[]{:S(2)}) copy-start(bf16[24,3072]{1,0:T(8,128)(2,1)} %param.27) | copy-start | bytes 442372
  11.0 42.4 %copy-start.18 = (bf16[24,768]{1,0:T(8,128)(2,1)S(1)}, bf16[24,768]{1,0:T(8,128)(2,1)}, u32[]{:S(2)}) copy-start(bf16[24,768]{1,0:T(8,128)(2,1)} %param.23) | copy-start | bytes 110596
  46.5 1.8 copy-start
  48.3 44.1 %copy-start.4 = (bf16[2,256,768]{2,1,0:T(8,128)(2,1)}, bf16[2,256,768]{2,1,0:T(8,128)(2,1)S(1)}, u32[]{:S(2)}) copy-start(bf16[2,256,768]{2,1,0:T(8,128)(2,1)S(1)} %get-tuple-element.49.x_ref) | copy-start | bytes 2359300
  48.3 5.1 %copy-start.12 = (bf16[96,768]{1,0:T(8,128)(2,1)S(1)}, bf16[96,768]{1,0:T(8,128)(2,1)}, u32[]{:S(2)}) copy-start(bf16[96,768]{1,0:T(8,128)(2,1)} %s_down_ref.1) | copy-start | bytes 442372
  48.6 43.8 %copy-start.11 = (f32[8,768]{1,0:T(8,128)}, f32[8,768]{1,0:T(8,128)S(1)}, u32[]{:S(2)}) copy-start(f32[8,768]{1,0:T(8,128)S(1)} %reshape.151.vec_ref) | copy-start | bytes 73732
  53.3 42.5 %copy-start.8 = (bf16[512,768]{1,0:T(8,128)(2,1)}, bf16[512,768]{1,0:T(8,128)(2,1)S(1)}, u32[]{:S(2)}) copy-start(bf16[512,768]{1,0:T(8,128)(2,1)S(1)} %get-tuple-element.63.normed_ref) | copy-start | bytes 2359300
  92.4 1.7 copy-start.1
  94.1 0.9 copy-start.9
  95.0 0.8 copy-start.10
  161.5 52.5 %copy-start.13 = (s32[1,192]{1,0:T(1,128)S(1)}, s32[1,192]{1,0:T(1,128)}, u32[]{:S(2)}) copy-start(s32[1,192]{1,0:T(1,128)} %dynamic-slice_bitcast_fusion.table_ref) | copy-start | bytes 2308
  197.2 16.8 %copy-start.5 = (f32[64,64,128]{2,1,0:T(8,128)S(1)}, f32[64,64,128]{2,1,0:T(8,128)}, u32[]{:S(2)}) copy-start(f32[64,64,128]{2,1,0:T(8,128)} %get-tuple-element.62.lse_ref) | copy-start | bytes 6291460
  197.2 1.4 copy-start.6
  261.6 1.9 copy-start.2
  300.2 1.6 copy-start.3
  301.9 14.6 %copy-start.19 = (f32[4,768]{1,0:T(4,128)S(1)}, f32[4,768]{1,0:T(4,128)}, u32[]{:S(2)}) copy-start(f32[4,768]{1,0:T(4,128)} %get-tuple-element.68) | copy-start | bytes 36868
  301.9 15.7 %copy-start.20 = (f32[12,1,256]{2,1,0:T(1,128)S(1)}, f32[12,1,256]{2,1,0:T(1,128)}, u32[]{:S(2)}) copy-start(f32[12,1,256]{2,1,0:T(1,128)} %get-tuple-element.69) | copy-start | bytes 36868
  397.4 7.1 %copy-start.15 = (bf16[2,256,768]{2,1,0:T(8,128)(2,1)S(1)}, bf16[2,256,768]{2,1,0:T(8,128)(2,1)}, u32[]{:S(2)}) copy-start(bf16[2,256,768]{2,1,0:T(8,128)(2,1)} %get-tuple-element.75) | copy-start | bytes 2359300
  397.4 8.4 %copy-start.21 = (f32[8,128]{1,0:T(8,128)S(1)}, f32[8,128]{1,0:T(8,128)}, u32[]{:S(2)}) copy-start(f32[8,128]{1,0:T(8,128)} %get-tuple-element.76) | copy-start | bytes 12292
  397.4 9.5 %copy-start.14 = (bf16[2,256,768]{2,1,0:T(8,128)(2,1)S(1)}, bf16[2,256,768]{2,1,0:T(8,128)(2,1)}, u32[]{:S(2)}) copy-start(bf16[2,256,768]{2,1,0:T(8,128)(2,1)} %get-tuple-element.200) | copy-start | bytes 2359300
  399.3 8.6 %copy-start.16 = (f32[96,768]{1,0:T(8,128)S(1)}, f32[96,768]{1,0:T(8,128)}, u32[]{:S(2)}) copy-start(f32[96,768]{1,0:T(8,128)} %get-tuple-element.213) | copy-start | bytes 884740

commit v4 on v3

--- a/solution.py
+++ b/solution.py
@@ -1402,7 +1402,26 @@
             copy.wait_send()
 
 
-def plane_qkv_kernel(x_ref, vec_ref, w_ref, bias_ref, normed_ref, send_ref):
+def sort_entries(table_ref, sorted_ref):
+    count = table_ref.shape[1]
+    along = jnp.broadcast_to(table_ref[...].astype(F32), (count, count))
+    down = along.T
+    lane = lax.broadcasted_iota(jnp.int32, (count, count), 1).astype(F32)
+    row = lax.broadcasted_iota(jnp.int32, (count, count), 0).astype(F32)
+    before = (along < down) | ((along == down) & (lane < row))
+    rank = jnp.sum(jnp.where(before, 1.0, 0.0), axis=1, keepdims=True)
+    sorted_ref[0:1] = jnp.sum(jnp.where(rank == lane, row, 0.0), axis=0, keepdims=True).astype(
+        jnp.int32
+    )
+    sorted_ref[1:2] = jnp.sum(jnp.where(down <= lane, 1.0, 0.0), axis=0, keepdims=True).astype(
+        jnp.int32
+    )
+
+
+def plane_qkv_kernel(
+    x_ref, vec_ref, w_ref, bias_ref, table_ref, normed_ref, send_ref, sorted_ref
+):
+    sort_entries(table_ref, sorted_ref)
     pieces, rows, _ = x_ref.shape
     values = x_ref[...].reshape(pieces * rows, D).astype(F32)
     normal, _ = norm_parts(values)
@@ -1438,19 +1457,20 @@
                         send_ref[1, spot, piece, 2] = part.astype(BF16)
 
 
-def plane_qkv(x, vec, w, bias):
+def plane_qkv(x, vec, w, bias, table):
     pieces, rows, _ = x.shape
     return pl.pallas_call(
         plane_qkv_kernel,
         out_shape=(
             jax.ShapeDtypeStruct((pieces * rows, D), BF16),
             jax.ShapeDtypeStruct((2, SPOTS, PIECES, 3, rows, LANES), BF16),
+            jax.ShapeDtypeStruct((2, table.shape[1]), jnp.int32),
         ),
-        in_specs=[whole()] * 4,
-        out_specs=(whole(), whole()),
+        in_specs=[whole()] * 5,
+        out_specs=(whole(), whole(), whole()),
         compiler_params=params_of(48),
         name="plane_qkv",
-    )(x, vec, w, bias)
+    )(x, vec, w, bias, table)
 
 
 def plane_attend_kernel(
@@ -1650,34 +1670,202 @@
     )(table, qkv, dy, c_ou, c_down)
 
 
-def plane_attend_back_kernel(
-    table_ref, qkv_ref, grad_ref, lse_ref, out_ref, sums_ref, pa_ref, da_ref, pb_ref, db_ref
-):
+def inward_targets(core, spot):
+    for side in (3, 1, 2, 0):
+        for other in (core, 1 - core):
+            yield side, other, flip(spot, side), side == 0 and other is core
+
+
+class Inward:
+    def __init__(self, source, target, send_sem, recv_sem, local_sem):
+        self.source, self.target = source, target
+        self.send_sem, self.recv_sem, self.local_sem = send_sem, recv_sem, local_sem
+        self.core, self.plane, self.spot = place_here()
+        self.sends, self.keeps = [], []
+
+    def send(self, other, goal, stays, piece, part, parts):
+        source = self.source.at[2 * other + piece, goal, parts]
+        target = self.target.at[self.core, self.spot, piece, parts]
+        if stays:
+            copy = pltpu.make_async_copy(source, target, self.local_sem.at[part, piece])
+            self.keeps.append(copy)
+        else:
+            copy = remote(
+                source,
+                target,
+                self.send_sem.at[len(self.sends)],
+                self.recv_sem.at[self.core, self.spot, piece, part],
+                (other, rank_of(self.plane, goal)),
+            )
+            self.sends.append(copy)
+        copy.start()
+
+    def finish(self, widths):
+        for side, other, goal, stays in inward_targets(self.core, self.spot):
+            if stays:
+                continue
+            for piece in range(PIECES):
+                for part, parts in enumerate(widths):
+                    target = self.target.at[other, goal, piece, parts]
+                    remote(
+                        target,
+                        target,
+                        self.send_sem.at[0],
+                        self.recv_sem.at[other, goal, piece, part],
+                        (self.core, rank_of(self.plane, self.spot)),
+                    ).wait_recv()
+        for copy in self.sends:
+            copy.wait_send()
+        for copy in self.keeps:
+            copy.wait()
+
+
+def plane_attend_back_kernel(count, *refs):
+    table_ref, sorted_ref, qkv_ref, grad_source_ref, lse_ref, hidden_ref = refs[:6]
+    sources, refs = refs[6 : 6 + count], refs[6 + count :]
+    back_ref, hidden_out_ref = refs[:2]
+    outs, refs = refs[2 : 2 + count], refs[2 + count :]
+    buffers, refs = refs[: 7 * count], refs[7 * count :]
+    grad_ref, out_ref, sums_ref, shares_ref, walked_ref = refs[:5]
+    reduce_send, reduce_recv, reduce_local = refs[5:8]
+    grad_sems, back_sems, move_sems = refs[8:11], refs[11:14], refs[14:17]
+
     groups, _, local, _, _ = qkv_ref.shape
     blocks = groups * local
     half = blocks // 2
-    core = lax.axis_index("gx")
+    core, plane, spot = place_here()
     low = low_lanes(BLOCK)
     masks = [half_mask(True), half_mask(False)]
 
+    greet(both_partners(core, plane, spot))
+    finish_grad = outward_send(grad_source_ref, grad_ref, *grad_sems)
+    reduces = [
+        Reduce(
+            source,
+            *buffers[7 * number : 7 * number + 7],
+            out,
+            (reduce_send.at[number], reduce_recv.at[number], reduce_local.at[number]),
+        )
+        for number, (source, out) in enumerate(zip(sources, outs))
+    ]
+    for one in reduces:
+        one.start()
+    finish_hidden = from_planes(hidden_ref, hidden_out_ref, *move_sems)
+
     def load(component, block):
         return qkv_ref[lax.div(block, local), component, lax.rem(block, local)]
 
     def load_grad(block):
-        return grad_ref[lax.div(block, local), lax.rem(block, local)]
+        rank = lax.div(block, local)
+        return grad_ref[lax.div(rank, SPOTS), lax.rem(rank, SPOTS), lax.rem(block, local)]
 
     def store(component, block, value):
-        out_ref[lax.div(block, local), component, lax.rem(block, local)] = value.astype(BF16)
+        rank = lax.div(block, local)
+        out_ref[
+            lax.div(rank, SPOTS), lax.rem(rank, SPOTS), component, lax.rem(block, local)
+        ] = value.astype(BF16)
+
+    nothing = jnp.zeros((BLOCK, LANES), F32)
 
     def clear(block, carry):
         for slot in range(2):
-            sums_ref[slot, block] = jnp.zeros((BLOCK, LANES), F32)
+            sums_ref[slot, block] = nothing
         return carry
 
     lax.fori_loop(0, blocks, clear, 0)
-
-    def one(block, slot, ids, bias):
-        keys = jnp.concatenate([load(1 + slot, spot) for spot in ids], axis=0)
+    finish_grad()
+
+    spans = blocks // SPAN
+    ends = (0, blocks - 1)
+    end = core * (blocks - 1)
+    both_a = jnp.concatenate(
+        [load(0, number) * masks[0] for number in ends]
+        + [load_grad(number) * masks[1] for number in ends],
+        axis=0,
+    )
+    both_b = jnp.concatenate([load(0, end) * masks[1], load_grad(end) * masks[0]], axis=0)
+    logs_a = jnp.concatenate([lse_ref[number][:, 0:1] for number in ends], axis=0)
+    logs_b = lse_ref[end][:, HEAD_DIM : HEAD_DIM + 1]
+    wide = SPAN * BLOCK // LANES
+    sides = ((0, both_a, logs_a), (1, both_b, logs_b))
+
+    def keys_at(span, slot):
+        return jnp.concatenate(
+            [load(1 + slot, span * SPAN + number) for number in range(SPAN)], axis=0
+        )
+
+    def put(slot, first, value):
+        for piece in range(value.shape[0] // BLOCK):
+            for column in range(wide):
+                shares_ref[slot, first + piece * wide + column] = value[
+                    piece * BLOCK : (piece + 1) * BLOCK, column * LANES : (column + 1) * LANES
+                ]
+
+    def get(slot, first, pieces):
+        return jnp.concatenate(
+            [
+                jnp.concatenate(
+                    [shares_ref[slot, first + piece * wide + column] for column in range(wide)],
+                    axis=1,
+                )
+                for piece in range(pieces)
+            ],
+            axis=0,
+        )
+
+    def first_pass(span, carry):
+        deltas = []
+        for slot, both, logs in sides:
+            rows = both.shape[0] // 2
+            size = rows // BLOCK * wide
+            products = dot_rt(both, keys_at(span, slot))
+            weights = jnp.exp(products[:rows] - logs)
+            grad_weights = products[rows:]
+            put(slot, span * size, weights)
+            put(slot, (spans + span) * size, grad_weights)
+            deltas.append(carry[slot] + jnp.sum(weights * grad_weights, axis=1, keepdims=True))
+        return tuple(deltas)
+
+    deltas = lax.fori_loop(
+        0, spans, first_pass, (jnp.zeros((2 * BLOCK, 1), F32), jnp.zeros((BLOCK, 1), F32))
+    )
+
+    def second_pass(span, carry):
+        totals = []
+        for slot, both, logs in sides:
+            rows = both.shape[0] // 2
+            size = rows // BLOCK * wide
+            weights = get(slot, span * size, rows // BLOCK)
+            grad_scores = weights * (
+                get(slot, (spans + span) * size, rows // BLOCK) - deltas[slot]
+            )
+            stacked = jnp.concatenate([grad_scores, weights], axis=0).astype(BF16)
+            shares = dot_lt(stacked, both)
+            for number in range(SPAN):
+                sums_ref[slot, span * SPAN + number] += shares[
+                    number * BLOCK : (number + 1) * BLOCK
+                ]
+            totals.append(carry[slot] + dot(stacked[:rows], keys_at(span, slot)))
+        return tuple(totals)
+
+    query_a, query_b = lax.fori_loop(
+        0,
+        spans,
+        second_pass,
+        (jnp.zeros((2 * BLOCK, LANES), F32), nothing),
+    )
+    for place, number in enumerate(ends):
+        rows = slice(place * BLOCK, (place + 1) * BLOCK)
+        store(0, number, jnp.where(low, query_a[rows], query_b) * SCALE)
+        for slot in range(2):
+            for pick in range(RANDOM):
+                shares_ref[slot, number * RANDOM + pick] = nothing
+
+    for one in reduces:
+        one.corners()
+
+    def one_block(block, slot, ids, bias):
+        keys = jnp.concatenate([load(1 + slot, number) for number in ids], axis=0)
         both = jnp.concatenate(
             [load(0, block) * masks[slot], load_grad(block) * masks[1 - slot]], axis=0
         )
@@ -1690,110 +1878,136 @@
         stacked = jnp.concatenate([grad_scores, weights], axis=0).astype(BF16)
         return dot(stacked[:BLOCK], keys), dot_lt(stacked, both)
 
-    def add(slot, ids, shares):
-        for place, spot in enumerate(ids):
-            sums_ref[slot, spot] += shares[place * BLOCK : (place + 1) * BLOCK]
+    def add(block, slot, shares):
+        fixed = (block - 1, block, block + 1, 0, blocks - 1)
+        for place, number in enumerate(fixed):
+            sums_ref[slot, number] += shares[place * BLOCK : (place + 1) * BLOCK]
+        for pick in range(RANDOM):
+            place = len(fixed) + pick
+            shares_ref[slot, block * RANDOM + pick] = shares[
+                place * BLOCK : (place + 1) * BLOCK
+            ]
 
     def sparse(step, carry):
         mine = 1 + step + core * (half - 1)
         other = 1 + step + (1 - core) * (half - 1)
         ids, bias = slots_of(table_ref, 0, mine, blocks)
         far_ids, far_bias = slots_of(table_ref, 0, other, blocks)
-        query_a, shares_a = one(mine, 0, ids, bias)
-        query_b, shares_b = one(mine, 1, ids, bias)
-        query_c, shares_c = one(other, 0, far_ids, far_bias)
+        query_a, shares_a = one_block(mine, 0, ids, bias)
+        query_b, shares_b = one_block(mine, 1, ids, bias)
+        query_c, shares_c = one_block(other, 0, far_ids, far_bias)
         store(0, mine, jnp.where(low, query_a, query_b) * SCALE)
         store(0, other, query_c * SCALE)
-        add(0, ids, shares_a)
-        add(1, ids, shares_b)
-        add(0, far_ids, shares_c)
+        add(mine, 0, shares_a)
+        add(mine, 1, shares_b)
+        add(other, 0, shares_c)
+        for pick in range(RANDOM):
+            shares_ref[1, other * RANDOM + pick] = nothing
         return carry
 
-    lax.fori_loop(0, half - 1, sparse, 0)
-
-    spans = blocks // SPAN
-    ends = (0, blocks - 1)
-    end = core * (blocks - 1)
-    both_a = jnp.concatenate(
-        [load(0, number) * masks[0] for number in ends]
-        + [load_grad(number) * masks[1] for number in ends],
-        axis=0,
-    )
-    both_b = jnp.concatenate([load(0, end) * masks[1], load_grad(end) * masks[0]], axis=0)
-    logs_a = jnp.concatenate([lse_ref[number][:, 0:1] for number in ends], axis=0)
-    logs_b = lse_ref[end][:, HEAD_DIM : HEAD_DIM + 1]
-
-    def keys_at(span, slot):
-        return jnp.concatenate(
-            [load(1 + slot, span * SPAN + number) for number in range(SPAN)], axis=0
-        )
-
-    def first_pass(span, carry):
-        deltas = []
-        for slot, both, logs, p_ref, d_ref in (
-            (0, both_a, logs_a, pa_ref, da_ref),
-            (1, both_b, logs_b, pb_ref, db_ref),
-        ):
-            rows = both.shape[0] // 2
-            products = dot_rt(both, keys_at(span, slot))
-            weights = jnp.exp(products[:rows] - logs)
-            grad_weights = products[rows:]
-            p_ref[span] = weights
-            d_ref[span] = grad_weights
-            deltas.append(carry[slot] + jnp.sum(weights * grad_weights, axis=1, keepdims=True))
-        return tuple(deltas)
-
-    deltas = lax.fori_loop(
-        0, spans, first_pass, (jnp.zeros((2 * BLOCK, 1), F32), jnp.zeros((BLOCK, 1), F32))
-    )
-
-    def second_pass(span, carry):
+    back = Inward(out_ref, back_ref, *back_sems)
+    widths = (slice(0, 1), slice(1, 3))
+
+    def send_queries(piece):
+        for side, other, goal, stays in inward_targets(core, spot):
+            back.send(other, goal, stays, piece, 0, widths[0])
+
+    lax.fori_loop(0, half // 2, sparse, 0)
+    for one in reduces:
+        one.sides()
+    send_queries(0)
+    lax.fori_loop(half // 2, half - 1, sparse, 0)
+    send_queries(1)
+    for one in reduces:
+        one.columns()
+
+    def walk(number, carry):
+        entry = sorted_ref[0, number]
+        earlier = sorted_ref[0, jnp.maximum(number - 1, 0)]
+        keep = jnp.where(table_ref[0, entry] == table_ref[0, earlier], 1.0, 0.0).astype(F32)
         totals = []
-        for slot, both, p_ref, d_ref in (
-            (0, both_a, pa_ref, da_ref),
-            (1, both_b, pb_ref, db_ref),
-        ):
-            rows = both.shape[0] // 2
-            weights = p_ref[span]
-            grad_scores = weights * (d_ref[span] - deltas[slot])
-            stacked = jnp.concatenate([grad_scores, weights], axis=0).astype(BF16)
-            add(slot, [span * SPAN + number for number in range(SPAN)], dot_lt(stacked, both))
-            totals.append(carry[slot] + dot(stacked[:rows], keys_at(span, slot)))
+        for slot in range(2):
+            total = carry[slot] * keep + shares_ref[slot, entry]
+            walked_ref[slot, number] = total.astype(BF16)
+            totals.append(total)
         return tuple(totals)
 
-    query_a, query_b = lax.fori_loop(
-        0,
-        spans,
-        second_pass,
-        (jnp.zeros((2 * BLOCK, LANES), F32), jnp.zeros((BLOCK, LANES), F32)),
-    )
-    for place, number in enumerate(ends):
-        rows = slice(place * BLOCK, (place + 1) * BLOCK)
-        store(0, number, jnp.where(low, query_a[rows], query_b) * SCALE)
-
-    def finish(block, carry):
-        for slot in range(2):
-            store(1 + slot, block, sums_ref[slot, block])
-        return carry
-
-    lax.fori_loop(0, blocks, finish, 0)
-
-
-def plane_attention_back(table, qkv, grad, lse):
+    lax.fori_loop(0, blocks * RANDOM, walk, (nothing, nothing))
+
+    for side, other, goal, stays in inward_targets(core, spot):
+        for piece in range(PIECES):
+            first = ((2 * other + piece) * SPOTS + goal) * local
+
+            def close(number, carry, first=first):
+                block = first + number
+                stop = sorted_ref[1, block]
+                start = jnp.where(block == 0, 0, sorted_ref[1, jnp.maximum(block - 1, 0)])
+                some = jnp.where(stop > start, 1.0, 0.0).astype(F32)
+                for slot in range(2):
+                    share = walked_ref[slot, jnp.maximum(stop - 1, 0)].astype(F32)
+                    store(1 + slot, block, sums_ref[slot, block] + share * some)
+                return carry
+
+            lax.fori_loop(0, local, close, 0)
+            back.send(other, goal, stays, piece, 1, widths[1])
+
+    for one in reduces:
+        one.finish()
+    finish_hidden()
+    back.finish(widths)
+
+
+def plane_attention_back(table, sorted_table, qkv, grad_source, lse, hidden, sources):
     groups, _, local, _, _ = qkv.shape
     blocks = groups * local
-    spans = blocks // SPAN
-    wide = VMEM((spans, 2 * BLOCK, SPAN * BLOCK), F32)
-    thin = VMEM((spans, BLOCK, SPAN * BLOCK), F32)
+    count = len(sources)
+    buffers = []
+    for source in sources:
+        buffers += reduce_scratch(source.shape, source.dtype)
+    tile = (local, BLOCK, LANES)
+    dma = pltpu.SemaphoreType.DMA
     return pl.pallas_call(
-        plane_attend_back_kernel,
-        out_shape=jax.ShapeDtypeStruct(qkv.shape, BF16),
-        in_specs=[whole(pltpu.SMEM), whole(), whole(), whole()],
-        out_specs=whole(),
-        scratch_shapes=[VMEM((2, blocks, BLOCK, LANES), F32), wide, wide, thin, thin],
-        compiler_params=params_of(48),
+        functools.partial(plane_attend_back_kernel, count),
+        out_shape=(
+            jax.ShapeDtypeStruct((2, SPOTS, PIECES, 3) + tile, BF16),
+            jax.ShapeDtypeStruct(hidden.shape, BF16),
+        )
+        + tuple(jax.ShapeDtypeStruct(source.shape[3:], F32) for source in sources),
+        in_specs=[
+            whole(pltpu.SMEM),
+            whole(pltpu.SMEM),
+            whole(),
+            whole(ANY),
+            whole(),
+            whole(ANY),
+        ]
+        + [whole(ANY)] * count,
+        out_specs=(whole(ANY), whole(ANY)) + (whole(),) * count,
+        scratch_shapes=buffers
+        + [
+            VMEM((PLANES, SPOTS) + tile, BF16),
+            VMEM((PLANES, SPOTS, 3) + tile, BF16),
+            VMEM((2, blocks, BLOCK, LANES), F32),
+            VMEM((2, blocks * RANDOM, BLOCK, LANES), F32),
+            VMEM((2, blocks * RANDOM, BLOCK, LANES), BF16),
+            dma((count, REDUCE_SEMS)),
+            dma((count, REDUCE_SEMS)),
+            dma((count, 4)),
+        ]
+        + exchange_sems((PLANES, SPOTS))
+        + [
+            dma((28,)),
+            dma((2, SPOTS, PIECES, 2)),
+            dma((2, PIECES)),
+            dma((2,)),
+            dma((2,)),
+            dma((2,)),
+        ],
+        compiler_params=pltpu.CompilerParams(
+            vmem_limit_bytes=60 * 1024 * 1024, collective_id=5, has_side_effects=True
+        ),
         name="plane_attention_back",
-    )(table, qkv, grad, lse)
+    )(table, sorted_table, qkv, grad_source, lse, hidden, *sources)
 
 
 def by_owner(out_ref, values):
@@ -2224,11 +2438,11 @@
 
 
 def spread_kernel(count, *refs):
-    hidden_ref, grad_ref = refs[:2]
-    sources = refs[2 : 2 + count]
-    hidden_out_ref, grad_out_ref = refs[2 + count : 4 + count]
-    outs = refs[4 + count : 4 + 2 * count]
-    scratch = refs[4 + 2 * count :]
+    grad_ref = refs[0]
+    sources = refs[1 : 1 + count]
+    grad_out_ref = refs[1 + count]
+    outs = refs[2 + count : 2 + 2 * count]
+    scratch = refs[2 + 2 * count :]
     buffers = scratch[: 7 * count]
     send_sem, recv_sem, local_sem, move_send, move_recv, move_local = scratch[7 * count :]
     core, plane, spot = place_here()
@@ -2244,10 +2458,7 @@
     ]
     for one in sums:
         one.start()
-    finish_grad = from_planes(grad_ref, grad_out_ref, move_send.at[0], move_recv.at[0], move_local.at[0])
-    finish_hidden = from_planes(
-        hidden_ref, hidden_out_ref, move_send.at[1], move_recv.at[1], move_local.at[1]
-    )
+    finish_grad = from_planes(grad_ref, grad_out_ref, move_send, move_recv, move_local)
     for one in sums:
         one.corners()
     for one in sums:
@@ -2257,37 +2468,33 @@
     for one in sums:
         one.finish()
     finish_grad()
-    finish_hidden()
-
-
-def spread(hidden, grad, sources):
+
+
+def spread(grad, sources):
     count = len(sources)
     buffers = []
     for source in sources:
         buffers += reduce_scratch(source.shape, source.dtype)
     return pl.pallas_call(
         functools.partial(spread_kernel, count),
-        out_shape=(
-            jax.ShapeDtypeStruct(hidden.shape, BF16),
-            jax.ShapeDtypeStruct(grad.shape, BF16),
-        )
+        out_shape=(jax.ShapeDtypeStruct(grad.shape, BF16),)
         + tuple(jax.ShapeDtypeStruct(source.shape[3:], F32) for source in sources),
-        in_specs=[whole(ANY)] * (2 + count),
-        out_specs=(whole(ANY), whole(ANY)) + (whole(),) * count,
+        in_specs=[whole(ANY)] * (1 + count),
+        out_specs=(whole(ANY),) + (whole(),) * count,
         scratch_shapes=buffers
         + [
             pltpu.SemaphoreType.DMA((count, REDUCE_SEMS)),
             pltpu.SemaphoreType.DMA((count, REDUCE_SEMS)),
             pltpu.SemaphoreType.DMA((count, 4)),
-            pltpu.SemaphoreType.DMA((2, 2)),
-            pltpu.SemaphoreType.DMA((2, 2)),
-            pltpu.SemaphoreType.DMA((2, 2)),
+            pltpu.SemaphoreType.DMA((2,)),
+            pltpu.SemaphoreType.DMA((2,)),
+            pltpu.SemaphoreType.DMA((2,)),
         ],
         compiler_params=pltpu.CompilerParams(
             vmem_limit_bytes=56 * 1024 * 1024, collective_id=2, has_side_effects=True
         ),
         name="spread",
-    )(hidden, grad, *sources)
+    )(grad, *sources)
 
 
 def fold_columns(array):
@@ -2353,8 +2560,10 @@
     tables = vecs[:, small : small + entries].reshape(2, PLANES * SPOTS, 2, local * RANDOM)
     tables = tables.astype(jnp.int32).transpose(2, 0, 1, 3).reshape(PLANES, 1, -1)
     table = lax.dynamic_index_in_dim(tables, plane, 0, keepdims=False)
-
-    normed, send = plane_qkv(x, vectors, w_qkv_all, bias)
+    spare = -table.shape[1] % LANES
+    table = jnp.pad(table, ((0, 0), (0, spare)), constant_values=2 * LANES)
+
+    normed, send, sorted_table = plane_qkv(x, vectors, w_qkv_all, bias, table)
     s_ou = jnp.concatenate([fold_columns(w_out), fold_columns(w_up)], axis=1)
     qkv, c_ou, c_down = exchange_qkv(send, s_ou, w_down)
     qkv = qkv.reshape(PLANES * SPOTS, 3, local, BLOCK, LANES)
@@ -2372,10 +2581,21 @@
         w_up_all,
         w_down_all.reshape(2, FF // 2, D),
     )
-    grad_mixed = outward(grad_send, 5, "exchange_dmixed")
-    grad_mixed = grad_mixed.reshape(PLANES * SPOTS, local, BLOCK, LANES)
-    dqkv = plane_attention_back(table, qkv, grad_mixed, lse)
-    dqkv = inward(dqkv.reshape(PLANES, SPOTS, 3, rows, LANES), 6, "exchange_dqkv")
+    grid = (2, PLANES, SPOTS)
+    dqkv, hidden_out, t_out, t_up, t_down = plane_attention_back(
+        table,
+        sorted_table,
+        qkv,
+        grad_send.reshape(2, SPOTS, PIECES, local, BLOCK, LANES),
+        lse,
+        hidden,
+        [
+            g_out.reshape(grid + g_out.shape[1:]),
+            g_up.reshape(grid + g_up.shape[1:]),
+            g_down.reshape(grid + (FF // RANKS, D)),
+        ],
+    )
+    dqkv = dqkv.reshape(2, SPOTS, PIECES, 3, rows, LANES)
     grad, g_qkv, g_bias, g_first = plane_qkv_back(dqkv, normed, x, dres, vectors, w_qkv_all)
 
     g_bias = g_bias.reshape(HALF_TILES, 2, LANES).swapaxes(0, 1).reshape(1, 3 * D)
@@ -2388,17 +2608,9 @@
     singles = jnp.concatenate(
         [singles, g_up_bias, jnp.zeros((RANKS, 8 * LANES - small), F32)], axis=1
     )
-    grid = (2, PLANES, SPOTS)
-    hidden_out, grad_hidden, singles, t_qkv, t_out, t_up, t_down = spread(
-        hidden,
+    grad_hidden, singles, t_qkv = spread(
         grad,
-        [
-            singles.reshape(grid + (8, LANES)),
-            g_qkv.reshape(grid + g_qkv.shape[1:]),
-            g_out.reshape(grid + g_out.shape[1:]),
-            g_up.reshape(grid + g_up.shape[1:]),
-            g_down.reshape(grid + (FF // RANKS, D)),
-        ],
+        [singles.reshape(grid + (8, LANES)), g_qkv.reshape(grid + g_qkv.shape[1:])],
     )
     singles = singles.reshape(8 * LANES)
     parts = [singles[number * own : (number + 1) * own] for number in range(8)]

time: 409 us -> 371 us (0.907)
  Pallas kernels: 371 us -> 336 us
  local copies, waits for them, and re-layouts: 32.4 us -> 27.4 us
    pallas_call x1, Pallas kernels: 78.9 us -> 33.8 us  [spread(): pl.pallas_call(functools.partial(spread_kernel, count), out_shape=(jax.Sh...]
    pallas_call x3 -> x1, Pallas kernels: 99.7 us -> 110 us  [plane_attention_back(): pl.pallas_call(functools.partial(plane_attend_back_kernel, count), out_sh...]
    unnamed x49 -> x41, local copies, waits for them, and re-layouts: 13.7 us -> 9.34 us
where the time goes in v4:
time: 371 us; the launch traced here: 370 us
  Pallas kernels  336 us (91%)
  local copies, waits for them, and re-layouts  27.4 us (7%)
  other arithmetic  5.66 us (2%)
    pallas_call x1, Pallas kernels, plane_attention_back(): pl.pallas_call(functools.partial(plane_attend_back_kernel, count), out_sh...  110 us
    pallas_call x1, Pallas kernels, plane_attention(): pl.pallas_call(plane_attend_kernel, out_shape=(jax.ShapeDtypeStruct((2, S...  63.8 us
    pallas_call x1, Pallas kernels, exchange_qkv(): pl.pallas_call(exchange_qkv_kernel, out_shape=(jax.ShapeDtypeStruct((PLAN...  39 us
    pallas_call x1, Pallas kernels, plane_middle(): pl.pallas_call(plane_middle_kernel, grid=(steps,), out_shape=(jax.ShapeDt...  35.6 us
    pallas_call x1, Pallas kernels, collect(): pl.pallas_call(collect_kernel, out_shape=(jax.ShapeDtypeStruct(x.shape, B...  35.5 us
    pallas_call x1, Pallas kernels, spread(): pl.pallas_call(functools.partial(spread_kernel, count), out_shape=(jax.Sh...  33.8 us
    pallas_call x1, Pallas kernels, plane_qkv_back(): pl.pallas_call(plane_qkv_back_kernel, grid=(HALF_TILES,), out_shape=(jax....  13.5 us
    unnamed x41, local copies, waits for them, and re-layouts  9.34 us

profile of v4, /device:TPU:0, one launch (start us, length us, event | category | flops | bytes accessed | tf_op | source)
XLA Modules:
  0.0 369.8 jit_solution(13165032251311899149)
XLA Ops:
  0.6 0.9 fusion.6
  1.6 0.9 fusion.5
  2.5 0.1 concatenate.52
  2.6 0.1 concatenate.53
  2.8 0.7 convert_element_type.23
  3.5 0.1 copy.45
  3.6 0.1 convert_element_type.24
  3.7 6.1 %concatenate.51 = bf16[2048]{0:T(1024)(128)(2,1)S(1)} concatenate(bf16[24]{0:T(256)(128)(2,1)} %param.18, bf16[24]{0:T(256)(128)(2,1)} %param.19, bf16[24]{0:T(256)(128)(2,1)} %param.21, bf16[24]{0:T(256)(128)(2,1)} %param.22, bf16[24]{0:T(256)(128)(2,1)} %param.24, bf16[24]{0:T(256)(128)(2,1)} %param.25, bf16[24]{0:T(256)(128)(2,1)} %param.26, bf16[24]{0:T(256)(128)(2,1)} %param.30, ...), dimensions={0} | concatenate | bytes 8192 | tf_op jit(solution)/shard_map/concatenate | solution.py:2536
  9.8 1.1 copy-done.3
  11.0 35.5 %collect.1 = (bf16[2,256,768]{2,1,0:T(8,128)(2,1)S(1)}, bf16[2,4,4,16,128]{4,3,2,1,0:T(8,128)(2,1)S(1)}, bf16[768,2304]{1,0:T(8,128)(2,1)S(1)}) custom-call(bf16[2,256,768]{2,1,0:T(8,128)(2,1)S(1)} %copy-done.3, bf16[16,128]{1,0:T(8,128)(2,1)S(1)} %bitcast.47, bf16[48,1152]{1,0:T(8,128)(2,1)S(1)} %pad_maximum_fusion.1.s_qkv_ref), custom_call_target="tpu_custom_call" | custom-call | tf_op jit(solution)/shard_map/collect/pallas_call | solution.py:1073
  46.5 1.8 copy-done
  48.4 0.1 reshape.158
  48.5 0.1 reshape.151.vec_ref
  48.8 0.1 concatenate.55
  49.2 0.1 copy.47
  49.3 0.1 reshape.150
  49.5 4.4 %plane_qkv.1 = (bf16[512,768]{1,0:T(8,128)(2,1)S(1)}, bf16[2,4,2,3,256,128]{5,4,3,2,1,0:T(8,128)(2,1)S(1)}, s32[2,256]{1,0:T(2,128)S(1)}) custom-call(bf16[2,256,768]{2,1,0:T(8,128)(2,1)S(1)} %get-tuple-element.51.x_ref, f32[8,768]{1,0:T(8,128)S(1)} %reshape.151.vec_ref, bf16[768,2304]{1,0:T(8,128)(2,1)} %copy-done, f32[1,2304]{1,0:T(1,128)S(1)} %bitcast.46, ...), custom_call_target="tpu_custom_call" | custom-call | tf_op jit(solution)/shard_map/plane_qkv/pallas_call | solution.py:1462
  53.9 0.6 copy-done.10
  54.5 39.0 %exchange_qkv.1 = (bf16[4,4,3,256,128]{4,3,2,1,0:T(8,128)(2,1)S(1)}, bf16[4,48,1920]{2,1,0:T(8,128)(2,1)S(1)}, bf16[4,96,768]{2,1,0:T(8,128)(2,1)S(1)}) custom-call(bf16[2,4,2,3,256,128]{5,4,3,2,1,0:T(8,128)(2,1)S(1)} %get-tuple-element.54.source_ref, bf16[48,1920]{1,0:T(8,128)(2,1)S(1)} %maximum_maximum_fusion.s_ou_ref, bf16[96,768]{1,0:T(8,128)(2,1)S(1)} %copy-done.8), custom_call_target="tpu_custom_call" | custom-call | tf_op jit(solution)/shard_map/exchange_qkv/pallas_call | solution.py:1313
  93.6 1.7 copy-done.1
  95.2 0.9 copy-done.5
  96.1 0.8 copy-done.6
  96.9 63.8 %plane_attention.1 = (bf16[2,4,2,4,64,128]{5,4,3,2,1,0:T(8,128)(2,1)}, f32[64,64,128]{2,1,0:T(8,128)}, bf16[2,256,768]{2,1,0:T(8,128)(2,1)}, bf16[768,768]{1,0:T...) custom-call(s32[1,256]{1,0:T(1,128)} %copy-done.9, bf16[16,3,4,64,128]{4,3,2,1,0:T(8,128)(2,1)} %bitcast.43, ...), custom_call_target="tpu_custom_call" | custom-call | tf_op jit(solution)/shard_map/plane_attention/pallas_call | solution.py:1639
  160.9 0.6 copy.50
  161.5 35.6 %plane_middle.1 = (bf16[2,256,768]{2,1,0:T(8,128)(2,1)}, bf16[2,4,2,256,128]{4,3,2,1,0:T(8,128)(2,1)}, f32[512,768]{1,0:T(8,128)}, bf16[32,48,384]{2,1,0:T(8,128...) custom-call(bf16[2,4,2,256,128]{4,3,2,1,0:T(8,128)(2,1)} %bitcast.55, ...), custom_call_target="tpu_custom_call" | custom-call | tf_op jit(solution)/shard_map/plane_middle/pallas_call | solution.py:2140
  197.2 110.0 %plane_attention_back.1 = (bf16[2,4,2,3,4,64,128]{6,5,4,3,2,1,0:T(8,128)(2,1)}, bf16[2,256,768]{2,1,0:T(8,128)(2,1)}, f32[48,384]{1,0:T(8,128)}, f32[48,1536]{1,0:T(8,128)}, f32[96,768]{1,0:T(8,128)}) custom-call(s32[1,256]{1,0:T(1,128)} %copy-done.9, s32[2,256]{1,0:T(2,128)} %copy-done.10, bf16[16,3,4,64,128]{4,3,2,1,0:T(8,128)(2,1)} %bitcast.44, ...), custom_call_target="tpu_custom_call" | custom-call | tf_op jit(solution)/shard_map/plane_attention_back/pallas_call | solution.py:1969
  307.2 1.0 fusion
  308.2 0.7 pad_maximum_fusion
  308.9 0.8 fusion.7
  309.7 0.6 pad_maximum_fusion.2
  310.3 13.5 %plane_qkv_back.1 = (bf16[2,256,768]{2,1,0:T(8,128)(2,1)}, bf16[32,48,1152]{2,1,0:T(8,128)(2,1)}, f32[9,1,256]{2,1,0:T(1,128)}, f32[2,768]{1,0:T(2,128)}) custom-call(bf16[2,4,2,3,256,128]{5,4,3,2,1,0:T(8,128)(2,1)} %bitcast.52, bf16[512,768]{1,0:T(8,128)(2,1)} %copy-done.4, bf16[2,256,768]{2,1,0:T(8,128)(2,1)} %copy-done.2, ...), custom_call_target="tpu_custom_call" | custom-call | tf_op jit(solution)/shard_map/plane_qkv_back/pallas_call | solution.py:2261
  323.8 0.7 copy.62
  324.7 0.1 concatenate.60
  324.8 0.1 concatenate.59
  324.9 0.7 concatenate.61
  325.6 0.1 reshape.142
  325.9 0.1 reshape.143
  326.2 0.7 copy.56
  326.9 33.8 %spread.1 = (bf16[2,256,768]{2,1,0:T(8,128)(2,1)}, f32[8,128]{1,0:T(8,128)}, f32[48,1152]{1,0:T(8,128)}) custom-call(bf16[2,256,768]{2,1,0:T(8,128)(2,1)} %get-tuple-element.73.refs_0_, f32[2,4,4,8,128]{4,3,2,1,0:T(8,128)} %bitcast.57, bf16[2,4,4,48,1152]{4,3,2,1,0:T(8,128)(2,1)} %bitcast.51), custom_call_target="tpu_custom_call" | custom-call | tf_op jit(solution)/shard_map/spread/pallas_call | solution.py:2478
  360.7 1.1 fusion.3
  361.8 1.0 fusion.1
  362.8 1.0 fusion.2
  363.8 0.8 concatenate.64
  364.6 2.4 convert_element_type.30
  367.0 0.6 fusion.13
  367.6 0.6 slice.492
  368.2 0.9 copy.65
  369.0 0.7 copy.66
  (65 shorter events, 1.4 us)
Async XLA Ops:
  9.8 1.1 copy-start.3
  11.0 43.5 %copy-start.13 = (bf16[24,3072]{1,0:T(8,128)(2,1)S(1)}, bf16[24,3072]{1,0:T(8,128)(2,1)}, u32[]{:S(2)}) copy-start(bf16[24,3072]{1,0:T(8,128)(2,1)} %param.27) | copy-start | bytes 442372
  46.5 1.8 copy-start
  48.3 6.2 %copy-start.2 = (bf16[2,256,768]{2,1,0:T(8,128)(2,1)}, bf16[2,256,768]{2,1,0:T(8,128)(2,1)S(1)}, u32[]{:S(2)}) copy-start(bf16[2,256,768]{2,1,0:T(8,128)(2,1)S(1)} %get-tuple-element.51.x_ref) | copy-start | bytes 2359300
  48.3 6.2 %copy-start.14 = (bf16[24,768]{1,0:T(8,128)(2,1)S(1)}, bf16[24,768]{1,0:T(8,128)(2,1)}, u32[]{:S(2)}) copy-start(bf16[24,768]{1,0:T(8,128)(2,1)} %param.23) | copy-start | bytes 110596
  48.3 6.2 %copy-start.8 = (bf16[96,768]{1,0:T(8,128)(2,1)S(1)}, bf16[96,768]{1,0:T(8,128)(2,1)}, u32[]{:S(2)}) copy-start(bf16[96,768]{1,0:T(8,128)(2,1)} %s_down_ref.1) | copy-start | bytes 442372
  48.6 44.9 %copy-start.7 = (f32[8,768]{1,0:T(8,128)}, f32[8,768]{1,0:T(8,128)S(1)}, u32[]{:S(2)}) copy-start(f32[8,768]{1,0:T(8,128)S(1)} %reshape.151.vec_ref) | copy-start | bytes 73732
  49.5 44.1 %copy-start.9 = (s32[1,256]{1,0:T(1,128)}, s32[1,256]{1,0:T(1,128)S(1)}, u32[]{:S(2)}) copy-start(s32[1,256]{1,0:T(1,128)S(1)} %pad.4.table_ref.refs_0_) | copy-start | bytes 3076
  53.9 0.6 copy-start.10
  54.4 39.1 %copy-start.4 = (bf16[512,768]{1,0:T(8,128)(2,1)}, bf16[512,768]{1,0:T(8,128)(2,1)S(1)}, u32[]{:S(2)}) copy-start(bf16[512,768]{1,0:T(8,128)(2,1)S(1)} %get-tuple-element.71.normed_ref) | copy-start | bytes 2359300
  93.5 1.7 copy-start.1
  95.2 0.9 copy-start.5
  96.1 0.8 copy-start.6
  310.3 14.6 %copy-start.15 = (f32[4,768]{1,0:T(4,128)S(1)}, f32[4,768]{1,0:T(4,128)}, u32[]{:S(2)}) copy-start(f32[4,768]{1,0:T(4,128)} %get-tuple-element.76) | copy-start | bytes 36868
  310.3 15.6 %copy-start.16 = (f32[12,1,256]{2,1,0:T(1,128)S(1)}, f32[12,1,256]{2,1,0:T(1,128)}, u32[]{:S(2)}) copy-start(f32[12,1,256]{2,1,0:T(1,128)} %get-tuple-element.77) | copy-start | bytes 36868
  360.7 6.2 %copy-start.17 = (f32[8,128]{1,0:T(8,128)S(1)}, f32[8,128]{1,0:T(8,128)}, u32[]{:S(2)}) copy-start(f32[8,128]{1,0:T(8,128)} %get-tuple-element.80) | copy-start | bytes 12292
  360.7 7.4 %copy-start.11 = (bf16[2,256,768]{2,1,0:T(8,128)(2,1)S(1)}, bf16[2,256,768]{2,1,0:T(8,128)(2,1)}, u32[]{:S(2)}) copy-start(bf16[2,256,768]{2,1,0:T(8,128)(2,1)} %get-tuple-element.204) | copy-start | bytes 2359300
  360.7 8.3 %copy-start.12 = (f32[96,768]{1,0:T(8,128)S(1)}, f32[96,768]{1,0:T(8,128)}, u32[]{:S(2)}) copy-start(f32[96,768]{1,0:T(8,128)} %get-tuple-element.217) | copy-start | bytes 884740

commit v5 on v4

--- a/solution.py
+++ b/solution.py
@@ -118,6 +118,14 @@
     lane = lax.broadcasted_iota(jnp.int32, (1, LANES), 1)
     keep = (lane < HEAD_DIM) if low_half else (lane >= HEAD_DIM)
     return jnp.where(keep, 1.0, 0.0).astype(BF16)
+
+
+def inner_slots(table_ref, block, blocks):
+    ids, bias = slots_of(table_ref, 0, block, blocks)
+    edge = (block == 0) | (block == blocks - 1)
+    ids[0] = jnp.maximum(ids[0], 0)
+    ids[2] = jnp.minimum(ids[2], blocks - 1)
+    return ids, bias + jnp.where(edge, NEGATIVE, 0.0).astype(F32)
 
 
 def slots_of(table_ref, micro, block, blocks):
@@ -1402,27 +1410,30 @@
             copy.wait_send()
 
 
-def sort_entries(table_ref, sorted_ref):
+def sort_entries(table_ref, sorted_ref, entries):
     count = table_ref.shape[1]
-    along = jnp.broadcast_to(table_ref[...].astype(F32), (count, count))
-    down = along.T
-    lane = lax.broadcasted_iota(jnp.int32, (count, count), 1).astype(F32)
+    core = lax.axis_index("gx")
+    lane = lax.broadcasted_iota(jnp.int32, (count, count), 1)
     row = lax.broadcasted_iota(jnp.int32, (count, count), 0).astype(F32)
-    before = (along < down) | ((along == down) & (lane < row))
-    rank = jnp.sum(jnp.where(before, 1.0, 0.0), axis=1, keepdims=True)
-    sorted_ref[0:1] = jnp.sum(jnp.where(rank == lane, row, 0.0), axis=0, keepdims=True).astype(
-        jnp.int32
-    )
-    sorted_ref[1:2] = jnp.sum(jnp.where(down <= lane, 1.0, 0.0), axis=0, keepdims=True).astype(
-        jnp.int32
-    )
+    everything = jnp.broadcast_to(table_ref[...].astype(F32), (count, count))
+    half = entries // 2
+    inside = (lane >= core * half) & (lane < (core + 1) * half)
+    lane = lane.astype(F32)
+    for number, along in enumerate((everything, jnp.where(inside, everything, 2.0 * LANES))):
+        down = along.T
+        before = (along < down) | ((along == down) & (lane < row))
+        rank = jnp.sum(jnp.where(before, 1.0, 0.0), axis=1, keepdims=True)
+        order = jnp.sum(jnp.where(rank == lane, row, 0.0), axis=0, keepdims=True)
+        upto = jnp.sum(jnp.where(down <= lane, 1.0, 0.0), axis=0, keepdims=True)
+        sorted_ref[2 * number : 2 * number + 1] = order.astype(jnp.int32)
+        sorted_ref[2 * number + 1 : 2 * number + 2] = upto.astype(jnp.int32)
 
 
 def plane_qkv_kernel(
     x_ref, vec_ref, w_ref, bias_ref, table_ref, normed_ref, send_ref, sorted_ref
 ):
-    sort_entries(table_ref, sorted_ref)
     pieces, rows, _ = x_ref.shape
+    sort_entries(table_ref, sorted_ref, PLANES * SPOTS * (rows // BLOCK) * RANDOM)
     values = x_ref[...].reshape(pieces * rows, D).astype(F32)
     normal, _ = norm_parts(values)
     normed_ref[...] = (normal * vec_ref[0:1] + vec_ref[1:2]).astype(BF16)
@@ -1464,7 +1475,7 @@
         out_shape=(
             jax.ShapeDtypeStruct((pieces * rows, D), BF16),
             jax.ShapeDtypeStruct((2, SPOTS, PIECES, 3, rows, LANES), BF16),
-            jax.ShapeDtypeStruct((2, table.shape[1]), jnp.int32),
+            jax.ShapeDtypeStruct((4, table.shape[1]), jnp.int32),
         ),
         in_specs=[whole()] * 5,
         out_specs=(whole(), whole(), whole()),
@@ -1670,6 +1681,52 @@
     )(table, qkv, dy, c_ou, c_down)
 
 
+class Outward:
+    def __init__(self, source, target, send_sem, recv_sem, local_sem):
+        self.target, self.recv_sem, self.send_sem = target, recv_sem, send_sem
+        self.core, self.plane, self.spot = place_here()
+        self.sends, self.keeps = [], []
+        for side in (3, 1, 2, 0):
+            for other in (self.core, 1 - self.core):
+                goal = flip(self.spot, side)
+                for piece in range(PIECES):
+                    start = source.at[other, goal, piece]
+                    stop = target.at[2 * self.core + piece, self.spot]
+                    if side == 0 and other is self.core:
+                        copy = pltpu.make_async_copy(start, stop, local_sem.at[piece])
+                        self.keeps.append(copy)
+                    else:
+                        copy = remote(
+                            start,
+                            stop,
+                            send_sem.at[len(self.sends)],
+                            recv_sem.at[2 * self.core + piece, self.spot],
+                            (other, rank_of(self.plane, goal)),
+                        )
+                        self.sends.append(copy)
+                    copy.start()
+
+    def arrive(self, side):
+        for other in (self.core, 1 - self.core):
+            if side == 0 and other is self.core:
+                for copy in self.keeps:
+                    copy.wait()
+                continue
+            for piece in range(PIECES):
+                place = (2 * other + piece, flip(self.spot, side))
+                remote(
+                    self.target.at[place],
+                    self.target.at[place],
+                    self.send_sem.at[0],
+                    self.recv_sem.at[place],
+                    (self.core, rank_of(self.plane, self.spot)),
+                ).wait_recv()
+
+    def finish(self):
+        for copy in self.sends:
+            copy.wait_send()
+
+
 def inward_targets(core, spot):
     for side in (3, 1, 2, 0):
         for other in (core, 1 - core):
@@ -1700,12 +1757,12 @@
             self.sends.append(copy)
         copy.start()
 
-    def finish(self, widths):
+    def finish(self, parts_of):
         for side, other, goal, stays in inward_targets(self.core, self.spot):
             if stays:
                 continue
             for piece in range(PIECES):
-                for part, parts in enumerate(widths):
+                for part, parts in enumerate(parts_of[0 if other is self.core else 1]):
                     target = self.target.at[other, goal, piece, parts]
                     remote(
                         target,
@@ -1720,25 +1777,28 @@
             copy.wait()
 
 
+KEYS_A, QUERIES, KEYS_B = range(3)
+
+
 def plane_attend_back_kernel(count, *refs):
     table_ref, sorted_ref, qkv_ref, grad_source_ref, lse_ref, hidden_ref = refs[:6]
     sources, refs = refs[6 : 6 + count], refs[6 + count :]
     back_ref, hidden_out_ref = refs[:2]
     outs, refs = refs[2 : 2 + count], refs[2 + count :]
     buffers, refs = refs[: 7 * count], refs[7 * count :]
-    grad_ref, out_ref, sums_ref, shares_ref, walked_ref = refs[:5]
-    reduce_send, reduce_recv, reduce_local = refs[5:8]
-    grad_sems, back_sems, move_sems = refs[8:11], refs[11:14], refs[14:17]
+    grad_ref, out_ref, sums_ref, shares_ref, walked_ref, sibling_ref = refs[:6]
+    scores_refs, refs = refs[6:10], refs[10:]
+    reduce_send, reduce_recv, reduce_local = refs[:3]
+    grad_sems, back_sems, move_sems, sibling_sems = refs[3:6], refs[6:9], refs[9:12], refs[12:14]
 
     groups, _, local, _, _ = qkv_ref.shape
     blocks = groups * local
-    half = blocks // 2
     core, plane, spot = place_here()
     low = low_lanes(BLOCK)
     masks = [half_mask(True), half_mask(False)]
 
     greet(both_partners(core, plane, spot))
-    finish_grad = outward_send(grad_source_ref, grad_ref, *grad_sems)
+    grads = Outward(grad_source_ref, grad_ref, *grad_sems)
     reduces = [
         Reduce(
             source,
@@ -1765,6 +1825,12 @@
             lax.div(rank, SPOTS), lax.rem(rank, SPOTS), component, lax.rem(block, local)
         ] = value.astype(BF16)
 
+    def stored(component, block):
+        rank = lax.div(block, local)
+        return out_ref[
+            lax.div(rank, SPOTS), lax.rem(rank, SPOTS), component, lax.rem(block, local)
+        ].astype(F32)
+
     nothing = jnp.zeros((BLOCK, LANES), F32)
 
     def clear(block, carry):
@@ -1773,98 +1839,9 @@
         return carry
 
     lax.fori_loop(0, blocks, clear, 0)
-    finish_grad()
-
-    spans = blocks // SPAN
-    ends = (0, blocks - 1)
-    end = core * (blocks - 1)
-    both_a = jnp.concatenate(
-        [load(0, number) * masks[0] for number in ends]
-        + [load_grad(number) * masks[1] for number in ends],
-        axis=0,
-    )
-    both_b = jnp.concatenate([load(0, end) * masks[1], load_grad(end) * masks[0]], axis=0)
-    logs_a = jnp.concatenate([lse_ref[number][:, 0:1] for number in ends], axis=0)
-    logs_b = lse_ref[end][:, HEAD_DIM : HEAD_DIM + 1]
-    wide = SPAN * BLOCK // LANES
-    sides = ((0, both_a, logs_a), (1, both_b, logs_b))
-
-    def keys_at(span, slot):
-        return jnp.concatenate(
-            [load(1 + slot, span * SPAN + number) for number in range(SPAN)], axis=0
-        )
-
-    def put(slot, first, value):
-        for piece in range(value.shape[0] // BLOCK):
-            for column in range(wide):
-                shares_ref[slot, first + piece * wide + column] = value[
-                    piece * BLOCK : (piece + 1) * BLOCK, column * LANES : (column + 1) * LANES
-                ]
-
-    def get(slot, first, pieces):
-        return jnp.concatenate(
-            [
-                jnp.concatenate(
-                    [shares_ref[slot, first + piece * wide + column] for column in range(wide)],
-                    axis=1,
-                )
-                for piece in range(pieces)
-            ],
-            axis=0,
-        )
-
-    def first_pass(span, carry):
-        deltas = []
-        for slot, both, logs in sides:
-            rows = both.shape[0] // 2
-            size = rows // BLOCK * wide
-            products = dot_rt(both, keys_at(span, slot))
-            weights = jnp.exp(products[:rows] - logs)
-            grad_weights = products[rows:]
-            put(slot, span * size, weights)
-            put(slot, (spans + span) * size, grad_weights)
-            deltas.append(carry[slot] + jnp.sum(weights * grad_weights, axis=1, keepdims=True))
-        return tuple(deltas)
-
-    deltas = lax.fori_loop(
-        0, spans, first_pass, (jnp.zeros((2 * BLOCK, 1), F32), jnp.zeros((BLOCK, 1), F32))
-    )
-
-    def second_pass(span, carry):
-        totals = []
-        for slot, both, logs in sides:
-            rows = both.shape[0] // 2
-            size = rows // BLOCK * wide
-            weights = get(slot, span * size, rows // BLOCK)
-            grad_scores = weights * (
-                get(slot, (spans + span) * size, rows // BLOCK) - deltas[slot]
-            )
-            stacked = jnp.concatenate([grad_scores, weights], axis=0).astype(BF16)
-            shares = dot_lt(stacked, both)
-            for number in range(SPAN):
-                sums_ref[slot, span * SPAN + number] += shares[
-                    number * BLOCK : (number + 1) * BLOCK
-                ]
-            totals.append(carry[slot] + dot(stacked[:rows], keys_at(span, slot)))
-        return tuple(totals)
-
-    query_a, query_b = lax.fori_loop(
-        0,
-        spans,
-        second_pass,
-        (jnp.zeros((2 * BLOCK, LANES), F32), nothing),
-    )
-    for place, number in enumerate(ends):
-        rows = slice(place * BLOCK, (place + 1) * BLOCK)
-        store(0, number, jnp.where(low, query_a[rows], query_b) * SCALE)
-        for slot in range(2):
-            for pick in range(RANDOM):
-                shares_ref[slot, number * RANDOM + pick] = nothing
-
-    for one in reduces:
-        one.corners()
-
-    def one_block(block, slot, ids, bias):
+
+    def one_block(block, slot):
+        ids, bias = inner_slots(table_ref, block, blocks)
         keys = jnp.concatenate([load(1 + slot, number) for number in ids], axis=0)
         both = jnp.concatenate(
             [load(0, block) * masks[slot], load_grad(block) * masks[1 - slot]], axis=0
@@ -1878,93 +1855,191 @@
         stacked = jnp.concatenate([grad_scores, weights], axis=0).astype(BF16)
         return dot(stacked[:BLOCK], keys), dot_lt(stacked, both)
 
-    def add(block, slot, shares):
-        fixed = (block - 1, block, block + 1, 0, blocks - 1)
-        for place, number in enumerate(fixed):
-            sums_ref[slot, number] += shares[place * BLOCK : (place + 1) * BLOCK]
-        for pick in range(RANDOM):
-            place = len(fixed) + pick
-            shares_ref[slot, block * RANDOM + pick] = shares[
-                place * BLOCK : (place + 1) * BLOCK
+    fixed = 5
+
+    def rank_blocks(rank, slot):
+        first = rank * local
+        results = [one_block(first + number, slot) for number in range(local)]
+
+        def share(number, place):
+            return results[number][1][place * BLOCK : (place + 1) * BLOCK]
+
+        for shift in range(-1, local + 1):
+            parts = [
+                share(number, shift - number + 1)
+                for number in range(local)
+                if 0 <= shift - number + 1 <= 2
             ]
-
-    def sparse(step, carry):
-        mine = 1 + step + core * (half - 1)
-        other = 1 + step + (1 - core) * (half - 1)
-        ids, bias = slots_of(table_ref, 0, mine, blocks)
-        far_ids, far_bias = slots_of(table_ref, 0, other, blocks)
-        query_a, shares_a = one_block(mine, 0, ids, bias)
-        query_b, shares_b = one_block(mine, 1, ids, bias)
-        query_c, shares_c = one_block(other, 0, far_ids, far_bias)
-        store(0, mine, jnp.where(low, query_a, query_b) * SCALE)
-        store(0, other, query_c * SCALE)
-        add(mine, 0, shares_a)
-        add(mine, 1, shares_b)
-        add(other, 0, shares_c)
-        for pick in range(RANDOM):
-            shares_ref[1, other * RANDOM + pick] = nothing
+            target = jnp.minimum(jnp.maximum(first + shift, 0), blocks - 1)
+            sums_ref[slot, target] += functools.reduce(jnp.add, parts)
+        for place, target in ((3, 0), (4, blocks - 1)):
+            sums_ref[slot, target] += functools.reduce(
+                jnp.add, [share(number, place) for number in range(local)]
+            )
+        for number in range(local):
+            for pick in range(RANDOM):
+                shares_ref[slot, (first + number) * RANDOM + pick] = share(number, fixed + pick)
+        return [result[0] for result in results]
+
+    def head_a(side):
+        def body(number, carry):
+            rank = number * SPOTS + flip(spot, side)
+            for place, query in enumerate(rank_blocks(rank, 0)):
+                store(QUERIES, rank * local + place, query * SCALE)
+            return carry
+
+        lax.fori_loop(0, PLANES, body, 0)
+
+    def head_b(number, carry):
+        rank = core * (groups // 2) + number
+        for place, query in enumerate(rank_blocks(rank, 1)):
+            block = rank * local + place
+            store(QUERIES, block, jnp.where(low, stored(QUERIES, block), query * SCALE))
         return carry
 
+    spans = blocks // SPAN
+    ends = (0, blocks - 1)
+
+    def dense(slot, p_ref, d_ref, numbers):
+        both = jnp.concatenate(
+            [load(0, number) * masks[slot] for number in numbers]
+            + [load_grad(number) * masks[1 - slot] for number in numbers],
+            axis=0,
+        )
+        rows = len(numbers) * BLOCK
+        column = slot * HEAD_DIM
+        logs = jnp.concatenate(
+            [lse_ref[number][:, column : column + 1] for number in numbers], axis=0
+        )
+
+        def keys_at(span):
+            return jnp.concatenate(
+                [load(1 + slot, span * SPAN + number) for number in range(SPAN)], axis=0
+            )
+
+        def first_pass(span, delta):
+            products = dot_rt(both, keys_at(span))
+            weights = jnp.exp(products[:rows] - logs)
+            grad_weights = products[rows:]
+            p_ref[span] = weights
+            d_ref[span] = grad_weights
+            return delta + jnp.sum(weights * grad_weights, axis=1, keepdims=True)
+
+        delta = lax.fori_loop(0, spans, first_pass, jnp.zeros((rows, 1), F32), unroll=2)
+
+        def second_pass(span, total):
+            weights = p_ref[span]
+            grad_scores = weights * (d_ref[span] - delta)
+            stacked = jnp.concatenate([grad_scores, weights], axis=0).astype(BF16)
+            shares = dot_lt(stacked, both)
+            for number in range(SPAN):
+                sums_ref[slot, span * SPAN + number] += shares[
+                    number * BLOCK : (number + 1) * BLOCK
+                ]
+            return total + dot(stacked[:rows], keys_at(span))
+
+        total = lax.fori_loop(0, spans, second_pass, jnp.zeros((rows, LANES), F32), unroll=2)
+        for place, number in enumerate(numbers):
+            query = total[place * BLOCK : (place + 1) * BLOCK] * SCALE
+            if slot == 1:
+                query = jnp.where(low, stored(QUERIES, number), query)
+            store(QUERIES, number, query)
+
+    def walk(slot, length):
+        def body(number, total):
+            entry = sorted_ref[2 * slot, number]
+            earlier = sorted_ref[2 * slot, jnp.maximum(number - 1, 0)]
+            keep = jnp.where(table_ref[0, entry] == table_ref[0, earlier], 1.0, 0.0).astype(F32)
+            total = total * keep + shares_ref[slot, entry]
+            walked_ref[slot, number] = total.astype(BF16)
+            return total
+
+        lax.fori_loop(0, length, body, nothing, unroll=4)
+
+    def close(slot, rank, component):
+        def body(number, carry):
+            block = rank * local + number
+            stop = sorted_ref[2 * slot + 1, block]
+            start = jnp.where(block == 0, 0, sorted_ref[2 * slot + 1, jnp.maximum(block - 1, 0)])
+            some = jnp.where(stop > start, 1.0, 0.0).astype(F32)
+            share = walked_ref[slot, jnp.maximum(stop - 1, 0)].astype(F32)
+            store(component, block, sums_ref[slot, block] + share * some)
+            return carry
+
+        lax.fori_loop(0, local, body, 0, unroll=True)
+
     back = Inward(out_ref, back_ref, *back_sems)
-    widths = (slice(0, 1), slice(1, 3))
-
-    def send_queries(piece):
-        for side, other, goal, stays in inward_targets(core, spot):
-            back.send(other, goal, stays, piece, 0, widths[0])
-
-    lax.fori_loop(0, half // 2, sparse, 0)
+    own_parts = (slice(0, 1), slice(1, 2), slice(2, 3))
+    far_parts = (slice(0, 2),)
+
+    for side in range(SPOTS):
+        grads.arrive(side)
+        head_a(side)
+        if side == 1:
+            for one in reduces:
+                one.corners()
+    dense(0, scores_refs[0], scores_refs[1], ends)
     for one in reduces:
         one.sides()
-    send_queries(0)
-    lax.fori_loop(half // 2, half - 1, sparse, 0)
-    send_queries(1)
+    walk(0, blocks * RANDOM)
+    for side, other, goal, stays in inward_targets(core, spot):
+        for piece in range(PIECES):
+            close(0, (2 * other + piece) * SPOTS + goal, KEYS_A)
+            if other is core:
+                back.send(other, goal, stays, piece, 0, own_parts[0])
+            else:
+                back.send(other, goal, stays, piece, 0, far_parts[0])
+    lax.fori_loop(0, groups // 2, head_b, 0)
+    dense(1, scores_refs[2], scores_refs[3], (core * (blocks - 1),))
+    for side, other, goal, stays in inward_targets(core, spot):
+        if other is core:
+            for piece in range(PIECES):
+                back.send(other, goal, stays, piece, 1, own_parts[1])
+    walk(1, blocks * RANDOM // 2)
+    for number in range(PIECES):
+        for goal in range(SPOTS):
+            close(1, (2 * (1 - core) + number) * SPOTS + goal, KEYS_B)
+    across = remote(
+        out_ref.at[pl.ds(2 * (1 - core), PIECES), :, KEYS_B],
+        sibling_ref,
+        sibling_sems[0],
+        sibling_sems[1],
+        (1 - core, rank_of(plane, spot)),
+    )
+    across.start()
+    for number in range(PIECES):
+        for goal in range(SPOTS):
+            close(1, (2 * core + number) * SPOTS + goal, KEYS_B)
     for one in reduces:
         one.columns()
-
-    def walk(number, carry):
-        entry = sorted_ref[0, number]
-        earlier = sorted_ref[0, jnp.maximum(number - 1, 0)]
-        keep = jnp.where(table_ref[0, entry] == table_ref[0, earlier], 1.0, 0.0).astype(F32)
-        totals = []
-        for slot in range(2):
-            total = carry[slot] * keep + shares_ref[slot, entry]
-            walked_ref[slot, number] = total.astype(BF16)
-            totals.append(total)
-        return tuple(totals)
-
-    lax.fori_loop(0, blocks * RANDOM, walk, (nothing, nothing))
-
+    across.wait_recv()
     for side, other, goal, stays in inward_targets(core, spot):
-        for piece in range(PIECES):
-            first = ((2 * other + piece) * SPOTS + goal) * local
-
-            def close(number, carry, first=first):
-                block = first + number
-                stop = sorted_ref[1, block]
-                start = jnp.where(block == 0, 0, sorted_ref[1, jnp.maximum(block - 1, 0)])
-                some = jnp.where(stop > start, 1.0, 0.0).astype(F32)
-                for slot in range(2):
-                    share = walked_ref[slot, jnp.maximum(stop - 1, 0)].astype(F32)
-                    store(1 + slot, block, sums_ref[slot, block] + share * some)
-                return carry
-
-            lax.fori_loop(0, local, close, 0)
-            back.send(other, goal, stays, piece, 1, widths[1])
-
+        if other is core:
+            for piece in range(PIECES):
+                place = (2 * core + piece, goal, KEYS_B)
+                out_ref[place] = (
+                    out_ref[place].astype(F32) + sibling_ref[piece, goal].astype(F32)
+                ).astype(BF16)
+                back.send(other, goal, stays, piece, 2, own_parts[2])
     for one in reduces:
         one.finish()
     finish_hidden()
-    back.finish(widths)
+    grads.finish()
+    across.wait_send()
+    back.finish((own_parts, far_parts))
 
 
 def plane_attention_back(table, sorted_table, qkv, grad_source, lse, hidden, sources):
     groups, _, local, _, _ = qkv.shape
     blocks = groups * local
+    spans = blocks // SPAN
     count = len(sources)
     buffers = []
     for source in sources:
         buffers += reduce_scratch(source.shape, source.dtype)
     tile = (local, BLOCK, LANES)
+    wide = VMEM((spans, 2 * BLOCK, SPAN * BLOCK), F32)
+    thin = VMEM((spans, BLOCK, SPAN * BLOCK), F32)
     dma = pltpu.SemaphoreType.DMA
     return pl.pallas_call(
         functools.partial(plane_attend_back_kernel, count),
@@ -1990,21 +2065,28 @@
             VMEM((2, blocks, BLOCK, LANES), F32),
             VMEM((2, blocks * RANDOM, BLOCK, LANES), F32),
             VMEM((2, blocks * RANDOM, BLOCK, LANES), BF16),
+            VMEM((PIECES, SPOTS) + tile, BF16),
+            wide,
+            wide,
+            thin,
+            thin,
             dma((count, REDUCE_SEMS)),
             dma((count, REDUCE_SEMS)),
             dma((count, 4)),
         ]
         + exchange_sems((PLANES, SPOTS))
         + [
-            dma((28,)),
-            dma((2, SPOTS, PIECES, 2)),
-            dma((2, PIECES)),
+            dma((36,)),
+            dma((2, SPOTS, PIECES, 3)),
+            dma((3, PIECES)),
             dma((2,)),
             dma((2,)),
             dma((2,)),
+            dma,
+            dma,
         ],
         compiler_params=pltpu.CompilerParams(
-            vmem_limit_bytes=60 * 1024 * 1024, collective_id=5, has_side_effects=True
+            vmem_limit_bytes=62 * 1024 * 1024, collective_id=5, has_side_effects=True
         ),
         name="plane_attention_back",
     )(table, sorted_table, qkv, grad_source, lse, hidden, *sources)
@@ -2183,114 +2265,6 @@
     )(mixed_in, x, dy, vec, w_out, up_shift, w_up, w_down)
 
 
-def plane_qkv_back_kernel(
-    recv_ref,
-    normed_ref,
-    x_ref,
-    dres_ref,
-    vec_ref,
-    w_ref,
-    grad_ref,
-    g_qkv_ref,
-    g_bias_ref,
-    g_small_ref,
-    packed_ref,
-    normed_t_ref,
-    dnormed_ref,
-):
-    pieces, rows, _ = x_ref.shape
-    step = pl.program_id(0)
-    low = low_lanes(rows)
-
-    @pl.when(step == 0)
-    def _():
-        core = lax.axis_index("gx")
-
-        def put(tile, piece, value):
-            side, chunk = tile // HALF_TILES, tile % HALF_TILES
-            packed_ref[
-                chunk, piece * rows : (piece + 1) * rows, side * LANES : (side + 1) * LANES
-            ] = value.astype(BF16)
-
-        for piece in range(pieces):
-            seconds = []
-            for spot in range(SPOTS):
-                first = recv_ref[0, spot, piece, 0].astype(F32)
-                second = recv_ref[1, spot, piece, 0].astype(F32)
-                put(spot, piece, jnp.where(low, first, jnp.where(core == 0, first, second)))
-                seconds.append(second)
-                base = D // LANES + 3 * spot
-                put(base, piece, recv_ref[0, spot, piece, 1])
-                put(base + 1, piece, recv_ref[1, spot, piece, 1])
-                shared = recv_ref[0, spot, piece, 2].astype(F32) + recv_ref[
-                    1, spot, piece, 2
-                ].astype(F32)
-                put(base + 2, piece, shared)
-            for number in range(2):
-                put(
-                    SPOTS + number,
-                    piece,
-                    jnp.where(low, seconds[2 * number], swap_halves(seconds[2 * number + 1])),
-                )
-        normed_t_ref[...] = normed_ref[...].astype(F32).T.astype(BF16)
-        dnormed_ref[...] = jnp.zeros_like(dnormed_ref)
-
-    packed = packed_ref[step]
-    g_bias_ref[0] = jnp.sum(packed.astype(F32), axis=0, keepdims=True)
-    by_owner(g_qkv_ref, dot(normed_t_ref[...], packed))
-    dnormed_ref[...] += dot_rt(packed, w_ref[...])
-
-    @pl.when(step == pl.num_programs(0) - 1)
-    def _():
-        normal, inverse = norm_parts(x_ref[...].reshape(pieces * rows, D).astype(F32))
-        dnormed = dnormed_ref[...]
-        g_small_ref[0:1] = jnp.sum(dnormed * normal, axis=0, keepdims=True)
-        g_small_ref[1:2] = jnp.sum(dnormed, axis=0, keepdims=True)
-        grad = dres_ref[...] + norm_pull(dnormed, normal, inverse, vec_ref[0:1])
-        grad_ref[...] = grad.astype(BF16).reshape(x_ref.shape)
-
-
-def plane_qkv_back(recv, normed, x, dres, vec, w):
-    pieces, rows, _ = x.shape
-    tokens = pieces * rows
-    shard = D // RANKS
-
-    def fixed(shape):
-        return pl.BlockSpec(shape, lambda step: (0,) * len(shape))
-
-    return pl.pallas_call(
-        plane_qkv_back_kernel,
-        grid=(HALF_TILES,),
-        out_shape=(
-            jax.ShapeDtypeStruct(x.shape, BF16),
-            jax.ShapeDtypeStruct((RANKS, 2 * shard, 3 * D // 2), BF16),
-            jax.ShapeDtypeStruct((HALF_TILES, 1, CHUNK), F32),
-            jax.ShapeDtypeStruct((2, D), F32),
-        ),
-        in_specs=[
-            fixed(recv.shape),
-            fixed((tokens, D)),
-            fixed(x.shape),
-            fixed((tokens, D)),
-            fixed(vec.shape),
-            pl.BlockSpec((D, CHUNK), lambda step: (0, step)),
-        ],
-        out_specs=(
-            fixed(x.shape),
-            pl.BlockSpec((RANKS, 2 * shard, LANES), lambda step: (0, 0, step)),
-            pl.BlockSpec((1, 1, CHUNK), lambda step: (step, 0, 0)),
-            fixed((2, D)),
-        ),
-        scratch_shapes=[
-            VMEM((HALF_TILES, tokens, CHUNK), BF16),
-            VMEM((D, tokens), BF16),
-            VMEM((tokens, D), F32),
-        ],
-        compiler_params=params_of(56),
-        name="plane_qkv_back",
-    )(recv, normed, x, dres, vec, w)
-
-
 class Reduce:
     SENDS = 4 + 2 + 2 + 3
     RECVS = SENDS
@@ -2437,64 +2411,237 @@
     ]
 
 
-def spread_kernel(count, *refs):
-    grad_ref = refs[0]
-    sources = refs[1 : 1 + count]
-    grad_out_ref = refs[1 + count]
-    outs = refs[2 + count : 2 + 2 * count]
-    scratch = refs[2 + 2 * count :]
-    buffers = scratch[: 7 * count]
-    send_sem, recv_sem, local_sem, move_send, move_recv, move_local = scratch[7 * count :]
+class Doubling:
+    STEPS = 5
+
+    def __init__(self, totals, boxes, send_sem, recv_sem):
+        self.totals, self.boxes = totals, boxes
+        self.send_sem, self.recv_sem = send_sem, recv_sem
+        core, plane, spot = place_here()
+        self.partners = (
+            (1 - core, rank_of(plane, spot)),
+            (core, rank_of(plane, flip(spot, 1))),
+            (core, rank_of(plane, flip(spot, 2))),
+            (core, rank_of(flip(plane, 1), spot)),
+            (core, rank_of(flip(plane, 2), spot)),
+        )
+        self.copies = []
+
+    def start(self, step):
+        self.copies = []
+        for number, (total, box) in enumerate(zip(self.totals, self.boxes)):
+            copy = remote(
+                total,
+                box.at[step],
+                self.send_sem.at[step, number],
+                self.recv_sem.at[step, number],
+                self.partners[step],
+            )
+            copy.start()
+            self.copies.append(copy)
+
+    def finish(self, step):
+        for copy, total, box in zip(self.copies, self.totals, self.boxes):
+            copy.wait()
+            total[...] += box[step]
+
+
+PARTS = 3
+
+
+def finish_kernel(
+    recv_ref,
+    normed_ref,
+    x_ref,
+    dres_hbm,
+    vec_ref,
+    w_hbm,
+    g_mid_ref,
+    g_up_bias_ref,
+    grad_ref,
+    g_qkv_ref,
+    rows_out_ref,
+    tiles_out_ref,
+    *scratch,
+):
+    sources, scratch = scratch[:PARTS], scratch[PARTS:]
+    buffers, scratch = scratch[: 7 * PARTS], scratch[7 * PARTS :]
+    packed_ref, dnormed_ref, gradient_ref, dres_ref, w_ref = scratch[:5]
+    rows_ref, tiles_ref, rows_box, tiles_box = scratch[5:9]
+    send_sem, recv_sem, local_sem, load_sem, sum_send, sum_recv = scratch[9:15]
+    move_sems = scratch[15:18]
+    pieces, rows, _ = x_ref.shape
+    tokens = pieces * rows
     core, plane, spot = place_here()
+    low = low_lanes(rows)
+
+    load_w = pltpu.make_async_copy(w_hbm, w_ref, load_sem.at[0])
+    load_dres = pltpu.make_async_copy(dres_hbm, dres_ref, load_sem.at[1])
+    load_w.start()
+    load_dres.start()
     greet(all_partners(core, plane, spot))
-    sums = [
+
+    def put(tile, piece, value):
+        side, chunk = tile // HALF_TILES, tile % HALF_TILES
+        packed_ref[
+            piece * rows : (piece + 1) * rows,
+            chunk * CHUNK + side * LANES : chunk * CHUNK + (side + 1) * LANES,
+        ] = value.astype(BF16)
+
+    for piece in range(pieces):
+        seconds = []
+        for goal in range(SPOTS):
+            first = recv_ref[0, goal, piece, QUERIES].astype(F32)
+            second = recv_ref[1, goal, piece, QUERIES].astype(F32)
+            put(goal, piece, jnp.where(low, first, jnp.where(core == 0, first, second)))
+            seconds.append(second)
+            base = D // LANES + 3 * goal
+            put(base, piece, recv_ref[0, goal, piece, KEYS_A])
+            put(base + 1, piece, recv_ref[1, goal, piece, KEYS_A])
+            put(base + 2, piece, recv_ref[core, goal, piece, KEYS_B])
+        for number in range(2):
+            put(
+                SPOTS + number,
+                piece,
+                jnp.where(low, seconds[2 * number], swap_halves(seconds[2 * number + 1])),
+            )
+
+    load_w.wait()
+    for chunk in range(HALF_TILES):
+        columns = slice(chunk * CHUNK, (chunk + 1) * CHUNK)
+        share = dot_rt(packed_ref[:, columns], w_ref[:, columns])
+        if chunk == 0:
+            dnormed_ref[...] = share
+        else:
+            dnormed_ref[...] += share
+    normal, inverse = norm_parts(x_ref[...].reshape(tokens, D).astype(F32))
+    dnormed = dnormed_ref[...]
+    load_dres.wait()
+    gradient = dres_ref[...] + norm_pull(dnormed, normal, inverse, vec_ref[0:1])
+    gradient_ref[...] = gradient.astype(BF16).reshape(x_ref.shape)
+    finish_grad = from_planes(gradient_ref, grad_ref, *move_sems)
+
+    rows_ref[0:1] = jnp.sum(dnormed * normal, axis=0, keepdims=True)
+    rows_ref[1:2] = jnp.sum(dnormed, axis=0, keepdims=True)
+    rows_ref[2:6] = g_mid_ref[...]
+    rows_ref[6:8] = jnp.zeros((2, D), F32)
+    tiles_ref[...] = jnp.zeros_like(tiles_ref)
+    for step in range(FF // CHUNK):
+        tiles_ref[step : step + 1] = g_up_bias_ref[step]
+    for chunk in range(HALF_TILES):
+        number = FF // CHUNK + chunk
+        tiles_ref[number : number + 1] = jnp.sum(
+            packed_ref[:, chunk * CHUNK : (chunk + 1) * CHUNK].astype(F32), axis=0, keepdims=True
+        )
+    sums = Doubling((rows_ref, tiles_ref), (rows_box, tiles_box), sum_send, sum_recv)
+    sums.start(0)
+
+    width = HALF_TILES // PARTS * LANES
+    reduces = [
         Reduce(
-            source,
-            *buffers[7 * number : 7 * number + 7],
-            out,
-            (send_sem.at[number], recv_sem.at[number], local_sem.at[number]),
-        )
-        for number, (source, out) in enumerate(zip(sources, outs))
+            sources[part],
+            *buffers[7 * part : 7 * part + 7],
+            g_qkv_ref.at[:, part * width : (part + 1) * width],
+            (send_sem.at[part], recv_sem.at[part], local_sem.at[part]),
+        )
+        for part in range(PARTS)
     ]
-    for one in sums:
-        one.start()
-    finish_grad = from_planes(grad_ref, grad_out_ref, move_send, move_recv, move_local)
-    for one in sums:
-        one.corners()
-    for one in sums:
-        one.sides()
-    for one in sums:
-        one.columns()
-    for one in sums:
+    shard = D // RANKS
+    normed_t = normed_ref[...].astype(F32).T.astype(BF16)
+    for part in range(PARTS):
+        for number in range(HALF_TILES // PARTS):
+            chunk = part * (HALF_TILES // PARTS) + number
+            values = dot(normed_t, packed_ref[:, chunk * CHUNK : (chunk + 1) * CHUNK])
+            columns = slice(number * LANES, (number + 1) * LANES)
+            for owner in range(RANKS):
+                mine = values[owner * shard : (owner + 1) * shard]
+                sources[part][
+                    owner // (PLANES * SPOTS), owner // SPOTS % PLANES, owner % SPOTS, :, columns
+                ] = jnp.concatenate([mine[:, :LANES], mine[:, LANES:]], axis=0).astype(BF16)
+        reduces[part].start()
+        if part > 0:
+            reduces[part - 1].corners()
+        if part > 1:
+            reduces[part - 2].sides()
+    sums.finish(0)
+    sums.start(1)
+    reduces[2].corners()
+    reduces[1].sides()
+    sums.finish(1)
+    sums.start(2)
+    reduces[0].columns()
+    reduces[2].sides()
+    sums.finish(2)
+    sums.start(3)
+    reduces[1].columns()
+    sums.finish(3)
+    sums.start(4)
+    reduces[2].columns()
+    sums.finish(4)
+    for one in reduces:
         one.finish()
+    rows_out_ref[...] = rows_ref[...]
+    tiles_out_ref[...] = tiles_ref[...]
     finish_grad()
 
 
-def spread(grad, sources):
-    count = len(sources)
+def finish_layer(recv, normed, x, dres, vec, w, g_mid, g_up_bias):
+    pieces, rows, _ = x.shape
+    tokens = pieces * rows
+    shard = D // RANKS
+    grid = (2, PLANES, SPOTS)
+    part = grid + (2 * shard, HALF_TILES // PARTS * LANES)
     buffers = []
-    for source in sources:
-        buffers += reduce_scratch(source.shape, source.dtype)
+    for _ in range(PARTS):
+        buffers += reduce_scratch(part, BF16)
+    tiles = -(-(FF // CHUNK + HALF_TILES) // 8) * 8
+    dma = pltpu.SemaphoreType.DMA
     return pl.pallas_call(
-        functools.partial(spread_kernel, count),
-        out_shape=(jax.ShapeDtypeStruct(grad.shape, BF16),)
-        + tuple(jax.ShapeDtypeStruct(source.shape[3:], F32) for source in sources),
-        in_specs=[whole(ANY)] * (1 + count),
-        out_specs=(whole(ANY),) + (whole(),) * count,
-        scratch_shapes=buffers
+        finish_kernel,
+        out_shape=(
+            jax.ShapeDtypeStruct(x.shape, BF16),
+            jax.ShapeDtypeStruct((2 * shard, 3 * D // 2), F32),
+            jax.ShapeDtypeStruct((8, D), F32),
+            jax.ShapeDtypeStruct((tiles, CHUNK), F32),
+        ),
+        in_specs=[
+            whole(),
+            whole(),
+            whole(),
+            whole(ANY),
+            whole(),
+            whole(ANY),
+            whole(),
+            whole(),
+        ],
+        out_specs=(whole(ANY), whole(), whole(), whole()),
+        scratch_shapes=[VMEM(part, BF16)] * PARTS
+        + buffers
         + [
-            pltpu.SemaphoreType.DMA((count, REDUCE_SEMS)),
-            pltpu.SemaphoreType.DMA((count, REDUCE_SEMS)),
-            pltpu.SemaphoreType.DMA((count, 4)),
-            pltpu.SemaphoreType.DMA((2,)),
-            pltpu.SemaphoreType.DMA((2,)),
-            pltpu.SemaphoreType.DMA((2,)),
+            VMEM((tokens, 3 * D), BF16),
+            VMEM((tokens, D), F32),
+            VMEM(x.shape, BF16),
+            VMEM((tokens, D), F32),
+            VMEM(w.shape, BF16),
+            VMEM((8, D), F32),
+            VMEM((tiles, CHUNK), F32),
+            VMEM((Doubling.STEPS, 8, D), F32),
+            VMEM((Doubling.STEPS, tiles, CHUNK), F32),
+            dma((PARTS, REDUCE_SEMS)),
+            dma((PARTS, REDUCE_SEMS)),
+            dma((PARTS, 4)),
+            dma((2,)),
+            dma((Doubling.STEPS, 2)),
+            dma((Doubling.STEPS, 2)),
+            dma((2,)),
+            dma((2,)),
+            dma((2,)),
         ],
         compiler_params=pltpu.CompilerParams(
-            vmem_limit_bytes=56 * 1024 * 1024, collective_id=2, has_side_effects=True
+            vmem_limit_bytes=60 * 1024 * 1024, collective_id=2, has_side_effects=True
         ),
-        name="spread",
-    )(grad, *sources)
+        name="finish_layer",
+    )(recv, normed, x, dres, vec, w, g_mid, g_up_bias)
 
 
 def fold_columns(array):
@@ -2596,40 +2743,34 @@
         ],
     )
     dqkv = dqkv.reshape(2, SPOTS, PIECES, 3, rows, LANES)
-    grad, g_qkv, g_bias, g_first = plane_qkv_back(dqkv, normed, x, dres, vectors, w_qkv_all)
-
-    g_bias = g_bias.reshape(HALF_TILES, 2, LANES).swapaxes(0, 1).reshape(1, 3 * D)
+    grad_hidden, t_qkv, sum_rows, sum_tiles = finish_layer(
+        dqkv, normed, x, dres, vectors, w_qkv_all, g_mid, g_up_bias
+    )
+
+    mine = lax.axis_index("gx") * PLANES * SPOTS + lax.axis_index("gy")
+    sum_tiles = sum_tiles.reshape(-1, 2, LANES)
+    g_bias = sum_tiles[FF // CHUNK : FF // CHUNK + HALF_TILES].swapaxes(0, 1).reshape(1, 3 * D)
     g_bias = take_blocks(g_bias, inverse)
-    singles = jnp.concatenate(
-        [g_first, g_bias[:, :D], g_bias[:, 2 * D :], g_mid[3:4], g_mid[0:3]], axis=0
-    )
-    singles = singles.reshape(8, RANKS, own).swapaxes(0, 1).reshape(RANKS, 8 * own)
-    g_up_bias = g_up_bias.reshape(FF // CHUNK, 2, LANES).swapaxes(0, 1).reshape(RANKS, FF // RANKS)
-    singles = jnp.concatenate(
-        [singles, g_up_bias, jnp.zeros((RANKS, 8 * LANES - small), F32)], axis=1
-    )
-    grad_hidden, singles, t_qkv = spread(
-        grad,
-        [singles.reshape(grid + (8, LANES)), g_qkv.reshape(grid + g_qkv.shape[1:])],
-    )
-    singles = singles.reshape(8 * LANES)
-    parts = [singles[number * own : (number + 1) * own] for number in range(8)]
+    sum_rows = jnp.concatenate([sum_rows, g_bias[:, :D], g_bias[:, 2 * D :]], axis=0)
+    parts = lax.dynamic_slice_in_dim(sum_rows, mine * own, own, 1)
+    g_up_bias = sum_tiles[: FF // CHUNK].swapaxes(0, 1).reshape(FF)
+    g_up_bias = lax.dynamic_slice_in_dim(g_up_bias, mine * (FF // RANKS), FF // RANKS, 0)
     return (
         hidden_out,
         grad_hidden.astype(F32),
         parts[0],
         parts[1],
         take_blocks(unfold_columns(t_qkv), inverse),
+        parts[8],
+        parts[9],
+        unfold_columns(t_out),
+        parts[5],
         parts[2],
         parts[3],
-        unfold_columns(t_out),
+        unfold_columns(t_up),
+        g_up_bias,
+        t_down,
         parts[4],
-        parts[5],
-        parts[6],
-        unfold_columns(t_up),
-        singles[8 * own : small],
-        t_down,
-        parts[7],
     )
 
 

time: 371 us -> 351 us (0.946)
  Pallas kernels: 336 us -> 318 us
    pallas_call x1, Pallas kernels: 110 us -> 98.9 us  [plane_attention_back(): pl.pallas_call(functools.partial(plane_attend_back_kernel, count), out_sh...]
    pallas_call x2 -> x1, Pallas kernels: 47.3 us -> 40.8 us  [finish_layer(): pl.pallas_call(finish_kernel, out_shape=(jax.ShapeDtypeStruct(x.shape, BF...]
    unnamed x41 -> x36, local copies, waits for them, and re-layouts: 9.34 us -> 8.65 us
where the time goes in v5:
time: 351 us; the launch traced here: 350 us
  Pallas kernels  318 us (91%)
  local copies, waits for them, and re-layouts  26.2 us (7%)
  other arithmetic  5.25 us (1%)
    pallas_call x1, Pallas kernels, plane_attention_back(): pl.pallas_call(functools.partial(plane_attend_back_kernel, count), out_sh...  98.9 us
    pallas_call x1, Pallas kernels, plane_attention(): pl.pallas_call(plane_attend_kernel, out_shape=(jax.ShapeDtypeStruct((2, S...  63.8 us
    pallas_call x1, Pallas kernels, finish_layer(): pl.pallas_call(finish_kernel, out_shape=(jax.ShapeDtypeStruct(x.shape, BF...  40.8 us
    pallas_call x1, Pallas kernels, exchange_qkv(): pl.pallas_call(exchange_qkv_kernel, out_shape=(jax.ShapeDtypeStruct((PLAN...  38.9 us
    pallas_call x1, Pallas kernels, plane_middle(): pl.pallas_call(plane_middle_kernel, grid=(steps,), out_shape=(jax.ShapeDt...  35.7 us
    pallas_call x1, Pallas kernels, collect(): pl.pallas_call(collect_kernel, out_shape=(jax.ShapeDtypeStruct(x.shape, B...  35.5 us
    unnamed x36, local copies, waits for them, and re-layouts  8.65 us

profile of v5, /device:TPU:0, one launch (start us, length us, event | category | flops | bytes accessed | tf_op | source)
XLA Modules:
  0.0 350.4 jit_solution(11297125650294034513)
XLA Ops:
  0.7 0.7 convert_element_type.23
  1.3 0.1 copy.42
  1.5 0.1 convert_element_type.24
  1.6 6.1 %concatenate.48 = bf16[2048]{0:T(1024)(128)(2,1)S(1)} concatenate(bf16[24]{0:T(256)(128)(2,1)} %param.18, bf16[24]{0:T(256)(128)(2,1)} %param.19, bf16[24]{0:T(256)(128)(2,1)} %param.21, bf16[24]{0:T(256)(128)(2,1)} %param.22, bf16[24]{0:T(256)(128)(2,1)} %param.24, bf16[24]{0:T(256)(128)(2,1)} %param.25, bf16[24]{0:T(256)(128)(2,1)} %param.26, bf16[24]{0:T(256)(128)(2,1)} %param.30, ...), dimensions={0} | concatenate | bytes 8192 | tf_op jit(solution)/shard_map/concatenate | solution.py:2683
  7.7 0.7 fusion.10
  8.4 0.9 fusion.7
  9.3 0.9 fusion.8
  10.3 0.1 concatenate.49
  10.4 0.1 concatenate.50
  10.5 0.1 slice.499
  10.6 0.9 fusion.6
  11.6 1.1 copy-done.4
  12.7 35.5 %collect.1 = (bf16[2,256,768]{2,1,0:T(8,128)(2,1)S(1)}, bf16[2,4,4,16,128]{4,3,2,1,0:T(8,128)(2,1)S(1)}, bf16[768,2304]{1,0:T(8,128)(2,1)S(1)}) custom-call(bf16[2,256,768]{2,1,0:T(8,128)(2,1)S(1)} %copy-done.4, bf16[16,128]{1,0:T(8,128)(2,1)S(1)} %bitcast.53, bf16[48,1152]{1,0:T(8,128)(2,1)S(1)} %pad_maximum_fusion.1.s_qkv_ref), custom_call_target="tpu_custom_call" | custom-call | tf_op jit(solution)/shard_map/collect/pallas_call | solution.py:1081
  48.2 1.8 copy-done
  50.1 0.1 copy.50
  50.2 0.1 reshape.132
  50.3 0.1 copy.44
  50.4 0.1 reshape.125
  50.7 0.6 copy.47
  51.3 0.1 reshape.133
  51.4 0.1 reshape.126.vec_ref
  51.7 0.1 concatenate.52
  51.9 4.4 %plane_qkv.1 = (bf16[512,768]{1,0:T(8,128)(2,1)S(1)}, bf16[2,4,2,3,256,128]{5,4,3,2,1,0:T(8,128)(2,1)S(1)}, s32[4,256]{1,0:T(4,128)S(1)}) custom-call(bf16[2,256,768]{2,1,0:T(8,128)(2,1)S(1)} %get-tuple-element.48.x_ref, f32[8,768]{1,0:T(8,128)S(1)} %reshape.126.vec_ref, bf16[768,2304]{1,0:T(8,128)(2,1)} %copy-done, f32[1,2304]{1,0:T(1,128)S(1)} %bitcast.52, ...), custom_call_target="tpu_custom_call" | custom-call | tf_op jit(solution)/shard_map/plane_qkv/pallas_call | solution.py:1473
  56.3 0.6 copy-done.10
  56.9 38.9 %exchange_qkv.1 = (bf16[4,4,3,256,128]{4,3,2,1,0:T(8,128)(2,1)S(1)}, bf16[4,48,1920]{2,1,0:T(8,128)(2,1)S(1)}, bf16[4,96,768]{2,1,0:T(8,128)(2,1)S(1)}) custom-call(bf16[2,4,2,3,256,128]{5,4,3,2,1,0:T(8,128)(2,1)S(1)} %get-tuple-element.51.source_ref, bf16[48,1920]{1,0:T(8,128)(2,1)S(1)} %maximum_maximum_fusion.s_ou_ref, bf16[96,768]{1,0:T(8,128)(2,1)S(1)} %copy-done.8), custom_call_target="tpu_custom_call" | custom-call | tf_op jit(solution)/shard_map/exchange_qkv/pallas_call | solution.py:1321
  95.8 1.7 copy-done.1
  97.5 0.9 copy-done.5
  98.4 0.8 copy-done.6
  99.2 63.8 %plane_attention.1 = (bf16[2,4,2,4,64,128]{5,4,3,2,1,0:T(8,128)(2,1)}, f32[64,64,128]{2,1,0:T(8,128)}, bf16[2,256,768]{2,1,0:T(8,128)(2,1)}, bf16[768,768]{1,0:T...) custom-call(s32[1,256]{1,0:T(1,128)} %copy-done.9, bf16[16,3,4,64,128]{4,3,2,1,0:T(8,128)(2,1)} %bitcast.49, ...), custom_call_target="tpu_custom_call" | custom-call | tf_op jit(solution)/shard_map/plane_attention/pallas_call | solution.py:1650
  163.1 35.7 %plane_middle.1 = (bf16[2,256,768]{2,1,0:T(8,128)(2,1)}, bf16[2,4,2,256,128]{4,3,2,1,0:T(8,128)(2,1)}, f32[512,768]{1,0:T(8,128)}, bf16[32,48,384]{2,1,0:T(8,128...) custom-call(bf16[2,4,2,256,128]{4,3,2,1,0:T(8,128)(2,1)} %bitcast.60, ...), custom_call_target="tpu_custom_call" | custom-call | tf_op jit(solution)/shard_map/plane_middle/pallas_call | solution.py:2222
  198.8 98.9 %plane_attention_back.1 = (bf16[2,4,2,3,4,64,128]{6,5,4,3,2,1,0:T(8,128)(2,1)}, bf16[2,256,768]{2,1,0:T(8,128)(2,1)}, f32[48,384]{1,0:T(8,128)}, f32[48,1536]{1,0:T(8,128)}, f32[96,768]{1,0:T(8,128)}) custom-call(s32[1,256]{1,0:T(1,128)} %copy-done.9, s32[4,256]{1,0:T(4,128)} %copy-done.10, bf16[16,3,4,64,128]{4,3,2,1,0:T(8,128)(2,1)} %bitcast.50, ...), custom_call_target="tpu_custom_call" | custom-call | tf_op jit(solution)/shard_map/plane_attention_back/pallas_call | solution.py:2044
  297.7 40.8 %finish_layer.1 = (bf16[2,256,768]{2,1,0:T(8,128)(2,1)}, f32[48,1152]{1,0:T(8,128)}, f32[8,768]{1,0:T(8,128)}, f32[24,256]{1,0:T(8,128)}) custom-call(bf16[2,4,2,3,256,128]{5,4,3,2,1,0:T(8,128)(2,1)} %bitcast.57, bf16[512,768]{1,0:T(8,128)(2,1)} %copy-done.3, bf16[2,256,768]{2,1,0:T(8,128)(2,1)} %copy-done.2, f32[512,768]{1,0:T(8,128)} %get-tuple-element.69.dres_hbm, ...), custom_call_target="tpu_custom_call" | custom-call | tf_op jit(solution)/shard_map/finish_layer/pallas_call | solution.py:2599
  338.5 0.8 slice.495
  339.3 0.7 slice.437
  340.1 0.6 dynamic_slice.12
  340.9 0.1 concatenate.56
  341.0 0.1 concatenate.57
  341.1 0.8 fusion.1
  341.8 0.5 slice_bitcast_fusion
  342.4 0.6 pad_maximum_fusion.2
  343.0 1.0 fusion.4
  344.0 1.0 fusion.5
  345.0 1.0 fusion.3
  346.0 0.8 concatenate.60
  346.8 0.7 pad_maximum_fusion
  347.6 1.3 convert_element_type.30
  348.8 0.9 copy.60
  349.7 0.7 copy.61
  (56 shorter events, 0.8 us)
Async XLA Ops:
  11.5 1.1 copy-start.4
  12.7 44.2 %copy-start.8 = (bf16[96,768]{1,0:T(8,128)(2,1)S(1)}, bf16[96,768]{1,0:T(8,128)(2,1)}, u32[]{:S(2)}) copy-start(bf16[96,768]{1,0:T(8,128)(2,1)} %s_down_ref.1) | copy-start | bytes 442372
  48.2 1.8 copy-start
  50.0 45.8 %copy-start.2 = (bf16[2,256,768]{2,1,0:T(8,128)(2,1)}, bf16[2,256,768]{2,1,0:T(8,128)(2,1)S(1)}, u32[]{:S(2)}) copy-start(bf16[2,256,768]{2,1,0:T(8,128)(2,1)S(1)} %get-tuple-element.48.x_ref) | copy-start | bytes 2359300
  50.5 45.3 %copy-start.9 = (s32[1,256]{1,0:T(1,128)}, s32[1,256]{1,0:T(1,128)S(1)}, u32[]{:S(2)}) copy-start(s32[1,256]{1,0:T(1,128)S(1)} %pad.4.table_ref.refs_0_) | copy-start | bytes 3076
  51.6 44.3 %copy-start.7 = (f32[8,768]{1,0:T(8,128)}, f32[8,768]{1,0:T(8,128)S(1)}, u32[]{:S(2)}) copy-start(f32[8,768]{1,0:T(8,128)S(1)} %reshape.126.vec_ref) | copy-start | bytes 73732
  56.3 0.6 copy-start.10
  56.9 42.3 %copy-start.3 = (bf16[512,768]{1,0:T(8,128)(2,1)}, bf16[512,768]{1,0:T(8,128)(2,1)S(1)}, u32[]{:S(2)}) copy-start(bf16[512,768]{1,0:T(8,128)(2,1)S(1)} %get-tuple-element.68.normed_ref) | copy-start | bytes 2359300
  95.8 1.7 copy-start.1
  97.5 0.9 copy-start.5
  98.4 0.8 copy-start.6
  297.7 44.7 %copy-start.15 = (f32[48,384]{1,0:T(8,128)S(1)}, f32[48,384]{1,0:T(8,128)}, u32[]{:S(2)}) copy-start(f32[48,384]{1,0:T(8,128)} %get-tuple-element.76) | copy-start | bytes 221188
  297.7 49.1 %copy-start.14 = (f32[48,1536]{1,0:T(8,128)S(1)}, f32[48,1536]{1,0:T(8,128)}, u32[]{:S(2)}) copy-start(f32[48,1536]{1,0:T(8,128)} %get-tuple-element.77) | copy-start | bytes 884740
  338.5 9.1 %copy-start.12 = (bf16[2,256,768]{2,1,0:T(8,128)(2,1)S(1)}, bf16[2,256,768]{2,1,0:T(8,128)(2,1)}, u32[]{:S(2)}) copy-start(bf16[2,256,768]{2,1,0:T(8,128)(2,1)} %get-tuple-element.72) | copy-start | bytes 2359300
  338.5 10.4 %copy-start.11 = (bf16[2,256,768]{2,1,0:T(8,128)(2,1)S(1)}, bf16[2,256,768]{2,1,0:T(8,128)(2,1)}, u32[]{:S(2)}) copy-start(bf16[2,256,768]{2,1,0:T(8,128)(2,1)} %get-tuple-element.198) | copy-start | bytes 2359300
  345.0 4.7 %copy-start.13 = (f32[96,768]{1,0:T(8,128)S(1)}, f32[96,768]{1,0:T(8,128)}, u32[]{:S(2)}) copy-start(f32[96,768]{1,0:T(8,128)} %get-tuple-element.211) | copy-start | bytes 884740

commit v6 on v5

--- a/solution.py
+++ b/solution.py
@@ -120,8 +120,8 @@
     return jnp.where(keep, 1.0, 0.0).astype(BF16)
 
 
-def inner_slots(table_ref, block, blocks):
-    ids, bias = slots_of(table_ref, 0, block, blocks)
+def inner_slots(pick, block, blocks):
+    ids, bias = picked_slots([pick(block, number) for number in range(RANDOM)], block, blocks)
     edge = (block == 0) | (block == blocks - 1)
     ids[0] = jnp.maximum(ids[0], 0)
     ids[2] = jnp.minimum(ids[2], blocks - 1)
@@ -130,6 +130,10 @@
 
 def slots_of(table_ref, micro, block, blocks):
     picks = [table_ref[micro, block * RANDOM + number] for number in range(RANDOM)]
+    return picked_slots(picks, block, blocks)
+
+
+def picked_slots(picks, block, blocks):
     last = blocks - 1
     ids = [block - 1, block, block + 1, 0, last] + picks
     dropped = [None, None, None, block == 1, block == last - 1]
@@ -1039,70 +1043,6 @@
     return 2 * tile, 2 * tile + 1
 
 
-def collect_kernel(
-    x_ref,
-    vec_ref,
-    s_qkv_ref,
-    xs_ref,
-    vecs_ref,
-    w_qkv_ref,
-    g_qkv_ref,
-    send_sem,
-    recv_sem,
-    local_sem,
-    move_send,
-    move_recv,
-    move_local,
-):
-    core, plane, spot = place_here()
-    greet(all_partners(core, plane, spot))
-    gathers = []
-    for number, (source, target) in enumerate(((vec_ref, vecs_ref), (s_qkv_ref, g_qkv_ref))):
-        one = Gather(
-            source, target, send_sem.at[number], recv_sem.at[number], local_sem.at[number]
-        )
-        one.start()
-        gathers.append(one)
-    finish_x = to_planes(x_ref, xs_ref, move_send, move_recv, move_local)
-    for one in gathers:
-        one.column()
-    for one in gathers:
-        one.across()
-    for one in gathers:
-        one.corner()
-    for one in gathers:
-        one.finish()
-    settle(g_qkv_ref, [(tile, w_qkv_ref, alternate(tile)) for tile in range(HALF_TILES)])
-    finish_x()
-
-
-def collect(x, vec, s_qkv):
-    grid = (2, PLANES, SPOTS)
-    return pl.pallas_call(
-        collect_kernel,
-        out_shape=(
-            jax.ShapeDtypeStruct(x.shape, BF16),
-            jax.ShapeDtypeStruct(grid + vec.shape, BF16),
-            jax.ShapeDtypeStruct((D, 3 * D), BF16),
-        ),
-        in_specs=[whole(ANY)] * 3,
-        out_specs=(whole(ANY), whole(ANY), whole()),
-        scratch_shapes=[
-            VMEM(grid + s_qkv.shape, BF16),
-            pltpu.SemaphoreType.DMA((2, Gather.SENDS)),
-            pltpu.SemaphoreType.DMA((2,) + grid),
-            pltpu.SemaphoreType.DMA((2,)),
-            pltpu.SemaphoreType.DMA((2,)),
-            pltpu.SemaphoreType.DMA((2,)),
-            pltpu.SemaphoreType.DMA((2,)),
-        ],
-        compiler_params=pltpu.CompilerParams(
-            vmem_limit_bytes=48 * 1024 * 1024, collective_id=1, has_side_effects=True
-        ),
-        name="collect",
-    )(x, vec, s_qkv)
-
-
 def plane_partners(core, plane, spot):
     partners = []
     for other in (core, 1 - core):
@@ -1117,96 +1057,6 @@
     return plane_partners(core, plane, spot) + column_partners(core, plane, spot)[1:]
 
 
-def outward_send(source_ref, target_ref, send_sem, recv_sem, local_sem):
-    core, plane, spot = place_here()
-    sends, keeps = [], []
-    for side in (3, 1, 2, 0):
-        for other in (core, 1 - core):
-            goal = flip(spot, side)
-            for piece in range(PIECES):
-                source = source_ref.at[other, goal, piece]
-                target = target_ref.at[2 * core + piece, spot]
-                if side == 0 and other is core:
-                    copy = pltpu.make_async_copy(source, target, local_sem.at[piece])
-                    keeps.append(copy)
-                else:
-                    copy = remote(
-                        source,
-                        target,
-                        send_sem.at[len(sends)],
-                        recv_sem.at[2 * core + piece, spot],
-                        (other, rank_of(plane, goal)),
-                    )
-                    sends.append(copy)
-                copy.start()
-
-    def finish():
-        for side in range(SPOTS):
-            for other in (core, 1 - core):
-                if side == 0 and other is core:
-                    continue
-                for piece in range(PIECES):
-                    target = target_ref.at[2 * other + piece, flip(spot, side)]
-                    remote(
-                        target,
-                        target,
-                        send_sem.at[0],
-                        recv_sem.at[2 * other + piece, flip(spot, side)],
-                        (core, rank_of(plane, spot)),
-                    ).wait_recv()
-        for copy in sends:
-            copy.wait_send()
-        for copy in keeps:
-            copy.wait()
-
-    return finish
-
-
-def inward_send(source_ref, target_ref, send_sem, recv_sem, local_sem):
-    core, plane, spot = place_here()
-    sends, keeps = [], []
-    for side in (3, 1, 2, 0):
-        for other in (core, 1 - core):
-            goal = flip(spot, side)
-            for piece in range(PIECES):
-                source = source_ref.at[2 * other + piece, goal]
-                target = target_ref.at[core, spot, piece]
-                if side == 0 and other is core:
-                    copy = pltpu.make_async_copy(source, target, local_sem.at[piece])
-                    keeps.append(copy)
-                else:
-                    copy = remote(
-                        source,
-                        target,
-                        send_sem.at[len(sends)],
-                        recv_sem.at[core, spot, piece],
-                        (other, rank_of(plane, goal)),
-                    )
-                    sends.append(copy)
-                copy.start()
-
-    def finish():
-        for side in range(SPOTS):
-            for other in (core, 1 - core):
-                if side == 0 and other is core:
-                    continue
-                for piece in range(PIECES):
-                    target = target_ref.at[other, flip(spot, side), piece]
-                    remote(
-                        target,
-                        target,
-                        send_sem.at[0],
-                        recv_sem.at[other, flip(spot, side), piece],
-                        (core, rank_of(plane, spot)),
-                    ).wait_recv()
-        for copy in sends:
-            copy.wait_send()
-        for copy in keeps:
-            copy.wait()
-
-    return finish
-
-
 def exchange_sems(recv_shape):
     return [
         pltpu.SemaphoreType.DMA((14,)),
@@ -1215,207 +1065,12 @@
     ]
 
 
-def outward_kernel(source_ref, target_ref, send_sem, recv_sem, local_sem):
-    greet(plane_partners(*place_here()))
-    outward_send(source_ref, target_ref, send_sem, recv_sem, local_sem)()
-
-
-def inward_kernel(source_ref, target_ref, send_sem, recv_sem, local_sem):
-    greet(plane_partners(*place_here()))
-    inward_send(source_ref, target_ref, send_sem, recv_sem, local_sem)()
-
-
-def plane_exchange(kernel, source, shape, recv_shape, collective, name):
-    return pl.pallas_call(
-        kernel,
-        out_shape=jax.ShapeDtypeStruct(shape, source.dtype),
-        in_specs=[whole(ANY)],
-        out_specs=whole(ANY),
-        scratch_shapes=exchange_sems(recv_shape),
-        compiler_params=pltpu.CompilerParams(
-            vmem_limit_bytes=16 * 1024 * 1024, collective_id=collective, has_side_effects=True
-        ),
-        name=name,
-    )(source)
-
-
-def outward(source, collective, name):
-    shape = (PLANES, SPOTS) + source.shape[3:]
-    return plane_exchange(outward_kernel, source, shape, (PLANES, SPOTS), collective, name)
-
-
-def inward(source, collective, name):
-    shape = (2, SPOTS, PIECES) + source.shape[2:]
-    return plane_exchange(
-        inward_kernel, source, shape, (2, SPOTS, PIECES), collective, name
-    )
-
-
-def column_send(source, target, send_sem, recv_sem, local_sem):
-    core, plane, spot = place_here()
-    keep = pltpu.make_async_copy(source, target.at[plane], local_sem)
-    keep.start()
-    copies = []
-    for bits in range(1, PLANES):
-        copy = remote(
-            source,
-            target.at[plane],
-            send_sem.at[bits - 1],
-            recv_sem.at[plane],
-            (core, rank_of(flip(plane, bits), spot)),
-        )
-        copy.start()
-        copies.append(copy)
-
-    def finish():
-        for bits in range(1, PLANES):
-            other = flip(plane, bits)
-            remote(
-                source,
-                target.at[other],
-                send_sem.at[0],
-                recv_sem.at[other],
-                (core, rank_of(plane, spot)),
-            ).wait_recv()
-        for copy in copies:
-            copy.wait_send()
-        keep.wait()
-
-    return finish
-
-
-def exchange_qkv_kernel(
-    source_ref,
-    s_ou_ref,
-    s_down_ref,
-    target_ref,
-    c_ou_ref,
-    c_down_ref,
-    send_sem,
-    recv_sem,
-    local_sem,
-    column_send_sem,
-    column_recv_sem,
-    column_local_sem,
-):
-    greet(both_partners(*place_here()))
-    finish = outward_send(source_ref, target_ref, send_sem, recv_sem, local_sem)
-    finishes = [
-        column_send(
-            source,
-            target,
-            column_send_sem.at[number],
-            column_recv_sem.at[number],
-            column_local_sem.at[number],
-        )
-        for number, (source, target) in enumerate(
-            ((s_ou_ref, c_ou_ref), (s_down_ref, c_down_ref))
-        )
-    ]
-    finish()
-    for one in finishes:
-        one()
-
-
-def exchange_qkv(source, s_ou, s_down):
-    return pl.pallas_call(
-        exchange_qkv_kernel,
-        out_shape=(
-            jax.ShapeDtypeStruct((PLANES, SPOTS) + source.shape[3:], BF16),
-            jax.ShapeDtypeStruct((PLANES,) + s_ou.shape, BF16),
-            jax.ShapeDtypeStruct((PLANES,) + s_down.shape, BF16),
-        ),
-        in_specs=[whole(ANY)] * 3,
-        out_specs=(whole(ANY),) * 3,
-        scratch_shapes=exchange_sems((PLANES, SPOTS))
-        + [
-            pltpu.SemaphoreType.DMA((2, PLANES - 1)),
-            pltpu.SemaphoreType.DMA((2, PLANES)),
-            pltpu.SemaphoreType.DMA((2,)),
-        ],
-        compiler_params=pltpu.CompilerParams(
-            vmem_limit_bytes=16 * 1024 * 1024, collective_id=3, has_side_effects=True
-        ),
-        name="exchange_qkv",
-    )(source, s_ou, s_down)
-
-
-class PlaneGather:
-    SENDS = 3 + 4 + 2
-
-    def __init__(self, column, target, send_sem, recv_sem, local_sem):
-        self.column, self.target = column, target
-        self.send_sem, self.recv_sem = send_sem, recv_sem
-        self.core, self.plane, self.spot = place_here()
-        self.sends = []
-        self.own = pltpu.make_async_copy(column, target.at[self.core, :, self.spot], local_sem)
-        self.own.start()
-        for goal in (self.neighbour(1), self.neighbour(2), self.sibling()):
-            self.send(column, slice(0, PLANES), self.spot, 0, goal)
-
-    def neighbour(self, bits):
-        return (self.core, rank_of(self.plane, flip(self.spot, bits)))
-
-    def sibling(self):
-        return (1 - self.core, rank_of(self.plane, self.spot))
-
-    def piece(self, core, planes, spot):
-        return self.target.at[core, planes, spot]
-
-    def send(self, source, planes, spot, part, goal):
-        copy = remote(
-            source,
-            self.piece(self.core, planes, spot),
-            self.send_sem.at[len(self.sends)],
-            self.recv_sem.at[self.core, spot, part],
-            goal,
-        )
-        copy.start()
-        self.sends.append(copy)
-
-    def arrive(self, core, planes, spot, part):
-        piece = self.piece(core, planes, spot)
-        remote(
-            piece,
-            piece,
-            self.send_sem.at[0],
-            self.recv_sem.at[core, spot, part],
-            (self.core, rank_of(self.plane, self.spot)),
-        ).wait_recv()
-
-    def forward(self):
-        for side in (1, 2):
-            spot = flip(self.spot, side)
-            everything = slice(0, PLANES)
-            self.arrive(self.core, everything, spot, 0)
-            half = slice(0, 2) if side == 1 else slice(2, 4)
-            self.send(
-                self.piece(self.core, half, spot), half, spot, side - 1, self.neighbour(3 - side)
-            )
-            self.send(self.piece(self.core, everything, spot), everything, spot, 0, self.sibling())
-
-    def corner(self):
-        spot = flip(self.spot, 3)
-        for part, half in enumerate((slice(0, 2), slice(2, 4))):
-            self.arrive(self.core, half, spot, part)
-            self.send(self.piece(self.core, half, spot), half, spot, part, self.sibling())
-
-    def finish(self):
-        for side in range(3):
-            self.arrive(1 - self.core, slice(0, PLANES), flip(self.spot, side), 0)
-        for part, half in enumerate((slice(0, 2), slice(2, 4))):
-            self.arrive(1 - self.core, half, flip(self.spot, 3), part)
-        self.own.wait()
-        for copy in self.sends:
-            copy.wait_send()
-
-
-def sort_entries(table_ref, sorted_ref, entries):
-    count = table_ref.shape[1]
+def sort_entries(table, sorted_ref, entries):
+    count = table.shape[1]
     core = lax.axis_index("gx")
     lane = lax.broadcasted_iota(jnp.int32, (count, count), 1)
     row = lax.broadcasted_iota(jnp.int32, (count, count), 0).astype(F32)
-    everything = jnp.broadcast_to(table_ref[...].astype(F32), (count, count))
+    everything = jnp.broadcast_to(table, (count, count))
     half = entries // 2
     inside = (lane >= core * half) & (lane < (core + 1) * half)
     lane = lane.astype(F32)
@@ -1427,258 +1082,6 @@
         upto = jnp.sum(jnp.where(down <= lane, 1.0, 0.0), axis=0, keepdims=True)
         sorted_ref[2 * number : 2 * number + 1] = order.astype(jnp.int32)
         sorted_ref[2 * number + 1 : 2 * number + 2] = upto.astype(jnp.int32)
-
-
-def plane_qkv_kernel(
-    x_ref, vec_ref, w_ref, bias_ref, table_ref, normed_ref, send_ref, sorted_ref
-):
-    pieces, rows, _ = x_ref.shape
-    sort_entries(table_ref, sorted_ref, PLANES * SPOTS * (rows // BLOCK) * RANDOM)
-    values = x_ref[...].reshape(pieces * rows, D).astype(F32)
-    normal, _ = norm_parts(values)
-    normed_ref[...] = (normal * vec_ref[0:1] + vec_ref[1:2]).astype(BF16)
-    low = low_lanes(rows)
-    queries = D // LANES
-    for chunk in range(HALF_TILES):
-        columns = slice(chunk * CHUNK, (chunk + 1) * CHUNK)
-        packed = dot(normed_ref[...], w_ref[:, columns]) + bias_ref[:, columns]
-        for side in range(2):
-            tile = chunk + side * HALF_TILES
-            whole_tile = packed[:, side * LANES : (side + 1) * LANES]
-            if tile < queries:
-                whole_tile = whole_tile.astype(BF16).astype(F32) * SCALE
-            for piece in range(pieces):
-                part = whole_tile[piece * rows : (piece + 1) * rows]
-                if tile < SPOTS:
-                    send_ref[0, tile, piece, 0] = part.astype(BF16)
-                elif tile < queries:
-                    first = 2 * (tile - SPOTS)
-                    shared = send_ref[0, first, piece, 0].astype(F32)
-                    send_ref[1, first, piece, 0] = jnp.where(low, part, shared).astype(BF16)
-                    shared = send_ref[0, first + 1, piece, 0].astype(F32)
-                    send_ref[1, first + 1, piece, 0] = jnp.where(
-                        low, swap_halves(part), shared
-                    ).astype(BF16)
-                else:
-                    spot, role = (tile - queries) // 3, (tile - queries) % 3
-                    if role < 2:
-                        send_ref[role, spot, piece, 1] = part.astype(BF16)
-                    else:
-                        send_ref[0, spot, piece, 2] = part.astype(BF16)
-                        send_ref[1, spot, piece, 2] = part.astype(BF16)
-
-
-def plane_qkv(x, vec, w, bias, table):
-    pieces, rows, _ = x.shape
-    return pl.pallas_call(
-        plane_qkv_kernel,
-        out_shape=(
-            jax.ShapeDtypeStruct((pieces * rows, D), BF16),
-            jax.ShapeDtypeStruct((2, SPOTS, PIECES, 3, rows, LANES), BF16),
-            jax.ShapeDtypeStruct((4, table.shape[1]), jnp.int32),
-        ),
-        in_specs=[whole()] * 5,
-        out_specs=(whole(), whole(), whole()),
-        compiler_params=params_of(48),
-        name="plane_qkv",
-    )(x, vec, w, bias, table)
-
-
-def plane_attend_kernel(
-    table_ref,
-    qkv_ref,
-    dy_ref,
-    c_ou_ref,
-    c_down_ref,
-    back_ref,
-    lse_ref,
-    dys_ref,
-    w_out_ref,
-    w_up_ref,
-    w_down_ref,
-    g_ou_ref,
-    out_ref,
-    s_ref,
-    t_ref,
-    send_sem,
-    recv_sem,
-    local_sem,
-    gather_send,
-    gather_recv,
-    gather_local,
-    move_send,
-    move_recv,
-    move_local,
-):
-    greet(both_partners(*place_here()))
-    gathers = [
-        PlaneGather(
-            column,
-            target,
-            gather_send.at[number],
-            gather_recv.at[number],
-            gather_local.at[number],
-        )
-        for number, (column, target) in enumerate(
-            ((c_ou_ref, g_ou_ref), (c_down_ref, w_down_ref))
-        )
-    ]
-    finish_dy = to_planes(dy_ref, dys_ref, move_send, move_recv, move_local)
-    groups, _, local, _, _ = qkv_ref.shape
-    blocks = groups * local
-    half = blocks // 2
-    core = lax.axis_index("gx")
-    low = low_lanes(BLOCK)
-    masks = [half_mask(True), half_mask(False)]
-
-    def load(component, block):
-        return qkv_ref[lax.div(block, local), component, lax.rem(block, local)]
-
-    def store(block, value):
-        rank = lax.div(block, local)
-        out_ref[lax.div(rank, SPOTS), lax.rem(rank, SPOTS), lax.rem(block, local)] = value.astype(BF16)
-
-    def one(block, slot, ids, bias):
-        keys = jnp.concatenate([load(1 + slot, spot) for spot in ids], axis=0)
-        scores = dot_rt(load(0, block) * masks[slot], keys) + bias
-        top = jnp.max(scores, axis=1, keepdims=True)
-        powered = jnp.exp(scores - top)
-        total = jnp.sum(powered, axis=1, keepdims=True)
-        mixed = dot(powered.astype(BF16), keys) * (1.0 / total)
-        return mixed, top + jnp.log(total)
-
-    def sparse(step, carry):
-        mine = 1 + step + core * (half - 1)
-        other = 1 + step + (1 - core) * (half - 1)
-        ids, bias = slots_of(table_ref, 0, mine, blocks)
-        far_ids, far_bias = slots_of(table_ref, 0, other, blocks)
-        mixed_a, log_a = one(mine, 0, ids, bias)
-        mixed_b, log_b = one(mine, 1, ids, bias)
-        mixed_c, log_c = one(other, 0, far_ids, far_bias)
-        store(mine, jnp.where(low, mixed_b, mixed_a))
-        store(other, mixed_c)
-        lse_ref[mine] = jnp.where(low, log_a, log_b)
-        lse_ref[other] = jnp.where(low, log_c, 0.0)
-        return carry
-
-    lax.fori_loop(0, half // 2, sparse, 0)
-    gathers[0].forward()
-    lax.fori_loop(half // 2, half - 1, sparse, 0)
-
-    spans = blocks // SPAN
-    ends = (0, blocks - 1)
-    end = core * (blocks - 1)
-    query_a = jnp.concatenate([load(0, number) for number in ends], axis=0) * masks[0]
-    query_b = load(0, end) * masks[1]
-
-    def keys_at(span, slot):
-        return jnp.concatenate(
-            [load(1 + slot, span * SPAN + number) for number in range(SPAN)], axis=0
-        )
-
-    def first_pass(span, carry):
-        top_a, top_b = carry
-        scores_a = dot_rt(query_a, keys_at(span, 0))
-        scores_b = dot_rt(query_b, keys_at(span, 1))
-        s_ref[span] = scores_a
-        t_ref[span] = scores_b
-        return (
-            jnp.maximum(top_a, jnp.max(scores_a, axis=1, keepdims=True)),
-            jnp.maximum(top_b, jnp.max(scores_b, axis=1, keepdims=True)),
-        )
-
-    top_a, top_b = lax.fori_loop(
-        0,
-        spans,
-        first_pass,
-        (jnp.full((2 * BLOCK, 1), NEGATIVE, F32), jnp.full((BLOCK, 1), NEGATIVE, F32)),
-    )
-
-    def second_pass(span, carry):
-        total_a, mixed_a, total_b, mixed_b = carry
-        powered_a = jnp.exp(s_ref[span] - top_a)
-        powered_b = jnp.exp(t_ref[span] - top_b)
-        return (
-            total_a + jnp.sum(powered_a, axis=1, keepdims=True),
-            mixed_a + dot(powered_a.astype(BF16), keys_at(span, 0)),
-            total_b + jnp.sum(powered_b, axis=1, keepdims=True),
-            mixed_b + dot(powered_b.astype(BF16), keys_at(span, 1)),
-        )
-
-    total_a, mixed_a, total_b, mixed_b = lax.fori_loop(
-        0,
-        spans,
-        second_pass,
-        (
-            jnp.zeros((2 * BLOCK, 1), F32),
-            jnp.zeros((2 * BLOCK, LANES), F32),
-            jnp.zeros((BLOCK, 1), F32),
-            jnp.zeros((BLOCK, LANES), F32),
-        ),
-    )
-    mixed_a = mixed_a * (1.0 / total_a)
-    mixed_b = mixed_b * (1.0 / total_b)
-    log_a = top_a + jnp.log(total_a)
-    log_b = top_b + jnp.log(total_b)
-    for place, number in enumerate(ends):
-        rows = slice(place * BLOCK, (place + 1) * BLOCK)
-        store(number, jnp.where(low, mixed_b, mixed_a[rows]))
-        lse_ref[number] = jnp.where(low, log_a[rows], log_b)
-
-    gathers[1].forward()
-    finish_mixed = inward_send(out_ref, back_ref, send_sem, recv_sem, local_sem)
-    gathers[0].corner()
-    gathers[0].finish()
-    outs = D // LANES // 2
-    settle(
-        g_ou_ref,
-        [(tile, w_out_ref, (tile, outs + tile)) for tile in range(outs)]
-        + [(outs + tile, w_up_ref, alternate(tile)) for tile in range(FF // CHUNK)],
-    )
-    gathers[1].corner()
-    gathers[1].finish()
-    finish_dy()
-    finish_mixed()
-
-
-def plane_attention(table, qkv, dy, c_ou, c_down):
-    groups, _, local, _, _ = qkv.shape
-    blocks = groups * local
-    spans = blocks // SPAN
-    grid = (2, PLANES, SPOTS)
-    tile = (local, BLOCK, LANES)
-    return pl.pallas_call(
-        plane_attend_kernel,
-        out_shape=(
-            jax.ShapeDtypeStruct((2, SPOTS, PIECES) + tile, BF16),
-            jax.ShapeDtypeStruct((blocks, BLOCK, LANES), F32),
-            jax.ShapeDtypeStruct(dy.shape, BF16),
-            jax.ShapeDtypeStruct((D, D), BF16),
-            jax.ShapeDtypeStruct((D, FF), BF16),
-            jax.ShapeDtypeStruct(grid + c_down.shape[1:], BF16),
-        ),
-        in_specs=[whole(pltpu.SMEM), whole(), whole(ANY), whole(ANY), whole(ANY)],
-        out_specs=(whole(ANY), whole(), whole(ANY), whole(), whole(), whole(ANY)),
-        scratch_shapes=[
-            VMEM(grid + c_ou.shape[1:], BF16),
-            VMEM((PLANES, SPOTS) + tile, BF16),
-            VMEM((spans, 2 * BLOCK, SPAN * BLOCK), F32),
-            VMEM((spans, BLOCK, SPAN * BLOCK), F32),
-        ]
-        + exchange_sems((2, SPOTS, PIECES))
-        + [
-            pltpu.SemaphoreType.DMA((2, PlaneGather.SENDS)),
-            pltpu.SemaphoreType.DMA((2, 2, SPOTS, 2)),
-            pltpu.SemaphoreType.DMA((2,)),
-            pltpu.SemaphoreType.DMA((2,)),
-            pltpu.SemaphoreType.DMA((2,)),
-            pltpu.SemaphoreType.DMA((2,)),
-        ],
-        compiler_params=pltpu.CompilerParams(
-            vmem_limit_bytes=56 * 1024 * 1024, collective_id=4, has_side_effects=True
-        ),
-        name="plane_attention",
-    )(table, qkv, dy, c_ou, c_down)
 
 
 class Outward:
@@ -1781,8 +1184,8 @@
 
 
 def plane_attend_back_kernel(count, *refs):
-    table_ref, sorted_ref, qkv_ref, grad_source_ref, lse_ref, hidden_ref = refs[:6]
-    sources, refs = refs[6 : 6 + count], refs[6 + count :]
+    table_ref, sorted_ref, qk_ref, shared_ref, grad_source_ref, lse_ref, hidden_ref = refs[:7]
+    sources, refs = refs[7 : 7 + count], refs[7 + count :]
     back_ref, hidden_out_ref = refs[:2]
     outs, refs = refs[2 : 2 + count], refs[2 + count :]
     buffers, refs = refs[: 7 * count], refs[7 * count :]
@@ -1791,7 +1194,8 @@
     reduce_send, reduce_recv, reduce_local = refs[:3]
     grad_sems, back_sems, move_sems, sibling_sems = refs[3:6], refs[6:9], refs[9:12], refs[12:14]
 
-    groups, _, local, _, _ = qkv_ref.shape
+    local = qk_ref.shape[3]
+    groups = PLANES * SPOTS
     blocks = groups * local
     core, plane, spot = place_here()
     low = low_lanes(BLOCK)
@@ -1813,7 +1217,10 @@
     finish_hidden = from_planes(hidden_ref, hidden_out_ref, *move_sems)
 
     def load(component, block):
-        return qkv_ref[lax.div(block, local), component, lax.rem(block, local)]
+        rank, number = lax.div(block, local), lax.rem(block, local)
+        if component == 2:
+            return shared_ref[lax.div(rank, SPOTS), lax.rem(rank, SPOTS), number]
+        return qk_ref[lax.div(rank, SPOTS), lax.rem(rank, SPOTS), component, number]
 
     def load_grad(block):
         rank = lax.div(block, local)
@@ -1840,8 +1247,11 @@
 
     lax.fori_loop(0, blocks, clear, 0)
 
+    def picked(block, number):
+        return table_ref[0, block * RANDOM + number]
+
     def one_block(block, slot):
-        ids, bias = inner_slots(table_ref, block, blocks)
+        ids, bias = inner_slots(picked, block, blocks)
         keys = jnp.concatenate([load(1 + slot, number) for number in ids], axis=0)
         both = jnp.concatenate(
             [load(0, block) * masks[slot], load_grad(block) * masks[1 - slot]], axis=0
@@ -2029,9 +1439,9 @@
     back.finish((own_parts, far_parts))
 
 
-def plane_attention_back(table, sorted_table, qkv, grad_source, lse, hidden, sources):
-    groups, _, local, _, _ = qkv.shape
-    blocks = groups * local
+def plane_attention_back(table, sorted_table, qk, shared, grad_source, lse, hidden, sources):
+    local = qk.shape[3]
+    blocks = PLANES * SPOTS * local
     spans = blocks // SPAN
     count = len(sources)
     buffers = []
@@ -2051,6 +1461,7 @@
         in_specs=[
             whole(pltpu.SMEM),
             whole(pltpu.SMEM),
+            whole(),
             whole(),
             whole(ANY),
             whole(),
@@ -2089,7 +1500,639 @@
             vmem_limit_bytes=62 * 1024 * 1024, collective_id=5, has_side_effects=True
         ),
         name="plane_attention_back",
-    )(table, sorted_table, qkv, grad_source, lse, hidden, *sources)
+    )(table, sorted_table, qk, shared, grad_source, lse, hidden, *sources)
+
+
+class PlaneGather:
+    SENDS = 3 + 3 + 4 + 2
+
+    def __init__(self, source, target, send_sem, column_sem, recv_sem, local_sem):
+        self.source, self.target = source, target
+        self.send_sem, self.column_sem, self.recv_sem = send_sem, column_sem, recv_sem
+        self.core, self.plane, self.spot = place_here()
+        self.sends = []
+        self.own = pltpu.make_async_copy(
+            source, target.at[self.core, self.plane, self.spot], local_sem
+        )
+        self.own.start()
+        for bits in range(1, PLANES):
+            copy = remote(
+                source,
+                target.at[self.core, self.plane, self.spot],
+                send_sem.at[len(self.sends)],
+                column_sem.at[self.plane],
+                (self.core, rank_of(flip(self.plane, bits), self.spot)),
+            )
+            copy.start()
+            self.sends.append(copy)
+
+    def neighbour(self, bits):
+        return (self.core, rank_of(self.plane, flip(self.spot, bits)))
+
+    def sibling(self):
+        return (1 - self.core, rank_of(self.plane, self.spot))
+
+    def piece(self, core, planes, spot):
+        return self.target.at[core, planes, spot]
+
+    def send(self, planes, spot, part, goal):
+        piece = self.piece(self.core, planes, spot)
+        copy = remote(
+            piece,
+            piece,
+            self.send_sem.at[len(self.sends)],
+            self.recv_sem.at[self.core, spot, part],
+            goal,
+        )
+        copy.start()
+        self.sends.append(copy)
+
+    def arrive(self, core, planes, spot, part):
+        piece = self.piece(core, planes, spot)
+        remote(
+            piece,
+            piece,
+            self.send_sem.at[0],
+            self.recv_sem.at[core, spot, part],
+            (self.core, rank_of(self.plane, self.spot)),
+        ).wait_recv()
+
+    def columns(self):
+        self.own.wait()
+        for bits in range(1, PLANES):
+            other = flip(self.plane, bits)
+            shard = self.target.at[self.core, other, self.spot]
+            remote(
+                shard,
+                shard,
+                self.send_sem.at[0],
+                self.column_sem.at[other],
+                (self.core, rank_of(self.plane, self.spot)),
+            ).wait_recv()
+        for goal in (self.neighbour(1), self.neighbour(2), self.sibling()):
+            self.send(slice(0, PLANES), self.spot, 0, goal)
+
+    def forward(self):
+        everything = slice(0, PLANES)
+        for side in (1, 2):
+            spot = flip(self.spot, side)
+            self.arrive(self.core, everything, spot, 0)
+            half = slice(0, 2) if side == 1 else slice(2, 4)
+            self.send(half, spot, side - 1, self.neighbour(3 - side))
+            self.send(everything, spot, 0, self.sibling())
+
+    def corner(self):
+        spot = flip(self.spot, 3)
+        for part, half in enumerate((slice(0, 2), slice(2, 4))):
+            self.arrive(self.core, half, spot, part)
+            self.send(half, spot, part, self.sibling())
+
+    def finish(self):
+        for side in range(3):
+            self.arrive(1 - self.core, slice(0, PLANES), flip(self.spot, side), 0)
+        for part, half in enumerate((slice(0, 2), slice(2, 4))):
+            self.arrive(1 - self.core, half, flip(self.spot, 3), part)
+        for copy in self.sends:
+            copy.wait_send()
+
+
+def pair_of_blocks(read, first, second):
+    low = low_lanes(1)
+    tiles = []
+    for block, wanted in ((first, 0), (second, 1)):
+        tile = read(block // 2)
+        tiles.append(tile if block % 2 == wanted else swap_halves(tile))
+    return jnp.where(low, tiles[0], tiles[1])
+
+
+def fold_tiles(target_ref, start, tiles, read):
+    half = len(tiles) // 2
+    for number in range(half):
+        columns = slice((start + number) * LANES, (start + number + 1) * LANES)
+        target_ref[:, columns] = jnp.concatenate(
+            [read(tiles[number]), read(tiles[half + number])], axis=0
+        ).astype(BF16)
+
+
+VECTORS = 8
+
+
+def lay_vectors(vecs_ref, vectors_ref, up_ref):
+    rows = vecs_ref.shape[3]
+    own, wide = D // RANKS, FF // RANKS
+    values = vecs_ref[...].reshape(RANKS, rows, LANES).astype(F32)
+
+    def spread_out(count, width):
+        place = lax.broadcasted_iota(jnp.int32, (LANES, count), 1)
+        lane = lax.broadcasted_iota(jnp.int32, (LANES, count), 0)
+        start = lax.div(place, width) * width
+        return jnp.where(place - start == lane, 1.0, 0.0).astype(BF16)
+
+    laid = dot(vecs_ref[...].reshape(RANKS * rows, LANES), spread_out(D, own))
+    owner = lax.broadcasted_iota(jnp.int32, (RANKS, 1, D), 0)
+    column = lax.broadcasted_iota(jnp.int32, (RANKS, 1, D), 2)
+    laid = jnp.where(lax.div(column, own) == owner, laid.reshape(RANKS, rows, D), 0.0)
+    vectors_ref[...] = jnp.sum(laid, axis=0)[:VECTORS]
+    row = lax.broadcasted_iota(jnp.int32, (1, rows, LANES), 1)
+    last = jnp.sum(jnp.where(row == VECTORS, values, 0.0), axis=1)
+    laid = dot(last.astype(BF16), spread_out(FF, wide))
+    owner = lax.broadcasted_iota(jnp.int32, (RANKS, FF), 0)
+    column = lax.broadcasted_iota(jnp.int32, (RANKS, FF), 1)
+    laid = jnp.sum(jnp.where(lax.div(column, wide) == owner, laid, 0.0), axis=0, keepdims=True)
+    for chunk in range(FF // CHUNK):
+        for side in range(2):
+            start = side * (FF // 2) + chunk * LANES
+            up_ref[chunk, :, side * LANES : (side + 1) * LANES] = laid[:, start : start + LANES]
+
+
+def lay_table(tables_ref, core, micro, entries):
+    count = 2 * LANES
+    ranks = PLANES * SPOTS
+    values = tables_ref[core].reshape(ranks, tables_ref.shape[3], LANES).astype(F32)
+    row = lax.broadcasted_iota(jnp.int32, (1, tables_ref.shape[3], LANES), 1)
+    values = jnp.sum(jnp.where(row == micro, values, 0.0), axis=1)
+    place = lax.broadcasted_iota(jnp.int32, (LANES, count), 1)
+    lane = lax.broadcasted_iota(jnp.int32, (LANES, count), 0)
+    start = lax.div(place, entries) * entries
+    laid = dot(values.astype(BF16), jnp.where(place - start == lane, 1.0, 0.0).astype(BF16))
+    owner = lax.broadcasted_iota(jnp.int32, (ranks, count), 0)
+    column = lax.broadcasted_iota(jnp.int32, (ranks, count), 1)
+    laid = jnp.sum(jnp.where(lax.div(column, entries) == owner, laid, 0.0), axis=0, keepdims=True)
+    column = lax.broadcasted_iota(jnp.int32, (1, count), 1)
+    return jnp.where(column < ranks * entries, laid, 2.0 * LANES)
+
+
+def front_kernel(
+    x_in_ref,
+    dy_ref,
+    vec_ref,
+    tab_ref,
+    w_qkv_in_ref,
+    w_out_in_ref,
+    w_up_in_ref,
+    w_down_in_ref,
+    back_ref,
+    x_ref,
+    dys_ref,
+    w_down_ref,
+    w_qkv_hbm,
+    w_out_hbm,
+    w_up_hbm,
+    qk_hbm,
+    shared_hbm,
+    normed_ref,
+    lse_ref,
+    vectors_ref,
+    up_ref,
+    table_ref,
+    sorted_ref,
+    s_qkv_ref,
+    s_ou_ref,
+    g_qkv_ref,
+    g_ou_ref,
+    w_qkv_ref,
+    w_out_ref,
+    w_up_ref,
+    xs_ref,
+    vecs_ref,
+    tabs_ref,
+    bias_ref,
+    send_ref,
+    qk_ref,
+    shared_ref,
+    out_ref,
+    p_ref,
+    q_ref,
+    picks_ref,
+    *sems,
+):
+    gather_send, gather_recv, gather_local = sems[:3]
+    plane_send, plane_column, plane_recv, plane_local = sems[3:7]
+    x_sems, dy_sems = sems[7:10], sems[10:13]
+    qkv_send, qkv_recv, qkv_local, shared_send, shared_recv = sems[13:18]
+    back_sems, local_sem = sems[18:21], sems[21]
+    core, plane, spot = place_here()
+    micro, rows, _ = x_in_ref.shape
+    tokens = PIECES * rows
+    local = rows // BLOCK
+    blocks = PLANES * SPOTS * local
+
+    barrier = pltpu.get_barrier_semaphore()
+    partners = both_partners(core, plane, spot)
+    for partner in partners:
+        pl.semaphore_signal(barrier, inc=1, device_id=partner, device_id_type=MESH)
+
+    def natural(ref):
+        return lambda tile: ref[:, tile * LANES : (tile + 1) * LANES].astype(F32)
+
+    order = [natural_block(entry) for entry in column_order()]
+    read = natural(w_qkv_in_ref)
+    fold_tiles(
+        s_qkv_ref,
+        0,
+        list(range(TILES)),
+        lambda tile: pair_of_blocks(read, order[2 * tile], order[2 * tile + 1]),
+    )
+    pl.semaphore_wait(barrier, len(partners))
+
+    finish_x = to_planes(x_in_ref, xs_ref, *x_sems)
+    gathers = []
+    for number, (source, target) in enumerate(
+        ((tab_ref, tabs_ref), (vec_ref, vecs_ref), (s_qkv_ref, g_qkv_ref))
+    ):
+        one = Gather(
+            source, target, gather_send.at[number], gather_recv.at[number], gather_local.at[number]
+        )
+        one.start()
+        gathers.append(one)
+    outs = D // LANES // 2
+    fold_tiles(s_ou_ref, 0, list(range(D // LANES)), natural(w_out_in_ref))
+    fold_tiles(s_ou_ref, outs, list(range(FF // LANES)), natural(w_up_in_ref))
+    for one in gathers:
+        one.column()
+    for one in gathers:
+        one.across()
+    for one in gathers:
+        one.corner()
+    finish_x()
+    spreads = [
+        PlaneGather(
+            source,
+            target,
+            plane_send.at[number],
+            plane_column.at[number],
+            plane_recv.at[number],
+            plane_local.at[number],
+        )
+        for number, (source, target) in enumerate(
+            ((s_ou_ref, g_ou_ref), (w_down_in_ref, w_down_ref))
+        )
+    ]
+    finish_dy = to_planes(dy_ref, dys_ref, *dy_sems)
+    keep_x = pltpu.make_async_copy(xs_ref, x_ref, local_sem.at[0])
+    keep_x.start()
+    normal, _ = norm_parts(xs_ref[...].reshape(tokens, D).astype(F32))
+    for one in gathers[:2]:
+        one.finish()
+
+    window_core, window_micro = lax.rem(plane, 2), lax.div(plane, 2)
+    scalars = pltpu.make_async_copy(tabs_ref.at[window_core], picks_ref, local_sem.at[1])
+    scalars.start()
+    lay_vectors(vecs_ref, vectors_ref, up_ref)
+    normed_ref[...] = (normal * vectors_ref[0:1] + vectors_ref[1:2]).astype(BF16)
+    for tile in range(TILES):
+        halves = []
+        for entry in column_order()[2 * tile : 2 * tile + 2]:
+            halves.append(entry)
+
+        def bias_tile(number, halves=halves):
+            if number < D // LANES:
+                return vectors_ref[2:3, number * LANES : (number + 1) * LANES]
+            if number < 2 * D // LANES:
+                return jnp.zeros((1, LANES), F32)
+            start = (number - 2 * D // LANES) * LANES
+            return vectors_ref[3:4, start : start + LANES]
+
+        chunk, side = tile % HALF_TILES, tile // HALF_TILES
+        start = chunk * CHUNK + side * LANES
+        bias_ref[:, start : start + LANES] = pair_of_blocks(
+            bias_tile, order[2 * tile], order[2 * tile + 1]
+        )
+    gathers[2].finish()
+    settle(g_qkv_ref, [(tile, w_qkv_ref, alternate(tile)) for tile in range(HALF_TILES)])
+    keep_w = pltpu.make_async_copy(w_qkv_ref, w_qkv_hbm, local_sem.at[2])
+    keep_w.start()
+
+    def shaped(value):
+        return value.astype(BF16).reshape(local, BLOCK, LANES)
+
+    low = low_lanes(rows)
+    queries = D // LANES
+    for chunk in range(HALF_TILES):
+        columns = slice(chunk * CHUNK, (chunk + 1) * CHUNK)
+        packed = dot(normed_ref[...], w_qkv_ref[:, columns]) + bias_ref[:, columns]
+        for side in range(2):
+            tile = chunk + side * HALF_TILES
+            whole_tile = packed[:, side * LANES : (side + 1) * LANES]
+            if tile < queries:
+                whole_tile = whole_tile.astype(BF16).astype(F32) * SCALE
+            for piece in range(PIECES):
+                part = whole_tile[piece * rows : (piece + 1) * rows]
+                if tile < SPOTS:
+                    send_ref[0, tile, piece, 0] = shaped(part)
+                elif tile < queries:
+                    first = 2 * (tile - SPOTS)
+                    shared = send_ref[0, first, piece, 0].reshape(rows, LANES).astype(F32)
+                    send_ref[1, first, piece, 0] = shaped(jnp.where(low, part, shared))
+                    shared = send_ref[0, first + 1, piece, 0].reshape(rows, LANES).astype(F32)
+                    send_ref[1, first + 1, piece, 0] = shaped(
+                        jnp.where(low, swap_halves(part), shared)
+                    )
+                else:
+                    goal, role = (tile - queries) // 3, (tile - queries) % 3
+                    if role < 2:
+                        send_ref[role, goal, piece, 1] = shaped(part)
+                    else:
+                        send_ref[0, goal, piece, 2] = shaped(part)
+    sends, keeps = [], []
+    for part, (parts, landing) in enumerate(((slice(0, 2), qk_ref), (2, shared_ref))):
+        for side in (3, 1, 2, 0):
+            for other in (core, 1 - core) if part == 0 else (core,):
+                goal = flip(spot, side)
+                for piece in range(PIECES):
+                    source = send_ref.at[other if part == 0 else 0, goal, piece, parts]
+                    target = landing.at[2 * core + piece, spot]
+                    if side == 0 and other is core:
+                        copy = pltpu.make_async_copy(source, target, qkv_local.at[part, piece])
+                        keeps.append((part, copy))
+                    else:
+                        copy = remote(
+                            source,
+                            target,
+                            qkv_send.at[len(sends)],
+                            qkv_recv.at[2 * core + piece, spot, part],
+                            (other, rank_of(plane, goal)),
+                        )
+                        sends.append(copy)
+                    copy.start()
+    for one in spreads:
+        one.columns()
+    table = lay_table(tabs_ref, window_core, window_micro, local * RANDOM)
+    table_ref[...] = table.astype(jnp.int32)
+    sort_entries(table, sorted_ref, blocks * RANDOM)
+    scalars.wait()
+
+    def arrive(part, other, piece, goal):
+        target = (qk_ref, shared_ref)[part].at[2 * other + piece, goal]
+        remote(
+            target,
+            target,
+            qkv_send.at[0],
+            qkv_recv.at[2 * other + piece, goal, part],
+            (core, rank_of(plane, spot)),
+        ).wait_recv()
+
+    for side in range(SPOTS):
+        for other in (core, 1 - core):
+            if side > 0 or other is not core:
+                for piece in range(PIECES):
+                    arrive(0, other, piece, flip(spot, side))
+    for part, copy in keeps:
+        copy.wait()
+
+    low = low_lanes(BLOCK)
+    masks = [half_mask(True), half_mask(False)]
+
+    def tile_of(component, block):
+        rank, number = lax.div(block, local), lax.rem(block, local)
+        if component == 2:
+            return shared_ref[lax.div(rank, SPOTS), lax.rem(rank, SPOTS), number]
+        return qk_ref[lax.div(rank, SPOTS), lax.rem(rank, SPOTS), component, number]
+
+    def picked(block, number):
+        rank = lax.div(block, local)
+        return picks_ref[
+            lax.div(rank, SPOTS),
+            lax.rem(rank, SPOTS),
+            window_micro,
+            lax.rem(block, local) * RANDOM + number,
+        ]
+
+    def place_of(block):
+        rank = lax.div(block, local)
+        return lax.div(rank, SPOTS), lax.rem(rank, SPOTS), lax.rem(block, local)
+
+    def put(block, slot, mixed, log):
+        place = place_of(block)
+        if slot == 0:
+            out_ref[place] = mixed.astype(BF16)
+            lse_ref[block] = jnp.where(low, log, 0.0)
+        else:
+            out_ref[place] = jnp.where(low, mixed, out_ref[place].astype(F32)).astype(BF16)
+            lse_ref[block] = jnp.where(low, lse_ref[block], log)
+
+    def one_block(block, slot):
+        ids, bias = inner_slots(picked, block, blocks)
+        keys = jnp.concatenate([tile_of(1 + slot, number) for number in ids], axis=0)
+        scores = dot_rt(tile_of(0, block) * masks[slot], keys) + bias
+        top = jnp.max(scores, axis=1, keepdims=True)
+        powered = jnp.exp(scores - top)
+        total = jnp.sum(powered, axis=1, keepdims=True)
+        mixed = dot(powered.astype(BF16), keys) * (1.0 / total)
+        return mixed, top + jnp.log(total)
+
+    def rank_blocks(rank, slot):
+        results = [one_block(rank * local + number, slot) for number in range(local)]
+        for number, (mixed, log) in enumerate(results):
+            put(rank * local + number, slot, mixed, log)
+
+    spans = blocks // SPAN
+    ends = (0, blocks - 1)
+
+    def dense(slot, scores_ref, numbers):
+        size = len(numbers) * BLOCK
+        query = jnp.concatenate([tile_of(0, number) * masks[slot] for number in numbers], axis=0)
+
+        def keys_at(span):
+            return jnp.concatenate(
+                [tile_of(1 + slot, span * SPAN + number) for number in range(SPAN)], axis=0
+            )
+
+        def first_pass(span, top):
+            scores = dot_rt(query, keys_at(span))
+            scores_ref[span] = scores
+            return jnp.maximum(top, jnp.max(scores, axis=1, keepdims=True))
+
+        top = lax.fori_loop(
+            0, spans, first_pass, jnp.full((size, 1), NEGATIVE, F32), unroll=2
+        )
+
+        def second_pass(span, carry):
+            total, mixed = carry
+            powered = jnp.exp(scores_ref[span] - top)
+            return (
+                total + jnp.sum(powered, axis=1, keepdims=True),
+                mixed + dot(powered.astype(BF16), keys_at(span)),
+            )
+
+        total, mixed = lax.fori_loop(
+            0,
+            spans,
+            second_pass,
+            (jnp.zeros((size, 1), F32), jnp.zeros((size, LANES), F32)),
+            unroll=2,
+        )
+        mixed = mixed * (1.0 / total)
+        log = top + jnp.log(total)
+        for place, number in enumerate(numbers):
+            span = slice(place * BLOCK, (place + 1) * BLOCK)
+            put(number, slot, mixed[span], log[span])
+
+    def head_a(number, carry):
+        rank_blocks(number, 0)
+        return carry
+
+    def head_b(number, carry):
+        rank_blocks(core * (PLANES * SPOTS // 2) + number, 1)
+        return carry
+
+    shared = []
+    half_way = PLANES * SPOTS // 2
+    lax.fori_loop(0, half_way, head_a, 0)
+    for side in range(SPOTS):
+        goal = flip(spot, side)
+        for piece in range(PIECES):
+            if side > 0:
+                arrive(1, core, piece, goal)
+            source = shared_ref.at[2 * core + piece, goal]
+            copy = remote(
+                source,
+                source,
+                shared_send.at[2 * side + piece],
+                shared_recv.at[2 * core + piece, goal],
+                (1 - core, rank_of(plane, spot)),
+            )
+            copy.start()
+            shared.append(copy)
+    lax.fori_loop(half_way, PLANES * SPOTS, head_a, 0)
+    dense(0, p_ref, ends)
+    spreads[0].forward()
+    back = Inward(out_ref, back_ref, *back_sems)
+    everything = slice(0, local)
+    for side, other, goal, stays in inward_targets(core, spot):
+        if other is not core:
+            for piece in range(PIECES):
+                back.send(other, goal, stays, piece, 0, everything)
+    for side in range(SPOTS):
+        for piece in range(PIECES):
+            target = shared_ref.at[2 * (1 - core) + piece, flip(spot, side)]
+            remote(
+                target,
+                target,
+                shared_send.at[0],
+                shared_recv.at[2 * (1 - core) + piece, flip(spot, side)],
+                (core, rank_of(plane, spot)),
+            ).wait_recv()
+    keep_qk = pltpu.make_async_copy(qk_ref, qk_hbm, local_sem.at[3])
+    keep_qk.start()
+    keep_shared = pltpu.make_async_copy(shared_ref, shared_hbm, local_sem.at[6])
+    keep_shared.start()
+    lax.fori_loop(0, half_way, head_b, 0)
+    dense(1, q_ref, (core * (blocks - 1),))
+    spreads[1].forward()
+    for side, other, goal, stays in inward_targets(core, spot):
+        if other is core:
+            for piece in range(PIECES):
+                back.send(other, goal, stays, piece, 0, everything)
+    spreads[0].corner()
+    spreads[0].finish()
+    settle(
+        g_ou_ref,
+        [(tile, w_out_ref, (tile, outs + tile)) for tile in range(outs)]
+        + [(outs + tile, w_up_ref, alternate(tile)) for tile in range(FF // CHUNK)],
+    )
+    keep_out = pltpu.make_async_copy(w_out_ref, w_out_hbm, local_sem.at[4])
+    keep_out.start()
+    keep_up = pltpu.make_async_copy(w_up_ref, w_up_hbm, local_sem.at[5])
+    keep_up.start()
+    spreads[1].corner()
+    spreads[1].finish()
+    finish_dy()
+    for copy in sends:
+        copy.wait_send()
+    for copy in shared:
+        copy.wait_send()
+    back.finish(((everything,), (everything,)))
+    for copy in (keep_x, keep_w, keep_qk, keep_shared, keep_out, keep_up):
+        copy.wait()
+
+
+def front(x, dy, vec, tab, w_qkv, w_out, w_up, w_down):
+    micro, rows, _ = x.shape
+    tokens = PIECES * rows
+    local = rows // BLOCK
+    blocks = PLANES * SPOTS * local
+    spans = blocks // SPAN
+    grid = (2, PLANES, SPOTS)
+    shard = D // RANKS
+    tile = (local, BLOCK, LANES)
+    dma = pltpu.SemaphoreType.DMA
+    struct = jax.ShapeDtypeStruct
+    ou = (2 * shard, (D + FF) // 2)
+    return pl.pallas_call(
+        front_kernel,
+        out_shape=(
+            struct((2, SPOTS, PIECES) + tile, BF16),
+            struct(x.shape, BF16),
+            struct(dy.shape, BF16),
+            struct(grid + w_down.shape, BF16),
+            struct((D, 3 * D), BF16),
+            struct((D, D), BF16),
+            struct((D, FF), BF16),
+            struct((PLANES, SPOTS, 2) + tile, BF16),
+            struct((PLANES, SPOTS) + tile, BF16),
+            struct((tokens, D), BF16),
+            struct((blocks, BLOCK, LANES), F32),
+            struct((VECTORS, D), F32),
+            struct((FF // CHUNK, 1, CHUNK), F32),
+            struct((1, 2 * LANES), jnp.int32),
+            struct((4, 2 * LANES), jnp.int32),
+        ),
+        in_specs=[
+            whole(ANY),
+            whole(ANY),
+            whole(ANY),
+            whole(ANY),
+            whole(),
+            whole(),
+            whole(),
+            whole(ANY),
+        ],
+        out_specs=(whole(ANY),) * 9 + (whole(),) * 6,
+        scratch_shapes=[
+            VMEM((2 * shard, 3 * D // 2), BF16),
+            VMEM(ou, BF16),
+            VMEM(grid + (2 * shard, 3 * D // 2), BF16),
+            VMEM(grid + ou, BF16),
+            VMEM((D, 3 * D), BF16),
+            VMEM((D, D), BF16),
+            VMEM((D, FF), BF16),
+            VMEM((PIECES, rows, D), BF16),
+            VMEM(grid + vec.shape, BF16),
+            VMEM(grid + tab.shape, jnp.int32),
+            VMEM((1, 3 * D), F32),
+            VMEM((2, SPOTS, PIECES, 3) + tile, BF16),
+            VMEM((PLANES, SPOTS, 2) + tile, BF16),
+            VMEM((PLANES, SPOTS) + tile, BF16),
+            VMEM((PLANES, SPOTS) + tile, BF16),
+            VMEM((spans, 2 * BLOCK, SPAN * BLOCK), F32),
+            VMEM((spans, BLOCK, SPAN * BLOCK), F32),
+            pltpu.SMEM((PLANES, SPOTS) + tab.shape, jnp.int32),
+            dma((3, Gather.SENDS)),
+            dma((3,) + grid),
+            dma((3,)),
+            dma((2, PlaneGather.SENDS)),
+            dma((2, PLANES)),
+            dma((2, 2, SPOTS, 2)),
+            dma((2,)),
+        ]
+        + [dma((2,))] * 6
+        + [
+            dma((20,)),
+            dma((PLANES, SPOTS, 2)),
+            dma((2, PIECES)),
+            dma((2 * SPOTS,)),
+            dma((PLANES, SPOTS)),
+            dma((14,)),
+            dma((2, SPOTS, PIECES, 1)),
+            dma((1, PIECES)),
+            dma((7,)),
+        ],
+        compiler_params=pltpu.CompilerParams(
+            vmem_limit_bytes=60 * 1024 * 1024, collective_id=1, has_side_effects=True
+        ),
+        name="front",
+    )(x, dy, vec, tab, w_qkv, w_out, w_up, w_down)
 
 
 def by_owner(out_ref, values):
@@ -2677,46 +2720,49 @@
     own = norm1_gain.shape[0]
     order = [natural_block(entry) for entry in column_order()]
     inverse = [order.index(number) for number in range(len(order))]
-    small = (8 + FF // D) * own
-    entries = rand_table.size
-
-    vec = jnp.concatenate(
+
+    def in_row(vector, number):
+        return jnp.pad(vector[None], ((number, 15 - number), (0, LANES - vector.shape[0])))
+
+    vec = functools.reduce(
+        jnp.add,
         [
-            norm1_gain,
-            norm1_bias,
-            query_bias,
-            value_bias,
-            out_bias,
-            norm2_gain,
-            norm2_bias,
-            down_bias,
-            up_bias,
-            rand_table.reshape(entries).astype(BF16),
-            jnp.zeros((16 * LANES - small - entries,), BF16),
-        ]
-    ).reshape(16, LANES)
-    x, vecs, w_qkv_all = collect(hidden_in, vec, fold_columns(take_blocks(w_qkv, order)))
-    vecs = vecs.reshape(RANKS, 16 * LANES)
-    vectors = vecs[:, : 8 * own].reshape(RANKS, 8, own).swapaxes(0, 1).reshape(8, D).astype(F32)
-    up_shift = vecs[:, 8 * own : small].astype(F32).reshape(2, FF // CHUNK, LANES)
-    up_shift = up_shift.swapaxes(0, 1).reshape(FF // CHUNK, 1, CHUNK)
-    bias = jnp.concatenate([vectors[2:3], jnp.zeros((1, D), F32), vectors[3:4]], axis=1)
-    bias = take_blocks(bias, order).reshape(2, HALF_TILES, LANES)
-    bias = bias.swapaxes(0, 1).reshape(1, 3 * D)
-    plane = lax.div(lax.axis_index("gy"), SPOTS)
-    tables = vecs[:, small : small + entries].reshape(2, PLANES * SPOTS, 2, local * RANDOM)
-    tables = tables.astype(jnp.int32).transpose(2, 0, 1, 3).reshape(PLANES, 1, -1)
-    table = lax.dynamic_index_in_dim(tables, plane, 0, keepdims=False)
-    spare = -table.shape[1] % LANES
-    table = jnp.pad(table, ((0, 0), (0, spare)), constant_values=2 * LANES)
-
-    normed, send, sorted_table = plane_qkv(x, vectors, w_qkv_all, bias, table)
-    s_ou = jnp.concatenate([fold_columns(w_out), fold_columns(w_up)], axis=1)
-    qkv, c_ou, c_down = exchange_qkv(send, s_ou, w_down)
-    qkv = qkv.reshape(PLANES * SPOTS, 3, local, BLOCK, LANES)
-    mixed, lse, dy, w_out_all, w_up_all, w_down_all = plane_attention(
-        table, qkv, cotangent, c_ou, c_down
+            in_row(vector, number)
+            for number, vector in enumerate(
+                (
+                    norm1_gain,
+                    norm1_bias,
+                    query_bias,
+                    value_bias,
+                    out_bias,
+                    norm2_gain,
+                    norm2_bias,
+                    down_bias,
+                    up_bias,
+                )
+            )
+        ],
     )
+    tab = jnp.pad(
+        rand_table.reshape(micro, local * RANDOM), ((0, 8 - micro), (0, LANES - local * RANDOM))
+    )
+    (
+        mixed,
+        x,
+        dy,
+        w_down_all,
+        w_qkv_all,
+        w_out_all,
+        w_up_all,
+        qk,
+        shared,
+        normed,
+        lse,
+        vectors,
+        up_shift,
+        table,
+        sorted_table,
+    ) = front(hidden_in, cotangent, vec, tab, w_qkv, w_out, w_up, w_down)
     mixed = mixed.reshape(2, SPOTS, PIECES, rows, LANES)
     hidden, grad_send, dres, g_out, g_up, g_down, g_up_bias, g_mid = plane_middle(
         mixed,
@@ -2732,7 +2778,8 @@
     dqkv, hidden_out, t_out, t_up, t_down = plane_attention_back(
         table,
         sorted_table,
-        qkv,
+        qk,
+        shared,
         grad_send.reshape(2, SPOTS, PIECES, local, BLOCK, LANES),
         lse,
         hidden,

time: 351 us -> 333 us (0.949)
  local copies, waits for them, and re-layouts: 26.2 us -> 9.96 us
    unnamed x36 -> x9, local copies, waits for them, and re-layouts: 8.65 us -> 2.38 us
    concatenate x1 -> x0, local copies, waits for them, and re-layouts: 6.1 us -> none  [plane_shards(): jnp.concatenate([norm1_gain, norm1_bias, query_bias, value_bias, out_bias...]
    pallas_call x4 -> x1, Pallas kernels: 143 us -> 139 us  [front(): pl.pallas_call(front_kernel, out_shape=(struct((2, SPOTS, PIECES) + tile,...]
where the time goes in v6:
time: 333 us
  Pallas kernels  315 us (95%)
  local copies, waits for them, and re-layouts  9.96 us (3%)
  other arithmetic  6.91 us (2%)
    pallas_call x1, Pallas kernels, front(): pl.pallas_call(front_kernel, out_shape=(struct((2, SPOTS, PIECES) + tile,...  139 us
    pallas_call x1, Pallas kernels, plane_attention_back(): pl.pallas_call(functools.partial(plane_attend_back_kernel, count), out_sh...  99.6 us
    pallas_call x1, Pallas kernels, finish_layer(): pl.pallas_call(finish_kernel, out_shape=(jax.ShapeDtypeStruct(x.shape, BF...  40.5 us
    pallas_call x1, Pallas kernels, plane_middle(): pl.pallas_call(plane_middle_kernel, grid=(steps,), out_shape=(jax.ShapeDt...  35.9 us

profile of v6, /device:TPU:0, one launch (start us, length us, event | category | flops | bytes accessed | tf_op | source)
XLA Modules:
  0.0 332.8 jit_solution(12150407594722963996)
XLA Ops:
  0.6 0.8 copy.33
  1.4 0.1 reshape.66
  1.5 0.6 pad.49.tab_ref
  2.1 1.4 pad_add_fusion.vec_ref
  3.5 139.2 %front.1 = (bf16[2,4,2,4,64,128]{5,4,3,2,1,0:T(8,128)(2,1)}, bf16[2,256,768]{2,1,0:T(8,128)(2,1)}, bf16[2,256,768]{2,1,0:T(8,128)(2,1)}, bf16[2,4,4,96,768]{4,3,...) custom-call(bf16[2,256,768]{2,1,0:T(8,128)(2,1)} %x_in_ref.1, ...), custom_call_target="tpu_custom_call" | custom-call | tf_op jit(solution)/shard_map/front/pallas_call | solution.py:2062
  142.7 35.9 %plane_middle.1 = (bf16[2,256,768]{2,1,0:T(8,128)(2,1)}, bf16[2,4,2,256,128]{4,3,2,1,0:T(8,128)(2,1)}, f32[512,768]{1,0:T(8,128)}, bf16[32,48,384]{2,1,0:T(8,128...) custom-call(bf16[2,4,2,256,128]{4,3,2,1,0:T(8,128)(2,1)} %bitcast.44, ...), custom_call_target="tpu_custom_call" | custom-call | tf_op jit(solution)/shard_map/plane_middle/pallas_call | solution.py:2265
  178.6 99.6 %plane_attention_back.1 = (bf16[2,4,2,3,4,64,128]{6,5,4,3,2,1,0:T(8,128)(2,1)}, bf16[2,256,768]{2,1,0:T(8,128)(2,1)}, f32[48,384]{1,0:T(8,128)}, f32[48,1536]{1,0:T(8,128)}, f32[96,768]{1,0:T(8,128)}) custom-call(s32[1,256]{1,0:T(1,128)} %get-tuple-element.47.refs_0_, s32[4,256]{1,0:T(4,128)} %get-tuple-element.48.refs_1_, ...), custom_call_target="tpu_custom_call" | custom-call | tf_op jit(solution)/shard_map/plane_attention_back/pallas_call | solution.py:1454
  278.2 1.0 fusion.2
  279.2 0.7 pad_maximum_fusion
  280.0 0.8 fusion.6
  280.8 0.6 pad_maximum_fusion.1
  281.4 40.5 %finish_layer.1 = (bf16[2,256,768]{2,1,0:T(8,128)(2,1)}, f32[48,1152]{1,0:T(8,128)}, f32[8,768]{1,0:T(8,128)}, f32[24,256]{1,0:T(8,128)}) custom-call(bf16[2,4,2,3,256,128]{5,4,3,2,1,0:T(8,128)(2,1)} %bitcast.42, bf16[512,768]{1,0:T(8,128)(2,1)} %get-tuple-element.67.normed_ref, bf16[2,256,768]{2,1,0:T(8,128)(2,1)} %get-tuple-element.52.x_ref, ...), custom_call_target="tpu_custom_call" | custom-call | tf_op jit(solution)/shard_map/finish_layer/pallas_call | solution.py:2642
  321.9 0.0 copy-start.2
  321.9 0.0 copy-start
  321.9 0.0 copy-start.1
  321.9 1.1 fusion.5
  323.0 1.0 fusion.3
  323.9 1.0 fusion.4
  324.9 0.8 concatenate.25
  325.7 0.7 slice.208
  326.5 0.1 fusion.8
  326.6 0.1 fusion.7
  326.6 0.1 concatenate.22
  326.7 0.1 concatenate.21
  326.8 0.8 fusion.1
  327.6 0.5 slice_bitcast_fusion
  328.2 2.4 convert_element_type.21
  330.6 0.0 copy-done.2
  330.6 0.6 dynamic_slice.7
  331.2 0.0 copy-done
  331.2 0.9 copy.42
  332.1 0.0 copy-done.1
  332.1 0.7 copy.43
  (7 shorter events, 0.1 us)
Async XLA Ops:
  321.9 8.7 %copy-start.2 = (f32[24,256]{1,0:T(8,128)S(1)}, f32[24,256]{1,0:T(8,128)}, u32[]{:S(2)}) copy-start(f32[24,256]{1,0:T(8,128)} %get-tuple-element.74) | copy-start | bytes 73732
  321.9 9.3 %copy-start = (bf16[2,256,768]{2,1,0:T(8,128)(2,1)S(1)}, bf16[2,256,768]{2,1,0:T(8,128)(2,1)}, u32[]{:S(2)}) copy-start(bf16[2,256,768]{2,1,0:T(8,128)(2,1)} %get-tuple-element.151) | copy-start | bytes 2359300
  321.9 10.2 %copy-start.1 = (f32[96,768]{1,0:T(8,128)S(1)}, f32[96,768]{1,0:T(8,128)}, u32[]{:S(2)}) copy-start(f32[96,768]{1,0:T(8,128)} %get-tuple-element.164) | copy-start | bytes 884740

commit v7 on v6

--- a/solution.py
+++ b/solution.py
@@ -1596,6 +1596,125 @@
             copy.wait_send()
 
 
+class CrossGather:
+    SENDS = 2 + 1 + 3 + 3 * 4
+
+    def __init__(self, source, target, send_sem, spot_sem, recv_sem, local_sem):
+        self.target = target
+        self.send_sem, self.spot_sem, self.recv_sem = send_sem, spot_sem, recv_sem
+        self.core, self.plane, self.spot = place_here()
+        self.sends = []
+        self.own = pltpu.make_async_copy(
+            source, target.at[self.core, self.plane, self.spot], local_sem
+        )
+        self.own.start()
+        for side in (1, 2):
+            self.pass_on(source, self.spot, flip(self.spot, side))
+
+    def push(self, source, target, recv_sem, device):
+        copy = remote(source, target, self.send_sem.at[len(self.sends)], recv_sem, device)
+        copy.start()
+        self.sends.append(copy)
+
+    def pass_on(self, source, spot, goal):
+        self.push(
+            source,
+            self.target.at[self.core, self.plane, spot],
+            self.spot_sem.at[spot],
+            (self.core, rank_of(self.plane, goal)),
+        )
+
+    def await_spot(self, spot):
+        shard = self.target.at[self.core, self.plane, spot]
+        remote(
+            shard,
+            shard,
+            self.send_sem.at[0],
+            self.spot_sem.at[spot],
+            (self.core, rank_of(self.plane, self.spot)),
+        ).wait_recv()
+
+    def across(self):
+        beside, beyond = flip(self.spot, 1), flip(self.spot, 2)
+        for side in (1, 2):
+            self.await_spot(flip(self.spot, side))
+        spot = beside * (1 - self.core) + beyond * self.core
+        goal = beyond * (1 - self.core) + beside * self.core
+        self.pass_on(self.target.at[self.core, self.plane, spot], spot, goal)
+
+    def blocks(self):
+        self.own.wait()
+        self.await_spot(flip(self.spot, 3))
+        self.maybe = []
+        self.along(self.plane, 1, self.plane < PLANES - 1)
+        self.along(self.plane, -1, self.plane > 0)
+        self.to_sibling(self.plane, self.plane >= 0)
+
+    def along(self, plane, step, wanted):
+        block = self.target.at[self.core, plane]
+        copy = remote(
+            block,
+            block,
+            self.send_sem.at[3 + len(self.maybe)],
+            self.recv_sem.at[self.core, plane],
+            (self.core, rank_of(self.plane + step, self.spot)),
+        )
+        self.begin(copy, wanted)
+
+    def to_sibling(self, plane, wanted):
+        block = self.target.at[self.core, plane]
+        copy = remote(
+            block,
+            block,
+            self.send_sem.at[3 + len(self.maybe)],
+            self.recv_sem.at[self.core, plane],
+            (1 - self.core, rank_of(self.plane, self.spot)),
+        )
+        self.begin(copy, wanted)
+
+    def begin(self, copy, wanted):
+        self.maybe.append((copy, wanted))
+
+        @pl.when(wanted)
+        def _():
+            copy.start()
+
+    def arrive(self, core, plane):
+        block = self.target.at[core, plane]
+        remote(
+            block,
+            block,
+            self.send_sem.at[0],
+            self.recv_sem.at[core, plane],
+            (self.core, rank_of(self.plane, self.spot)),
+        ).wait_recv()
+
+    def hop(self, distance):
+        for step in (1, -1):
+            origin = self.plane - step * distance
+            here = (origin >= 0) & (origin < PLANES)
+            onward = self.plane + step
+            more = here & (onward >= 0) & (onward < PLANES)
+
+            @pl.when(here)
+            def _(origin=origin):
+                self.arrive(self.core, origin)
+
+            self.along(origin, step, more)
+            self.to_sibling(origin, here)
+
+    def finish(self):
+        for bits in range(PLANES):
+            self.arrive(1 - self.core, flip(self.plane, bits))
+        for copy in self.sends:
+            copy.wait_send()
+        for copy, wanted in self.maybe:
+
+            @pl.when(wanted)
+            def _(copy=copy):
+                copy.wait_send()
+
+
 def pair_of_blocks(read, first, second):
     low = low_lanes(1)
     tiles = []
@@ -1707,10 +1826,10 @@
     *sems,
 ):
     gather_send, gather_recv, gather_local = sems[:3]
-    plane_send, plane_column, plane_recv, plane_local = sems[3:7]
-    x_sems, dy_sems = sems[7:10], sems[10:13]
-    qkv_send, qkv_recv, qkv_local, shared_send, shared_recv = sems[13:18]
-    back_sems, local_sem = sems[18:21], sems[21]
+    plane_sems, cross_sems = sems[3:7], sems[7:11]
+    x_sems, dy_sems = sems[11:14], sems[14:17]
+    qkv_send, qkv_recv, qkv_local, shared_send, shared_recv = sems[17:22]
+    back_sems, local_sem = sems[22:25], sems[25]
     core, plane, spot = place_here()
     micro, rows, _ = x_in_ref.shape
     tokens = PIECES * rows
@@ -1750,25 +1869,14 @@
     fold_tiles(s_ou_ref, outs, list(range(FF // LANES)), natural(w_up_in_ref))
     for one in gathers:
         one.column()
+    cross = CrossGather(w_down_in_ref, w_down_ref, *cross_sems)
     for one in gathers:
         one.across()
     for one in gathers:
         one.corner()
+    cross.across()
     finish_x()
-    spreads = [
-        PlaneGather(
-            source,
-            target,
-            plane_send.at[number],
-            plane_column.at[number],
-            plane_recv.at[number],
-            plane_local.at[number],
-        )
-        for number, (source, target) in enumerate(
-            ((s_ou_ref, g_ou_ref), (w_down_in_ref, w_down_ref))
-        )
-    ]
-    finish_dy = to_planes(dy_ref, dys_ref, *dy_sems)
+    spread = PlaneGather(s_ou_ref, g_ou_ref, *plane_sems)
     keep_x = pltpu.make_async_copy(xs_ref, x_ref, local_sem.at[0])
     keep_x.start()
     normal, _ = norm_parts(xs_ref[...].reshape(tokens, D).astype(F32))
@@ -1855,8 +1963,8 @@
                         )
                         sends.append(copy)
                     copy.start()
-    for one in spreads:
-        one.columns()
+    spread.columns()
+    cross.blocks()
     table = lay_table(tabs_ref, window_core, window_micro, local * RANDOM)
     table_ref[...] = table.astype(jnp.int32)
     sort_entries(table, sorted_ref, blocks * RANDOM)
@@ -1879,6 +1987,7 @@
                     arrive(0, other, piece, flip(spot, side))
     for part, copy in keeps:
         copy.wait()
+    cross.hop(1)
 
     low = low_lanes(BLOCK)
     masks = [half_mask(True), half_mask(False)]
@@ -1994,9 +2103,11 @@
             )
             copy.start()
             shared.append(copy)
+    cross.hop(2)
+    finish_dy = to_planes(dy_ref, dys_ref, *dy_sems)
     lax.fori_loop(half_way, PLANES * SPOTS, head_a, 0)
     dense(0, p_ref, ends)
-    spreads[0].forward()
+    spread.forward()
     back = Inward(out_ref, back_ref, *back_sems)
     everything = slice(0, local)
     for side, other, goal, stays in inward_targets(core, spot):
@@ -2019,13 +2130,13 @@
     keep_shared.start()
     lax.fori_loop(0, half_way, head_b, 0)
     dense(1, q_ref, (core * (blocks - 1),))
-    spreads[1].forward()
+    spread.corner()
+    cross.hop(3)
     for side, other, goal, stays in inward_targets(core, spot):
         if other is core:
             for piece in range(PIECES):
                 back.send(other, goal, stays, piece, 0, everything)
-    spreads[0].corner()
-    spreads[0].finish()
+    spread.finish()
     settle(
         g_ou_ref,
         [(tile, w_out_ref, (tile, outs + tile)) for tile in range(outs)]
@@ -2035,8 +2146,7 @@
     keep_out.start()
     keep_up = pltpu.make_async_copy(w_up_ref, w_up_hbm, local_sem.at[5])
     keep_up.start()
-    spreads[1].corner()
-    spreads[1].finish()
+    cross.finish()
     finish_dy()
     for copy in sends:
         copy.wait_send()
@@ -2111,10 +2221,14 @@
             dma((3, Gather.SENDS)),
             dma((3,) + grid),
             dma((3,)),
-            dma((2, PlaneGather.SENDS)),
+            dma((PlaneGather.SENDS,)),
+            dma((PLANES,)),
+            dma((2, SPOTS, 2)),
+            dma,
+            dma((CrossGather.SENDS,)),
+            dma((SPOTS,)),
             dma((2, PLANES)),
-            dma((2, 2, SPOTS, 2)),
-            dma((2,)),
+            dma,
         ]
         + [dma((2,))] * 6
         + [

time: 333 us -> 325 us (0.976)
  Pallas kernels: 315 us -> 307 us
    pallas_call x1, Pallas kernels: 139 us -> 130 us  [front(): pl.pallas_call(front_kernel, out_shape=(struct((2, SPOTS, PIECES) + tile,...]
where the time goes in v7:
time: 325 us
  Pallas kernels  307 us (94%)
  local copies, waits for them, and re-layouts  9.96 us (3%)
  other arithmetic  6.91 us (2%)
    pallas_call x1, Pallas kernels, front(): pl.pallas_call(front_kernel, out_shape=(struct((2, SPOTS, PIECES) + tile,...  130 us
    pallas_call x1, Pallas kernels, plane_attention_back(): pl.pallas_call(functools.partial(plane_attend_back_kernel, count), out_sh...  101 us
    pallas_call x1, Pallas kernels, finish_layer(): pl.pallas_call(finish_kernel, out_shape=(jax.ShapeDtypeStruct(x.shape, BF...  40.5 us
    pallas_call x1, Pallas kernels, plane_middle(): pl.pallas_call(plane_middle_kernel, grid=(steps,), out_shape=(jax.ShapeDt...  35.9 us

profile of v7, /device:TPU:0, one launch (start us, length us, event | category | flops | bytes accessed | tf_op | source)
XLA Modules:
  0.0 324.8 jit_solution(5089599208471450185)
XLA Ops:
  0.6 0.8 copy.33
  1.4 0.1 reshape.66
  1.5 0.6 pad.49.tab_ref
  2.1 1.4 pad_add_fusion.vec_ref
  3.5 130.1 %front.1 = (bf16[2,4,2,4,64,128]{5,4,3,2,1,0:T(8,128)(2,1)}, bf16[2,256,768]{2,1,0:T(8,128)(2,1)}, bf16[2,256,768]{2,1,0:T(8,128)(2,1)}, bf16[2,4,4,96,768]{4,3,...) custom-call(bf16[2,256,768]{2,1,0:T(8,128)(2,1)} %x_in_ref.1, ...), custom_call_target="tpu_custom_call" | custom-call | tf_op jit(solution)/shard_map/front/pallas_call | solution.py:2172
  133.6 35.9 %plane_middle.1 = (bf16[2,256,768]{2,1,0:T(8,128)(2,1)}, bf16[2,4,2,256,128]{4,3,2,1,0:T(8,128)(2,1)}, f32[512,768]{1,0:T(8,128)}, bf16[32,48,384]{2,1,0:T(8,128...) custom-call(bf16[2,4,2,256,128]{4,3,2,1,0:T(8,128)(2,1)} %bitcast.44, ...), custom_call_target="tpu_custom_call" | custom-call | tf_op jit(solution)/shard_map/plane_middle/pallas_call | solution.py:2379
  169.5 100.8 %plane_attention_back.1 = (bf16[2,4,2,3,4,64,128]{6,5,4,3,2,1,0:T(8,128)(2,1)}, bf16[2,256,768]{2,1,0:T(8,128)(2,1)}, f32[48,384]{1,0:T(8,128)}, f32[48,1536]{1,0:T(8,128)}, f32[96,768]{1,0:T(8,128)}) custom-call(s32[1,256]{1,0:T(1,128)} %get-tuple-element.47.refs_0_, s32[4,256]{1,0:T(4,128)} %get-tuple-element.48.refs_1_, ...), custom_call_target="tpu_custom_call" | custom-call | tf_op jit(solution)/shard_map/plane_attention_back/pallas_call | solution.py:1454
  270.3 1.0 fusion.2
  271.3 0.7 pad_maximum_fusion
  272.0 0.8 fusion.6
  272.8 0.6 pad_maximum_fusion.1
  273.5 40.5 %finish_layer.1 = (bf16[2,256,768]{2,1,0:T(8,128)(2,1)}, f32[48,1152]{1,0:T(8,128)}, f32[8,768]{1,0:T(8,128)}, f32[24,256]{1,0:T(8,128)}) custom-call(bf16[2,4,2,3,256,128]{5,4,3,2,1,0:T(8,128)(2,1)} %bitcast.42, bf16[512,768]{1,0:T(8,128)(2,1)} %get-tuple-element.67.normed_ref, bf16[2,256,768]{2,1,0:T(8,128)(2,1)} %get-tuple-element.52.x_ref, ...), custom_call_target="tpu_custom_call" | custom-call | tf_op jit(solution)/shard_map/finish_layer/pallas_call | solution.py:2756
  313.9 0.0 copy-start.2
  313.9 0.0 copy-start
  313.9 0.0 copy-start.1
  314.0 1.1 fusion.5
  315.0 1.0 fusion.3
  316.0 1.0 fusion.4
  317.0 0.8 concatenate.25
  317.8 0.7 slice.208
  318.5 0.1 fusion.8
  318.6 0.1 fusion.7
  318.7 0.1 concatenate.22
  318.8 0.1 concatenate.21
  318.9 0.8 fusion.1
  319.7 0.5 slice_bitcast_fusion
  320.2 2.4 convert_element_type.21
  322.6 0.0 copy-done.2
  322.7 0.6 dynamic_slice.7
  323.2 0.0 copy-done
  323.2 0.9 copy.42
  324.1 0.0 copy-done.1
  324.1 0.7 copy.43
  (7 shorter events, 0.1 us)
Async XLA Ops:
  313.9 8.7 %copy-start.2 = (f32[24,256]{1,0:T(8,128)S(1)}, f32[24,256]{1,0:T(8,128)}, u32[]{:S(2)}) copy-start(f32[24,256]{1,0:T(8,128)} %get-tuple-element.74) | copy-start | bytes 73732
  313.9 9.3 %copy-start = (bf16[2,256,768]{2,1,0:T(8,128)(2,1)S(1)}, bf16[2,256,768]{2,1,0:T(8,128)(2,1)}, u32[]{:S(2)}) copy-start(bf16[2,256,768]{2,1,0:T(8,128)(2,1)} %get-tuple-element.151) | copy-start | bytes 2359300
  313.9 10.2 %copy-start.1 = (f32[96,768]{1,0:T(8,128)S(1)}, f32[96,768]{1,0:T(8,128)}, u32[]{:S(2)}) copy-start(f32[96,768]{1,0:T(8,128)} %get-tuple-element.164) | copy-start | bytes 884740

commit v8 on v7

--- a/solution.py
+++ b/solution.py
@@ -1183,16 +1183,19 @@
 KEYS_A, QUERIES, KEYS_B = range(3)
 
 
-def plane_attend_back_kernel(count, *refs):
+def plane_attend_back_kernel(*refs):
     table_ref, sorted_ref, qk_ref, shared_ref, grad_source_ref, lse_ref, hidden_ref = refs[:7]
-    sources, refs = refs[7 : 7 + count], refs[7 + count :]
-    back_ref, hidden_out_ref = refs[:2]
-    outs, refs = refs[2 : 2 + count], refs[2 + count :]
-    buffers, refs = refs[: 7 * count], refs[7 * count :]
-    grad_ref, out_ref, sums_ref, shares_ref, walked_ref, sibling_ref = refs[:6]
-    scores_refs, refs = refs[6:10], refs[10:]
-    reduce_send, reduce_recv, reduce_local = refs[:3]
-    grad_sems, back_sems, move_sems, sibling_sems = refs[3:6], refs[6:9], refs[9:12], refs[12:14]
+    sources, half_up_ref, half_down_ref, refs = refs[7:10], refs[10], refs[11], refs[12:]
+    sources = list(sources[:2]) + [sources[2].at[number] for number in range(LATE)]
+    back_ref, hidden_out_ref, t_out_ref, t_up_ref, t_down_ref = refs[:5]
+    count = 2 + LATE
+    refs = refs[5:]
+    buffers, mines, refs = refs[: 3 * count], refs[3 * count : 4 * count], refs[4 * count :]
+    part_out_ref, part_up_ref, part_down_ref, far_out_ref, far_up_ref, far_down_ref = refs[:6]
+    grad_ref, out_ref, sums_ref, shares_ref, walked_ref, sibling_ref = refs[6:12]
+    scores_refs, refs = refs[12:16], refs[16:]
+    reduce_send, reduce_recv, far_send, far_recv, load_sem = refs[:5]
+    grad_sems, back_sems, move_sems, sibling_sems = refs[5:8], refs[8:11], refs[11:14], refs[14:16]
 
     local = qk_ref.shape[3]
     groups = PLANES * SPOTS
@@ -1204,16 +1207,28 @@
     greet(both_partners(core, plane, spot))
     grads = Outward(grad_source_ref, grad_ref, *grad_sems)
     reduces = [
-        Reduce(
+        SpotReduce(
             source,
-            *buffers[7 * number : 7 * number + 7],
-            out,
-            (reduce_send.at[number], reduce_recv.at[number], reduce_local.at[number]),
+            *buffers[3 * number : 3 * number + 3],
+            reduce_send.at[number],
+            reduce_recv.at[number],
+            rows=FF // RANKS if number >= 2 else None,
+            mine=mine,
         )
-        for number, (source, out) in enumerate(zip(sources, outs))
+        for number, (source, mine) in enumerate(zip(sources, mines))
+    ]
+    ready = PER_STAGE * EARLY
+    loads = [
+        pltpu.make_async_copy(one.half(core), mine, load_sem.at[number])
+        for number, (one, mine) in enumerate(zip(reduces, mines))
+    ] + [
+        pltpu.make_async_copy(half_up_ref, part_up_ref.at[0:ready], load_sem.at[count]),
+        pltpu.make_async_copy(half_down_ref, part_down_ref.at[0:EARLY], load_sem.at[count + 1]),
     ]
     for one in reduces:
         one.start()
+    for copy in loads:
+        copy.start()
     finish_hidden = from_planes(hidden_ref, hidden_out_ref, *move_sems)
 
     def load(component, block):
@@ -1385,12 +1400,38 @@
     for side in range(SPOTS):
         grads.arrive(side)
         head_a(side)
-        if side == 1:
+        if side == 0:
+            for copy in loads:
+                copy.wait()
             for one in reduces:
                 one.corners()
+        if side == 2:
+            for one in reduces:
+                one.sides()
     dense(0, scores_refs[0], scores_refs[1], ends)
-    for one in reduces:
-        one.sides()
+    reduces[0].close(part_out_ref)
+    reduces[1].close(part_up_ref.at[ready : PER_STAGE * STAGES])
+    for number in range(LATE):
+        reduces[2 + number].close(part_down_ref.at[EARLY + number])
+    fars = []
+    for bits in range(1, PLANES):
+        goal = flip(plane, bits)
+        for number, (source, target) in enumerate(
+            (
+                (part_out_ref.at[:, goal], far_out_ref),
+                (part_up_ref.at[:, goal], far_up_ref),
+                (part_down_ref.at[goal], far_down_ref),
+            )
+        ):
+            copy = remote(
+                source,
+                target.at[bits - 1],
+                far_send.at[number, bits - 1],
+                far_recv.at[number, bits - 1],
+                (core, rank_of(goal, spot)),
+            )
+            copy.start()
+            fars.append(copy)
     walk(0, blocks * RANDOM)
     for side, other, goal, stays in inward_targets(core, spot):
         for piece in range(PIECES):
@@ -1420,8 +1461,6 @@
     for number in range(PIECES):
         for goal in range(SPOTS):
             close(1, (2 * core + number) * SPOTS + goal, KEYS_B)
-    for one in reduces:
-        one.columns()
     across.wait_recv()
     for side, other, goal, stays in inward_targets(core, spot):
         if other is core:
@@ -1431,33 +1470,67 @@
                     out_ref[place].astype(F32) + sibling_ref[piece, goal].astype(F32)
                 ).astype(BF16)
                 back.send(other, goal, stays, piece, 2, own_parts[2])
-    for one in reduces:
-        one.finish()
+    for copy in fars:
+        copy.wait()
+
+    def total(part, far, index):
+        value = part.astype(F32)
+        for bits in range(PLANES - 1):
+            value = value + far[(bits,) + index].astype(F32)
+        return value
+
+    t_out_ref[...] = total(part_out_ref[0, plane], far_out_ref, (0,))
+
+    def close_up(number, carry):
+        t_up_ref[number] = total(part_up_ref[number, plane], far_up_ref, (number,))
+        return carry
+
+    lax.fori_loop(0, PER_STAGE * STAGES, close_up, 0)
+    t_down_ref[...] = total(part_down_ref[plane], far_down_ref, ())
     finish_hidden()
     grads.finish()
     across.wait_send()
     back.finish((own_parts, far_parts))
 
 
-def plane_attention_back(table, sorted_table, qk, shared, grad_source, lse, hidden, sources):
+def plane_attention_back(
+    table, sorted_table, qk, shared, grad_source, lse, hidden, sources, half_up, half_down
+):
     local = qk.shape[3]
     blocks = PLANES * SPOTS * local
     spans = blocks // SPAN
-    count = len(sources)
-    buffers = []
-    for source in sources:
-        buffers += reduce_scratch(source.shape, source.dtype)
+    shard, rows = D // RANKS, FF // RANKS
+    up_count = PER_STAGE * STAGES
+    up_tail, out_tail = (2 * shard, LANES), (2 * shard, D // 2)
+    buffers = block_scratch(1, *out_tail) + block_scratch(PER_STAGE * LATE, *up_tail)
+    for _ in range(LATE):
+        buffers += row_scratch(rows, D)
+    count = 2 + LATE
+    mines = [
+        VMEM((1, PLANES, SPOTS) + out_tail, BF16),
+        VMEM((PER_STAGE * LATE, PLANES, SPOTS) + up_tail, BF16),
+    ] + [VMEM((SPOTS * rows, D), BF16)] * LATE
+    parts = [
+        VMEM((1, PLANES) + out_tail, BF16),
+        VMEM((up_count, PLANES) + up_tail, BF16),
+        VMEM((STAGES, rows, D), BF16),
+        VMEM((PLANES - 1, 1) + out_tail, BF16),
+        VMEM((PLANES - 1, up_count) + up_tail, BF16),
+        VMEM((PLANES - 1, rows, D), BF16),
+    ]
     tile = (local, BLOCK, LANES)
     wide = VMEM((spans, 2 * BLOCK, SPAN * BLOCK), F32)
     thin = VMEM((spans, BLOCK, SPAN * BLOCK), F32)
     dma = pltpu.SemaphoreType.DMA
     return pl.pallas_call(
-        functools.partial(plane_attend_back_kernel, count),
+        plane_attend_back_kernel,
         out_shape=(
             jax.ShapeDtypeStruct((2, SPOTS, PIECES, 3) + tile, BF16),
             jax.ShapeDtypeStruct(hidden.shape, BF16),
-        )
-        + tuple(jax.ShapeDtypeStruct(source.shape[3:], F32) for source in sources),
+            jax.ShapeDtypeStruct(out_tail, F32),
+            jax.ShapeDtypeStruct((up_count,) + up_tail, F32),
+            jax.ShapeDtypeStruct((rows, D), F32),
+        ),
         in_specs=[
             whole(pltpu.SMEM),
             whole(pltpu.SMEM),
@@ -1467,9 +1540,11 @@
             whole(),
             whole(ANY),
         ]
-        + [whole(ANY)] * count,
-        out_specs=(whole(ANY), whole(ANY)) + (whole(),) * count,
+        + [whole(ANY)] * 5,
+        out_specs=(whole(ANY), whole(ANY)) + (whole(),) * 3,
         scratch_shapes=buffers
+        + mines
+        + parts
         + [
             VMEM((PLANES, SPOTS) + tile, BF16),
             VMEM((PLANES, SPOTS, 3) + tile, BF16),
@@ -1481,9 +1556,11 @@
             wide,
             thin,
             thin,
-            dma((count, REDUCE_SEMS)),
-            dma((count, REDUCE_SEMS)),
-            dma((count, 4)),
+            dma((count, SpotReduce.SEMS)),
+            dma((count, SpotReduce.SEMS)),
+            dma((3, PLANES - 1)),
+            dma((3, PLANES - 1)),
+            dma((count + 2,)),
         ]
         + exchange_sems((PLANES, SPOTS))
         + [
@@ -1500,7 +1577,7 @@
             vmem_limit_bytes=62 * 1024 * 1024, collective_id=5, has_side_effects=True
         ),
         name="plane_attention_back",
-    )(table, sorted_table, qk, shared, grad_source, lse, hidden, *sources)
+    )(table, sorted_table, qk, shared, grad_source, lse, hidden, *sources, half_up, half_down)
 
 
 class PlaneGather:
@@ -2249,6 +2326,135 @@
     )(x, dy, vec, tab, w_qkv, w_out, w_up, w_down)
 
 
+class SpotReduce:
+    SEMS = 4
+
+    def __init__(self, source, near, corner, sides, send_sem, recv_sem, rows=None, mine=None):
+        self.source, self.near, self.corner, self.side = source, near, corner, sides
+        self.send_sem, self.recv_sem, self.rows, self.mine = send_sem, recv_sem, rows, mine
+        self.core, self.plane, self.spot = place_here()
+        beside, beyond = flip(self.spot, 1), flip(self.spot, 2)
+        self.via = beyond * (1 - self.core) + beside * self.core
+        self.other = beside * (1 - self.core) + beyond * self.core
+
+    def half(self, core):
+        return self.source.at[core] if self.rows else self.source.at[:, core]
+
+    def part(self, spot):
+        if self.rows:
+            start = pl.multiple_of(spot * self.rows, 16)
+            return self.near.at[pl.ds(start, self.rows)]
+        return self.near.at[:, :, spot]
+
+    def copy(self, number):
+        sibling = (1 - self.core, rank_of(self.plane, self.spot))
+        if number == 0:
+            source, target, device = self.half(1 - self.core), self.near, sibling
+        elif number == 1:
+            source, target = self.part(flip(self.spot, 3)), self.corner
+            device = (self.core, rank_of(self.plane, self.via))
+        else:
+            spot = flip(self.spot, number - 1)
+            source, target = self.part(spot), self.side.at[number - 2]
+            device = (self.core, rank_of(self.plane, spot))
+        return remote(source, target, self.send_sem.at[number], self.recv_sem.at[number], device)
+
+    def start(self):
+        self.copy(0).start()
+
+    def add(self, spot, terms, target=None):
+        if self.rows:
+            rows = self.rows
+
+            def slab(number, carry):
+                size = rows // 3
+                first = pl.multiple_of(spot * rows + number * size, 16)
+                place = pl.ds(first, size)
+                inner = pl.ds(pl.multiple_of(number * size, 16), size)
+                total = self.near[place].astype(F32)
+                for read in terms:
+                    total = total + read(place, inner).astype(F32)
+                if target is None:
+                    self.near[place] = total.astype(BF16)
+                else:
+                    target[inner] = total.astype(BF16)
+                return carry
+
+            lax.fori_loop(0, 3, slab, 0)
+            return
+        count = self.near.shape[0]
+
+        def block(number, carry):
+            first, plane = lax.div(number, PLANES), lax.rem(number, PLANES)
+            total = self.near[first, plane, spot].astype(F32)
+            for read in terms:
+                total = total + read(first, plane).astype(F32)
+            if target is None:
+                self.near[first, plane, spot] = total.astype(BF16)
+            else:
+                target[first, plane] = total.astype(BF16)
+            return carry
+
+        lax.fori_loop(0, count * PLANES, block, 0)
+
+    def corners(self):
+        self.copy(0).wait_recv()
+        core = self.core
+        for spot in range(SPOTS):
+            if self.rows and self.mine is None:
+                self.add(spot, [lambda place, inner: self.source[core, place]])
+            elif self.rows:
+                self.add(spot, [lambda place, inner: self.mine[place]])
+            elif self.mine is None:
+                self.add(spot, [lambda first, plane, spot=spot: self.source[first, core, plane, spot]])
+            else:
+                self.add(spot, [lambda first, plane, spot=spot: self.mine[first, plane, spot]])
+        self.copy(1).start()
+
+    def sides(self):
+        self.copy(1).wait_recv()
+        if self.rows:
+            self.add(self.other, [lambda place, inner: self.corner[inner]])
+        else:
+            self.add(self.other, [lambda first, plane: self.corner[first, plane]])
+        self.copy(2).start()
+        self.copy(3).start()
+
+    def close(self, target):
+        self.copy(2).wait_recv()
+        self.copy(3).wait_recv()
+        if self.rows:
+            terms = [lambda place, inner, n=n: self.side[n, inner] for n in range(2)]
+        else:
+            terms = [lambda first, plane, n=n: self.side[n, first, plane] for n in range(2)]
+        self.add(self.spot, terms, target)
+        for number in range(self.SEMS):
+            self.copy(number).wait_send()
+
+
+def block_scratch(count, rows, width):
+    return [
+        VMEM((count, PLANES, SPOTS, rows, width), BF16),
+        VMEM((count, PLANES, rows, width), BF16),
+        VMEM((2, count, PLANES, rows, width), BF16),
+    ]
+
+
+def row_scratch(rows, width):
+    return [
+        VMEM((SPOTS * rows, width), BF16),
+        VMEM((rows, width), BF16),
+        VMEM((2, rows, width), BF16),
+    ]
+
+
+STAGES = 4
+PER_STAGE = FF // CHUNK // STAGES
+EARLY = 2
+LATE = STAGES - EARLY
+WAITS = (2, 4, 6)
+
+
 def by_owner(out_ref, values):
     rows = D // RANKS
     width = values.shape[1] // 2
@@ -2270,8 +2476,10 @@
     send_ref,
     dres_ref,
     g_out_ref,
-    g_up_ref,
-    g_down_ref,
+    half_up_ref,
+    half_down_ref,
+    last_up_ref,
+    last_down_ref,
     g_up_bias_ref,
     g_small_ref,
     mixed_ref,
@@ -2280,7 +2488,31 @@
     second_t_ref,
     total_ref,
     dsecond_ref,
+    g_up_ref,
+    g_down_ref,
+    *scratch,
 ):
+    send_sem, recv_sem, local_sem = scratch[-3:]
+    stages = []
+    for number in range(EARLY):
+        buffers = scratch[6 * number : 6 * number + 6]
+        stages.append(
+            (
+                SpotReduce(
+                    g_up_ref.at[PER_STAGE * number : PER_STAGE * (number + 1)],
+                    *buffers[:3],
+                    send_sem.at[number, 0],
+                    recv_sem.at[number, 0],
+                ),
+                SpotReduce(
+                    g_down_ref.at[number],
+                    *buffers[3:],
+                    send_sem.at[number, 1],
+                    recv_sem.at[number, 1],
+                    rows=FF // RANKS,
+                ),
+            )
+        )
     pieces, rows, _ = x_ref.shape
     tokens = pieces * rows
     step = pl.program_id(0)
@@ -2289,7 +2521,14 @@
 
     @pl.when(step == 0)
     def _():
-        core = lax.axis_index("gx")
+        core, plane, spot = place_here()
+        greet(
+            [
+                (1 - core, rank_of(plane, spot)),
+                (core, rank_of(plane, flip(spot, 1))),
+                (core, rank_of(plane, flip(spot, 2))),
+            ]
+        )
         for piece in range(pieces):
             span = slice(piece * rows, (piece + 1) * rows)
             for spot in (0, 2):
@@ -2328,14 +2567,58 @@
     )
     dy = dy_ref[...]
     total_ref[...] += dot(active, w_down)
-    g_down_ref[...] = dot_lt(active, dy).astype(BF16).reshape(g_down_ref.shape)
+    stage, turn = lax.div(step, PER_STAGE), lax.rem(step, PER_STAGE)
+    down_share = dot_lt(active, dy).astype(BF16)
+    place = pl.ds(pl.multiple_of(turn * LANES, LANES), LANES)
+    for side in range(2):
+        g_down_ref[stage, side, place] = down_share[side * LANES : (side + 1) * LANES]
     dupper = (dot_rt(dy, w_down) * slope).astype(BF16)
     g_up_bias_ref[0] = jnp.sum(dupper.astype(F32), axis=0, keepdims=True)
-    by_owner(g_up_ref, dot(second_t_ref[...], dupper))
+    up_share = dot(second_t_ref[...], dupper)
+    shard = D // RANKS
+    for owner in range(RANKS):
+        part = up_share[owner * shard : (owner + 1) * shard]
+        g_up_ref[step, owner // (PLANES * SPOTS), owner // SPOTS % PLANES, owner % SPOTS] = (
+            jnp.concatenate([part[:, :LANES], part[:, LANES:]], axis=0).astype(BF16)
+        )
     dsecond_ref[...] += dot_rt(dupper, w_up_ref[...])
 
-    @pl.when(step == pl.num_programs(0) - 1)
+    last = FF // CHUNK - 1
+    for number, pair in enumerate(stages):
+        done = PER_STAGE * (number + 1) - 1
+
+        @pl.when(step == done)
+        def _(pair=pair):
+            for one in pair:
+                one.start()
+
+        @pl.when(step == done + WAITS[0])
+        def _(pair=pair):
+            for one in pair:
+                one.corners()
+
+        @pl.when(step == done + WAITS[1])
+        def _(pair=pair):
+            for one in pair:
+                one.sides()
+
+        if done + WAITS[2] < last:
+
+            @pl.when(step == done + WAITS[2])
+            def _(pair=pair, number=number):
+                pair[0].close(half_up_ref.at[PER_STAGE * number : PER_STAGE * (number + 1)])
+                pair[1].close(half_down_ref.at[number])
+
+    @pl.when(step == last)
     def _():
+        keep_up = pltpu.make_async_copy(
+            g_up_ref.at[PER_STAGE * EARLY : PER_STAGE * STAGES], last_up_ref, local_sem.at[0]
+        )
+        keep_up.start()
+        keep_down = pltpu.make_async_copy(
+            g_down_ref.at[EARLY:STAGES], last_down_ref, local_sem.at[1]
+        )
+        keep_down.start()
         residual = residual_ref[...]
         hidden_ref[...] = (
             (residual + (total_ref[...] + down_shift)).astype(BF16).reshape(x_ref.shape)
@@ -2364,6 +2647,12 @@
                 send_ref[1, spot, piece] = jnp.where(low, tiles[1], tiles[0]).astype(BF16)
                 send_ref[0, spot + 1, piece] = jnp.where(low, flipped[2], tiles[1]).astype(BF16)
                 send_ref[1, spot + 1, piece] = flipped[2].astype(BF16)
+        for number, pair in enumerate(stages):
+            if PER_STAGE * (number + 1) - 1 + WAITS[2] >= last:
+                pair[0].close(half_up_ref.at[PER_STAGE * number : PER_STAGE * (number + 1)])
+                pair[1].close(half_down_ref.at[number])
+        keep_up.wait()
+        keep_down.wait()
 
 
 def plane_middle(mixed_in, x, dy, vec, w_out, up_shift, w_up, w_down):
@@ -2375,6 +2664,13 @@
         return pl.BlockSpec(shape, lambda step: (0,) * len(shape))
 
     steps = FF // CHUNK
+    grid = (2, PLANES, SPOTS)
+    down_rows = FF // RANKS
+    half_up = (PER_STAGE * EARLY, PLANES, 2 * shard, LANES)
+    half_down = (EARLY, down_rows, D)
+    buffers = []
+    for _ in range(EARLY):
+        buffers += block_scratch(PER_STAGE, 2 * shard, LANES) + row_scratch(down_rows, D)
     down = pl.BlockSpec((2, LANES, D), lambda step: (0, step, 0))
     return pl.pallas_call(
         plane_middle_kernel,
@@ -2384,8 +2680,10 @@
             jax.ShapeDtypeStruct(mixed_in.shape, BF16),
             jax.ShapeDtypeStruct((tokens, D), F32),
             jax.ShapeDtypeStruct((RANKS, 2 * shard, D // 2), BF16),
-            jax.ShapeDtypeStruct((RANKS, 2 * shard, FF // 2), BF16),
-            jax.ShapeDtypeStruct((2, FF // 2, D), BF16),
+            jax.ShapeDtypeStruct(half_up, BF16),
+            jax.ShapeDtypeStruct(half_down, BF16),
+            jax.ShapeDtypeStruct((PER_STAGE * LATE,) + grid + (2 * shard, LANES), BF16),
+            jax.ShapeDtypeStruct((LATE, 2, FF // 2 // STAGES, D), BF16),
             jax.ShapeDtypeStruct((steps, 1, CHUNK), F32),
             jax.ShapeDtypeStruct((4, D), F32),
         ),
@@ -2404,8 +2702,10 @@
             fixed(mixed_in.shape),
             fixed((tokens, D)),
             fixed((RANKS, 2 * shard, D // 2)),
-            pl.BlockSpec((RANKS, 2 * shard, LANES), lambda step: (0, 0, step)),
-            down,
+            fixed(half_up),
+            fixed(half_down),
+            whole(ANY),
+            whole(ANY),
             pl.BlockSpec((1, 1, CHUNK), lambda step: (step, 0, 0)),
             fixed((4, D)),
         ),
@@ -2416,8 +2716,18 @@
             VMEM((D, tokens), BF16),
             VMEM((tokens, D), F32),
             VMEM((tokens, D), F32),
+            VMEM((steps,) + grid + (2 * shard, LANES), BF16),
+            VMEM((STAGES, 2, FF // 2 // STAGES, D), BF16),
+        ]
+        + buffers
+        + [
+            pltpu.SemaphoreType.DMA((EARLY, 2, SpotReduce.SEMS)),
+            pltpu.SemaphoreType.DMA((EARLY, 2, SpotReduce.SEMS)),
+            pltpu.SemaphoreType.DMA((2,)),
         ],
-        compiler_params=params_of(56),
+        compiler_params=pltpu.CompilerParams(
+            vmem_limit_bytes=60 * 1024 * 1024, collective_id=3, has_side_effects=True
+        ),
         name="plane_middle",
     )(mixed_in, x, dy, vec, w_out, up_shift, w_up, w_down)
 
@@ -2878,7 +3188,18 @@
         sorted_table,
     ) = front(hidden_in, cotangent, vec, tab, w_qkv, w_out, w_up, w_down)
     mixed = mixed.reshape(2, SPOTS, PIECES, rows, LANES)
-    hidden, grad_send, dres, g_out, g_up, g_down, g_up_bias, g_mid = plane_middle(
+    (
+        hidden,
+        grad_send,
+        dres,
+        g_out,
+        half_up,
+        half_down,
+        last_up,
+        last_down,
+        g_up_bias,
+        g_mid,
+    ) = plane_middle(
         mixed,
         x,
         dy.reshape(micro * rows, D),
@@ -2898,11 +3219,14 @@
         lse,
         hidden,
         [
-            g_out.reshape(grid + g_out.shape[1:]),
-            g_up.reshape(grid + g_up.shape[1:]),
-            g_down.reshape(grid + (FF // RANKS, D)),
+            g_out.reshape((1,) + grid + g_out.shape[1:]),
+            last_up,
+            last_down,
         ],
+        half_up,
+        half_down,
     )
+    t_up = t_up.swapaxes(0, 1).reshape(2 * own, FF // 2)
     dqkv = dqkv.reshape(2, SPOTS, PIECES, 3, rows, LANES)
     grad_hidden, t_qkv, sum_rows, sum_tiles = finish_layer(
         dqkv, normed, x, dres, vectors, w_qkv_all, g_mid, g_up_bias

time: 325 us -> 314 us (0.966)
  Pallas kernels: 307 us -> 297 us
    pallas_call x1, Pallas kernels: 101 us -> 82 us  [plane_attention_back(): pl.pallas_call(plane_attend_back_kernel, out_shape=(jax.ShapeDtypeStruct(...]
    pallas_call x1, Pallas kernels: 35.9 us -> 44.3 us  [plane_middle(): pl.pallas_call(plane_middle_kernel, grid=(steps,), out_shape=(jax.ShapeDt...]
where the time goes in v8:
time: 314 us; the launch traced here: 313 us
  Pallas kernels  297 us (95%)
  local copies, waits for them, and re-layouts  10 us (3%)
  other arithmetic  5.78 us (2%)
    pallas_call x1, Pallas kernels, front(): pl.pallas_call(front_kernel, out_shape=(struct((2, SPOTS, PIECES) + tile,...  130 us
    pallas_call x1, Pallas kernels, plane_attention_back(): pl.pallas_call(plane_attend_back_kernel, out_shape=(jax.ShapeDtypeStruct(...  82 us
    pallas_call x1, Pallas kernels, plane_middle(): pl.pallas_call(plane_middle_kernel, grid=(steps,), out_shape=(jax.ShapeDt...  44.3 us
    pallas_call x1, Pallas kernels, finish_layer(): pl.pallas_call(finish_kernel, out_shape=(jax.ShapeDtypeStruct(x.shape, BF...  40.4 us

profile of v8, /device:TPU:0, one launch (start us, length us, event | category | flops | bytes accessed | tf_op | source)
XLA Modules:
  0.0 313.3 jit_solution(5129331951938847324)
XLA Ops:
  0.6 0.8 copy.33
  1.4 0.1 reshape.63
  1.5 0.6 pad.49.tab_ref
  2.1 1.4 pad_add_fusion.vec_ref
  3.5 130.1 %front.1 = (bf16[2,4,2,4,64,128]{5,4,3,2,1,0:T(8,128)(2,1)}, bf16[2,256,768]{2,1,0:T(8,128)(2,1)}, bf16[2,256,768]{2,1,0:T(8,128)(2,1)}, bf16[2,4,4,96,768]{4,3,...) custom-call(bf16[2,256,768]{2,1,0:T(8,128)(2,1)} %x_in_ref.1, ...), custom_call_target="tpu_custom_call" | custom-call | tf_op jit(solution)/shard_map/front/pallas_call | solution.py:2249
  133.6 44.3 %plane_middle.1 = (bf16[2,256,768]{2,1,0:T(8,128)(2,1)}, bf16[2,4,2,256,128]{4,3,2,1,0:T(8,128)(2,1)}, f32[512,768]{1,0:T(8,128)}, bf16[32,48,384]{2,1,0:T(8,128...) custom-call(bf16[2,4,2,256,128]{4,3,2,1,0:T(8,128)(2,1)} %bitcast.49, ...), custom_call_target="tpu_custom_call" | custom-call | tf_op jit(solution)/shard_map/plane_middle/pallas_call | solution.py:2675
  177.9 82.0 %plane_attention_back.1 = (bf16[2,4,2,3,4,64,128]{6,5,4,3,2,1,0:T(8,128)(2,1)}, bf16[2,256,768]{2,1,0:T(8,128)(2,1)}, f32[48,384]{1,0:T(8,128)}, f32[12,48,128]{2,1,0:T(8,128)}, f32[96,768]{1,0:T(8,128)}) custom-call(s32[1,256]{1,0:T(1,128)} %get-tuple-element.49.refs_0_, s32[4,256]{1,0:T(4,128)} %get-tuple-element.50.refs_1_, ...), custom_call_target="tpu_custom_call" | custom-call | tf_op jit(solution)/shard_map/plane_attention_back/pallas_call | solution.py:1525
  259.9 1.0 slice_bitcast_fusion.1
  260.9 0.7 pad_maximum_fusion
  261.6 0.8 fusion.5
  262.4 0.6 pad_maximum_fusion.1
  263.1 40.4 %finish_layer.1 = (bf16[2,256,768]{2,1,0:T(8,128)(2,1)}, f32[48,1152]{1,0:T(8,128)}, f32[8,768]{1,0:T(8,128)}, f32[24,256]{1,0:T(8,128)}) custom-call(bf16[2,4,2,3,256,128]{5,4,3,2,1,0:T(8,128)(2,1)} %bitcast.47, bf16[512,768]{1,0:T(8,128)(2,1)} %get-tuple-element.71.normed_ref, bf16[2,256,768]{2,1,0:T(8,128)(2,1)} %get-tuple-element.54.x_ref, ...), custom_call_target="tpu_custom_call" | custom-call | tf_op jit(solution)/shard_map/finish_layer/pallas_call | solution.py:3066
  303.5 0.0 copy-start.1
  303.5 0.0 copy-start.3
  303.5 0.0 copy-start
  303.5 1.1 fusion.4
  304.6 1.0 fusion.2
  305.6 1.0 fusion.3
  306.6 0.0 copy-start.2
  306.6 0.8 concatenate.25
  307.4 0.7 slice.214
  308.2 0.1 fusion.7
  308.2 0.1 fusion.6
  308.3 0.1 concatenate.22
  308.4 0.1 concatenate.21
  308.5 0.8 fusion.1
  309.3 0.5 slice_bitcast_fusion.2
  309.8 0.0 copy-done.1
  309.8 1.3 convert_element_type.21
  311.1 0.0 copy-done.3
  311.1 0.6 dynamic_slice.7
  311.7 0.0 copy-done
  311.7 0.9 copy.48
  312.6 0.0 copy-done.2
  312.6 0.7 copy.49
  (8 shorter events, 0.1 us)
Async XLA Ops:
  303.5 6.3 %copy-start.1 = (bf16[2,256,768]{2,1,0:T(8,128)(2,1)S(1)}, bf16[2,256,768]{2,1,0:T(8,128)(2,1)}, u32[]{:S(2)}) copy-start(bf16[2,256,768]{2,1,0:T(8,128)(2,1)} %get-tuple-element.76) | copy-start | bytes 2359300
  303.5 7.6 %copy-start.3 = (f32[24,256]{1,0:T(8,128)S(1)}, f32[24,256]{1,0:T(8,128)}, u32[]{:S(2)}) copy-start(f32[24,256]{1,0:T(8,128)} %get-tuple-element.78) | copy-start | bytes 73732
  303.5 8.2 %copy-start = (bf16[2,256,768]{2,1,0:T(8,128)(2,1)S(1)}, bf16[2,256,768]{2,1,0:T(8,128)(2,1)}, u32[]{:S(2)}) copy-start(bf16[2,256,768]{2,1,0:T(8,128)(2,1)} %get-tuple-element.157) | copy-start | bytes 2359300
  306.6 6.0 %copy-start.2 = (f32[96,768]{1,0:T(8,128)S(1)}, f32[96,768]{1,0:T(8,128)}, u32[]{:S(2)}) copy-start(f32[96,768]{1,0:T(8,128)} %get-tuple-element.170) | copy-start | bytes 884740

commit v9 on v8

--- a/solution.py
+++ b/solution.py
@@ -758,18 +758,6 @@
     return "qkv".index(entry[0]) * HEADS + entry[1]
 
 
-def take_blocks(array, order):
-    parts = []
-    start = 0
-    while start < len(order):
-        stop = start + 1
-        while stop < len(order) and order[stop] == order[stop - 1] + 1:
-            stop += 1
-        parts.append(array[..., order[start] * HEAD_DIM : (order[start] + stop - start) * HEAD_DIM])
-        start = stop
-    return jnp.concatenate(parts, axis=-1)
-
-
 def flip(value, bits):
     if bits == 0:
         return value
@@ -1229,6 +1217,30 @@
         one.start()
     for copy in loads:
         copy.start()
+
+    def far(bits, number, source, target):
+        return remote(
+            source,
+            target,
+            far_send.at[number, bits - 1],
+            far_recv.at[number, bits - 1],
+            (core, rank_of(flip(plane, bits), spot)),
+        )
+
+    def far_down(bits, source):
+        return far(bits, 3, source, far_down_ref.at[bits - 1])
+
+    fars = []
+    for bits in range(1, PLANES):
+        goal = flip(plane, bits)
+        copy = far(bits, 0, half_up_ref.at[:, goal], far_up_ref.at[bits - 1, 0:ready])
+        copy.start()
+        fars.append(copy)
+
+        @pl.when(goal < EARLY)
+        def _(bits=bits, goal=goal):
+            far_down(bits, half_down_ref.at[jnp.minimum(goal, EARLY - 1)]).start()
+
     finish_hidden = from_planes(hidden_ref, hidden_out_ref, *move_sems)
 
     def load(component, block):
@@ -1413,25 +1425,21 @@
     reduces[1].close(part_up_ref.at[ready : PER_STAGE * STAGES])
     for number in range(LATE):
         reduces[2 + number].close(part_down_ref.at[EARLY + number])
-    fars = []
     for bits in range(1, PLANES):
         goal = flip(plane, bits)
-        for number, (source, target) in enumerate(
-            (
-                (part_out_ref.at[:, goal], far_out_ref),
-                (part_up_ref.at[:, goal], far_up_ref),
-                (part_down_ref.at[goal], far_down_ref),
-            )
+        late = slice(ready, PER_STAGE * STAGES)
+        for copy in (
+            far(bits, 1, part_out_ref.at[:, goal], far_out_ref.at[bits - 1]),
+            far(bits, 2, part_up_ref.at[late, goal], far_up_ref.at[bits - 1, late]),
         ):
-            copy = remote(
-                source,
-                target.at[bits - 1],
-                far_send.at[number, bits - 1],
-                far_recv.at[number, bits - 1],
-                (core, rank_of(goal, spot)),
-            )
             copy.start()
             fars.append(copy)
+
+        @pl.when(goal >= EARLY)
+        def _(bits=bits, goal=goal):
+            far_down(bits, part_down_ref.at[goal]).start()
+
+        fars.append(far_down(bits, part_down_ref.at[goal]))
     walk(0, blocks * RANDOM)
     for side, other, goal, stays in inward_targets(core, spot):
         for piece in range(PIECES):
@@ -1558,8 +1566,8 @@
             thin,
             dma((count, SpotReduce.SEMS)),
             dma((count, SpotReduce.SEMS)),
-            dma((3, PLANES - 1)),
-            dma((3, PLANES - 1)),
+            dma((4, PLANES - 1)),
+            dma((4, PLANES - 1)),
             dma((count + 2,)),
         ]
         + exchange_sems((PLANES, SPOTS))
@@ -1931,7 +1939,6 @@
     )
     pl.semaphore_wait(barrier, len(partners))
 
-    finish_x = to_planes(x_in_ref, xs_ref, *x_sems)
     gathers = []
     for number, (source, target) in enumerate(
         ((tab_ref, tabs_ref), (vec_ref, vecs_ref), (s_qkv_ref, g_qkv_ref))
@@ -1946,25 +1953,19 @@
     fold_tiles(s_ou_ref, outs, list(range(FF // LANES)), natural(w_up_in_ref))
     for one in gathers:
         one.column()
+    finish_x = to_planes(x_in_ref, xs_ref, *x_sems)
     cross = CrossGather(w_down_in_ref, w_down_ref, *cross_sems)
     for one in gathers:
         one.across()
     for one in gathers:
         one.corner()
     cross.across()
-    finish_x()
-    spread = PlaneGather(s_ou_ref, g_ou_ref, *plane_sems)
-    keep_x = pltpu.make_async_copy(xs_ref, x_ref, local_sem.at[0])
-    keep_x.start()
-    normal, _ = norm_parts(xs_ref[...].reshape(tokens, D).astype(F32))
     for one in gathers[:2]:
         one.finish()
-
     window_core, window_micro = lax.rem(plane, 2), lax.div(plane, 2)
     scalars = pltpu.make_async_copy(tabs_ref.at[window_core], picks_ref, local_sem.at[1])
     scalars.start()
     lay_vectors(vecs_ref, vectors_ref, up_ref)
-    normed_ref[...] = (normal * vectors_ref[0:1] + vectors_ref[1:2]).astype(BF16)
     for tile in range(TILES):
         halves = []
         for entry in column_order()[2 * tile : 2 * tile + 2]:
@@ -1987,6 +1988,13 @@
     settle(g_qkv_ref, [(tile, w_qkv_ref, alternate(tile)) for tile in range(HALF_TILES)])
     keep_w = pltpu.make_async_copy(w_qkv_ref, w_qkv_hbm, local_sem.at[2])
     keep_w.start()
+
+    finish_x()
+    spread = PlaneGather(s_ou_ref, g_ou_ref, *plane_sems)
+    keep_x = pltpu.make_async_copy(xs_ref, x_ref, local_sem.at[0])
+    keep_x.start()
+    normal, _ = norm_parts(xs_ref[...].reshape(tokens, D).astype(F32))
+    normed_ref[...] = (normal * vectors_ref[0:1] + vectors_ref[1:2]).astype(BF16)
 
     def shaped(value):
         return value.astype(BF16).reshape(local, BLOCK, LANES)
@@ -3111,14 +3119,135 @@
     )(recv, normed, x, dres, vec, w, g_mid, g_up_bias)
 
 
-def fold_columns(array):
-    half = array.shape[1] // 2
-    return jnp.concatenate([array[:, :half], array[:, half:]], axis=0)
-
-
-def unfold_columns(array):
-    half = array.shape[0] // 2
-    return jnp.concatenate([array[:half], array[half:]], axis=1)
+def present_kernel(
+    hidden_hbm,
+    grad_hbm,
+    t_qkv_hbm,
+    t_out_hbm,
+    t_up_hbm,
+    t_down_hbm,
+    rows_hbm,
+    tiles_hbm,
+    hidden_out_ref,
+    grad_out_ref,
+    g_qkv_ref,
+    g_out_ref,
+    g_up_ref,
+    g_down_ref,
+    *outs,
+):
+    singles, (grad_ref, t_qkv_ref, t_out_ref, t_up_ref, rows_ref, tiles_ref, copy_sem) = (
+        outs[:-7],
+        outs[-7:],
+    )
+    loads = [
+        pltpu.make_async_copy(source, target, copy_sem.at[number])
+        for number, (source, target) in enumerate(
+            (
+                (rows_hbm, rows_ref),
+                (tiles_hbm, tiles_ref),
+                (t_qkv_hbm, t_qkv_ref),
+                (t_out_hbm, t_out_ref),
+                (t_up_hbm, t_up_ref),
+                (grad_hbm, grad_ref),
+                (t_down_hbm, g_down_ref),
+                (hidden_hbm, hidden_out_ref),
+            )
+        )
+    ]
+    for copy in loads:
+        copy.start()
+    core, plane, spot = place_here()
+    mine = core * (PLANES * SPOTS) + rank_of(plane, spot)
+    own, wide = D // RANKS, FF // RANKS
+    order = [natural_block(entry) for entry in column_order()]
+    inverse = [order.index(number) for number in range(len(order))]
+
+    for copy in loads[:5]:
+        copy.wait()
+    half = D // 2
+    for side in range(2):
+        rows = slice(side * own, (side + 1) * own)
+        g_out_ref[:, side * half : (side + 1) * half] = t_out_ref[rows]
+        for chunk in range(FF // CHUNK):
+            start = side * (FF // 2) + chunk * LANES
+            g_up_ref[:, start : start + LANES] = t_up_ref[chunk, rows]
+
+    def folded(tile):
+        side, chunk = tile // HALF_TILES, tile % HALF_TILES
+        return t_qkv_ref[
+            side * own : (side + 1) * own, chunk * LANES : (chunk + 1) * LANES
+        ]
+
+    def bias_sum(tile):
+        side, chunk = tile // HALF_TILES, tile % HALF_TILES
+        row = FF // CHUNK + chunk
+        return tiles_ref[row : row + 1, side * LANES : (side + 1) * LANES]
+
+    biases = []
+    for tile in range(TILES):
+        blocks = inverse[2 * tile], inverse[2 * tile + 1]
+        g_qkv_ref[:, tile * LANES : (tile + 1) * LANES] = pair_of_blocks(folded, *blocks)
+        biases.append(pair_of_blocks(bias_sum, *blocks))
+    third = TILES // 3
+    query = jnp.concatenate(biases[:third], axis=1)
+    value = jnp.concatenate(biases[2 * third :], axis=1)
+    vectors = jnp.concatenate([rows_ref[0:6], query, value], axis=0)
+
+    def pick(values, first, wanted):
+        place = lax.broadcasted_iota(jnp.int32, (values.shape[1], LANES), 0) + first
+        lane = lax.broadcasted_iota(jnp.int32, (values.shape[1], LANES), 1)
+        one_hot = jnp.where(place == mine * wanted + lane, 1.0, 0.0)
+        return lax.dot_general(
+            values,
+            one_hot,
+            (((1,), (0,)), ((), ())),
+            precision=lax.Precision.HIGHEST,
+            preferred_element_type=F32,
+        )
+
+    picked = pick(vectors, 0, own)
+    for number in range(VECTORS):
+        singles[number][...] = picked[number : number + 1, :own]
+    total = jnp.zeros((1, LANES), F32)
+    for chunk in range(FF // CHUNK):
+        for side in range(2):
+            total = total + pick(
+                tiles_ref[chunk : chunk + 1, side * LANES : (side + 1) * LANES],
+                side * (FF // 2) + chunk * LANES,
+                wide,
+            )
+    singles[VECTORS][...] = total[:, :wide]
+    loads[5].wait()
+    grad_out_ref[...] = grad_ref[...].astype(F32)
+    for copy in loads[6:]:
+        copy.wait()
+
+
+def present(hidden, grad, t_qkv, t_out, t_up, t_down, rows, tiles):
+    own, wide = D // RANKS, FF // RANKS
+    struct = jax.ShapeDtypeStruct
+    return pl.pallas_call(
+        present_kernel,
+        out_shape=(
+            struct(hidden.shape, BF16),
+            struct(grad.shape, F32),
+            struct((own, 3 * D), F32),
+            struct((own, D), F32),
+            struct((own, FF), F32),
+            struct((wide, D), F32),
+        )
+        + (struct((1, own), F32),) * VECTORS
+        + (struct((1, wide), F32),),
+        in_specs=[whole(ANY)] * 8,
+        out_specs=(whole(),) * (7 + VECTORS),
+        scratch_shapes=[
+            VMEM(item.shape, item.dtype) for item in (grad, t_qkv, t_out, t_up, rows, tiles)
+        ]
+        + [pltpu.SemaphoreType.DMA((8,))],
+        compiler_params=params_of(63),
+        name="present",
+    )(hidden, grad, t_qkv, t_out, t_up, t_down, rows, tiles)
 
 
 def plane_shards(
@@ -3141,9 +3270,6 @@
 ):
     micro, rows, _ = hidden_in.shape
     local = rows // BLOCK
-    own = norm1_gain.shape[0]
-    order = [natural_block(entry) for entry in column_order()]
-    inverse = [order.index(number) for number in range(len(order))]
 
     def in_row(vector, number):
         return jnp.pad(vector[None], ((number, 15 - number), (0, LANES - vector.shape[0])))
@@ -3226,36 +3352,30 @@
         half_up,
         half_down,
     )
-    t_up = t_up.swapaxes(0, 1).reshape(2 * own, FF // 2)
     dqkv = dqkv.reshape(2, SPOTS, PIECES, 3, rows, LANES)
     grad_hidden, t_qkv, sum_rows, sum_tiles = finish_layer(
         dqkv, normed, x, dres, vectors, w_qkv_all, g_mid, g_up_bias
     )
 
-    mine = lax.axis_index("gx") * PLANES * SPOTS + lax.axis_index("gy")
-    sum_tiles = sum_tiles.reshape(-1, 2, LANES)
-    g_bias = sum_tiles[FF // CHUNK : FF // CHUNK + HALF_TILES].swapaxes(0, 1).reshape(1, 3 * D)
-    g_bias = take_blocks(g_bias, inverse)
-    sum_rows = jnp.concatenate([sum_rows, g_bias[:, :D], g_bias[:, 2 * D :]], axis=0)
-    parts = lax.dynamic_slice_in_dim(sum_rows, mine * own, own, 1)
-    g_up_bias = sum_tiles[: FF // CHUNK].swapaxes(0, 1).reshape(FF)
-    g_up_bias = lax.dynamic_slice_in_dim(g_up_bias, mine * (FF // RANKS), FF // RANKS, 0)
+    results = present(hidden_out, grad_hidden, t_qkv, t_out, t_up, t_down, sum_rows, sum_tiles)
+    hidden_out, grad_hidden, g_qkv, g_out, g_up, g_down = results[:6]
+    n1g, n1b, n2g, n2b, db, ob, qb, vb, ub = (item.reshape(item.size) for item in results[6:])
     return (
         hidden_out,
-        grad_hidden.astype(F32),
-        parts[0],
-        parts[1],
-        take_blocks(unfold_columns(t_qkv), inverse),
-        parts[8],
-        parts[9],
-        unfold_columns(t_out),
-        parts[5],
-        parts[2],
-        parts[3],
-        unfold_columns(t_up),
-        g_up_bias,
-        t_down,
-        parts[4],
+        grad_hidden,
+        n1g,
+        n1b,
+        g_qkv,
+        qb,
+        vb,
+        g_out,
+        ob,
+        n2g,
+        n2b,
+        g_up,
+        ub,
+        g_down,
+        db,
     )
 
 

time: 314 us -> 299 us (0.952)
  local copies, waits for them, and re-layouts: 10 us -> 1.46 us
  other arithmetic: 5.78 us -> 1.39 us
    pallas_call x1, Pallas kernels: 130 us -> 121 us  [front(): pl.pallas_call(front_kernel, out_shape=(struct((2, SPOTS, PIECES) + tile,...]
    pallas_call x0 -> x1, Pallas kernels: none -> 4.65 us  [present(): pl.pallas_call(present_kernel, out_shape=(struct(hidden.shape, BF16), str...]
    slice x12 -> x0, local copies, waits for them, and re-layouts: 3.78 us -> none  [the longest x3 1.89 us: unfold_columns(): return jnp.concatenate([array[:half], array[half:]], axis=1)]
where the time goes in v9:
time: 299 us
  Pallas kernels  295 us (99%)
    pallas_call x1, Pallas kernels, front(): pl.pallas_call(front_kernel, out_shape=(struct((2, SPOTS, PIECES) + tile,...  121 us
    pallas_call x1, Pallas kernels, plane_attention_back(): pl.pallas_call(plane_attend_back_kernel, out_shape=(jax.ShapeDtypeStruct(...  83.5 us
    pallas_call x1, Pallas kernels, plane_middle(): pl.pallas_call(plane_middle_kernel, grid=(steps,), out_shape=(jax.ShapeDt...  44.9 us
    pallas_call x1, Pallas kernels, finish_layer(): pl.pallas_call(finish_kernel, out_shape=(jax.ShapeDtypeStruct(x.shape, BF...  40.6 us

profile of v9, /device:TPU:0, one launch (start us, length us, event | category | flops | bytes accessed | tf_op | source)
XLA Modules:
  0.0 298.6 jit_solution(14538242514315480142)
XLA Ops:
  0.6 0.8 copy.32
  1.4 0.1 reshape.78
  1.5 0.6 pad.49.tab_ref
  2.1 1.4 pad_add_fusion.vec_ref
  3.5 121.3 %front.1 = (bf16[2,4,2,4,64,128]{5,4,3,2,1,0:T(8,128)(2,1)}, bf16[2,256,768]{2,1,0:T(8,128)(2,1)}, bf16[2,256,768]{2,1,0:T(8,128)(2,1)}, bf16[2,4,4,96,768]{4,3,...) custom-call(bf16[2,256,768]{2,1,0:T(8,128)(2,1)} %x_in_ref.1, ...), custom_call_target="tpu_custom_call" | custom-call | tf_op jit(solution)/shard_map/front/pallas_call | solution.py:2257
  124.8 44.9 %plane_middle.1 = (bf16[2,256,768]{2,1,0:T(8,128)(2,1)}, bf16[2,4,2,256,128]{4,3,2,1,0:T(8,128)(2,1)}, f32[512,768]{1,0:T(8,128)}, bf16[32,48,384]{2,1,0:T(8,128...) custom-call(bf16[2,4,2,256,128]{4,3,2,1,0:T(8,128)(2,1)} %bitcast.27, ...), custom_call_target="tpu_custom_call" | custom-call | tf_op jit(solution)/shard_map/plane_middle/pallas_call | solution.py:2683
  169.7 83.5 %plane_attention_back.1 = (bf16[2,4,2,3,4,64,128]{6,5,4,3,2,1,0:T(8,128)(2,1)}, bf16[2,256,768]{2,1,0:T(8,128)(2,1)}, f32[48,384]{1,0:T(8,128)}, f32[12,48,128]{2,1,0:T(8,128)}, f32[96,768]{1,0:T(8,128)}) custom-call(s32[1,256]{1,0:T(1,128)} %get-tuple-element.64.refs_0_, s32[4,256]{1,0:T(4,128)} %get-tuple-element.65.refs_1_, ...), custom_call_target="tpu_custom_call" | custom-call | tf_op jit(solution)/shard_map/plane_attention_back/pallas_call | solution.py:1533
  253.2 40.6 %finish_layer.1 = (bf16[2,256,768]{2,1,0:T(8,128)(2,1)}, f32[48,1152]{1,0:T(8,128)}, f32[8,768]{1,0:T(8,128)}, f32[24,256]{1,0:T(8,128)}) custom-call(bf16[2,4,2,3,256,128]{5,4,3,2,1,0:T(8,128)(2,1)} %bitcast.25, bf16[512,768]{1,0:T(8,128)(2,1)} %get-tuple-element.86.normed_ref, bf16[2,256,768]{2,1,0:T(8,128)(2,1)} %get-tuple-element.69.x_ref, ...), custom_call_target="tpu_custom_call" | custom-call | tf_op jit(solution)/shard_map/finish_layer/pallas_call | solution.py:3074
  293.8 4.6 %present.1 = (bf16[2,256,768]{2,1,0:T(8,128)(2,1)}, f32[2,256,768]{2,1,0:T(8,128)}, f32[24,2304]{1,0:T(8,128)}, f32[24,768]{1,0:T(8,128)}, f32[24,3072]{1,0:T(8,...) custom-call(bf16[2,256,768]{2,1,0:T(8,128)(2,1)} %get-tuple-element., ...), custom_call_target="tpu_custom_call" | custom-call | tf_op jit(solution)/shard_map/present/pallas_call | solution.py:3230

commit v10 on v9

--- a/solution.py
+++ b/solution.py
@@ -865,11 +865,12 @@
     return finish
 
 
-def from_planes(source, target, send_sem, recv_sem, local_sem):
+def from_planes(source, target, send_sem, recv_sem, local_sem, later=False):
     core, plane, spot = place_here()
     micro, odd = lax.div(plane, 2), lax.rem(plane, 2)
     sends, keeps = [], []
-    for piece in range(PIECES):
+
+    def start(piece):
         goal = 2 * core + piece
         here = (goal == plane) & (odd == core)
         send = remote(
@@ -891,6 +892,9 @@
 
         sends.append((here, send))
         keeps.append((here, keep))
+
+    for piece in () if later else range(PIECES):
+        start(piece)
 
     def finish():
         for number in range(2):
@@ -917,7 +921,7 @@
             def _(keep=keep):
                 keep.wait()
 
-    return finish
+    return (start, finish) if later else finish
 
 
 class Gather:
@@ -1072,18 +1076,29 @@
         sorted_ref[2 * number + 1 : 2 * number + 2] = upto.astype(jnp.int32)
 
 
+def pack_halves(read, target_ref, place, local, low, half):
+    for number in range(local // 2):
+        first = read(2 * number).astype(F32)
+        second = swap_halves(read(2 * number + 1).astype(F32))
+        kept = (first, second) if half == 0 else (second, first)
+        target_ref[place + (number,)] = jnp.where(low, *kept).astype(BF16)
+
+
 class Outward:
-    def __init__(self, source, target, send_sem, recv_sem, local_sem):
-        self.target, self.recv_sem, self.send_sem = target, recv_sem, send_sem
+    def __init__(self, source, far_source, target, packed, send_sem, recv_sem, local_sem):
+        self.target, self.packed = target, packed
+        self.recv_sem, self.send_sem = recv_sem, send_sem
         self.core, self.plane, self.spot = place_here()
         self.sends, self.keeps = [], []
         for side in (3, 1, 2, 0):
+            goal = flip(self.spot, side)
             for other in (self.core, 1 - self.core):
-                goal = flip(self.spot, side)
+                near = other is self.core
                 for piece in range(PIECES):
-                    start = source.at[other, goal, piece]
-                    stop = target.at[2 * self.core + piece, self.spot]
-                    if side == 0 and other is self.core:
+                    start = (source if near else far_source).at[goal, piece]
+                    place = (2 * self.core + piece, self.spot)
+                    stop = (target if near else packed).at[place]
+                    if side == 0 and near:
                         copy = pltpu.make_async_copy(start, stop, local_sem.at[piece])
                         self.keeps.append(copy)
                     else:
@@ -1091,27 +1106,37 @@
                             start,
                             stop,
                             send_sem.at[len(self.sends)],
-                            recv_sem.at[2 * self.core + piece, self.spot],
+                            recv_sem.at[place],
                             (other, rank_of(self.plane, goal)),
                         )
                         self.sends.append(copy)
                     copy.start()
 
     def arrive(self, side):
+        goal = flip(self.spot, side)
         for other in (self.core, 1 - self.core):
-            if side == 0 and other is self.core:
+            near = other is self.core
+            if side == 0 and near:
                 for copy in self.keeps:
                     copy.wait()
                 continue
             for piece in range(PIECES):
-                place = (2 * other + piece, flip(self.spot, side))
+                place = (2 * other + piece, goal)
+                landed = (self.target if near else self.packed).at[place]
                 remote(
-                    self.target.at[place],
-                    self.target.at[place],
+                    landed,
+                    landed,
                     self.send_sem.at[0],
                     self.recv_sem.at[place],
                     (self.core, rank_of(self.plane, self.spot)),
                 ).wait_recv()
+                if not near:
+                    for number in range(self.packed.shape[2]):
+                        tile = self.packed[place + (number,)]
+                        self.target[place + (2 * number,)] = tile
+                        self.target[place + (2 * number + 1,)] = swap_halves(
+                            tile.astype(F32)
+                        ).astype(BF16)
 
     def finish(self):
         for copy in self.sends:
@@ -1172,16 +1197,18 @@
 
 
 def plane_attend_back_kernel(*refs):
-    table_ref, sorted_ref, qk_ref, shared_ref, grad_source_ref, lse_ref, hidden_ref = refs[:7]
-    sources, half_up_ref, half_down_ref, refs = refs[7:10], refs[10], refs[11], refs[12:]
+    table_ref, sorted_ref, qk_ref, shared_ref, near_grad_ref, far_grad_ref, lse_ref, hidden_ref = (
+        refs[:8]
+    )
+    sources, half_up_ref, half_down_ref, refs = refs[8:11], refs[11], refs[12], refs[13:]
     sources = list(sources[:2]) + [sources[2].at[number] for number in range(LATE)]
     back_ref, hidden_out_ref, t_out_ref, t_up_ref, t_down_ref = refs[:5]
     count = 2 + LATE
     refs = refs[5:]
     buffers, mines, refs = refs[: 3 * count], refs[3 * count : 4 * count], refs[4 * count :]
     part_out_ref, part_up_ref, part_down_ref, far_out_ref, far_up_ref, far_down_ref = refs[:6]
-    grad_ref, out_ref, sums_ref, shares_ref, walked_ref, sibling_ref = refs[6:12]
-    scores_refs, refs = refs[12:16], refs[16:]
+    grad_ref, packed_ref, out_ref, sums_ref, shares_ref, walked_ref, sibling_ref = refs[6:13]
+    scores_refs, refs = refs[13:17], refs[17:]
     reduce_send, reduce_recv, far_send, far_recv, load_sem = refs[:5]
     grad_sems, back_sems, move_sems, sibling_sems = refs[5:8], refs[8:11], refs[11:14], refs[14:16]
 
@@ -1193,7 +1220,7 @@
     masks = [half_mask(True), half_mask(False)]
 
     greet(both_partners(core, plane, spot))
-    grads = Outward(grad_source_ref, grad_ref, *grad_sems)
+    grads = Outward(near_grad_ref, far_grad_ref, grad_ref, packed_ref, *grad_sems)
     reduces = [
         SpotReduce(
             source,
@@ -1502,7 +1529,7 @@
 
 
 def plane_attention_back(
-    table, sorted_table, qk, shared, grad_source, lse, hidden, sources, half_up, half_down
+    table, sorted_table, qk, shared, near, far, lse, hidden, sources, half_up, half_down
 ):
     local = qk.shape[3]
     blocks = PLANES * SPOTS * local
@@ -1545,6 +1572,7 @@
             whole(),
             whole(),
             whole(ANY),
+            whole(ANY),
             whole(),
             whole(ANY),
         ]
@@ -1555,6 +1583,7 @@
         + parts
         + [
             VMEM((PLANES, SPOTS) + tile, BF16),
+            VMEM((PLANES, SPOTS, local // 2, BLOCK, LANES), BF16),
             VMEM((PLANES, SPOTS, 3) + tile, BF16),
             VMEM((2, blocks, BLOCK, LANES), F32),
             VMEM((2, blocks * RANDOM, BLOCK, LANES), F32),
@@ -1585,7 +1614,7 @@
             vmem_limit_bytes=62 * 1024 * 1024, collective_id=5, has_side_effects=True
         ),
         name="plane_attention_back",
-    )(table, sorted_table, qk, shared, grad_source, lse, hidden, *sources, half_up, half_down)
+    )(table, sorted_table, qk, shared, near, far, lse, hidden, *sources, half_up, half_down)
 
 
 class PlaneGather:
@@ -1876,6 +1905,7 @@
     w_up_in_ref,
     w_down_in_ref,
     back_ref,
+    far_back_ref,
     x_ref,
     dys_ref,
     w_down_ref,
@@ -1905,6 +1935,7 @@
     qk_ref,
     shared_ref,
     out_ref,
+    pack_ref,
     p_ref,
     q_ref,
     picks_ref,
@@ -1914,7 +1945,7 @@
     plane_sems, cross_sems = sems[3:7], sems[7:11]
     x_sems, dy_sems = sems[11:14], sems[14:17]
     qkv_send, qkv_recv, qkv_local, shared_send, shared_recv = sems[17:22]
-    back_sems, local_sem = sems[22:25], sems[25]
+    back_send, back_recv, back_local, far_send, far_recv, local_sem = sems[22:28]
     core, plane, spot = place_here()
     micro, rows, _ = x_in_ref.shape
     tokens = PIECES * rows
@@ -2188,17 +2219,33 @@
             )
             copy.start()
             shared.append(copy)
-    cross.hop(2)
     finish_dy = to_planes(dy_ref, dys_ref, *dy_sems)
     lax.fori_loop(half_way, PLANES * SPOTS, head_a, 0)
     dense(0, p_ref, ends)
     spread.forward()
-    back = Inward(out_ref, back_ref, *back_sems)
-    everything = slice(0, local)
-    for side, other, goal, stays in inward_targets(core, spot):
-        if other is not core:
-            for piece in range(PIECES):
-                back.send(other, goal, stays, piece, 0, everything)
+    backs, stay = [], []
+    for side in (3, 1, 2, 0):
+        goal = flip(spot, side)
+        for piece in range(PIECES):
+            pack_halves(
+                lambda number, piece=piece, goal=goal: out_ref[
+                    2 * (1 - core) + piece, goal, number
+                ],
+                pack_ref,
+                (piece, goal),
+                local,
+                low,
+                1,
+            )
+            copy = remote(
+                pack_ref.at[piece, goal],
+                far_back_ref.at[spot, piece],
+                far_send.at[piece, side],
+                far_recv.at[spot, piece],
+                (1 - core, rank_of(plane, goal)),
+            )
+            copy.start()
+            backs.append(copy)
     for side in range(SPOTS):
         for piece in range(PIECES):
             target = shared_ref.at[2 * (1 - core) + piece, flip(spot, side)]
@@ -2209,6 +2256,7 @@
                 shared_recv.at[2 * (1 - core) + piece, flip(spot, side)],
                 (core, rank_of(plane, spot)),
             ).wait_recv()
+    cross.hop(2)
     keep_qk = pltpu.make_async_copy(qk_ref, qk_hbm, local_sem.at[3])
     keep_qk.start()
     keep_shared = pltpu.make_async_copy(shared_ref, shared_hbm, local_sem.at[6])
@@ -2216,11 +2264,24 @@
     lax.fori_loop(0, half_way, head_b, 0)
     dense(1, q_ref, (core * (blocks - 1),))
     spread.corner()
+    for side in (3, 1, 2, 0):
+        goal = flip(spot, side)
+        for piece in range(PIECES):
+            source, target = out_ref.at[2 * core + piece, goal], back_ref.at[spot, piece]
+            if side == 0:
+                copy = pltpu.make_async_copy(source, target, back_local.at[piece])
+                stay.append(copy)
+            else:
+                copy = remote(
+                    source,
+                    target,
+                    back_send.at[piece, side],
+                    back_recv.at[spot, piece],
+                    (core, rank_of(plane, goal)),
+                )
+                backs.append(copy)
+            copy.start()
     cross.hop(3)
-    for side, other, goal, stays in inward_targets(core, spot):
-        if other is core:
-            for piece in range(PIECES):
-                back.send(other, goal, stays, piece, 0, everything)
     spread.finish()
     settle(
         g_ou_ref,
@@ -2237,7 +2298,19 @@
         copy.wait_send()
     for copy in shared:
         copy.wait_send()
-    back.finish(((everything,), (everything,)))
+    for side in range(SPOTS):
+        goal = flip(spot, side)
+        for piece in range(PIECES):
+            here = (core, rank_of(plane, spot))
+            if side > 0:
+                target = back_ref.at[goal, piece]
+                remote(target, target, back_send.at[0, 0], back_recv.at[goal, piece], here).wait_recv()
+            target = far_back_ref.at[goal, piece]
+            remote(target, target, far_send.at[0, 0], far_recv.at[goal, piece], here).wait_recv()
+    for copy in backs:
+        copy.wait_send()
+    for copy in stay:
+        copy.wait()
     for copy in (keep_x, keep_w, keep_qk, keep_shared, keep_out, keep_up):
         copy.wait()
 
@@ -2257,7 +2330,8 @@
     return pl.pallas_call(
         front_kernel,
         out_shape=(
-            struct((2, SPOTS, PIECES) + tile, BF16),
+            struct((SPOTS, PIECES) + tile, BF16),
+            struct((SPOTS, PIECES, local // 2, BLOCK, LANES), BF16),
             struct(x.shape, BF16),
             struct(dy.shape, BF16),
             struct(grid + w_down.shape, BF16),
@@ -2283,7 +2357,7 @@
             whole(),
             whole(ANY),
         ],
-        out_specs=(whole(ANY),) * 9 + (whole(),) * 6,
+        out_specs=(whole(ANY),) * 10 + (whole(),) * 6,
         scratch_shapes=[
             VMEM((2 * shard, 3 * D // 2), BF16),
             VMEM(ou, BF16),
@@ -2300,6 +2374,7 @@
             VMEM((PLANES, SPOTS, 2) + tile, BF16),
             VMEM((PLANES, SPOTS) + tile, BF16),
             VMEM((PLANES, SPOTS) + tile, BF16),
+            VMEM((PIECES, SPOTS, local // 2, BLOCK, LANES), BF16),
             VMEM((spans, 2 * BLOCK, SPAN * BLOCK), F32),
             VMEM((spans, BLOCK, SPAN * BLOCK), F32),
             pltpu.SMEM((PLANES, SPOTS) + tab.shape, jnp.int32),
@@ -2322,9 +2397,11 @@
             dma((2, PIECES)),
             dma((2 * SPOTS,)),
             dma((PLANES, SPOTS)),
-            dma((14,)),
-            dma((2, SPOTS, PIECES, 1)),
-            dma((1, PIECES)),
+            dma((PIECES, SPOTS)),
+            dma((SPOTS, PIECES)),
+            dma((PIECES,)),
+            dma((PIECES, SPOTS)),
+            dma((SPOTS, PIECES)),
             dma((7,)),
         ],
         compiler_params=pltpu.CompilerParams(
@@ -2388,7 +2465,7 @@
                     target[inner] = total.astype(BF16)
                 return carry
 
-            lax.fori_loop(0, 3, slab, 0)
+            lax.fori_loop(0, 3, slab, 0, unroll=True)
             return
         count = self.near.shape[0]
 
@@ -2403,7 +2480,7 @@
                 target[first, plane] = total.astype(BF16)
             return carry
 
-        lax.fori_loop(0, count * PLANES, block, 0)
+        lax.fori_loop(0, count * PLANES, block, 0, unroll=4)
 
     def corners(self):
         self.copy(0).wait_recv()
@@ -2473,6 +2550,7 @@
 
 def plane_middle_kernel(
     mixed_in_ref,
+    far_in_ref,
     x_ref,
     dy_ref,
     vec_ref,
@@ -2482,6 +2560,7 @@
     w_down_ref,
     hidden_ref,
     send_ref,
+    far_ref,
     dres_ref,
     g_out_ref,
     half_up_ref,
@@ -2537,17 +2616,25 @@
                 (core, rank_of(plane, flip(spot, 2))),
             ]
         )
+        def received(spot, piece):
+            own = mixed_in_ref[spot, piece].astype(F32)
+            halves = far_in_ref[spot, piece].astype(F32)
+            parts = []
+            for number in range(rows // BLOCK // 2):
+                part = halves[number * BLOCK : (number + 1) * BLOCK]
+                parts += [part, swap_halves(part)]
+            other = jnp.concatenate(parts, axis=0)
+            return (jnp.where(core == 0, own, other), jnp.where(core == 0, other, own)), own
+
         for piece in range(pieces):
             span = slice(piece * rows, (piece + 1) * rows)
             for spot in (0, 2):
-                first = [mixed_in_ref[side, spot, piece].astype(F32) for side in range(2)]
-                last = [mixed_in_ref[side, spot + 1, piece].astype(F32) for side in range(2)]
-                own_first = jnp.where(core == 0, first[0], first[1])
-                own_last = jnp.where(core == 0, last[0], last[1])
+                first, own_first = received(spot, piece)
+                last_two, own_last = received(spot + 1, piece)
                 tiles = (
                     jnp.where(low, swap_halves(first[0]), first[1]),
-                    jnp.where(low, own_first, last[0]),
-                    swap_halves(jnp.where(low, own_last, last[1])),
+                    jnp.where(low, own_first, last_two[0]),
+                    swap_halves(jnp.where(low, own_last, last_two[1])),
                 )
                 for number, tile in enumerate(tiles):
                     spread = 3 * (spot // 2) + number
@@ -2643,6 +2730,19 @@
         g_small_ref[3:4] = jnp.sum(branch.astype(F32), axis=0, keepdims=True)
         by_owner(g_out_ref, dot_lt(mixed_ref[...], branch))
         dmixed = dot_rt(branch, w_out_ref[...])
+        core = lax.axis_index("gx")
+
+        def hand_over(spot, piece, first, second):
+            send_ref[spot, piece] = jnp.where(core == 0, first, second).astype(BF16)
+            far = jnp.where(core == 0, second, first)
+            for number in range(rows // BLOCK // 2):
+                start = 2 * number * BLOCK
+                far_ref[spot, piece, number * BLOCK : (number + 1) * BLOCK] = jnp.where(
+                    low_lanes(BLOCK),
+                    swap_halves(far[start + BLOCK : start + 2 * BLOCK]),
+                    far[start : start + BLOCK],
+                ).astype(BF16)
+
         for piece in range(pieces):
             span = slice(piece * rows, (piece + 1) * rows)
             for spot in (0, 2):
@@ -2651,10 +2751,15 @@
                     for number in range(3 * (spot // 2), 3 * (spot // 2) + 3)
                 ]
                 flipped = [swap_halves(tile) for tile in tiles]
-                send_ref[0, spot, piece] = jnp.where(low, tiles[1], flipped[0]).astype(BF16)
-                send_ref[1, spot, piece] = jnp.where(low, tiles[1], tiles[0]).astype(BF16)
-                send_ref[0, spot + 1, piece] = jnp.where(low, flipped[2], tiles[1]).astype(BF16)
-                send_ref[1, spot + 1, piece] = flipped[2].astype(BF16)
+                hand_over(
+                    spot,
+                    piece,
+                    jnp.where(low, tiles[1], flipped[0]),
+                    jnp.where(low, tiles[1], tiles[0]),
+                )
+                hand_over(
+                    spot + 1, piece, jnp.where(low, flipped[2], tiles[1]), flipped[2]
+                )
         for number, pair in enumerate(stages):
             if PER_STAGE * (number + 1) - 1 + WAITS[2] >= last:
                 pair[0].close(half_up_ref.at[PER_STAGE * number : PER_STAGE * (number + 1)])
@@ -2663,7 +2768,7 @@
         keep_down.wait()
 
 
-def plane_middle(mixed_in, x, dy, vec, w_out, up_shift, w_up, w_down):
+def plane_middle(mixed_in, far_in, x, dy, vec, w_out, up_shift, w_up, w_down):
     pieces, rows, _ = x.shape
     tokens = pieces * rows
     shard = D // RANKS
@@ -2686,6 +2791,7 @@
         out_shape=(
             jax.ShapeDtypeStruct(x.shape, BF16),
             jax.ShapeDtypeStruct(mixed_in.shape, BF16),
+            jax.ShapeDtypeStruct(far_in.shape, BF16),
             jax.ShapeDtypeStruct((tokens, D), F32),
             jax.ShapeDtypeStruct((RANKS, 2 * shard, D // 2), BF16),
             jax.ShapeDtypeStruct(half_up, BF16),
@@ -2697,6 +2803,7 @@
         ),
         in_specs=[
             fixed(mixed_in.shape),
+            fixed(far_in.shape),
             fixed(x.shape),
             fixed((tokens, D)),
             fixed(vec.shape),
@@ -2708,6 +2815,7 @@
         out_specs=(
             fixed(x.shape),
             fixed(mixed_in.shape),
+            fixed(far_in.shape),
             fixed((tokens, D)),
             fixed((RANKS, 2 * shard, D // 2)),
             fixed(half_up),
@@ -2737,7 +2845,7 @@
             vmem_limit_bytes=60 * 1024 * 1024, collective_id=3, has_side_effects=True
         ),
         name="plane_middle",
-    )(mixed_in, x, dy, vec, w_out, up_shift, w_up, w_down)
+    )(mixed_in, far_in, x, dy, vec, w_out, up_shift, w_up, w_down)
 
 
 class Reduce:
@@ -2786,7 +2894,7 @@
             ).astype(self.total.dtype)
             return carry
 
-        lax.fori_loop(0, PLANES, add, 0)
+        lax.fori_loop(0, PLANES, add, 0, unroll=True)
 
     def corners(self):
         self.take(0, 3)
@@ -2844,7 +2952,7 @@
             ).astype(self.total.dtype)
             return carry
 
-        lax.fori_loop(0, PLANES, add, 0)
+        lax.fori_loop(0, PLANES, add, 0, unroll=True)
         self.far_copies = []
         for bits in range(1, PLANES):
             plane = flip(self.plane, bits)
@@ -2963,6 +3071,7 @@
             chunk * CHUNK + side * LANES : chunk * CHUNK + (side + 1) * LANES,
         ] = value.astype(BF16)
 
+    start_piece, finish_grad = from_planes(gradient_ref, grad_ref, *move_sems, later=True)
     for piece in range(pieces):
         seconds = []
         for goal in range(SPOTS):
@@ -2980,24 +3089,26 @@
                 piece,
                 jnp.where(low, seconds[2 * number], swap_halves(seconds[2 * number + 1])),
             )
-
-    load_w.wait()
-    for chunk in range(HALF_TILES):
-        columns = slice(chunk * CHUNK, (chunk + 1) * CHUNK)
-        share = dot_rt(packed_ref[:, columns], w_ref[:, columns])
-        if chunk == 0:
-            dnormed_ref[...] = share
-        else:
-            dnormed_ref[...] += share
-    normal, inverse = norm_parts(x_ref[...].reshape(tokens, D).astype(F32))
-    dnormed = dnormed_ref[...]
-    load_dres.wait()
-    gradient = dres_ref[...] + norm_pull(dnormed, normal, inverse, vec_ref[0:1])
-    gradient_ref[...] = gradient.astype(BF16).reshape(x_ref.shape)
-    finish_grad = from_planes(gradient_ref, grad_ref, *move_sems)
-
-    rows_ref[0:1] = jnp.sum(dnormed * normal, axis=0, keepdims=True)
-    rows_ref[1:2] = jnp.sum(dnormed, axis=0, keepdims=True)
+        if piece == 0:
+            load_w.wait()
+            load_dres.wait()
+        span = slice(piece * rows, (piece + 1) * rows)
+        share = dot_rt(packed_ref[span], w_ref[...])
+        dnormed_ref[span] = share
+        normal, inverse = norm_parts(x_ref[piece].astype(F32))
+        gradient = dres_ref[span] + norm_pull(share, normal, inverse, vec_ref[0:1])
+        gradient_ref[piece] = gradient.astype(BF16)
+        start_piece(piece)
+        sums = [
+            jnp.sum(share * normal, axis=0, keepdims=True),
+            jnp.sum(share, axis=0, keepdims=True),
+        ]
+        for number in range(2):
+            if piece == 0:
+                rows_ref[number : number + 1] = sums[number]
+            else:
+                rows_ref[number : number + 1] += sums[number]
+
     rows_ref[2:6] = g_mid_ref[...]
     rows_ref[6:8] = jnp.zeros((2, D), F32)
     tiles_ref[...] = jnp.zeros_like(tiles_ref)
@@ -3298,6 +3409,7 @@
     )
     (
         mixed,
+        far_mixed,
         x,
         dy,
         w_down_all,
@@ -3313,10 +3425,12 @@
         table,
         sorted_table,
     ) = front(hidden_in, cotangent, vec, tab, w_qkv, w_out, w_up, w_down)
-    mixed = mixed.reshape(2, SPOTS, PIECES, rows, LANES)
+    mixed = mixed.reshape(SPOTS, PIECES, rows, LANES)
+    far_mixed = far_mixed.reshape(SPOTS, PIECES, rows // 2, LANES)
     (
         hidden,
-        grad_send,
+        near_grad,
+        far_grad,
         dres,
         g_out,
         half_up,
@@ -3327,6 +3441,7 @@
         g_mid,
     ) = plane_middle(
         mixed,
+        far_mixed,
         x,
         dy.reshape(micro * rows, D),
         vectors,
@@ -3341,7 +3456,8 @@
         sorted_table,
         qk,
         shared,
-        grad_send.reshape(2, SPOTS, PIECES, local, BLOCK, LANES),
+        near_grad.reshape(SPOTS, PIECES, local, BLOCK, LANES),
+        far_grad.reshape(SPOTS, PIECES, local // 2, BLOCK, LANES),
         lse,
         hidden,
         [
@@ -3382,7 +3498,7 @@
 def shards(*arrays):
     micro, rows, _ = arrays[0].shape
     fits = lax.axis_size("gx") == 2 and lax.axis_size("gy") == PLANES * SPOTS
-    fits = fits and micro == 2 and rows % BLOCK == 0
+    fits = fits and micro == 2 and rows == 4 * BLOCK
     return (plane_shards if fits else general_shards)(*arrays)
 
 

time: 299 us -> 288 us (0.963)
  Pallas kernels: 295 us -> 284 us
    pallas_call x1, Pallas kernels: 83.5 us -> 78.5 us  [plane_attention_back(): pl.pallas_call(plane_attend_back_kernel, out_shape=(jax.ShapeDtypeStruct(...]
where the time goes in v10:
time: 288 us
  Pallas kernels  284 us (99%)
    pallas_call x1, Pallas kernels, front(): pl.pallas_call(front_kernel, out_shape=(struct((SPOTS, PIECES) + tile, BF...  118 us
    pallas_call x1, Pallas kernels, plane_attention_back(): pl.pallas_call(plane_attend_back_kernel, out_shape=(jax.ShapeDtypeStruct(...  78.5 us
    pallas_call x1, Pallas kernels, plane_middle(): pl.pallas_call(plane_middle_kernel, grid=(steps,), out_shape=(jax.ShapeDt...  43.6 us
    pallas_call x1, Pallas kernels, finish_layer(): pl.pallas_call(finish_kernel, out_shape=(jax.ShapeDtypeStruct(x.shape, BF...  39.4 us

profile of v10, /device:TPU:0, one launch (start us, length us, event | category | flops | bytes accessed | tf_op | source)
XLA Modules:
  0.0 288.2 jit_solution(18063032109427811320)
XLA Ops:
  0.6 0.8 copy.32
  1.4 0.1 reshape.84
  1.5 0.6 pad.49.tab_ref
  2.1 1.4 pad_add_fusion.vec_ref
  3.5 118.4 %front.1 = (bf16[4,2,4,64,128]{4,3,2,1,0:T(8,128)(2,1)}, bf16[4,2,2,64,128]{4,3,2,1,0:T(8,128)(2,1)}, bf16[2,256,768]{2,1,0:T(8,128)(2,1)}, bf16[2,256,768]{2,1,...) custom-call(bf16[2,256,768]{2,1,0:T(8,128)(2,1)} %x_in_ref.1, ...), custom_call_target="tpu_custom_call" | custom-call | tf_op jit(solution)/shard_map/front/pallas_call | solution.py:2330
  121.9 43.6 %plane_middle.1 = (bf16[2,256,768]{2,1,0:T(8,128)(2,1)}, bf16[4,2,256,128]{3,2,1,0:T(8,128)(2,1)}, bf16[4,2,128,128]{3,2,1,0:T(8,128)(2,1)}, f32[512,768]{1,0:T(...) custom-call(bf16[4,2,256,128]{3,2,1,0:T(8,128)(2,1)} %bitcast.30, ...), custom_call_target="tpu_custom_call" | custom-call | tf_op jit(solution)/shard_map/plane_middle/pallas_call | solution.py:2788
  165.5 78.5 %plane_attention_back.1 = (bf16[2,4,2,3,4,64,128]{6,5,4,3,2,1,0:T(8,128)(2,1)}, bf16[2,256,768]{2,1,0:T(8,128)(2,1)}, f32[48,384]{1,0:T(8,128)}, f32[12,48,128]{2,1,0:T(8,128)}, f32[96,768]{1,0:T(8,128)}) custom-call(s32[1,256]{1,0:T(1,128)} %get-tuple-element.66.refs_0_, s32[4,256]{1,0:T(4,128)} %get-tuple-element.67.refs_1_, ...), custom_call_target="tpu_custom_call" | custom-call | tf_op jit(solution)/shard_map/plane_attention_back/pallas_call | solution.py:1560
  244.0 39.4 %finish_layer.1 = (bf16[2,256,768]{2,1,0:T(8,128)(2,1)}, f32[48,1152]{1,0:T(8,128)}, f32[8,768]{1,0:T(8,128)}, f32[24,256]{1,0:T(8,128)}) custom-call(bf16[2,4,2,3,256,128]{5,4,3,2,1,0:T(8,128)(2,1)} %bitcast.27, bf16[512,768]{1,0:T(8,128)(2,1)} %get-tuple-element.90.normed_ref, bf16[2,256,768]{2,1,0:T(8,128)(2,1)} %get-tuple-element.72.x_ref, ...), custom_call_target="tpu_custom_call" | custom-call | tf_op jit(solution)/shard_map/finish_layer/pallas_call | solution.py:3185
  283.4 4.6 %present.1 = (bf16[2,256,768]{2,1,0:T(8,128)(2,1)}, f32[2,256,768]{2,1,0:T(8,128)}, f32[24,2304]{1,0:T(8,128)}, f32[24,768]{1,0:T(8,128)}, f32[24,3072]{1,0:T(8,...) custom-call(bf16[2,256,768]{2,1,0:T(8,128)(2,1)} %get-tuple-element., ...), custom_call_target="tpu_custom_call" | custom-call | tf_op jit(solution)/shard_map/present/pallas_call | solution.py:3341

commit v11 on v10

--- a/solution.py
+++ b/solution.py
@@ -1202,15 +1202,16 @@
     )
     sources, half_up_ref, half_down_ref, refs = refs[8:11], refs[11], refs[12], refs[13:]
     sources = list(sources[:2]) + [sources[2].at[number] for number in range(LATE)]
-    back_ref, hidden_out_ref, t_out_ref, t_up_ref, t_down_ref = refs[:5]
+    back_ref, far_back_ref, hidden_out_ref, t_out_ref, t_up_ref, t_down_ref = refs[:6]
     count = 2 + LATE
-    refs = refs[5:]
+    refs = refs[6:]
     buffers, mines, refs = refs[: 3 * count], refs[3 * count : 4 * count], refs[4 * count :]
     part_out_ref, part_up_ref, part_down_ref, far_out_ref, far_up_ref, far_down_ref = refs[:6]
     grad_ref, packed_ref, out_ref, sums_ref, shares_ref, walked_ref, sibling_ref = refs[6:13]
-    scores_refs, refs = refs[13:17], refs[17:]
+    pack_ref, scores_refs, refs = refs[13], refs[14:18], refs[18:]
     reduce_send, reduce_recv, far_send, far_recv, load_sem = refs[:5]
     grad_sems, back_sems, move_sems, sibling_sems = refs[5:8], refs[8:11], refs[11:14], refs[14:16]
+    pack_send, pack_recv = refs[16:18]
 
     local = qk_ref.shape[3]
     groups = PLANES * SPOTS
@@ -1434,7 +1435,8 @@
 
     back = Inward(out_ref, back_ref, *back_sems)
     own_parts = (slice(0, 1), slice(1, 2), slice(2, 3))
-    far_parts = (slice(0, 2),)
+    far_parts = (slice(0, 1),)
+    packs = []
 
     for side in range(SPOTS):
         grads.arrive(side)
@@ -1444,10 +1446,9 @@
                 copy.wait()
             for one in reduces:
                 one.corners()
-        if side == 2:
+        if side == 1:
             for one in reduces:
                 one.sides()
-    dense(0, scores_refs[0], scores_refs[1], ends)
     reduces[0].close(part_out_ref)
     reduces[1].close(part_up_ref.at[ready : PER_STAGE * STAGES])
     for number in range(LATE):
@@ -1467,6 +1468,7 @@
             far_down(bits, part_down_ref.at[goal]).start()
 
         fars.append(far_down(bits, part_down_ref.at[goal]))
+    dense(0, scores_refs[0], scores_refs[1], ends)
     walk(0, blocks * RANDOM)
     for side, other, goal, stays in inward_targets(core, spot):
         for piece in range(PIECES):
@@ -1475,6 +1477,25 @@
                 back.send(other, goal, stays, piece, 0, own_parts[0])
             else:
                 back.send(other, goal, stays, piece, 0, far_parts[0])
+                pack_halves(
+                    lambda number, other=other, goal=goal, piece=piece: out_ref[
+                        2 * other + piece, goal, QUERIES, number
+                    ],
+                    pack_ref,
+                    (piece, goal),
+                    local,
+                    low,
+                    0,
+                )
+                copy = remote(
+                    pack_ref.at[piece, goal],
+                    far_back_ref.at[spot, piece],
+                    pack_send.at[piece, side],
+                    pack_recv.at[spot, piece],
+                    (other, rank_of(plane, goal)),
+                )
+                copy.start()
+                packs.append(copy)
     lax.fori_loop(0, groups // 2, head_b, 0)
     dense(1, scores_refs[2], scores_refs[3], (core * (blocks - 1),))
     for side, other, goal, stays in inward_targets(core, spot):
@@ -1526,6 +1547,18 @@
     grads.finish()
     across.wait_send()
     back.finish((own_parts, far_parts))
+    for copy in packs:
+        copy.wait_send()
+    for goal in range(SPOTS):
+        for piece in range(PIECES):
+            target = far_back_ref.at[goal, piece]
+            remote(
+                target,
+                target,
+                pack_send.at[0, 0],
+                pack_recv.at[goal, piece],
+                (core, rank_of(plane, spot)),
+            ).wait_recv()
 
 
 def plane_attention_back(
@@ -1561,6 +1594,7 @@
         plane_attend_back_kernel,
         out_shape=(
             jax.ShapeDtypeStruct((2, SPOTS, PIECES, 3) + tile, BF16),
+            jax.ShapeDtypeStruct((SPOTS, PIECES, local // 2, BLOCK, LANES), BF16),
             jax.ShapeDtypeStruct(hidden.shape, BF16),
             jax.ShapeDtypeStruct(out_tail, F32),
             jax.ShapeDtypeStruct((up_count,) + up_tail, F32),
@@ -1577,7 +1611,7 @@
             whole(ANY),
         ]
         + [whole(ANY)] * 5,
-        out_specs=(whole(ANY), whole(ANY)) + (whole(),) * 3,
+        out_specs=(whole(ANY),) * 3 + (whole(),) * 3,
         scratch_shapes=buffers
         + mines
         + parts
@@ -1589,6 +1623,7 @@
             VMEM((2, blocks * RANDOM, BLOCK, LANES), F32),
             VMEM((2, blocks * RANDOM, BLOCK, LANES), BF16),
             VMEM((PIECES, SPOTS) + tile, BF16),
+            VMEM((PIECES, SPOTS, local // 2, BLOCK, LANES), BF16),
             wide,
             wide,
             thin,
@@ -1609,6 +1644,8 @@
             dma((2,)),
             dma,
             dma,
+            dma((PIECES, SPOTS)),
+            dma((SPOTS, PIECES)),
         ],
         compiler_params=pltpu.CompilerParams(
             vmem_limit_bytes=62 * 1024 * 1024, collective_id=5, has_side_effects=True
@@ -3034,6 +3071,7 @@
 
 def finish_kernel(
     recv_ref,
+    far_ref,
     normed_ref,
     x_ref,
     dres_hbm,
@@ -3075,9 +3113,15 @@
     for piece in range(pieces):
         seconds = []
         for goal in range(SPOTS):
-            first = recv_ref[0, goal, piece, QUERIES].astype(F32)
-            second = recv_ref[1, goal, piece, QUERIES].astype(F32)
-            put(goal, piece, jnp.where(low, first, jnp.where(core == 0, first, second)))
+            own = recv_ref[core, goal, piece, QUERIES].astype(F32)
+            halves = far_ref[goal, piece].astype(F32)
+            parts = []
+            for number in range(rows // BLOCK // 2):
+                part = halves[number * BLOCK : (number + 1) * BLOCK]
+                parts += [part, swap_halves(part)]
+            other = jnp.concatenate(parts, axis=0)
+            second = jnp.where(core == 0, other, own)
+            put(goal, piece, jnp.where(low & (core == 1), other, own))
             seconds.append(second)
             base = D // LANES + 3 * goal
             put(base, piece, recv_ref[0, goal, piece, KEYS_A])
@@ -3171,7 +3215,7 @@
     finish_grad()
 
 
-def finish_layer(recv, normed, x, dres, vec, w, g_mid, g_up_bias):
+def finish_layer(recv, far, normed, x, dres, vec, w, g_mid, g_up_bias):
     pieces, rows, _ = x.shape
     tokens = pieces * rows
     shard = D // RANKS
@@ -3191,6 +3235,7 @@
             jax.ShapeDtypeStruct((tiles, CHUNK), F32),
         ),
         in_specs=[
+            whole(),
             whole(),
             whole(),
             whole(),
@@ -3227,7 +3272,7 @@
             vmem_limit_bytes=60 * 1024 * 1024, collective_id=2, has_side_effects=True
         ),
         name="finish_layer",
-    )(recv, normed, x, dres, vec, w, g_mid, g_up_bias)
+    )(recv, far, normed, x, dres, vec, w, g_mid, g_up_bias)
 
 
 def present_kernel(
@@ -3451,7 +3496,7 @@
         w_down_all.reshape(2, FF // 2, D),
     )
     grid = (2, PLANES, SPOTS)
-    dqkv, hidden_out, t_out, t_up, t_down = plane_attention_back(
+    dqkv, far_dq, hidden_out, t_out, t_up, t_down = plane_attention_back(
         table,
         sorted_table,
         qk,
@@ -3469,8 +3514,9 @@
         half_down,
     )
     dqkv = dqkv.reshape(2, SPOTS, PIECES, 3, rows, LANES)
+    far_dq = far_dq.reshape(SPOTS, PIECES, rows // 2, LANES)
     grad_hidden, t_qkv, sum_rows, sum_tiles = finish_layer(
-        dqkv, normed, x, dres, vectors, w_qkv_all, g_mid, g_up_bias
+        dqkv, far_dq, normed, x, dres, vectors, w_qkv_all, g_mid, g_up_bias
     )
 
     results = present(hidden_out, grad_hidden, t_qkv, t_out, t_up, t_down, sum_rows, sum_tiles)

time: 288 us -> 284 us (0.986)
  Pallas kernels: 284 us -> 280 us
    pallas_call x1, Pallas kernels: 78.5 us -> 74.4 us  [plane_attention_back(): pl.pallas_call(plane_attend_back_kernel, out_shape=(jax.ShapeDtypeStruct(...]
where the time goes in v11:
time: 284 us
  Pallas kernels  280 us (99%)
    pallas_call x1, Pallas kernels, front(): pl.pallas_call(front_kernel, out_shape=(struct((SPOTS, PIECES) + tile, BF...  118 us
    pallas_call x1, Pallas kernels, plane_attention_back(): pl.pallas_call(plane_attend_back_kernel, out_shape=(jax.ShapeDtypeStruct(...  74.4 us
    pallas_call x1, Pallas kernels, plane_middle(): pl.pallas_call(plane_middle_kernel, grid=(steps,), out_shape=(jax.ShapeDt...  43.6 us
    pallas_call x1, Pallas kernels, finish_layer(): pl.pallas_call(finish_kernel, out_shape=(jax.ShapeDtypeStruct(x.shape, BF...  39.1 us

profile of v11, /device:TPU:0, one launch (start us, length us, event | category | flops | bytes accessed | tf_op | source)
XLA Modules:
  0.0 283.9 jit_solution(16438770323120058247)
XLA Ops:
  0.6 0.8 copy.32
  1.4 0.1 reshape.87
  1.5 0.6 pad.49.tab_ref
  2.1 1.4 pad_add_fusion.vec_ref
  3.5 118.4 %front.1 = (bf16[4,2,4,64,128]{4,3,2,1,0:T(8,128)(2,1)}, bf16[4,2,2,64,128]{4,3,2,1,0:T(8,128)(2,1)}, bf16[2,256,768]{2,1,0:T(8,128)(2,1)}, bf16[2,256,768]{2,1,...) custom-call(bf16[2,256,768]{2,1,0:T(8,128)(2,1)} %x_in_ref.1, ...), custom_call_target="tpu_custom_call" | custom-call | tf_op jit(solution)/shard_map/front/pallas_call | solution.py:2367
  121.9 43.6 %plane_middle.1 = (bf16[2,256,768]{2,1,0:T(8,128)(2,1)}, bf16[4,2,256,128]{3,2,1,0:T(8,128)(2,1)}, bf16[4,2,128,128]{3,2,1,0:T(8,128)(2,1)}, f32[512,768]{1,0:T(...) custom-call(bf16[4,2,256,128]{3,2,1,0:T(8,128)(2,1)} %bitcast.31, ...), custom_call_target="tpu_custom_call" | custom-call | tf_op jit(solution)/shard_map/plane_middle/pallas_call | solution.py:2825
  165.5 74.4 %plane_attention_back.1 = (bf16[2,4,2,3,4,64,128]{6,5,4,3,2,1,0:T(8,128)(2,1)}, bf16[4,2,2,64,128]{4,3,2,1,0:T(8,128)(2,1)}, bf16[2,256,768]{2,1,0:T(8,128)(2,1)...) custom-call(s32[1,256]{1,0:T(1,128)} %get-tuple-element.67.refs_0_, ...), custom_call_target="tpu_custom_call" | custom-call | tf_op jit(solution)/shard_map/plane_attention_back/pallas_call | solution.py:1593
  239.9 39.1 %finish_layer.1 = (bf16[2,256,768]{2,1,0:T(8,128)(2,1)}, f32[48,1152]{1,0:T(8,128)}, f32[8,768]{1,0:T(8,128)}, f32[24,256]{1,0:T(8,128)}) custom-call(bf16[2,4,2,3,256,128]{5,4,3,2,1,0:T(8,128)(2,1)} %bitcast.28, bf16[4,2,128,128]{3,2,1,0:T(8,128)(2,1)} %bitcast.33, bf16[512,768]{1,0:T(8,128)(2,1)} %get-tuple-element.92.normed_ref, ...), custom_call_target="tpu_custom_call" | custom-call | tf_op jit(solution)/shard_map/finish_layer/pallas_call | solution.py:3229
  279.0 4.6 %present.1 = (bf16[2,256,768]{2,1,0:T(8,128)(2,1)}, f32[2,256,768]{2,1,0:T(8,128)}, f32[24,2304]{1,0:T(8,128)}, f32[24,768]{1,0:T(8,128)}, f32[24,3072]{1,0:T(8,...) custom-call(bf16[2,256,768]{2,1,0:T(8,128)(2,1)} %get-tuple-element., ...), custom_call_target="tpu_custom_call" | custom-call | tf_op jit(solution)/shard_map/present/pallas_call | solution.py:3386

commit v12 on v11

--- a/solution.py
+++ b/solution.py
@@ -2057,8 +2057,8 @@
     keep_w = pltpu.make_async_copy(w_qkv_ref, w_qkv_hbm, local_sem.at[2])
     keep_w.start()
 
+    spread = PlaneGather(s_ou_ref, g_ou_ref, *plane_sems)
     finish_x()
-    spread = PlaneGather(s_ou_ref, g_ou_ref, *plane_sems)
     keep_x = pltpu.make_async_copy(xs_ref, x_ref, local_sem.at[0])
     keep_x.start()
     normal, _ = norm_parts(xs_ref[...].reshape(tokens, D).astype(F32))

time: 284 us -> 283 us (level)
  no operation moved by 1% of the time
where the time goes in v12:
time: 283 us; the launch traced here: 282 us
  Pallas kernels  279 us (99%)
    pallas_call x1, Pallas kernels, front(): pl.pallas_call(front_kernel, out_shape=(struct((SPOTS, PIECES) + tile, BF...  116 us
    pallas_call x1, Pallas kernels, plane_attention_back(): pl.pallas_call(plane_attend_back_kernel, out_shape=(jax.ShapeDtypeStruct(...  74.1 us
    pallas_call x1, Pallas kernels, plane_middle(): pl.pallas_call(plane_middle_kernel, grid=(steps,), out_shape=(jax.ShapeDt...  44.5 us
    pallas_call x1, Pallas kernels, finish_layer(): pl.pallas_call(finish_kernel, out_shape=(jax.ShapeDtypeStruct(x.shape, BF...  39.4 us

profile of v12, /device:TPU:0, one launch (start us, length us, event | category | flops | bytes accessed | tf_op | source)
XLA Modules:
  0.0 282.3 jit_solution(4242860718848867595)
XLA Ops:
  0.6 0.8 copy.32
  1.4 0.1 reshape.87
  1.5 0.6 pad.49.tab_ref
  2.1 1.4 pad_add_fusion.vec_ref
  3.5 115.9 %front.1 = (bf16[4,2,4,64,128]{4,3,2,1,0:T(8,128)(2,1)}, bf16[4,2,2,64,128]{4,3,2,1,0:T(8,128)(2,1)}, bf16[2,256,768]{2,1,0:T(8,128)(2,1)}, bf16[2,256,768]{2,1,...) custom-call(bf16[2,256,768]{2,1,0:T(8,128)(2,1)} %x_in_ref.1, ...), custom_call_target="tpu_custom_call" | custom-call | tf_op jit(solution)/shard_map/front/pallas_call | solution.py:2367
  119.4 44.5 %plane_middle.1 = (bf16[2,256,768]{2,1,0:T(8,128)(2,1)}, bf16[4,2,256,128]{3,2,1,0:T(8,128)(2,1)}, bf16[4,2,128,128]{3,2,1,0:T(8,128)(2,1)}, f32[512,768]{1,0:T(...) custom-call(bf16[4,2,256,128]{3,2,1,0:T(8,128)(2,1)} %bitcast.31, ...), custom_call_target="tpu_custom_call" | custom-call | tf_op jit(solution)/shard_map/plane_middle/pallas_call | solution.py:2825
  163.9 74.1 %plane_attention_back.1 = (bf16[2,4,2,3,4,64,128]{6,5,4,3,2,1,0:T(8,128)(2,1)}, bf16[4,2,2,64,128]{4,3,2,1,0:T(8,128)(2,1)}, bf16[2,256,768]{2,1,0:T(8,128)(2,1)...) custom-call(s32[1,256]{1,0:T(1,128)} %get-tuple-element.67.refs_0_, ...), custom_call_target="tpu_custom_call" | custom-call | tf_op jit(solution)/shard_map/plane_attention_back/pallas_call | solution.py:1593
  238.1 39.4 %finish_layer.1 = (bf16[2,256,768]{2,1,0:T(8,128)(2,1)}, f32[48,1152]{1,0:T(8,128)}, f32[8,768]{1,0:T(8,128)}, f32[24,256]{1,0:T(8,128)}) custom-call(bf16[2,4,2,3,256,128]{5,4,3,2,1,0:T(8,128)(2,1)} %bitcast.28, bf16[4,2,128,128]{3,2,1,0:T(8,128)(2,1)} %bitcast.33, bf16[512,768]{1,0:T(8,128)(2,1)} %get-tuple-element.92.normed_ref, ...), custom_call_target="tpu_custom_call" | custom-call | tf_op jit(solution)/shard_map/finish_layer/pallas_call | solution.py:3229
  277.5 4.6 %present.1 = (bf16[2,256,768]{2,1,0:T(8,128)(2,1)}, f32[2,256,768]{2,1,0:T(8,128)}, f32[24,2304]{1,0:T(8,128)}, f32[24,768]{1,0:T(8,128)}, f32[24,3072]{1,0:T(8,...) custom-call(bf16[2,256,768]{2,1,0:T(8,128)(2,1)} %get-tuple-element., ...), custom_call_target="tpu_custom_call" | custom-call | tf_op jit(solution)/shard_map/present/pallas_call | solution.py:3386

commit v13 on v12

--- a/solution.py
+++ b/solution.py
@@ -2052,12 +2052,12 @@
         bias_ref[:, start : start + LANES] = pair_of_blocks(
             bias_tile, order[2 * tile], order[2 * tile + 1]
         )
+    spread = PlaneGather(s_ou_ref, g_ou_ref, *plane_sems)
     gathers[2].finish()
     settle(g_qkv_ref, [(tile, w_qkv_ref, alternate(tile)) for tile in range(HALF_TILES)])
     keep_w = pltpu.make_async_copy(w_qkv_ref, w_qkv_hbm, local_sem.at[2])
     keep_w.start()
 
-    spread = PlaneGather(s_ou_ref, g_ou_ref, *plane_sems)
     finish_x()
     keep_x = pltpu.make_async_copy(xs_ref, x_ref, local_sem.at[0])
     keep_x.start()

time: 283 us -> 283 us (level)
  no operation moved by 1% of the time
where the time goes in v13:
time: 283 us
  Pallas kernels  279 us (99%)
    pallas_call x1, Pallas kernels, front(): pl.pallas_call(front_kernel, out_shape=(struct((SPOTS, PIECES) + tile, BF...  116 us
    pallas_call x1, Pallas kernels, plane_attention_back(): pl.pallas_call(plane_attend_back_kernel, out_shape=(jax.ShapeDtypeStruct(...  75.2 us
    pallas_call x1, Pallas kernels, plane_middle(): pl.pallas_call(plane_middle_kernel, grid=(steps,), out_shape=(jax.ShapeDt...  44.9 us
    pallas_call x1, Pallas kernels, finish_layer(): pl.pallas_call(finish_kernel, out_shape=(jax.ShapeDtypeStruct(x.shape, BF...  39.1 us

profile of v13, /device:TPU:0, one launch (start us, length us, event | category | flops | bytes accessed | tf_op | source)
XLA Modules:
  0.0 283.2 jit_solution(12002223744306097408)
XLA Ops:
  0.6 0.8 copy.32
  1.4 0.1 reshape.87
  1.5 0.6 pad.49.tab_ref
  2.1 1.4 pad_add_fusion.vec_ref
  3.5 115.5 %front.1 = (bf16[4,2,4,64,128]{4,3,2,1,0:T(8,128)(2,1)}, bf16[4,2,2,64,128]{4,3,2,1,0:T(8,128)(2,1)}, bf16[2,256,768]{2,1,0:T(8,128)(2,1)}, bf16[2,256,768]{2,1,...) custom-call(bf16[2,256,768]{2,1,0:T(8,128)(2,1)} %x_in_ref.1, ...), custom_call_target="tpu_custom_call" | custom-call | tf_op jit(solution)/shard_map/front/pallas_call | solution.py:2367
  119.1 44.9 %plane_middle.1 = (bf16[2,256,768]{2,1,0:T(8,128)(2,1)}, bf16[4,2,256,128]{3,2,1,0:T(8,128)(2,1)}, bf16[4,2,128,128]{3,2,1,0:T(8,128)(2,1)}, f32[512,768]{1,0:T(...) custom-call(bf16[4,2,256,128]{3,2,1,0:T(8,128)(2,1)} %bitcast.31, ...), custom_call_target="tpu_custom_call" | custom-call | tf_op jit(solution)/shard_map/plane_middle/pallas_call | solution.py:2825
  164.0 75.2 %plane_attention_back.1 = (bf16[2,4,2,3,4,64,128]{6,5,4,3,2,1,0:T(8,128)(2,1)}, bf16[4,2,2,64,128]{4,3,2,1,0:T(8,128)(2,1)}, bf16[2,256,768]{2,1,0:T(8,128)(2,1)...) custom-call(s32[1,256]{1,0:T(1,128)} %get-tuple-element.67.refs_0_, ...), custom_call_target="tpu_custom_call" | custom-call | tf_op jit(solution)/shard_map/plane_attention_back/pallas_call | solution.py:1593
  239.2 39.1 %finish_layer.1 = (bf16[2,256,768]{2,1,0:T(8,128)(2,1)}, f32[48,1152]{1,0:T(8,128)}, f32[8,768]{1,0:T(8,128)}, f32[24,256]{1,0:T(8,128)}) custom-call(bf16[2,4,2,3,256,128]{5,4,3,2,1,0:T(8,128)(2,1)} %bitcast.28, bf16[4,2,128,128]{3,2,1,0:T(8,128)(2,1)} %bitcast.33, bf16[512,768]{1,0:T(8,128)(2,1)} %get-tuple-element.92.normed_ref, ...), custom_call_target="tpu_custom_call" | custom-call | tf_op jit(solution)/shard_map/finish_layer/pallas_call | solution.py:3229
  278.3 4.6 %present.1 = (bf16[2,256,768]{2,1,0:T(8,128)(2,1)}, f32[2,256,768]{2,1,0:T(8,128)}, f32[24,2304]{1,0:T(8,128)}, f32[24,768]{1,0:T(8,128)}, f32[24,3072]{1,0:T(8,...) custom-call(bf16[2,256,768]{2,1,0:T(8,128)(2,1)} %get-tuple-element., ...), custom_call_target="tpu_custom_call" | custom-call | tf_op jit(solution)/shard_map/present/pallas_call | solution.py:3386
